TPU v7x, 32 devices: a whole 2x2x4 slice. The times are simulated.
32 devices in a mesh: seq: 8 (over z, x), batch: 4 (over y, core).
Axes of the slice: x: 2, y: 2, z: 4, core: 2. Of those that a mesh axis runs over, the one named last changes fastest.
Arguments:
- inputs: bfloat16 [1024, 4, 2048], P('seq', 'batch'), may hold values from -6 to 6
- positions: int32 [1024, 4], P('seq', 'batch'), may hold values from 0 to 1023, as said below
- ln1_gain: float32 [2048], replicated, may hold values from 0.5 to 1.5
- ln1_bias: float32 [2048], replicated, may hold values from -1.75 to 1.75
- w_qkv: bfloat16 [2048, 6144], P('seq'), may hold values from -0.125 to 0.125
- qkv_bias: float32 [6144], replicated, may hold values from -1.75 to 1.75
- w_out: bfloat16 [2048, 2048], P('seq'), may hold values from -0.75 to 0.75
- ln2_gain: float32 [2048], replicated, may hold values from 0.5 to 1.5
- ln2_bias: float32 [2048], replicated, may hold values from -1.75 to 1.75
- w_gate: bfloat16 [2048, 5632], P(None, 'seq'), may hold values from -0.125 to 0.125
- w_up: bfloat16 [2048, 5632], P(None, 'seq'), may hold values from -0.125 to 0.125
- w_down: bfloat16 [5632, 2048], P('seq'), may hold values from -0.078125 to 0.078125
- cotangent: bfloat16 [1024, 4, 2048], P('seq', 'batch'), may hold values from -6 to 6
Outputs:
- output: bfloat16 [1024, 4, 2048], P('seq', 'batch')
- grad_input: float32 [1024, 4, 2048], P('seq', 'batch')
- grad_ln1_gain: float32 [2048], replicated
- grad_ln1_bias: float32 [2048], replicated
- grad_w_qkv: float32 [2048, 6144], P('seq')
- grad_qkv_bias: float32 [6144], replicated
- grad_w_out: float32 [2048, 2048], P('seq')
- grad_ln2_gain: float32 [2048], replicated
- grad_ln2_bias: float32 [2048], replicated
- grad_w_gate: float32 [2048, 5632], P(None, 'seq')
- grad_w_up: float32 [2048, 5632], P(None, 'seq')
- grad_w_down: float32 [5632, 2048], P('seq')
Inputs may be any that keep to these rules, and one draw needn't show every extreme that they name: positions[t, r] is 0 where a document of packed row r begins (always at t = 0) and positions[t - 1, r] + 1 elsewhere.
All inputs are finite; a program needn't handle non-finite values.
Results may differ from a plain program's by a relative error of at most 0.019.
Values may be sent and summed in bfloat16 or wider, within the bound.
No kernel may reach another device: no remote copies, remote signals or barrier semaphores. Data moves between devices by JAX's collectives and lax.ppermute only.
A program may use at most 512 MiB of HBM per device.

v0:
```python
import jax
import jax.numpy as jnp
from jax import lax
from jax.sharding import PartitionSpec as P

HEADS = 32
KEY_BLOCK = 512


eps_norm = 1e-05
theta_base = 10000.0
masked_score = -1e30


def norm_parts(values, gain_vector, shift_vector):
    mean_value = jnp.mean(values, axis=-1, keepdims=True)
    centred = values - mean_value
    inverse = lax.rsqrt(jnp.mean(centred * centred, axis=-1, keepdims=True) + eps_norm)
    unit_value = centred * inverse
    return (unit_value * gain_vector + shift_vector, unit_value, inverse)


def norm_back(gradient, unit_value, inverse, gain_vector):
    scaled = gradient * gain_vector
    back_value = inverse * (
        scaled
        - jnp.mean(scaled, axis=-1, keepdims=True)
        - unit_value * jnp.mean(scaled * unit_value, axis=-1, keepdims=True)
    )
    return (back_value, jnp.sum(gradient * unit_value, axis=(0, 1)), jnp.sum(gradient, axis=(0, 1)))


def rotary_tables(positions, rotated):
    half_dim = rotated // 2
    frequency = theta_base ** (-(jnp.arange(half_dim, dtype=jnp.float32) * 2.0 / rotated))
    angles = positions.astype(jnp.float32)[:, :, None] * frequency
    return (jnp.cos(angles)[:, :, None, :], jnp.sin(angles)[:, :, None, :])


def rotate(values, cosine_table, sine_table, rotated):
    half_dim = rotated // 2
    first_half = values[..., :half_dim]
    second_half = values[..., half_dim:rotated]
    return jnp.concatenate(
        [
            first_half * cosine_table - second_half * sine_table,
            second_half * cosine_table + first_half * sine_table,
            values[..., rotated:],
        ],
        axis=-1,
    )


def contract_rows(left_side, right_side):
    return lax.dot_general(
        left_side, right_side, (((0,), (0,)), ((), ())), preferred_element_type=jnp.float32
    )


def contract_last(left_side, right_side):
    return lax.dot_general(
        left_side, right_side, (((1,), (1,)), ((), ())), preferred_element_type=jnp.float32
    )


def on_device(
    inputs,
    positions,
    ln1_gain,
    ln1_bias,
    w_qkv,
    qkv_bias,
    w_out,
    ln2_gain,
    ln2_bias,
    w_gate,
    w_up,
    w_down,
    cotangent,
):
    shard_len, row_count, model_width = inputs.shape
    head_dim = model_width // HEADS
    rotated = head_dim // 4
    score_scale = head_dim ** (-0.5)
    length = shard_len * lax.axis_size("seq")
    blocks = length // KEY_BLOCK
    ffn_local = w_gate.shape[1]
    local_tokens = shard_len * row_count
    full_qkv, full_out = (
        lax.all_gather(w_qkv, "seq", axis=0, tiled=True),
        lax.all_gather(w_out, "seq", axis=0, tiled=True),
    )
    resid = inputs.astype(jnp.float32)
    normed, unit_one, inverse_one = norm_parts(resid, ln1_gain, ln1_bias)
    normed_low = normed.astype(jnp.bfloat16).reshape(local_tokens, model_width)
    joined = jnp.dot(normed_low, full_qkv, preferred_element_type=jnp.float32) + qkv_bias
    joined = joined.reshape(shard_len, row_count, 3, HEADS, head_dim)
    cosine_table, sine_table = rotary_tables(positions, rotated)
    queries = rotate(joined[:, :, 0], cosine_table, sine_table, rotated).astype(jnp.bfloat16)
    key_flat = (
        rotate(joined[:, :, 1], cosine_table, sine_table, rotated)
        .astype(jnp.bfloat16)
        .reshape(shard_len, row_count, model_width)
    )
    value_flat = joined[:, :, 2].astype(jnp.bfloat16).reshape(shard_len, row_count, model_width)
    keys_all, values_all = (
        lax.all_gather(key_flat, "seq", axis=0, tiled=True),
        lax.all_gather(value_flat, "seq", axis=0, tiled=True),
    )
    query_place = lax.axis_index("seq") * shard_len + jnp.arange(shard_len, dtype=jnp.int32)
    doc_first = (query_place[:, None] - positions).T

    def slice_block(whole_rows, block_index):
        return lax.dynamic_slice_in_dim(whole_rows, block_index * KEY_BLOCK, KEY_BLOCK, 0).reshape(
            KEY_BLOCK, row_count, HEADS, head_dim
        )

    def block_scores(key_block, block_index):
        scores = (
            jnp.einsum("qrhd,krhd->rhqk", queries, key_block, preferred_element_type=jnp.float32)
            * score_scale
        )
        key_pos = block_index * KEY_BLOCK + jnp.arange(KEY_BLOCK, dtype=jnp.int32)
        visible = (key_pos[None, None, :] <= query_place[None, :, None]) & (
            key_pos[None, None, :] >= doc_first[:, :, None]
        )
        return jnp.where(visible[:, None], scores, masked_score)

    def max_step(carried, block_index):
        running_max, denominator = carried
        scores = block_scores(slice_block(keys_all, block_index), block_index)
        new_max = jnp.maximum(running_max, jnp.max(scores, axis=-1))
        denominator = denominator * jnp.exp(running_max - new_max) + jnp.sum(
            jnp.exp(scores - new_max[..., None]), axis=-1
        )
        return ((new_max, denominator), None)

    start_max = jnp.full((row_count, HEADS, shard_len), masked_score, jnp.float32)
    start_total = jnp.zeros((row_count, HEADS, shard_len), jnp.float32)
    (final_max, final_total), unused = lax.scan(
        max_step, (start_max, start_total), jnp.arange(blocks)
    )
    log_total = final_max + jnp.log(final_total)

    def value_step(accum, block_index):
        scores = block_scores(slice_block(keys_all, block_index), block_index)
        probability = jnp.exp(scores - log_total[..., None]).astype(jnp.bfloat16)
        value_block = slice_block(values_all, block_index)
        return (
            accum
            + jnp.einsum(
                "rhqk,krhd->qrhd", probability, value_block, preferred_element_type=jnp.float32
            ),
            None,
        )

    attended, unused = lax.scan(
        value_step,
        jnp.zeros((shard_len, row_count, HEADS, head_dim), jnp.float32),
        jnp.arange(blocks),
    )
    mixed_low = attended.reshape(local_tokens, model_width).astype(jnp.bfloat16)
    branch = jnp.dot(mixed_low, full_out, preferred_element_type=jnp.float32)
    middle = resid + branch.reshape(shard_len, row_count, model_width)
    normed_two, unit_two, inverse_two = norm_parts(middle, ln2_gain, ln2_bias)
    tokens_all = lax.all_gather(normed_two.astype(jnp.bfloat16), "seq", axis=0, tiled=True)
    flat_tokens = tokens_all.reshape(length * row_count, model_width)
    gate_proj = jnp.dot(flat_tokens, w_gate, preferred_element_type=jnp.float32)
    up_proj = jnp.dot(flat_tokens, w_up, preferred_element_type=jnp.float32)
    hidden_low = (
        (jax.nn.silu(gate_proj) * up_proj)
        .astype(jnp.bfloat16)
        .reshape(length, row_count, ffn_local)
    )
    row_total = lax.axis_size("seq") * shard_len
    hidden_rows = hidden_low.reshape(row_total * row_count, ffn_local)
    mlp_part = lax.psum_scatter(
        jnp.dot(hidden_rows, w_down, preferred_element_type=jnp.float32)
        .reshape(row_total, row_count, model_width)
        .astype(jnp.bfloat16),
        "seq",
        scatter_dimension=0,
        tiled=True,
    ).astype(jnp.float32)
    output = (middle + mlp_part).astype(jnp.bfloat16)
    piece_rows = lax.all_gather(cotangent, "seq", axis=0, tiled=True)
    piece_count = piece_rows.shape[0]
    flat_piece = piece_rows.reshape(piece_count * row_count, model_width)
    act_rows = hidden_low.reshape(piece_count * row_count, ffn_local)
    act_piece = contract_last(flat_piece, w_down).reshape(piece_count, row_count, ffn_local)
    grad_hidden = act_piece
    grad_down = contract_rows(act_rows, flat_piece)
    grad_hidden = grad_hidden.reshape(length * row_count, ffn_local)
    sigmoid_gate = jax.nn.sigmoid(gate_proj)
    grad_gate_low = (
        grad_hidden * up_proj * sigmoid_gate * (1.0 + gate_proj * (1.0 - sigmoid_gate))
    ).astype(jnp.bfloat16)
    grad_up_low = (grad_hidden * gate_proj * sigmoid_gate).astype(jnp.bfloat16)
    grad_gate = contract_rows(flat_tokens, grad_gate_low)
    grad_up = contract_rows(flat_tokens, grad_up_low)
    gate_grid = grad_gate_low.reshape(length, row_count, ffn_local)
    up_grid = grad_up_low.reshape(length, row_count, ffn_local)
    row_total = lax.axis_size("seq") * shard_len
    gate_piece = gate_grid.reshape(row_total * row_count, ffn_local)
    up_piece = up_grid.reshape(row_total * row_count, ffn_local)
    summed = contract_last(gate_piece, w_gate) + contract_last(up_piece, w_up)
    grad_normed_two = lax.psum_scatter(
        summed.reshape(row_total, row_count, model_width).astype(jnp.bfloat16),
        "seq",
        scatter_dimension=0,
        tiled=True,
    ).astype(jnp.float32)
    back_two, gain_two_grad, bias_two_grad = norm_back(
        grad_normed_two, unit_two, inverse_two, ln2_gain
    )
    grad_middle = cotangent.astype(jnp.float32) + back_two
    grad_branch = grad_middle.reshape(local_tokens, model_width).astype(jnp.bfloat16)
    grad_mixed_flat = contract_last(grad_branch, full_out).astype(jnp.bfloat16)
    grad_mixed = grad_mixed_flat.reshape(shard_len, row_count, HEADS, head_dim)
    delta = jnp.einsum("qrhd,qrhd->rhq", grad_mixed.astype(jnp.float32), attended)

    def grad_step(accum, block_index):
        key_block = slice_block(keys_all, block_index)
        value_block = slice_block(values_all, block_index)
        scores = block_scores(key_block, block_index)
        probability = jnp.exp(scores - log_total[..., None])
        grad_prob = jnp.einsum(
            "qrhd,krhd->rhqk", grad_mixed, value_block, preferred_element_type=jnp.float32
        )
        grad_score = (probability * (grad_prob - delta[..., None])).astype(jnp.bfloat16)
        accum = accum + jnp.einsum(
            "rhqk,krhd->qrhd", grad_score, key_block, preferred_element_type=jnp.float32
        )
        grad_key = (
            jnp.einsum("rhqk,qrhd->krhd", grad_score, queries, preferred_element_type=jnp.float32)
            * score_scale
        )
        grad_value = jnp.einsum(
            "rhqk,qrhd->krhd",
            probability.astype(jnp.bfloat16),
            grad_mixed,
            preferred_element_type=jnp.float32,
        )
        joined_grads = jnp.concatenate(
            [
                grad_key.reshape(KEY_BLOCK, row_count, model_width),
                grad_value.reshape(KEY_BLOCK, row_count, model_width),
            ],
            axis=-1,
        )
        return (accum, joined_grads)

    query_accum, block_grads = lax.scan(
        grad_step,
        jnp.zeros((shard_len, row_count, HEADS, head_dim), jnp.float32),
        jnp.arange(blocks),
    )
    kv_partial = block_grads.reshape(length, row_count, 2 * model_width)
    kv_grads = lax.psum_scatter(
        kv_partial.astype(jnp.bfloat16), "seq", scatter_dimension=0, tiled=True
    ).astype(jnp.float32)
    grad_query = rotate(query_accum * score_scale, cosine_table, -sine_table, rotated).reshape(
        shard_len, row_count, model_width
    )
    grad_key_local = rotate(
        kv_grads[..., :model_width].reshape(shard_len, row_count, HEADS, head_dim),
        cosine_table,
        -sine_table,
        rotated,
    ).reshape(shard_len, row_count, model_width)
    grad_value_local = kv_grads[..., model_width:]
    grad_joined = (
        jnp.concatenate([grad_query, grad_key_local, grad_value_local], axis=-1)
        .astype(jnp.bfloat16)
        .reshape(local_tokens, 3 * model_width)
    )
    bias_grad = jnp.sum(grad_joined.astype(jnp.float32), axis=0)
    grad_normed = contract_last(grad_joined, full_qkv).reshape(shard_len, row_count, model_width)
    back_one, gain_one_grad, bias_one_grad = norm_back(grad_normed, unit_one, inverse_one, ln1_gain)
    grad_input = grad_middle + back_one
    weight_part = lax.psum_scatter(
        jnp.concatenate(
            [contract_rows(normed_low, grad_joined), contract_rows(mixed_low, grad_branch)], axis=1
        ).astype(jnp.bfloat16),
        "seq",
        scatter_dimension=0,
        tiled=True,
    ).astype(jnp.float32)
    grad_qkv_w, grad_out_w, grad_gate_w, grad_up_w, grad_down_w = (
        lax.psum(weight_part[:, : 3 * model_width].astype(jnp.bfloat16), "batch").astype(
            jnp.float32
        ),
        lax.psum(weight_part[:, 3 * model_width :].astype(jnp.bfloat16), "batch").astype(
            jnp.float32
        ),
        lax.psum(grad_gate.astype(jnp.bfloat16), "batch").astype(jnp.float32),
        lax.psum(grad_up.astype(jnp.bfloat16), "batch").astype(jnp.float32),
        lax.psum(grad_down.astype(jnp.bfloat16), "batch").astype(jnp.float32),
    )
    gain_one_sum, bias_one_sum, qkv_bias_sum, gain_two_sum, bias_two_sum = lax.psum(
        (gain_one_grad, bias_one_grad, bias_grad, gain_two_grad, bias_two_grad), ("seq", "batch")
    )
    return (
        output,
        grad_input,
        gain_one_sum,
        bias_one_sum,
        grad_qkv_w,
        qkv_bias_sum,
        grad_out_w,
        gain_two_sum,
        bias_two_sum,
        grad_gate_w,
        grad_up_w,
        grad_down_w,
    )


def solution(mesh):
    in_specs = (
        P("seq", "batch", None),
        P("seq", "batch"),
        P(),
        P(),
        P("seq", None),
        P(),
        P("seq", None),
        P(),
        P(),
        P(None, "seq"),
        P(None, "seq"),
        P("seq", None),
        P("seq", "batch", None),
    )
    out_specs = (
        P("seq", "batch", None),
        P("seq", "batch", None),
        P(),
        P(),
        P("seq", None),
        P(),
        P("seq", None),
        P(),
        P(),
        P(None, "seq"),
        P(None, "seq"),
        P("seq", None),
    )
    return jax.shard_map(
        on_device, mesh=mesh, in_specs=in_specs, out_specs=out_specs, check_vma=False
    )
```

profile of v0, /device:TPU:0, one launch (start us, length us, event | category | flops | bytes accessed | tf_op | source)
XLA Modules:
  0.0 2195.7 jit_solution(8508946311102204932)
XLA Ops:
  9.6 483.2 %all-gather.7.cloned.1.call-done = bf16[2048,6144]{1,0:T(8,128)(2,1)} async-done(((bf16[256,6144]{1,0:T(8,128)(2,1)}), bf16[2048,6144]{1,0:T(8,128)(2,1)}) %all-gather.7.cloned.1.call-update) | async-done | bytes 25165840 | tf_op jit(solution)/shard_map/all_gather | solution.py:90
  492.8 13.4 convolution_add_fusion
  506.2 3.5 copy.39
  514.0 2.1 slice.127
  519.1 2.5 copy.40
  521.6 67.5 %all-gather.11.cloned.1.call-done = bf16[1024,1,2048]{0,2,1:T(8,128)(2,1)} async-done(((bf16[128,1,2048]{0,2,1:T(8,128)(2,1)}), bf16[1024,1,2048]{0,2,1:T(8,128)(2,1)}) %all-gather.11.cloned.1.call-update) | async-done | bytes 4194320 | tf_op jit(solution)/shard_map/all_gather | solution.py:107
  589.1 13.8 while.37
  592.2 1.9 fusion.155
  599.2 1.9 fusion.155
  602.9 62.4 %all-gather.9.cloned.1.call-done = bf16[1024,1,2048]{0,2,1:T(8,128)(2,1)} async-done(((bf16[128,1,2048]{0,2,1:T(8,128)(2,1)}), bf16[1024,1,2048]{0,2,1:T(8,128)(2,1)}) %all-gather.9.cloned.1.call-update) | async-done | bytes 4194320 | tf_op jit(solution)/shard_map/all_gather | solution.py:108
  665.4 27.1 %while.38 = (s32[]{:T(128)}, f32[128,1,32,64]{0,3,2,1:T(8,128)}, s32[2]{0:T(128)S(1)}, bf16[1024,1,2048]{0,2,1:T(8,128)(2,1)}, s32[128,1]{0,1:T(1,128)S(1)}, /*i...) while((s32[]{:T(128)}, f32[128,1,32,64]{0,3,2,1:T(8,128)}, ...), condition=%wide.region_7.8_spmd.clone, body=%wide.region_6.7_spmd.clone.sunk | while | flops 545981056 | bytes 15357653 | solution.py:157
  666.8 4.5 constant_dynamic-slice_fusion.9
  671.3 7.8 fusion.160
  680.4 4.5 constant_dynamic-slice_fusion.9
  684.9 7.5 fusion.160
  692.5 2.1 convert_element_type.165
  694.6 95.9 %all-gather.13.cloned.1.call-done = bf16[2048,2048]{1,0:T(8,128)(2,1)} async-done(((bf16[256,2048]{1,0:T(8,128)(2,1)}), bf16[2048,2048]{1,0:T(8,128)(2,1)}) %all-gather.13.cloned.1.call-update) | async-done | bytes 8388624 | tf_op jit(solution)/shard_map/all_gather | solution.py:91
  790.5 5.0 fusion.105
  798.6 70.6 %all-gather.15.cloned.1.call-done = bf16[1024,1,2048]{2,0,1:T(8,128)(2,1)} async-done(((bf16[128,1,2048]{2,0,1:T(8,128)(2,1)}), bf16[1024,1,2048]{2,0,1:T(8,128)(2,1)}) %all-gather.15.cloned.1.call-update) | async-done | bytes 4194320 | tf_op jit(solution)/shard_map/all_gather | solution.py:166
  869.2 8.0 fusion.57
  877.2 4.8 fusion.59
  882.0 60.9 %all-gather.17.cloned.1.call-done = bf16[1024,1,2048]{2,0,1:T(8,128)(2,1)} async-done(((bf16[128,1,2048]{2,0,1:T(8,128)(2,1)}), bf16[1024,1,2048]{2,0,1:T(8,128)(2,1)}) %all-gather.17.cloned.1.call-update) | async-done | bytes 4194320 | tf_op jit(solution)/shard_map/all_gather | solution.py:186
  942.9 8.4 multiply_convert_fusion
  951.4 3.5 fusion.106
  955.0 5.3 fusion.48
  960.4 6.4 convert_bitcast_fusion
  967.0 79.6 %reduce-scatter.7.cloned.1.call-done = bf16[128,1,2048]{2,0,1:T(8,128)(2,1)} async-done(((bf16[1024,1,2048]{2,0,1:T(8,128)(2,1)}), bf16[128,1,2048]{2,0,1:T(8,128)(2,1)}) %reduce-scatter.7.cloned.1.call-update) | async-done | bytes 524304 | tf_op jit(solution)/shard_map/reduce_scatter | solution.py:207
  1046.6 2.1 fusion.92
  1048.7 90.4 %reduce-scatter.5.cloned.1.call-done = bf16[128,1,2048]{2,0,1:T(8,128)(2,1)} async-done(((bf16[1024,1,2048]{2,0,1:T(8,128)(2,1)}), bf16[128,1,2048]{2,0,1:T(8,128)(2,1)}) %reduce-scatter.5.cloned.1.call-update) | async-done | bytes 524304 | tf_op jit(solution)/shard_map/reduce_scatter | solution.py:177
  1139.1 2.6 fusion.90
  1141.7 7.5 convolution_convert_fusion.2
  1150.7 54.6 %while.39 = (s32[]{:T(128)}, f32[128,1,32,64]{0,3,2,1:T(8,128)}, bf16[2,512,1,4096]{3,1,0,2:T(8,128)(2,1)}, s32[2]{0:T(128)S(1)}, bf16[1024,1,2048]{0,2,1:T(8,12...) while((s32[]{:T(128)}, f32[128,1,32,64]{0,3,2,1:T(8,128)}, ...), condition=%wide.region_15.16_spmd.clone, body=%wide.region_14.15_spmd.clone.sunk | while | flops 1374356096 | bytes 94623528 | solution.py:253
  1152.1 2.5 constant_dynamic-slice_fusion.10
  1155.9 3.4 fusion.172
  1159.4 2.4 fusion.174
  1164.8 2.3 maximum_bitcast_fusion.2
  1167.0 6.3 copy.84
  1173.4 4.7 constant_dynamic-update-slice_fusion.2
  1179.5 2.5 constant_dynamic-slice_fusion.10
  1183.3 3.4 fusion.172
  1186.7 2.4 fusion.174
  1192.1 2.3 maximum_bitcast_fusion.2
  1194.4 6.3 copy.84
  1200.7 4.6 constant_dynamic-update-slice_fusion.2
  1208.4 5.9 convolution_convert_fusion.1
  1214.3 140.0 %reduce-scatter.9.cloned.1.call-done = bf16[128,1,4096]{2,0,1:T(8,128)(2,1)} async-done(((bf16[1024,1,4096]{2,0,1:T(8,128)(2,1)}), bf16[128,1,4096]{2,0,1:T(8,128)(2,1)}) %reduce-scatter.9.cloned.1.call-update) | async-done | bytes 1048592 | tf_op jit(solution)/shard_map/reduce_scatter | solution.py:259
  1359.2 1.9 pad_maximum_fusion.5
  1362.3 12.0 convolution_convert_fusion
  1374.3 22.8 %pad_maximum_fusion = bf16[2048,8192]{1,0:T(8,128)(2,1)} fusion(bf16[2048,2048]{1,0:T(8,128)(2,1)} %convolution_convert_fusion.1, bf16[2048,6144]{1,0:T(8,128)(2,1)} %convolution_convert_fusion), kind=kLoop, calls=%fused_computation.63 | loop fusion | flops 67108864 | bytes 67108864 | tf_op jit(solution)/shard_map/concatenate | solution.py:282
  1397.5 7.5 fusion.67
  1405.0 4.5 fusion.61
  1409.5 4.5 fusion.64
  1413.9 525.1 %reduce-scatter.11.cloned.1.call-done = bf16[256,8192]{1,0:T(8,128)(2,1)} async-done(((bf16[2048,8192]{1,0:T(8,128)(2,1)}), bf16[256,8192]{1,0:T(8,128)(2,1)}) %reduce-scatter.11.cloned.1.call-update) | async-done | bytes 4194320 | tf_op jit(solution)/shard_map/reduce_scatter | solution.py:281
  1939.0 2.3 slice.103
  1941.3 3.9 slice.102
  1945.2 15.1 fusion.86
  1963.5 2.0 copy.48
  1965.8 41.3 %all-reduce = (f32[2048]{0:T(1024)}, f32[2048]{0:T(1024)}, f32[6144]{0:T(1024)}, f32[2048]{0:T(1024)}, f32[2048]{0:T(1024)}) all-reduce(f32[2048]{0:T(1024)S(1)} %get-tuple-element.331, f32[2048]{0:T(1024)S(1)} %get-tuple-element.333, f32[6144]{0:T(1024)S(1)} %convert_reduce_fusion, ...), channel_id=1, replica_groups=mesh['seq'=8,'batch'=4] {'seq','batch'}, use_global_device_ids=true, to_apply=%region_20.21 | all-reduce | flops 14336 | bytes 114688 | tf_op jit(solution)/shard_map/psum | solution.py:300
  2007.1 165.2 %all-reduce.4.cloned.1.call-done = (bf16[256,6144]{1,0:T(8,128)(2,1)}, bf16[256,2048]{1,0:T(8,128)(2,1)}, bf16[2048,704]{0,1:T(8,128)(2,1)}, bf16[2048,704]{0,1:T(8,128)(2,1)}, bf16[704,2048]{1,0:T(8,128)(2,1)}) async-done(((bf16[256,6144]{1,0:T(8,128)(2,1)}, bf16[256,2048]{1,0:T(8,128)(2,1)}, bf16[2048,704]{0,1:T(8,128)(2,1)}, bf16[2048,704]{0,1:T(8,128)(2,1)}, bf16[704,2048]{1,0:T(8,128)(2,1)}), ...) | async-done | bytes 12845072 | tf_op jit(solution)/shard_map/psum | solution.py:290
  2172.3 2.9 convert_element_type.186
  2175.3 3.4 convert_element_type.184
  2178.7 3.3 convert_element_type.188
  2182.0 3.3 convert_element_type.190
  2185.3 3.3 convert_element_type.192
  (202 shorter events, 47.4 us)
Async XLA Ops:
  7.2 935.7 %copy-start = (bf16[704,2048]{1,0:T(8,128)(2,1)S(1)}, bf16[704,2048]{1,0:T(8,128)(2,1)}, u32[]{:S(2)}) copy-start(bf16[704,2048]{1,0:T(8,128)(2,1)} %param.30) | copy-start | bytes 8650756
  7.2 1.2 copy-start.7
  7.2 1.6 copy-start.36
  7.2 485.6 %copy-start.20 = (f32[2048]{0:T(1024)S(1)}, f32[2048]{0:T(1024)}, u32[]{:S(2)}) copy-start(f32[2048]{0:T(1024)} %param.21) | copy-start | bytes 24580
  7.2 485.6 %copy-start.22 = (f32[2048]{0:T(1024)S(1)}, f32[2048]{0:T(1024)}, u32[]{:S(2)}) copy-start(f32[2048]{0:T(1024)} %param.22) | copy-start | bytes 24580
  7.2 485.5 %copy-start.33 = (f32[6144]{0:T(1024)S(1)}, f32[6144]{0:T(1024)}, u32[]{:S(2)}) copy-start(f32[6144]{0:T(1024)} %param.24) | copy-start | bytes 73732
  7.3 485.5 %all-gather.7.cloned.1.call-start = ((), (), s32[]{:S(2)}) async-start(), calls=%async_computation.4 | async-start | bytes 28311552 | tf_op jit(solution)/shard_map/all_gather | solution.py:90
  8.0 581.1 %all-gather.11.cloned.1.call-start = ((), (), s32[]{:S(2)}) async-start(), calls=%async_computation.6 | async-start | bytes 4718592 | tf_op jit(solution)/shard_map/all_gather | solution.py:107
  8.6 497.6 %copy-start.27 = (f32[128]{0:T(128)}, f32[128]{0:T(128)S(1)}, u32[]{:S(2)}) copy-start(f32[128]{0:T(128)S(1)} %broadcast_multiply_fusion.6) | copy-start | bytes 1540
  8.9 497.3 %copy-start.31 = (f32[128]{0:T(128)}, f32[128]{0:T(128)S(1)}, u32[]{:S(2)}) copy-start(f32[128]{0:T(128)S(1)} %add_rsqrt_fusion.1) | copy-start | bytes 1540
  9.6 501.9 %copy-start.25 = (f32[128,8]{0,1:T(8,128)}, f32[128,8]{0,1:T(8,128)S(1)}, u32[]{:S(2)}) copy-start(f32[128,8]{0,1:T(8,128)S(1)} %get-tuple-element.434) | copy-start | bytes 12292
  511.4 1.0 copy-start.18
  514.0 151.4 %all-gather.9.cloned.1.call-start = ((), (), s32[]{:S(2)}) async-start(), calls=%async_computation.5 | async-start | bytes 4718592 | tf_op jit(solution)/shard_map/all_gather | solution.py:108
  516.1 274.4 %all-gather.13.cloned.1.call-start = ((), (), s32[]{:S(2)}) async-start(), calls=%async_computation.7 | async-start | bytes 9437184 | tf_op jit(solution)/shard_map/all_gather | solution.py:91
  516.7 352.5 %all-gather.15.cloned.1.call-start = ((), (), s32[]{:S(2)}) async-start(), calls=%async_computation.8 | async-start | bytes 4718592 | tf_op jit(solution)/shard_map/all_gather | solution.py:166
  790.5 5.9 copy-start.24
  790.5 5.9 copy-start.35
  795.4 1.0 copy-start.5
  797.5 145.4 %all-gather.17.cloned.1.call-start = ((), (), s32[]{:S(2)}) async-start(), calls=%async_computation.10 | async-start | bytes 4718592 | tf_op jit(solution)/shard_map/all_gather | solution.py:186
  798.1 248.6 %reduce-scatter.7.cloned.1.call-start = ((), (), s32[]{:S(2)}) async-start(), calls=%async_computation.11 | async-start | bytes 4718592 | tf_op jit(solution)/shard_map/reduce_scatter | solution.py:207
  869.2 8.0 copy-start.37
  869.2 8.0 copy-start.39
  942.9 8.5 copy-start.40
  951.4 3.6 copy-start.42
  951.4 3.6 copy-start.44
  951.4 3.6 copy-start.41
  960.3 178.8 %reduce-scatter.5.cloned.1.call-start = ((), (), s32[]{:S(2)}) async-start(), calls=%async_computation.9 | async-start | bytes 4718592 | tf_op jit(solution)/shard_map/reduce_scatter | solution.py:177
  966.8 79.9 %copy-start.6 = (f32[128,1,2048]{2,0,1:T(8,128)S(1)}, f32[128,1,2048]{2,0,1:T(8,128)}, u32[]{:S(2)}) copy-start(f32[128,1,2048]{2,0,1:T(8,128)} %copy-done.5) | copy-start | bytes 3145732
  966.8 172.4 %copy-start.19 = (bf16[128,1,2048]{2,0,1:T(8,128)(2,1)S(1)}, bf16[128,1,2048]{2,0,1:T(8,128)(2,1)}, u32[]{:S(2)}) copy-start(bf16[128,1,2048]{2,0,1:T(8,128)(2,1)} %param.31) | copy-start | bytes 1572868
  966.8 387.5 %reduce-scatter.9.cloned.1.call-start = ((), (), s32[]{:S(2)}) async-start(), calls=%async_computation.12 | async-start | bytes 9437184 | tf_op jit(solution)/shard_map/reduce_scatter | solution.py:259
  1141.7 7.5 copy-start.9
  1141.7 8.8 copy-start.12
  1159.3 2.4 copy-start.2
  1163.1 1.6 copy-start.3
  1186.7 2.4 copy-start.2
  1190.5 1.6 copy-start.3
  1205.3 1.2 copy-start.4
  1205.3 3.1 copy-start.10
  1205.3 3.1 copy-start.11
  1205.4 733.7 %reduce-scatter.11.cloned.1.call-start = ((), (), s32[]{:S(2)}) async-start(), calls=%async_computation.13 | async-start | bytes 37748736 | tf_op jit(solution)/shard_map/reduce_scatter | solution.py:281
  1206.6 1.0 copy-start.17
  1214.3 142.5 %copy-start.26 = (f32[128,8]{0,1:T(8,128)S(1)}, f32[128,8]{0,1:T(8,128)}, u32[]{:S(2)}) copy-start(f32[128,8]{0,1:T(8,128)} %copy-done.25) | copy-start | bytes 12292
  1214.3 142.5 %copy-start.34 = (f32[128,8]{0,1:T(8,128)S(1)}, f32[128,8]{0,1:T(8,128)}, u32[]{:S(2)}) copy-start(f32[128,8]{0,1:T(8,128)} %get-tuple-element.432) | copy-start | bytes 12292
  1356.6 5.6 copy-start.8
  1356.6 5.6 copy-start.21
  1356.6 5.6 copy-start.23
  1356.6 5.7 copy-start.28
  1356.6 5.7 copy-start.32
  1397.2 775.1 %all-reduce.4.cloned.1.call-start = ((), (), s32[]{:S(2)}) async-start(), calls=%async_computation.14 | async-start | bytes 25690112 | tf_op jit(solution)/shard_map/psum | solution.py:290
  1397.5 7.5 copy-start.38
  1397.5 7.5 copy-start.45
  1405.0 4.5 copy-start.43
  1961.7 4.1 copy-start.29
  1961.7 4.1 copy-start.30
  2172.3 2.9 copy-start.13
  2175.2 3.5 copy-start.16
  2178.7 3.3 copy-start.15
  2182.0 3.3 copy-start.14
  2185.3 3.3 copy-start.1
Sparse Core Ops, SparseCore 0:
  9.6 483.1 all-gather.6
  514.1 74.9 all-gather.10
  591.7 73.5 all-gather.8
  667.3 123.1 all-gather.12
  797.6 71.5 all-gather.14
  871.2 71.6 all-gather.16
  960.4 86.1 reduce-scatter.6
  1051.3 87.7 reduce-scatter.4
  1205.5 148.7 reduce-scatter.8
  1397.3 541.6 reduce-scatter.10
  1945.4 226.9 all-reduce.3
where the time goes:
time: 2200 us
  waiting for transfers between devices  1840 us (84%)
  matrix products  151 us (7%)
  local copies, waits for them, and re-layouts  72.3 us (3%)
  other arithmetic  67.6 us (3%)
  blocking collectives  41.3 us (2%)
    reduce_scatter x1, waiting for transfers between devices, on_device(): lax.psum_scatter(jnp.concatenate([contract_rows(normed_low, grad_joined),...  525 us
    all_gather x1, waiting for transfers between devices, on_device(): lax.all_gather(w_qkv, 'seq', axis=0, tiled=True)  483 us
    psum x1, waiting for transfers between devices, on_device(): lax.psum(weight_part[:, :3 * model_width].astype(jnp.bfloat16), 'batch')  165 us
    reduce_scatter x1, waiting for transfers between devices, on_device(): lax.psum_scatter(kv_partial.astype(jnp.bfloat16), 'seq', scatter_dimensio...  140 us
    all_gather x1, waiting for transfers between devices, on_device(): lax.all_gather(w_out, 'seq', axis=0, tiled=True)  95.9 us
    reduce_scatter x1, waiting for transfers between devices, on_device(): lax.psum_scatter(jnp.dot(hidden_rows, w_down, preferred_element_type=jnp....  90.4 us
    reduce_scatter x1, waiting for transfers between devices, on_device(): lax.psum_scatter(summed.reshape(row_total, row_count, model_width).astype...  79.6 us
    all_gather x1, waiting for transfers between devices, on_device(): lax.all_gather(normed_two.astype(jnp.bfloat16), 'seq', axis=0, tiled=True)  70.6 us
  transfers between devices with their start and end apart: 11, of which 11 were waited for; matrix products, arithmetic and copies ran while one was open for 5% of the time, Pallas kernels for 0%

commit v1 on v0

v1 whole, which is shorter than its diff:
```python
import functools

import jax
import jax.numpy as jnp
from jax import lax
from jax.experimental import pallas as pl
from jax.experimental.pallas import tpu as pltpu
from jax.sharding import PartitionSpec as P

HEADS = 32
HEAD_DIM = 64
ROT = 16
BLOCK = 128
TILE = 256

eps_norm = 1e-05
theta_base = 10000.0
masked_score = -1e30
bf16 = jnp.bfloat16
f32 = jnp.float32


def ring_order(n):
    return [0, 2, 4, 6, 7, 5, 3, 1] if n == 8 else list(range(n))


class Ring:
    def __init__(self, axis):
        self.axis = axis
        self.n = n = lax.axis_size(axis)
        order = ring_order(n)
        self.ahead = [(order[i], order[(i + 1) % n]) for i in range(n)]
        self.behind = [(b, a) for a, b in self.ahead]
        place = jnp.array([order.index(i) for i in range(n)], jnp.int32)
        offset = (place - place[lax.axis_index(axis)]) % n
        half = n // 2
        self.slot = jnp.where(
            offset == 0, 0, jnp.where(offset == half, n - 1, jnp.where(offset < half, 2 * offset, 2 * (n - offset) - 1))
        ).astype(jnp.int32)

    def up(self, v):
        return lax.ppermute(v, self.axis, self.ahead)

    def down(self, v):
        return lax.ppermute(v, self.axis, self.behind)

    def gather(self, v):
        half = v.shape[0] // 2
        blocks, first, second = [v], v, v
        for _ in range(1, self.n // 2):
            first, second = self.up(first), self.down(second)
            blocks += [first, second]
        return blocks + [jnp.concatenate([self.up(first[:half]), self.down(second[half:])])]

    def scatter(self, parts):
        far = parts[-1]().astype(bf16)
        half = far.shape[0] // 2
        first, second = self.up(far[:half]), self.down(far[half:])
        for d in range(self.n // 2 - 1, 0, -1):
            first, second = first.astype(f32), second.astype(f32)
            if d == self.n // 2 - 1:
                first = jnp.pad(first, ((0, half), (0, 0)))
                second = jnp.pad(second, ((half, 0), (0, 0)))
            first = self.up((parts[2 * d]() + first).astype(bf16))
            second = self.down((parts[2 * d - 1]() + second).astype(bf16))
        return parts[0]() + first.astype(f32) + second.astype(f32)


def swap(v, axis, bit):
    n = lax.axis_size(axis)
    return lax.ppermute(v, axis, [(i, i ^ bit) for i in range(n)])


def bits_of(n):
    return [1 << i for i in range(n.bit_length() - 1)]


def batch_scatter(v, axis="batch"):
    n = lax.axis_size(axis)
    me = lax.axis_index(axis)
    rest = v
    for bit in bits_of(n):
        pairs = rest.reshape((rest.shape[0] // 2, 2) + rest.shape[1:])
        mine = (me // bit) % 2
        keep = lax.dynamic_index_in_dim(pairs, mine, 1, keepdims=False)
        give = lax.dynamic_index_in_dim(pairs, 1 - mine, 1, keepdims=False)
        rest = keep.astype(f32) + swap(give.astype(bf16), axis, bit).astype(f32)
    return rest[0]


def batch_gather(v, axis="batch"):
    n = lax.axis_size(axis)
    me = lax.axis_index(axis)
    held = v[None]
    for bit in reversed(bits_of(n)):
        other = swap(held, axis, bit)
        low = (me // bit) % 2 == 0
        pair = jnp.stack([jnp.where(low, held, other), jnp.where(low, other, held)], 1)
        held = pair.reshape((-1,) + v.shape)
    return held


def sum_all(v, axes):
    for axis in axes:
        for bit in bits_of(lax.axis_size(axis)):
            v = v + swap(v, axis, bit)
    return v


def norm_parts(values, gain_vector, shift_vector):
    mean_value = jnp.mean(values, axis=-1, keepdims=True)
    centred = values - mean_value
    inverse = lax.rsqrt(jnp.mean(centred * centred, axis=-1, keepdims=True) + eps_norm)
    unit_value = centred * inverse
    return (unit_value * gain_vector + shift_vector, unit_value, inverse)


def norm_back(gradient, unit_value, inverse, gain_vector):
    scaled = gradient * gain_vector
    return inverse * (
        scaled
        - jnp.mean(scaled, axis=-1, keepdims=True)
        - unit_value * jnp.mean(scaled * unit_value, axis=-1, keepdims=True)
    )


def dot(a, b):
    return jnp.dot(a, b, preferred_element_type=f32)


def dot_rows(a, b):
    return lax.dot_general(a, b, (((0,), (0,)), ((), ())), preferred_element_type=f32)


def dot_last(a, b):
    return lax.dot_general(a, b, (((1,), (1,)), ((), ())), preferred_element_type=f32)


def rotary_tables(positions, width):
    half = ROT // 2
    frequency = theta_base ** (-(jnp.arange(half, dtype=f32) * 2.0 / ROT))
    angles = positions.astype(f32)[:, None] * frequency
    cosine, sine = jnp.cos(angles), jnp.sin(angles)
    rest = jnp.zeros((positions.shape[0], HEAD_DIM - ROT), f32)
    own = jnp.concatenate([cosine, cosine, rest + 1.0], 1)
    other = jnp.concatenate([-sine, sine, rest], 1)
    return jnp.tile(own, (1, width // HEAD_DIM)), jnp.tile(other, (1, width // HEAD_DIM))


def rotate_lanes(x, own, other):
    half = ROT // 2
    width = x.shape[1]
    lane = lax.broadcasted_iota(jnp.int32, x.shape, 1) % HEAD_DIM
    partner = jnp.where(lane < half, pltpu.roll(x, width - half, 1), pltpu.roll(x, half, 1))
    return x * own + partner * other


def visible_to(first_ref, start, keys, tile):
    key = lax.broadcasted_iota(jnp.int32, (keys, tile), 0)
    query = lax.broadcasted_iota(jnp.int32, (keys, tile), 1) + start
    return (key <= query) & (key >= first_ref[0:1, start : start + tile])


def head_rows(x, h):
    if x.shape[0] == HEAD_DIM:
        return x
    row = lax.broadcasted_iota(jnp.int32, x.shape, 0) // HEAD_DIM
    return jnp.where(row == h, x, jnp.zeros_like(x))


def head_lanes(x, h):
    if x.shape[1] == HEAD_DIM:
        return x
    lane = lax.broadcasted_iota(jnp.int32, x.shape, 1) // HEAD_DIM
    return jnp.where(lane == h, x, jnp.zeros_like(x))


def attend_kernel(slot_ref, joined_ref, own_ref, other_ref, first_ref, qkv_ref, mixed_ref, lse_ref, q_t, v_t):
    length, width3 = joined_ref.shape
    width = width3 // 3
    heads = width // HEAD_DIM
    scale = HEAD_DIM ** (-0.5)
    for j in range(length // BLOCK):
        rows = pl.ds(pl.multiple_of(slot_ref[j] * BLOCK, BLOCK), BLOCK)
        here = slice(j * BLOCK, (j + 1) * BLOCK)
        x = joined_ref[rows, :]
        own, other = own_ref[here, :], other_ref[here, :]
        q = rotate_lanes(x[:, :width], own, other).astype(bf16)
        k = rotate_lanes(x[:, width : 2 * width], own, other).astype(bf16)
        v = x[:, 2 * width :].astype(bf16)
        qkv_ref[0, here, :] = q
        qkv_ref[1, here, :] = k
        qkv_ref[2, here, :] = v
        q_t[:, here] = (q.astype(f32) * scale).T.astype(bf16)
        v_t[:, here] = v.astype(f32).T.astype(bf16)
    lse_ref[...] = jnp.zeros_like(lse_ref)
    tile = min(TILE, length)
    for start in range(0, length, tile):
        keys = start + tile
        seen = visible_to(first_ref, start, keys, tile)
        queries = q_t[:, start : start + tile]
        outs = []
        for h in range(heads):
            scores = dot(qkv_ref[1, :keys, :], head_rows(queries, h))
            scores = jnp.where(seen, scores, masked_score)
            top = jnp.max(scores, axis=0, keepdims=True)
            weights = jnp.exp(scores - top)
            total = jnp.sum(weights, axis=0, keepdims=True)
            lse_ref[h : h + 1, start : start + tile] = top + jnp.log(total)
            prob = (weights * (1.0 / total)).astype(bf16)
            outs.append(dot(v_t[h * HEAD_DIM : (h + 1) * HEAD_DIM, :keys], prob))
        out = jnp.concatenate(outs, 0).T.astype(bf16)
        for i in range(tile // BLOCK):
            rows = pl.ds(pl.multiple_of(slot_ref[start // BLOCK + i] * BLOCK, BLOCK), BLOCK)
            mixed_ref[rows, :] = out[i * BLOCK : (i + 1) * BLOCK]


def attend_back_kernel(
    slot_ref, qkv_ref, mixed_ref, grad_ref, lse_ref, own_ref, other_ref, first_ref, out_ref,
    q_t, k_t, g_t, grads, delta, dk, dv,
):
    length, width = mixed_ref.shape
    heads = width // HEAD_DIM
    scale = HEAD_DIM ** (-0.5)
    for j in range(length // BLOCK):
        rows = pl.ds(pl.multiple_of(slot_ref[j] * BLOCK, BLOCK), BLOCK)
        here = slice(j * BLOCK, (j + 1) * BLOCK)
        g = grad_ref[rows, :]
        g_flip = g.astype(f32).T
        o_flip = mixed_ref[rows, :].astype(f32).T
        both = g_flip * o_flip
        for h in range(heads):
            delta[h : h + 1, here] = jnp.sum(both[h * HEAD_DIM : (h + 1) * HEAD_DIM], axis=0, keepdims=True)
        grads[here, :] = g
        g_t[:, here] = g_flip.astype(bf16)
        q_t[:, here] = (qkv_ref[0, here, :].astype(f32) * scale).T.astype(bf16)
        k_t[:, here] = qkv_ref[1, here, :].astype(f32).T.astype(bf16)
    dk[...] = jnp.zeros_like(dk)
    dv[...] = jnp.zeros_like(dv)
    tile = min(TILE, length)
    for start in range(0, length, tile):
        keys = start + tile
        here = slice(start, keys)
        seen = visible_to(first_ref, start, keys, tile)
        q_tile, g_tile = q_t[:, here], g_t[:, here]
        q_rows, g_rows = qkv_ref[0, here, :], grads[here, :]
        dq, dk_sum, dv_sum = [], dk[:keys, :], dv[:keys, :]
        for h in range(heads):
            scores = dot(qkv_ref[1, :keys, :], head_rows(q_tile, h))
            prob = jnp.where(seen, jnp.exp(scores - lse_ref[h : h + 1, here]), 0.0)
            grad_prob = dot(qkv_ref[2, :keys, :], head_rows(g_tile, h))
            grad_score = (prob * (grad_prob - delta[h : h + 1, here])).astype(bf16)
            dv_sum += dot(prob.astype(bf16), head_lanes(g_rows, h))
            dk_sum += dot(grad_score, head_lanes(q_rows, h))
            dq.append(dot(k_t[h * HEAD_DIM : (h + 1) * HEAD_DIM, :keys], grad_score))
        dk[:keys, :] = dk_sum
        dv[:keys, :] = dv_sum
        dq = jnp.concatenate(dq, 0).T * scale
        for i in range(tile // BLOCK):
            at = slice(i * BLOCK, (i + 1) * BLOCK)
            place = slice(start + i * BLOCK, start + (i + 1) * BLOCK)
            rows = pl.ds(pl.multiple_of(slot_ref[start // BLOCK + i] * BLOCK, BLOCK), BLOCK)
            turned = rotate_lanes(dq[at], own_ref[place, :], -other_ref[place, :])
            out_ref[rows, :width] = turned.astype(bf16)
    for j in range(length // BLOCK):
        rows = pl.ds(pl.multiple_of(slot_ref[j] * BLOCK, BLOCK), BLOCK)
        here = slice(j * BLOCK, (j + 1) * BLOCK)
        turned = rotate_lanes(dk[here, :] * scale, own_ref[here, :], -other_ref[here, :])
        out_ref[rows, width : 2 * width] = turned.astype(bf16)
        out_ref[rows, 2 * width :] = dv[here, :].astype(bf16)


def in_vmem(count):
    return [pl.BlockSpec(memory_space=pltpu.SMEM)] + [pl.BlockSpec(memory_space=pltpu.VMEM)] * count


def attend(slot, joined, own, other, first):
    length, width3 = joined.shape
    width = width3 // 3
    rows = max(8, width // HEAD_DIM)
    return pl.pallas_call(
        attend_kernel,
        out_shape=(
            jax.ShapeDtypeStruct((3, length, width), bf16),
            jax.ShapeDtypeStruct((length, width), bf16),
            jax.ShapeDtypeStruct((rows, length), f32),
        ),
        in_specs=in_vmem(4),
        out_specs=(pl.BlockSpec(memory_space=pltpu.VMEM),) * 3,
        scratch_shapes=[pltpu.VMEM((width, length), bf16), pltpu.VMEM((width, length), bf16)],
        compiler_params=pltpu.CompilerParams(vmem_limit_bytes=48 * 2**20),
        name="attend",
    )(slot, joined, own, other, first)


def attend_back(slot, qkv, mixed, grad, lse, own, other, first):
    length, width = mixed.shape
    rows = lse.shape[0]
    return pl.pallas_call(
        attend_back_kernel,
        out_shape=jax.ShapeDtypeStruct((length, 3 * width), bf16),
        in_specs=in_vmem(7),
        out_specs=pl.BlockSpec(memory_space=pltpu.VMEM),
        scratch_shapes=[
            pltpu.VMEM((width, length), bf16),
            pltpu.VMEM((width, length), bf16),
            pltpu.VMEM((width, length), bf16),
            pltpu.VMEM((length, width), bf16),
            pltpu.VMEM((rows, length), f32),
            pltpu.VMEM((length, width), f32),
            pltpu.VMEM((length, width), f32),
        ],
        compiler_params=pltpu.CompilerParams(vmem_limit_bytes=48 * 2**20),
        name="attend_back",
    )(slot, qkv, mixed, grad, lse, own, other, first)


def on_device(
    inputs, positions, ln1_gain, ln1_bias, w_qkv, qkv_bias, w_out, ln2_gain, ln2_bias, w_gate, w_up, w_down, cotangent
):
    n, rows = lax.axis_size("seq"), lax.axis_size("batch")
    me, my_row = lax.axis_index("seq"), lax.axis_index("batch")
    ring = Ring("seq")
    tokens, model = inputs.shape[0], inputs.shape[2]
    length = tokens * n
    width = model // n
    depth = w_qkv.shape[0]
    x = inputs.reshape(tokens, model).astype(f32)
    cot = cotangent.reshape(tokens, model)

    share = depth // rows
    mine = lax.dynamic_slice_in_dim(w_qkv, my_row * share, share, 0).reshape(share, 3, n, width)
    mine = mine.transpose(2, 0, 1, 3).reshape(n, share, 3 * width)
    fetched = lax.all_to_all(mine, "seq", split_axis=0, concat_axis=0, tiled=True)
    w_heads = batch_gather(fetched).transpose(1, 0, 2, 3).reshape(model, 3 * width)
    bias_heads = lax.dynamic_index_in_dim(qkv_bias.reshape(3, n, width), me, 1, keepdims=False).reshape(3 * width)

    places = lax.all_gather(positions.reshape(tokens), "seq", axis=0, tiled=True)
    own, other = rotary_tables(places, width)
    first = (jnp.arange(length, dtype=jnp.int32) - places)[None]

    normed, unit_one, inverse_one = norm_parts(x, ln1_gain, ln1_bias)
    normed_blocks = ring.gather(normed.astype(bf16))
    joined = jnp.concatenate([dot(b, w_heads) + bias_heads for b in normed_blocks])
    qkv, mixed, lse = attend(ring.slot, joined, own, other, first)

    def block(v, i):
        return v[i * tokens : (i + 1) * tokens]

    branch = ring.scatter([functools.partial(lambda i: dot(block(mixed, i), w_out), i) for i in range(n)])
    middle = x + branch
    normed_two, unit_two, inverse_two = norm_parts(middle, ln2_gain, ln2_bias)
    cot_blocks = ring.gather(cot)
    two_blocks = ring.gather(normed_two.astype(bf16))

    hidden, grad_gate, grad_up = [], [], []
    for b, c in zip(two_blocks, cot_blocks, strict=True):
        gate, up = dot(b, w_gate), dot(b, w_up)
        grad_hidden = dot_last(c, w_down)
        sigmoid = jax.nn.sigmoid(gate)
        silu = gate * sigmoid
        hidden.append((silu * up).astype(bf16))
        grad_gate.append((grad_hidden * up * sigmoid * (1.0 + gate * (1.0 - sigmoid))).astype(bf16))
        grad_up.append((grad_hidden * silu).astype(bf16))

    grad_two = ring.scatter(
        [
            functools.partial(lambda i: dot_last(grad_gate[i], w_gate) + dot_last(grad_up[i], w_up), i)
            for i in range(n)
        ]
    )
    out_sum = ring.scatter([functools.partial(lambda i: dot(hidden[i], w_down), i) for i in range(n)])
    output = (middle + out_sum).astype(bf16)

    all_two, all_cot = jnp.concatenate(two_blocks), jnp.concatenate(cot_blocks)
    grad_w_down = dot_rows(jnp.concatenate(hidden), all_cot).astype(bf16)
    grad_w_gate = dot_rows(all_two, jnp.concatenate(grad_gate)).astype(bf16)
    grad_w_up = dot_rows(all_two, jnp.concatenate(grad_up)).astype(bf16)

    def over_rows(v):
        parts = v.reshape((rows, v.shape[0] // rows) + v.shape[1:])
        return batch_gather(batch_scatter(parts).astype(bf16)).reshape(v.shape).astype(f32)

    grad_w_down, grad_w_gate, grad_w_up = over_rows(grad_w_down), over_rows(grad_w_gate), over_rows(grad_w_up)

    grad_middle = cot.astype(f32) + norm_back(grad_two, unit_two, inverse_two, ln2_gain)
    gain_two_grad = jnp.sum(grad_two * unit_two, axis=0)
    bias_two_grad = jnp.sum(grad_two, axis=0)
    branch_blocks = ring.gather(grad_middle.astype(bf16))
    grad_mixed = jnp.concatenate([dot_last(b, w_out).astype(bf16) for b in branch_blocks])
    grad_w_out = over_rows(dot_rows(mixed, jnp.concatenate(branch_blocks)).astype(bf16))

    grad_joined = attend_back(ring.slot, qkv, mixed, grad_mixed, lse, own, other, first)
    bias_heads_grad = jnp.sum(grad_joined.astype(f32), axis=0)
    grad_one = ring.scatter(
        [functools.partial(lambda i: dot_last(block(grad_joined, i), w_heads), i) for i in range(n)]
    )
    grad_input = grad_middle + norm_back(grad_one, unit_one, inverse_one, ln1_gain)
    gain_one_grad = jnp.sum(grad_one * unit_one, axis=0)
    bias_one_grad = jnp.sum(grad_one, axis=0)

    grad_w_heads = dot_rows(jnp.concatenate(normed_blocks), grad_joined).astype(bf16)
    parts = grad_w_heads.reshape(n, rows, share, 3 * width).transpose(1, 0, 2, 3)
    mine = batch_scatter(parts).astype(bf16)
    mine = lax.all_to_all(mine, "seq", split_axis=0, concat_axis=0, tiled=True)
    mine = mine.reshape(n, share, 3, width).transpose(1, 2, 0, 3).reshape(share, 3 * model)
    grad_w_qkv = batch_gather(mine).reshape(depth, 3 * model).astype(f32)

    bias_all = jnp.zeros((3, n, width), f32)
    bias_all = lax.dynamic_update_slice(bias_all, bias_heads_grad.reshape(3, 1, width), (0, me, 0)).reshape(-1)
    vectors = jnp.concatenate([gain_one_grad, bias_one_grad, gain_two_grad, bias_two_grad, bias_all]).reshape(-1, 128)
    vectors = sum_all(vectors, ("seq", "batch")).reshape(-1)
    gain_one_sum, bias_one_sum, gain_two_sum, bias_two_sum, qkv_bias_sum = jnp.split(
        vectors, [model, 2 * model, 3 * model, 4 * model]
    )
    return (
        output.reshape(tokens, 1, model),
        grad_input.reshape(tokens, 1, model),
        gain_one_sum,
        bias_one_sum,
        grad_w_qkv,
        qkv_bias_sum,
        grad_w_out,
        gain_two_sum,
        bias_two_sum,
        grad_w_gate,
        grad_w_up,
        grad_w_down,
    )


def solution(mesh):
    token, shard, column, whole = P("seq", "batch", None), P("seq", None), P(None, "seq"), P()
    in_specs = (
        token, P("seq", "batch"), whole, whole, shard, whole, shard, whole, whole, column, column, shard, token
    )
    out_specs = (token, token, whole, whole, shard, whole, shard, whole, whole, column, column, shard)
    return jax.shard_map(on_device, mesh=mesh, in_specs=in_specs, out_specs=out_specs, check_vma=False)
```

time: 2200 us -> 667 us (0.30)
  waiting for transfers between devices: 1840 us -> 208 us
  starting transfers between devices: 1.76 us -> 97.2 us
  local copies, waits for them, and re-layouts: 72.3 us -> 133 us
  matrix products: 151 us -> 106 us
  Pallas kernels: 0 us -> 22.2 us
    all_gather x6 -> x0, waiting for transfers between devices: 841 us -> none  [the longest x1 483 us: on_device(): lax.all_gather(w_qkv, 'seq', axis=0, tiled=True)]
    reduce_scatter x4 -> x0, waiting for transfers between devices: 835 us -> none  [the longest x1 525 us: on_device(): lax.psum_scatter(jnp.concatenate([contract_rows(normed_low, grad_joined),...]
    ppermute x0 -> x91, waiting for transfers between devices: none -> 200 us  [the longest x32 108 us: down(): return lax.ppermute(v, self.axis, self.behind)]
    psum x1 -> x0, waiting for transfers between devices: 165 us -> none  [on_device(): lax.psum(weight_part[:, :3 * model_width].astype(jnp.bfloat16), 'batch')]
    ppermute x0 -> x91, starting transfers between devices: none -> 85.5 us  [the longest x32 65.2 us: up(): return lax.ppermute(v, self.axis, self.ahead)]
    dot_general x29 -> x85, matrix products: 151 us -> 106 us  [the longest x40 51.8 us: dot_last(): lax.dot_general(a, b, (((1,), (1,)), ((), ())), preferred_element_type=f32)]
    all_gather x0 -> x1, blocking collectives: none -> 43.9 us  [on_device(): lax.all_gather(positions.reshape(tokens), 'seq', axis=0, tiled=True)]
    convert_element_type x1 -> x12, local copies, waits for them, and re-layouts: 1.31 us -> 43.5 us  [the longest x6 38.2 us: over_rows(): batch_gather(batch_scatter(parts).astype(bf16)).reshape(v.shape).astype(f32)]
  transfers between devices with their start and end apart: 11 -> 93, of which waited for: 11 -> 33; matrix products, arithmetic and copies ran while one was open for 5% -> 40% of each run, Pallas kernels for 0% -> 3%
where the time goes in v1:
time: 667 us; the launch traced here: 660 us
  waiting for transfers between devices  208 us (31%)
  local copies, waits for them, and re-layouts  133 us (20%)
  matrix products  106 us (16%)
  starting transfers between devices  97.2 us (15%)
  other arithmetic  46.5 us (7%)
  blocking collectives  43.9 us (7%)
  Pallas kernels  22.2 us (3%)
    ppermute x32, waiting for transfers between devices, down(): return lax.ppermute(v, self.axis, self.behind)  108 us
    ppermute x32, starting transfers between devices, up(): return lax.ppermute(v, self.axis, self.ahead)  65.2 us
    ppermute x27, waiting for transfers between devices, swap(): return lax.ppermute(v, axis, [(i, i ^ bit) for i in range(n)])  57.5 us
    dot_general x40, matrix products, dot_last(): lax.dot_general(a, b, (((1,), (1,)), ((), ())), preferred_element_type=f32)  51.8 us
    all_gather x1, blocking collectives, on_device(): lax.all_gather(positions.reshape(tokens), 'seq', axis=0, tiled=True)  43.9 us
    convert_element_type x6, local copies, waits for them, and re-layouts, over_rows(): batch_gather(batch_scatter(parts).astype(bf16)).reshape(v.shape).astype(f32)  38.2 us
    dot_general x40, matrix products, dot(): return jnp.dot(a, b, preferred_element_type=f32)  36.2 us
    ppermute x32, waiting for transfers between devices, up(): return lax.ppermute(v, self.axis, self.ahead)  34.9 us
  transfers between devices with their start and end apart: 93, of which 33 were waited for; matrix products, arithmetic and copies ran while one was open for 40% of the time, Pallas kernels for 3%

profile of v1, /device:TPU:0, one launch (start us, length us, event | category | flops | bytes accessed | tf_op | source)
XLA Modules:
  0.0 660.2 jit_solution(10708891134777032803)
XLA Ops:
  4.9 7.3 %all-to-all-start = ((bf16[8,64,768]{2,1,0:T(8,128)(2,1)}), bf16[8,64,768]{2,1,0:T(8,128)(2,1)}, u32[]{:S(2)}, u32[]{:S(2)}) async-start(bf16[8,64,768]{2,1,0:T(8,128)(2,1)} %reshape.236), calls=%async_computation | async-start | bytes 1572864 | tf_op jit(solution)/shard_map/all_to_all | solution.py:334
  18.0 43.9 %all-gather = s32[1024,1]{0,1:T(1,128)S(1)} all-gather(s32[128,1]{0,1:T(1,128)S(1)} %copy-done.94), channel_id=2, replica_groups=mesh['seq'=8,'batch'=4] {'seq'}, dimensions={0}, use_global_device_ids=true | all-gather | bytes 4608 | tf_op jit(solution)/shard_map/all_gather | solution.py:338
  67.8 3.1 fusion.108
  70.9 2.5 collective-permute-start.4
  75.5 2.3 collective-permute-done
  82.1 4.0 collective-permute-done.4
  86.1 2.4 collective-permute-start.6
  88.5 8.9 %collective-permute-done.38 = bf16[128,2048]{1,0:T(8,128)(2,1)S(1)} collective-permute-done((bf16[128,2048]{1,0:T(8,128)(2,1)}, bf16[128,2048]{1,0:T(8,128)(2,1)S(1)}, u32[]{:S(2)}, u32[]{:S(2)}) %collective-permute-start.38) | collective-permute-done | bytes 524320 | tf_op jit(solution)/shard_map/ppermute | solution.py:42
  97.4 2.4 collective-permute-start.39
  103.5 7.5 %collective-permute-done.7 = bf16[128,2048]{1,0:T(8,128)(2,1)S(1)} collective-permute-done((bf16[128,2048]{1,0:T(8,128)(2,1)S(1)}, bf16[128,2048]{1,0:T(8,128)(2,1)S(1)}, u32[]{:S(2)}, u32[]{:S(2)}) %collective-permute-start.7) | collective-permute-done | bytes 524320 | tf_op jit(solution)/shard_map/ppermute | solution.py:45
  113.1 8.9 %collective-permute-done.36 = bf16[128,2048]{1,0:T(8,128)(2,1)S(1)} collective-permute-done((bf16[128,2048]{1,0:T(8,128)(2,1)S(1)}, bf16[128,2048]{1,0:T(8,128)(2,1)S(1)}, u32[]{:S(2)}, u32[]{:S(2)}) %collective-permute-start.36) | collective-permute-done | bytes 524320 | tf_op jit(solution)/shard_map/ppermute | solution.py:45
  137.7 12.1 %attend.1 = (bf16[3,1024,256]{2,1,0:T(8,128)(2,1)S(1)}, bf16[1024,256]{1,0:T(8,128)(2,1)S(1)}, f32[8,1024]{1,0:T(8,128)S(1)}) custom-call(s32[8]{0:T(128)S(1)} %compare_select_fusion.4.slot_ref, f32[1024,768]{1,0:T(8,128)} %copy-done.48, f32[1024,256]{1,0:T(8,128)S(1)} %copy.74.own_ref, f32[1024,256]{1,0:T(8,128)S(1)} %copy.75.other_ref, s32[1,1024]{1,0:T(1,128)S(1)} %bitcast.370), custom_call_target="tpu_custom_call" | custom-call | tf_op jit(solution)/shard_map/attend/pallas_call | solution.py:281
  152.9 5.9 collective-permute-done.14
  161.9 9.6 %collective-permute-done.15 = bf16[128,2048]{1,0:T(8,128)(2,1)S(1)} collective-permute-done((bf16[128,2048]{1,0:T(8,128)(2,1)S(1)}, bf16[128,2048]{1,0:T(8,128)(2,1)S(1)}, u32[]{:S(2)}, u32[]{:S(2)}) %collective-permute-start.15) | collective-permute-done | bytes 524320 | tf_op jit(solution)/shard_map/ppermute | solution.py:45
  171.7 2.3 collective-permute-start.12
  174.4 7.3 %collective-permute-done.16 = bf16[128,2048]{1,0:T(8,128)(2,1)S(1)} collective-permute-done((bf16[128,2048]{1,0:T(8,128)(2,1)S(1)}, bf16[128,2048]{1,0:T(8,128)(2,1)S(1)}, u32[]{:S(2)}, u32[]{:S(2)}) %collective-permute-start.16) | collective-permute-done | bytes 524320 | tf_op jit(solution)/shard_map/ppermute | solution.py:45
  184.0 2.5 collective-permute-start.13
  188.4 3.7 collective-permute-done.17
  194.2 2.5 collective-permute-start.21
  217.8 2.5 collective-permute-start.22
  222.1 8.3 %collective-permute-done.22 = bf16[128,2048]{1,0:T(8,128)(2,1)S(1)} collective-permute-done((bf16[128,2048]{1,0:T(8,128)(2,1)S(1)}, bf16[128,2048]{1,0:T(8,128)(2,1)S(1)}, u32[]{:S(2)}, u32[]{:S(2)}) %collective-permute-start.22) | collective-permute-done | bytes 524320 | tf_op jit(solution)/shard_map/ppermute | solution.py:42
  242.4 2.5 collective-permute-start.23
  246.6 5.0 collective-permute-done.23
  251.6 2.5 collective-permute-start.24
  274.1 2.4 collective-permute-start.26
  276.5 4.4 convolution_convert_fusion.2
  281.0 7.7 %reshape_reshape.18 = bf16[2,2,512,704]{2,1,0,3:T(2,128)(2,1)} reshape(bf16[2048,704]{0,1:T(8,128)(2,1)} %convolution_convert_fusion.2) | data formatting | bytes 5767168 | tf_op jit(solution)/shard_map/reshape;reshape | solution.py:83
  288.7 10.3 %constant_dynamic-slice_fusion.3 = (bf16[2,1,512,704]{2,1,0,3:T(2,128)(2,1)}, bf16[2,1,512,704]{2,1,0,3:T(2,128)(2,1)S(1)}) fusion(bf16[2,2,512,704]{2,1,0,3:T(2,128)(2,1)} %reshape_reshape.18, s32[]{:T(128)S(6)} %select_n.291, s32[]{:T(128)S(6)} %select_n.292), kind=kLoop, calls=%fused_computation.330 | loop fusion | bytes 5767176 | tf_op jit(solution)/shard_map/jit(dynamic_index_in_dim)/dynamic_slice | solution.py:85
  301.7 4.5 convolution_convert_fusion.1
  306.2 7.9 %reshape_reshape.19 = bf16[2,2,512,704]{2,1,0,3:T(2,128)(2,1)} reshape(bf16[2048,704]{0,1:T(8,128)(2,1)} %convolution_convert_fusion.1) | data formatting | bytes 5767168 | tf_op jit(solution)/shard_map/reshape;reshape | solution.py:83
  314.0 8.6 %constant_dynamic-slice_fusion.1 = (bf16[2,1,512,704]{2,1,0,3:T(2,128)(2,1)S(1)}, bf16[2,1,512,704]{2,1,0,3:T(2,128)(2,1)S(1)}) fusion(bf16[2,2,512,704]{2,1,0,3:T(2,128)(2,1)} %reshape_reshape.19, s32[]{:T(128)S(6)} %select_n.291, s32[]{:T(128)S(6)} %select_n.292), kind=kLoop, calls=%fused_computation.328 | loop fusion | bytes 5767176 | tf_op jit(solution)/shard_map/jit(dynamic_index_in_dim)/dynamic_slice | solution.py:85
  332.6 8.7 %collective-permute-done.47 = bf16[128,2048]{1,0:T(8,128)(2,1)S(1)} collective-permute-done((bf16[128,2048]{1,0:T(8,128)(2,1)S(1)}, bf16[128,2048]{1,0:T(8,128)(2,1)S(1)}, u32[]{:S(2)}, u32[]{:S(2)}) %collective-permute-start.47) | collective-permute-done | bytes 524320 | tf_op jit(solution)/shard_map/ppermute | solution.py:45
  343.6 8.8 %collective-permute-done.31 = bf16[128,2048]{1,0:T(8,128)(2,1)S(1)} collective-permute-done((bf16[128,2048]{1,0:T(8,128)(2,1)S(1)}, bf16[128,2048]{1,0:T(8,128)(2,1)S(1)}, u32[]{:S(2)}, u32[]{:S(2)}) %collective-permute-start.31) | collective-permute-done | bytes 524320 | tf_op jit(solution)/shard_map/ppermute | solution.py:45
  354.9 8.8 %collective-permute-done.48 = bf16[128,2048]{1,0:T(8,128)(2,1)S(1)} collective-permute-done((bf16[128,2048]{1,0:T(8,128)(2,1)S(1)}, bf16[128,2048]{1,0:T(8,128)(2,1)S(1)}, u32[]{:S(2)}, u32[]{:S(2)}) %collective-permute-start.48) | collective-permute-done | bytes 524320 | tf_op jit(solution)/shard_map/ppermute | solution.py:45
  366.3 8.6 %collective-permute-done.32 = bf16[128,2048]{1,0:T(8,128)(2,1)S(1)} collective-permute-done((bf16[128,2048]{1,0:T(8,128)(2,1)S(1)}, bf16[128,2048]{1,0:T(8,128)(2,1)S(1)}, u32[]{:S(2)}, u32[]{:S(2)}) %collective-permute-start.32) | collective-permute-done | bytes 524320 | tf_op jit(solution)/shard_map/ppermute | solution.py:45
  382.7 3.5 collective-permute-done.49
  386.7 3.1 collective-permute-done.45
  389.8 6.2 collective-permute-done.33
  406.9 3.4 convolution_convert_fusion.3
  416.9 13.4 %collective-permute-done.81 = bf16[1,512,704]{1,2,0:T(8,128)(2,1)S(1)} collective-permute-done((bf16[1,512,704]{1,2,0:T(8,128)(2,1)S(1)}, bf16[1,512,704]{1,2,0:T(8,128)(2,1)S(1)}, u32[]{:S(2)}, u32[]{:S(2)}) %collective-permute-start.81) | collective-permute-done | bytes 720928 | tf_op jit(solution)/shard_map/ppermute | solution.py:71
  431.7 13.6 %collective-permute-done.85 = bf16[1,512,704]{1,2,0:T(8,128)(2,1)S(1)} collective-permute-done((bf16[1,512,704]{1,2,0:T(8,128)(2,1)S(1)}, bf16[1,512,704]{1,2,0:T(8,128)(2,1)S(1)}, u32[]{:S(2)}, u32[]{:S(2)}) %collective-permute-start.85) | collective-permute-done | bytes 720928 | tf_op jit(solution)/shard_map/ppermute | solution.py:71
  452.2 10.2 %collective-permute-done.55 = bf16[128,2048]{1,0:T(8,128)(2,1)S(1)} collective-permute-done((bf16[128,2048]{1,0:T(8,128)(2,1)S(1)}, bf16[128,2048]{1,0:T(8,128)(2,1)S(1)}, u32[]{:S(2)}, u32[]{:S(2)}) %collective-permute-start.55) | collective-permute-done | bytes 524320 | tf_op jit(solution)/shard_map/ppermute | solution.py:45
  466.1 4.1 collective-permute-done.57
  471.5 10.1 %attend_back.1 = bf16[1024,768]{1,0:T(8,128)(2,1)S(1)} custom-call(s32[8]{0:T(128)S(1)} %compare_select_fusion.4.slot_ref, bf16[3,1024,256]{2,1,0:T(8,128)(2,1)} %copy-done.4, bf16[1024,256]{1,0:T(8,128)(2,1)S(1)} %get-tuple-element.15.mixed_ref, bf16[1024,256]{1,0:T(8,128)(2,1)S(1)} %fusion.17.grad_ref, f32[8,1024]{1,0:T(8,128)S(1)} %get-tuple-element.17.lse_ref, ...), custom_call_target="tpu_custom_call" | custom-call | tf_op jit(solution)/shard_map/attend_back/pallas_call | solution.py:299
  495.4 4.9 convolution_convert_fusion
  508.0 2.3 copy-done.7
  510.3 2.9 add_convert_fusion.6
  525.5 2.9 maximum_convert_fusion.2
  528.4 7.0 %copy.84 = f32[2,2,512,704]{2,1,0,3:T(2,128)} copy(f32[2,2,512,704]{2,3,0,1:T(8,128)S(1)} %maximum_convert_fusion.1) | data formatting | bytes 11534336 | tf_op jit(solution)/shard_map/convert_element_type | solution.py:382
  535.4 8.7 %reshape.261 = f32[2048,704]{0,1:T(8,128)} reshape(f32[2,2,512,704]{2,1,0,3:T(2,128)} %copy.84) | data formatting | bytes 11534336 | tf_op jit(solution)/shard_map/convert_element_type | solution.py:382
  544.1 9.6 %copy.87 = f32[2,2,512,704]{2,1,0,3:T(2,128)} copy(f32[2,2,512,704]{2,3,0,1:T(8,128)} %maximum_convert_fusion.2) | data formatting | bytes 11534336 | tf_op jit(solution)/shard_map/convert_element_type | solution.py:382
  553.7 8.6 %reshape.263 = f32[2048,704]{0,1:T(8,128)} reshape(f32[2,2,512,704]{2,1,0,3:T(2,128)} %copy.87) | data formatting | bytes 11534336 | tf_op jit(solution)/shard_map/convert_element_type | solution.py:382
  569.7 6.1 collective-permute-done.64
  583.1 14.0 %collective-permute-done.72 = bf16[1,8,64,768]{3,2,1,0:T(8,128)(2,1)S(1)} collective-permute-done((bf16[1,8,64,768]{3,2,1,0:T(8,128)(2,1)S(1)}, bf16[1,8,64,768]{3,2,1,0:T(8,128)(2,1)S(1)}, u32[]{:S(2)}, u32[]{:S(2)}) %collective-permute-start.72) | collective-permute-done | bytes 786464 | tf_op jit(solution)/shard_map/ppermute | solution.py:71
  598.1 4.5 all-to-all-start.1
  602.7 2.7 fusion.32
  609.5 2.7 collective-permute-done.66
  613.3 7.4 %all-to-all-done.1 = bf16[8,64,768]{2,1,0:T(8,128)(2,1)} async-done(((bf16[8,64,768]{2,1,0:T(8,128)(2,1)}), bf16[8,64,768]{2,1,0:T(8,128)(2,1)}, u32[]{:S(2)}, u32[]{:S(2)}) %all-to-all-start.1) | async-done | bytes 786464 | tf_op jit(solution)/shard_map/all_to_all | solution.py:405
  620.7 3.4 reshape.250
  624.1 2.9 copy.79
  633.6 5.1 collective-permute-done.68
  641.7 5.2 collective-permute-done.73
  653.0 2.9 copy.88
  656.6 3.1 copy.80
  (589 shorter events, 241.7 us)
Async XLA Ops:
  4.9 57.0 %all-to-all-start = ((bf16[8,64,768]{2,1,0:T(8,128)(2,1)}), bf16[8,64,768]{2,1,0:T(8,128)(2,1)}, u32[]{:S(2)}, u32[]{:S(2)}) async-start(bf16[8,64,768]{2,1,0:T(8,128)(2,1)} %reshape.236), calls=%async_computation | async-start | bytes 1572864 | tf_op jit(solution)/shard_map/all_to_all | solution.py:334
  14.0 57.0 %collective-permute-start.2 = (bf16[128,2048]{1,0:T(8,128)(2,1)}, bf16[128,2048]{1,0:T(8,128)(2,1)}, u32[]{:S(2)}, u32[]{:S(2)}) collective-permute-start(bf16[128,2048]{1,0:T(8,128)(2,1)} %get-tuple-element.128), channel_id=1, source_target_pairs={{0,8},{8,16},{16,24},{24,28},{28,20},{20,12},{12,4},{4,0},{1,9},{9... | collective-permute-start | bytes 1572872 | tf_op jit(solution)/shard_map/ppermute | solution.py:42
  16.0 57.4 %collective-permute-start.3 = (bf16[128,2048]{1,0:T(8,128)(2,1)}, bf16[128,2048]{1,0:T(8,128)(2,1)}, u32[]{:S(2)}, u32[]{:S(2)}) collective-permute-start(bf16[128,2048]{1,0:T(8,128)(2,1)} %get-tuple-element.128), channel_id=1, source_target_pairs={{8,0},{16,8},{24,16},{28,24},{20,28},{12,20},{4,12},{0,4},{9,1},{1... | collective-permute-start | bytes 1572872 | tf_op jit(solution)/shard_map/ppermute | solution.py:45
  16.0 57.4 %collective-permute-start.37 = (bf16[128,2048]{1,0:T(8,128)(2,1)S(1)}, bf16[128,2048]{1,0:T(8,128)(2,1)}, u32[]{:S(2)}, u32[]{:S(2)}) collective-permute-start(bf16[128,2048]{1,0:T(8,128)(2,1)S(1)} %bitcast.401), channel_id=1, source_target_pairs={{0,8},{8,16},{16,24},{24,28},{28,20},{20,12},{12,4},{4,0},{1,9},{9... | collective-permute-start | bytes 1572872 | tf_op jit(solution)/shard_map/ppermute | solution.py:42
  18.0 57.5 %collective-permute-start.34 = (bf16[128,2048]{1,0:T(8,128)(2,1)S(1)}, bf16[128,2048]{1,0:T(8,128)(2,1)}, u32[]{:S(2)}, u32[]{:S(2)}) collective-permute-start(bf16[128,2048]{1,0:T(8,128)(2,1)S(1)} %bitcast.402), channel_id=1, source_target_pairs={{8,0},{16,8},{24,16},{28,24},{20,28},{12,20},{4,12},{0,4},{9,1},{1... | collective-permute-start | bytes 1572872 | tf_op jit(solution)/shard_map/ppermute | solution.py:45
  61.9 16.0 %collective-permute-start = (bf16[1,8,64,768]{3,2,1,0:T(8,128)(2,1)}, bf16[1,8,64,768]{3,2,1,0:T(8,128)(2,1)}, u32[]{:S(2)}, u32[]{:S(2)}) collective-permute-start(bf16[1,8,64,768]{3,2,1,0:T(8,128)(2,1)} %bitcast.4), channel_id=1, source_target_pairs={{0,2},{1,3},{2,0},{3,1},{4,6},{5,7},{6,4},{7,5},{8,10},{9,11},{10,... | collective-permute-start | bytes 2359304 | tf_op jit(solution)/shard_map/ppermute | solution.py:71
  70.9 15.2 %collective-permute-start.4 = (bf16[128,2048]{1,0:T(8,128)(2,1)}, bf16[128,2048]{1,0:T(8,128)(2,1)S(1)}, u32[]{:S(2)}, u32[]{:S(2)}) collective-permute-start(bf16[128,2048]{1,0:T(8,128)(2,1)} %collective-permute-done.2), channel_id=1, source_target_pairs={{0,8},{8,16},{16,24},{24,28},{28,20},{20,12},{12,4},{4,0},{1,9},{9... | collective-permute-start | bytes 1572872 | tf_op jit(solution)/shard_map/ppermute | solution.py:42
  73.4 15.1 %collective-permute-start.5 = (bf16[128,2048]{1,0:T(8,128)(2,1)}, bf16[128,2048]{1,0:T(8,128)(2,1)S(1)}, u32[]{:S(2)}, u32[]{:S(2)}) collective-permute-start(bf16[128,2048]{1,0:T(8,128)(2,1)} %collective-permute-done.3), channel_id=1, source_target_pairs={{8,0},{16,8},{24,16},{28,24},{20,28},{12,20},{4,12},{0,4},{9,1},{1... | collective-permute-start | bytes 1572872 | tf_op jit(solution)/shard_map/ppermute | solution.py:45
  73.4 23.9 %collective-permute-start.38 = (bf16[128,2048]{1,0:T(8,128)(2,1)}, bf16[128,2048]{1,0:T(8,128)(2,1)S(1)}, u32[]{:S(2)}, u32[]{:S(2)}) collective-permute-start(bf16[128,2048]{1,0:T(8,128)(2,1)} %collective-permute-done.37), channel_id=1, source_target_pairs={{0,8},{8,16},{16,24},{24,28},{28,20},{20,12},{12,4},{4,0},{1,9},{9... | collective-permute-start | bytes 1572872 | tf_op jit(solution)/shard_map/ppermute | solution.py:42
  75.5 24.3 %collective-permute-start.35 = (bf16[128,2048]{1,0:T(8,128)(2,1)}, bf16[128,2048]{1,0:T(8,128)(2,1)S(1)}, u32[]{:S(2)}, u32[]{:S(2)}) collective-permute-start(bf16[128,2048]{1,0:T(8,128)(2,1)} %collective-permute-done.34), channel_id=1, source_target_pairs={{8,0},{16,8},{24,16},{28,24},{20,28},{12,20},{4,12},{0,4},{9,1},{1... | collective-permute-start | bytes 1572872 | tf_op jit(solution)/shard_map/ppermute | solution.py:45
  79.5 48.0 %collective-permute-start.1 = (bf16[2,8,64,768]{3,2,1,0:T(8,128)(2,1)S(1)}, bf16[2,8,64,768]{3,2,1,0:T(8,128)(2,1)S(1)}, u32[]{:S(2)}, u32[]{:S(2)}) collective-permute-start(bf16[2,8,64,768]{3,2,1,0:T(8,128)(2,1)S(1)} %maximum_bitcast_fusion), channel_id=1, source_target_pairs={{0,1},{1,0},{2,3},{3,2},{4,5},{5,4},{6,7},{7,6},{8,9},{9,8},{10,11... | collective-permute-start | bytes 4718600 | tf_op jit(solution)/shard_map/ppermute | solution.py:71
  86.1 24.9 %collective-permute-start.6 = (bf16[128,2048]{1,0:T(8,128)(2,1)S(1)}, bf16[128,2048]{1,0:T(8,128)(2,1)S(1)}, u32[]{:S(2)}, u32[]{:S(2)}) collective-permute-start(bf16[128,2048]{1,0:T(8,128)(2,1)S(1)} %collective-permute-done.4), channel_id=1, source_target_pairs={{0,8},{8,16},{16,24},{24,28},{28,20},{20,12},{12,4},{4,0},{1,9},{9... | collective-permute-start | bytes 1572872 | tf_op jit(solution)/shard_map/ppermute | solution.py:42
  88.5 22.5 %collective-permute-start.7 = (bf16[128,2048]{1,0:T(8,128)(2,1)S(1)}, bf16[128,2048]{1,0:T(8,128)(2,1)S(1)}, u32[]{:S(2)}, u32[]{:S(2)}) collective-permute-start(bf16[128,2048]{1,0:T(8,128)(2,1)S(1)} %collective-permute-done.5), channel_id=1, source_target_pairs={{8,0},{16,8},{24,16},{28,24},{20,28},{12,20},{4,12},{0,4},{9,1},{1... | collective-permute-start | bytes 1572872 | tf_op jit(solution)/shard_map/ppermute | solution.py:45
  97.4 25.6 %collective-permute-start.39 = (bf16[128,2048]{1,0:T(8,128)(2,1)S(1)}, bf16[128,2048]{1,0:T(8,128)(2,1)S(1)}, u32[]{:S(2)}, u32[]{:S(2)}) collective-permute-start(bf16[128,2048]{1,0:T(8,128)(2,1)S(1)} %collective-permute-done.38), channel_id=1, source_target_pairs={{0,8},{8,16},{16,24},{24,28},{28,20},{20,12},{12,4},{4,0},{1,9},{9... | collective-permute-start | bytes 1572872 | tf_op jit(solution)/shard_map/ppermute | solution.py:42
  99.7 22.3 %collective-permute-start.36 = (bf16[128,2048]{1,0:T(8,128)(2,1)S(1)}, bf16[128,2048]{1,0:T(8,128)(2,1)S(1)}, u32[]{:S(2)}, u32[]{:S(2)}) collective-permute-start(bf16[128,2048]{1,0:T(8,128)(2,1)S(1)} %collective-permute-done.35), channel_id=1, source_target_pairs={{8,0},{16,8},{24,16},{28,24},{20,28},{12,20},{4,12},{0,4},{9,1},{1... | collective-permute-start | bytes 1572872 | tf_op jit(solution)/shard_map/ppermute | solution.py:45
  111.0 24.4 %collective-permute-start.9 = (bf16[64,2048]{1,0:T(8,128)(2,1)S(1)}, bf16[64,2048]{1,0:T(8,128)(2,1)S(1)}, u32[]{:S(2)}, u32[]{:S(2)}) collective-permute-start(bf16[64,2048]{1,0:T(8,128)(2,1)S(1)} %slice.134), channel_id=1, source_target_pairs={{8,0},{16,8},{24,16},{28,24},{20,28},{12,20},{4,12},{0,4},{9,1},{1... | collective-permute-start | bytes 786440 | tf_op jit(solution)/shard_map/ppermute | solution.py:45
  111.1 24.3 %collective-permute-start.8 = (bf16[64,2048]{1,0:T(8,128)(2,1)S(1)}, bf16[64,2048]{1,0:T(8,128)(2,1)S(1)}, u32[]{:S(2)}, u32[]{:S(2)}) collective-permute-start(bf16[64,2048]{1,0:T(8,128)(2,1)S(1)} %slice.133), channel_id=1, source_target_pairs={{0,8},{8,16},{16,24},{24,28},{28,20},{20,12},{12,4},{4,0},{1,9},{9... | collective-permute-start | bytes 786440 | tf_op jit(solution)/shard_map/ppermute | solution.py:42
  122.8 144.2 %collective-permute-start.41 = (bf16[64,2048]{1,0:T(8,128)(2,1)}, bf16[64,2048]{1,0:T(8,128)(2,1)S(1)}, u32[]{:S(2)}, u32[]{:S(2)}) collective-permute-start(bf16[64,2048]{1,0:T(8,128)(2,1)} %slice.142), channel_id=1, source_target_pairs={{8,0},{16,8},{24,16},{28,24},{20,28},{12,20},{4,12},{0,4},{9,1},{1... | collective-permute-start | bytes 786440 | tf_op jit(solution)/shard_map/ppermute | solution.py:45
  123.7 143.3 %collective-permute-start.40 = (bf16[64,2048]{1,0:T(8,128)(2,1)}, bf16[64,2048]{1,0:T(8,128)(2,1)S(1)}, u32[]{:S(2)}, u32[]{:S(2)}) collective-permute-start(bf16[64,2048]{1,0:T(8,128)(2,1)} %slice.141), channel_id=1, source_target_pairs={{0,8},{8,16},{16,24},{24,28},{28,20},{20,12},{12,4},{4,0},{1,9},{9... | collective-permute-start | bytes 786440 | tf_op jit(solution)/shard_map/ppermute | solution.py:42
  220.3 13.8 %collective-permute-start.19 = (bf16[128,2048]{1,0:T(8,128)(2,1)S(1)}, bf16[128,2048]{1,0:T(8,128)(2,1)S(1)}, u32[]{:S(2)}, u32[]{:S(2)}) collective-permute-start(bf16[128,2048]{1,0:T(8,128)(2,1)S(1)} %collective-permute-done.18), channel_id=1, source_target_pairs={{8,0},{16,8},{24,16},{28,24},{20,28},{12,20},{4,12},{0,4},{9,1},{1... | collective-permute-start | bytes 1572872 | tf_op jit(solution)/shard_map/ppermute | solution.py:45
  270.6 52.5 %collective-permute-start.46 = (bf16[64,2048]{1,0:T(8,128)(2,1)}, bf16[64,2048]{1,0:T(8,128)(2,1)}, u32[]{:S(2)}, u32[]{:S(2)}) collective-permute-start(bf16[64,2048]{1,0:T(8,128)(2,1)} %get-tuple-element.198), channel_id=1, source_target_pairs={{8,0},{16,8},{24,16},{28,24},{20,28},{12,20},{4,12},{0,4},{9,1},{1... | collective-permute-start | bytes 786440 | tf_op jit(solution)/shard_map/ppermute | solution.py:45
  270.6 55.7 %collective-permute-start.42 = (bf16[64,2048]{1,0:T(8,128)(2,1)}, bf16[64,2048]{1,0:T(8,128)(2,1)S(1)}, u32[]{:S(2)}, u32[]{:S(2)}) collective-permute-start(bf16[64,2048]{1,0:T(8,128)(2,1)} %get-tuple-element.197), channel_id=1, source_target_pairs={{0,8},{8,16},{16,24},{24,28},{28,20},{20,12},{12,4},{4,0},{1,9},{9... | collective-permute-start | bytes 786440 | tf_op jit(solution)/shard_map/ppermute | solution.py:42
  274.1 52.9 %collective-permute-start.30 = (bf16[64,2048]{1,0:T(8,128)(2,1)}, bf16[64,2048]{1,0:T(8,128)(2,1)}, u32[]{:S(2)}, u32[]{:S(2)}) collective-permute-start(bf16[64,2048]{1,0:T(8,128)(2,1)} %get-tuple-element.200), channel_id=1, source_target_pairs={{8,0},{16,8},{24,16},{28,24},{20,28},{12,20},{4,12},{0,4},{9,1},{1... | collective-permute-start | bytes 786440 | tf_op jit(solution)/shard_map/ppermute | solution.py:45
  274.1 56.6 %collective-permute-start.26 = (bf16[64,2048]{1,0:T(8,128)(2,1)}, bf16[64,2048]{1,0:T(8,128)(2,1)}, u32[]{:S(2)}, u32[]{:S(2)}) collective-permute-start(bf16[64,2048]{1,0:T(8,128)(2,1)} %get-tuple-element.199), channel_id=1, source_target_pairs={{0,8},{8,16},{16,24},{24,28},{28,20},{20,12},{12,4},{4,0},{1,9},{9... | collective-permute-start | bytes 786440 | tf_op jit(solution)/shard_map/ppermute | solution.py:42
  300.5 76.8 %collective-permute-start.79 = (bf16[2,512,704]{1,2,0:T(8,128)(2,1)}, bf16[2,512,704]{1,2,0:T(8,128)(2,1)}, u32[]{:S(2)}, u32[]{:S(2)}) collective-permute-start(bf16[2,512,704]{1,2,0:T(8,128)(2,1)} %bitcast.368), channel_id=1, source_target_pairs={{0,1},{1,0},{2,3},{3,2},{4,5},{5,4},{6,7},{7,6},{8,9},{9,8},{10,11... | collective-permute-start | bytes 4325384 | tf_op jit(solution)/shard_map/ppermute | solution.py:71
  323.2 58.3 %collective-permute-start.83 = (bf16[2,512,704]{1,2,0:T(8,128)(2,1)S(1)}, bf16[2,512,704]{1,2,0:T(8,128)(2,1)S(1)}, u32[]{:S(2)}, u32[]{:S(2)}) collective-permute-start(bf16[2,512,704]{1,2,0:T(8,128)(2,1)S(1)} %bitcast.404), channel_id=1, source_target_pairs={{0,1},{1,0},{2,3},{3,2},{4,5},{5,4},{6,7},{7,6},{8,9},{9,8},{10,11... | collective-permute-start | bytes 4325384 | tf_op jit(solution)/shard_map/ppermute | solution.py:71
  326.4 14.9 %collective-permute-start.47 = (bf16[128,2048]{1,0:T(8,128)(2,1)S(1)}, bf16[128,2048]{1,0:T(8,128)(2,1)S(1)}, u32[]{:S(2)}, u32[]{:S(2)}) collective-permute-start(bf16[128,2048]{1,0:T(8,128)(2,1)S(1)} %add_convert_fusion.12), channel_id=1, source_target_pairs={{8,0},{16,8},{24,16},{28,24},{20,28},{12,20},{4,12},{0,4},{9,1},{1... | collective-permute-start | bytes 1572872 | tf_op jit(solution)/shard_map/ppermute | solution.py:45
  327.1 16.4 %collective-permute-start.43 = (bf16[128,2048]{1,0:T(8,128)(2,1)S(1)}, bf16[128,2048]{1,0:T(8,128)(2,1)S(1)}, u32[]{:S(2)}, u32[]{:S(2)}) collective-permute-start(bf16[128,2048]{1,0:T(8,128)(2,1)S(1)} %add_convert_fusion.15), channel_id=1, source_target_pairs={{0,8},{8,16},{16,24},{24,28},{28,20},{20,12},{12,4},{4,0},{1,9},{9... | collective-permute-start | bytes 1572872 | tf_op jit(solution)/shard_map/ppermute | solution.py:42
  330.8 21.7 %collective-permute-start.31 = (bf16[128,2048]{1,0:T(8,128)(2,1)S(1)}, bf16[128,2048]{1,0:T(8,128)(2,1)S(1)}, u32[]{:S(2)}, u32[]{:S(2)}) collective-permute-start(bf16[128,2048]{1,0:T(8,128)(2,1)S(1)} %add_convert_fusion.19), channel_id=1, source_target_pairs={{8,0},{16,8},{24,16},{28,24},{20,28},{12,20},{4,12},{0,4},{9,1},{1... | collective-permute-start | bytes 1572872 | tf_op jit(solution)/shard_map/ppermute | solution.py:45
  343.5 20.3 %collective-permute-start.48 = (bf16[128,2048]{1,0:T(8,128)(2,1)S(1)}, bf16[128,2048]{1,0:T(8,128)(2,1)S(1)}, u32[]{:S(2)}, u32[]{:S(2)}) collective-permute-start(bf16[128,2048]{1,0:T(8,128)(2,1)S(1)} %add_convert_fusion.11), channel_id=1, source_target_pairs={{8,0},{16,8},{24,16},{28,24},{20,28},{12,20},{4,12},{0,4},{9,1},{1... | collective-permute-start | bytes 1572872 | tf_op jit(solution)/shard_map/ppermute | solution.py:45
  354.7 20.3 %collective-permute-start.32 = (bf16[128,2048]{1,0:T(8,128)(2,1)S(1)}, bf16[128,2048]{1,0:T(8,128)(2,1)S(1)}, u32[]{:S(2)}, u32[]{:S(2)}) collective-permute-start(bf16[128,2048]{1,0:T(8,128)(2,1)S(1)} %add_convert_fusion.18), channel_id=1, source_target_pairs={{8,0},{16,8},{24,16},{28,24},{20,28},{12,20},{4,12},{0,4},{9,1},{1... | collective-permute-start | bytes 1572872 | tf_op jit(solution)/shard_map/ppermute | solution.py:45
  366.1 20.1 %collective-permute-start.49 = (bf16[128,2048]{1,0:T(8,128)(2,1)S(1)}, bf16[128,2048]{1,0:T(8,128)(2,1)S(1)}, u32[]{:S(2)}, u32[]{:S(2)}) collective-permute-start(bf16[128,2048]{1,0:T(8,128)(2,1)S(1)} %add_convert_fusion.10), channel_id=1, source_target_pairs={{8,0},{16,8},{24,16},{28,24},{20,28},{12,20},{4,12},{0,4},{9,1},{1... | collective-permute-start | bytes 1572872 | tf_op jit(solution)/shard_map/ppermute | solution.py:45
  375.0 14.9 %collective-permute-start.45 = (bf16[128,2048]{1,0:T(8,128)(2,1)S(1)}, bf16[128,2048]{1,0:T(8,128)(2,1)S(1)}, u32[]{:S(2)}, u32[]{:S(2)}) collective-permute-start(bf16[128,2048]{1,0:T(8,128)(2,1)S(1)} %add_convert_fusion.13), channel_id=1, source_target_pairs={{0,8},{8,16},{16,24},{24,28},{28,20},{20,12},{12,4},{4,0},{1,9},{9... | collective-permute-start | bytes 1572872 | tf_op jit(solution)/shard_map/ppermute | solution.py:42
  377.1 18.9 %collective-permute-start.33 = (bf16[128,2048]{1,0:T(8,128)(2,1)S(1)}, bf16[128,2048]{1,0:T(8,128)(2,1)S(1)}, u32[]{:S(2)}, u32[]{:S(2)}) collective-permute-start(bf16[128,2048]{1,0:T(8,128)(2,1)S(1)} %add_convert_fusion.17), channel_id=1, source_target_pairs={{8,0},{16,8},{24,16},{28,24},{20,28},{12,20},{4,12},{0,4},{9,1},{1... | collective-permute-start | bytes 1572872 | tf_op jit(solution)/shard_map/ppermute | solution.py:45
  377.3 20.2 %collective-permute-start.29 = (bf16[128,2048]{1,0:T(8,128)(2,1)S(1)}, bf16[128,2048]{1,0:T(8,128)(2,1)S(1)}, u32[]{:S(2)}, u32[]{:S(2)}) collective-permute-start(bf16[128,2048]{1,0:T(8,128)(2,1)S(1)} %add_convert_fusion.20), channel_id=1, source_target_pairs={{0,8},{8,16},{16,24},{24,28},{28,20},{20,12},{12,4},{4,0},{1,9},{9... | collective-permute-start | bytes 1572872 | tf_op jit(solution)/shard_map/ppermute | solution.py:42
  381.5 29.5 %collective-permute-start.80 = (bf16[1,512,704]{1,2,0:T(8,128)(2,1)S(1)}, bf16[1,512,704]{1,2,0:T(8,128)(2,1)S(1)}, u32[]{:S(2)}, u32[]{:S(2)}) collective-permute-start(bf16[1,512,704]{1,2,0:T(8,128)(2,1)S(1)} %dynamic-slice_convert_fusion.3), channel_id=1, source_target_pairs={{0,2},{1,3},{2,0},{3,1},{4,6},{5,7},{6,4},{7,5},{8,10},{9,11},{10,... | collective-permute-start | bytes 2162696 | tf_op jit(solution)/shard_map/ppermute | solution.py:71
  386.2 25.6 %collective-permute-start.84 = (bf16[1,512,704]{1,2,0:T(8,128)(2,1)S(1)}, bf16[1,512,704]{1,2,0:T(8,128)(2,1)S(1)}, u32[]{:S(2)}, u32[]{:S(2)}) collective-permute-start(bf16[1,512,704]{1,2,0:T(8,128)(2,1)S(1)} %dynamic-slice_convert_fusion.2), channel_id=1, source_target_pairs={{0,2},{1,3},{2,0},{3,1},{4,6},{5,7},{6,4},{7,5},{8,10},{9,11},{10,... | collective-permute-start | bytes 2162696 | tf_op jit(solution)/shard_map/ppermute | solution.py:71
  410.9 39.1 %collective-permute-start.87 = (bf16[2,176,2048]{2,1,0:T(8,128)(2,1)S(1)}, bf16[2,176,2048]{2,1,0:T(8,128)(2,1)S(1)}, u32[]{:S(2)}, u32[]{:S(2)}) collective-permute-start(bf16[2,176,2048]{2,1,0:T(8,128)(2,1)S(1)} %dynamic-slice_bitcast_fusion.1), channel_id=1, source_target_pairs={{0,1},{1,0},{2,3},{3,2},{4,5},{5,4},{6,7},{7,6},{8,9},{9,8},{10,11... | collective-permute-start | bytes 4325384 | tf_op jit(solution)/shard_map/ppermute | solution.py:71
  411.2 19.0 %collective-permute-start.81 = (bf16[1,512,704]{1,2,0:T(8,128)(2,1)S(1)}, bf16[1,512,704]{1,2,0:T(8,128)(2,1)S(1)}, u32[]{:S(2)}, u32[]{:S(2)}) collective-permute-start(bf16[1,512,704]{1,2,0:T(8,128)(2,1)S(1)} %add_convert_fusion.3), channel_id=1, source_target_pairs={{0,2},{1,3},{2,0},{3,1},{4,6},{5,7},{6,4},{7,5},{8,10},{9,11},{10,... | collective-permute-start | bytes 2162696 | tf_op jit(solution)/shard_map/ppermute | solution.py:71
  412.1 33.2 %collective-permute-start.85 = (bf16[1,512,704]{1,2,0:T(8,128)(2,1)S(1)}, bf16[1,512,704]{1,2,0:T(8,128)(2,1)S(1)}, u32[]{:S(2)}, u32[]{:S(2)}) collective-permute-start(bf16[1,512,704]{1,2,0:T(8,128)(2,1)S(1)} %add_convert_fusion.2), channel_id=1, source_target_pairs={{0,2},{1,3},{2,0},{3,1},{4,6},{5,7},{6,4},{7,5},{8,10},{9,11},{10,... | collective-permute-start | bytes 2162696 | tf_op jit(solution)/shard_map/ppermute | solution.py:71
  413.7 33.2 %collective-permute-start.52 = (bf16[128,2048]{1,0:T(8,128)(2,1)S(1)}, bf16[128,2048]{1,0:T(8,128)(2,1)S(1)}, u32[]{:S(2)}, u32[]{:S(2)}) collective-permute-start(bf16[128,2048]{1,0:T(8,128)(2,1)S(1)} %collective-permute-done.50), channel_id=1, source_target_pairs={{0,8},{8,16},{16,24},{24,28},{28,20},{20,12},{12,4},{4,0},{1,9},{9... | collective-permute-start | bytes 1572872 | tf_op jit(solution)/shard_map/ppermute | solution.py:42
  415.6 32.7 %collective-permute-start.53 = (bf16[128,2048]{1,0:T(8,128)(2,1)S(1)}, bf16[128,2048]{1,0:T(8,128)(2,1)S(1)}, u32[]{:S(2)}, u32[]{:S(2)}) collective-permute-start(bf16[128,2048]{1,0:T(8,128)(2,1)S(1)} %collective-permute-done.51), channel_id=1, source_target_pairs={{8,0},{16,8},{24,16},{28,24},{20,28},{12,20},{4,12},{0,4},{9,1},{1... | collective-permute-start | bytes 1572872 | tf_op jit(solution)/shard_map/ppermute | solution.py:45
  431.7 87.9 %collective-permute-start.82 = (bf16[2,512,704]{1,2,0:T(8,128)(2,1)}, bf16[2,512,704]{1,2,0:T(8,128)(2,1)}, u32[]{:S(2)}, u32[]{:S(2)}) collective-permute-start(bf16[2,512,704]{1,2,0:T(8,128)(2,1)} %maximum_bitcast_fusion.2), channel_id=1, source_target_pairs={{0,1},{1,0},{2,3},{3,2},{4,5},{5,4},{6,7},{7,6},{8,9},{9,8},{10,11... | collective-permute-start | bytes 4325384 | tf_op jit(solution)/shard_map/ppermute | solution.py:71
  446.9 75.1 %collective-permute-start.86 = (bf16[2,512,704]{1,2,0:T(8,128)(2,1)}, bf16[2,512,704]{1,2,0:T(8,128)(2,1)}, u32[]{:S(2)}, u32[]{:S(2)}) collective-permute-start(bf16[2,512,704]{1,2,0:T(8,128)(2,1)} %maximum_bitcast_fusion.3), channel_id=1, source_target_pairs={{0,1},{1,0},{2,3},{3,2},{4,5},{5,4},{6,7},{7,6},{8,9},{9,8},{10,11... | collective-permute-start | bytes 4325384 | tf_op jit(solution)/shard_map/ppermute | solution.py:71
  446.9 16.2 %collective-permute-start.54 = (bf16[128,2048]{1,0:T(8,128)(2,1)S(1)}, bf16[128,2048]{1,0:T(8,128)(2,1)S(1)}, u32[]{:S(2)}, u32[]{:S(2)}) collective-permute-start(bf16[128,2048]{1,0:T(8,128)(2,1)S(1)} %collective-permute-done.52), channel_id=1, source_target_pairs={{0,8},{8,16},{16,24},{24,28},{28,20},{20,12},{12,4},{4,0},{1,9},{9... | collective-permute-start | bytes 1572872 | tf_op jit(solution)/shard_map/ppermute | solution.py:42
  448.3 14.1 %collective-permute-start.55 = (bf16[128,2048]{1,0:T(8,128)(2,1)S(1)}, bf16[128,2048]{1,0:T(8,128)(2,1)S(1)}, u32[]{:S(2)}, u32[]{:S(2)}) collective-permute-start(bf16[128,2048]{1,0:T(8,128)(2,1)S(1)} %collective-permute-done.53), channel_id=1, source_target_pairs={{8,0},{16,8},{24,16},{28,24},{20,28},{12,20},{4,12},{0,4},{9,1},{1... | collective-permute-start | bytes 1572872 | tf_op jit(solution)/shard_map/ppermute | solution.py:45
  451.7 63.6 %collective-permute-start.88 = (bf16[1,176,2048]{2,1,0:T(8,128)(2,1)}, bf16[1,176,2048]{2,1,0:T(8,128)(2,1)}, u32[]{:S(2)}, u32[]{:S(2)}) collective-permute-start(bf16[1,176,2048]{2,1,0:T(8,128)(2,1)} %dynamic-slice_convert_fusion.1), channel_id=1, source_target_pairs={{0,2},{1,3},{2,0},{3,1},{4,6},{5,7},{6,4},{7,5},{8,10},{9,11},{10,... | collective-permute-start | bytes 2162696 | tf_op jit(solution)/shard_map/ppermute | solution.py:71
  493.4 14.6 %collective-permute-start.62 = (bf16[64,2048]{1,0:T(8,128)(2,1)}, bf16[64,2048]{1,0:T(8,128)(2,1)}, u32[]{:S(2)}, u32[]{:S(2)}) collective-permute-start(bf16[64,2048]{1,0:T(8,128)(2,1)} %get-tuple-element.196), channel_id=1, source_target_pairs={{8,0},{16,8},{24,16},{28,24},{20,28},{12,20},{4,12},{0,4},{9,1},{1... | collective-permute-start | bytes 786440 | tf_op jit(solution)/shard_map/ppermute | solution.py:45
  494.0 19.2 %collective-permute-start.58 = (bf16[64,2048]{1,0:T(8,128)(2,1)}, bf16[64,2048]{1,0:T(8,128)(2,1)S(1)}, u32[]{:S(2)}, u32[]{:S(2)}) collective-permute-start(bf16[64,2048]{1,0:T(8,128)(2,1)} %get-tuple-element.195), channel_id=1, source_target_pairs={{0,8},{8,16},{16,24},{24,28},{28,20},{20,12},{12,4},{4,0},{1,9},{9... | collective-permute-start | bytes 786440 | tf_op jit(solution)/shard_map/ppermute | solution.py:42
  508.0 69.3 %collective-permute-start.71 = (bf16[2,8,64,768]{3,2,1,0:T(8,128)(2,1)}, bf16[2,8,64,768]{3,2,1,0:T(8,128)(2,1)}, u32[]{:S(2)}, u32[]{:S(2)}) collective-permute-start(bf16[2,8,64,768]{3,2,1,0:T(8,128)(2,1)} %dynamic-slice_bitcast_fusion), channel_id=1, source_target_pairs={{0,1},{1,0},{2,3},{3,2},{4,5},{5,4},{6,7},{7,6},{8,9},{9,8},{10,11... | collective-permute-start | bytes 4718600 | tf_op jit(solution)/shard_map/ppermute | solution.py:71
  515.3 47.0 %collective-permute-start.63 = (bf16[128,2048]{1,0:T(8,128)(2,1)}, bf16[128,2048]{1,0:T(8,128)(2,1)S(1)}, u32[]{:S(2)}, u32[]{:S(2)}) collective-permute-start(bf16[128,2048]{1,0:T(8,128)(2,1)} %add_convert_fusion.6), channel_id=1, source_target_pairs={{8,0},{16,8},{24,16},{28,24},{20,28},{12,20},{4,12},{0,4},{9,1},{1... | collective-permute-start | bytes 1572872 | tf_op jit(solution)/shard_map/ppermute | solution.py:45
  517.2 45.8 %collective-permute-start.59 = (bf16[128,2048]{1,0:T(8,128)(2,1)}, bf16[128,2048]{1,0:T(8,128)(2,1)}, u32[]{:S(2)}, u32[]{:S(2)}) collective-permute-start(bf16[128,2048]{1,0:T(8,128)(2,1)} %add_convert_fusion.9), channel_id=1, source_target_pairs={{0,8},{8,16},{16,24},{24,28},{28,20},{20,12},{12,4},{4,0},{1,9},{9... | collective-permute-start | bytes 1572872 | tf_op jit(solution)/shard_map/ppermute | solution.py:42
  519.9 47.4 %collective-permute-start.89 = (bf16[1,176,2048]{2,1,0:T(8,128)(2,1)S(1)}, bf16[1,176,2048]{2,1,0:T(8,128)(2,1)}, u32[]{:S(2)}, u32[]{:S(2)}) collective-permute-start(bf16[1,176,2048]{2,1,0:T(8,128)(2,1)S(1)} %add_convert_fusion.1), channel_id=1, source_target_pairs={{0,2},{1,3},{2,0},{3,1},{4,6},{5,7},{6,4},{7,5},{8,10},{9,11},{10,... | collective-permute-start | bytes 2162696 | tf_op jit(solution)/shard_map/ppermute | solution.py:71
  522.0 43.7 %collective-permute-start.76 = (bf16[1,64,2048]{2,1,0:T(8,128)(2,1)}, bf16[1,64,2048]{2,1,0:T(8,128)(2,1)}, u32[]{:S(2)}, u32[]{:S(2)}) collective-permute-start(bf16[1,64,2048]{2,1,0:T(8,128)(2,1)} %dynamic-slice_convert_fusion.4), channel_id=1, source_target_pairs={{0,2},{1,3},{2,0},{3,1},{4,6},{5,7},{6,4},{7,5},{8,10},{9,11},{10,... | collective-permute-start | bytes 786440 | tf_op jit(solution)/shard_map/ppermute | solution.py:71
  564.2 15.6 %collective-permute-start.60 = (bf16[128,2048]{1,0:T(8,128)(2,1)S(1)}, bf16[128,2048]{1,0:T(8,128)(2,1)S(1)}, u32[]{:S(2)}, u32[]{:S(2)}) collective-permute-start(bf16[128,2048]{1,0:T(8,128)(2,1)S(1)} %add_convert_fusion.8), channel_id=1, source_target_pairs={{0,8},{8,16},{16,24},{24,28},{28,20},{20,12},{12,4},{4,0},{1,9},{9... | collective-permute-start | bytes 1572872 | tf_op jit(solution)/shard_map/ppermute | solution.py:42
  566.7 15.5 %collective-permute-start.77 = (bf16[1,64,2048]{2,1,0:T(8,128)(2,1)S(1)}, bf16[1,64,2048]{2,1,0:T(8,128)(2,1)S(1)}, u32[]{:S(2)}, u32[]{:S(2)}) collective-permute-start(bf16[1,64,2048]{2,1,0:T(8,128)(2,1)S(1)} %add_convert_fusion.30), channel_id=1, source_target_pairs={{0,2},{1,3},{2,0},{3,1},{4,6},{5,7},{6,4},{7,5},{8,10},{9,11},{10,... | collective-permute-start | bytes 786440 | tf_op jit(solution)/shard_map/ppermute | solution.py:71
  569.7 81.4 %collective-permute-start.90 = (bf16[2,176,2048]{2,1,0:T(8,128)(2,1)}, bf16[2,176,2048]{2,1,0:T(8,128)(2,1)}, u32[]{:S(2)}, u32[]{:S(2)}) collective-permute-start(bf16[2,176,2048]{2,1,0:T(8,128)(2,1)} %maximum_bitcast_fusion.4), channel_id=1, source_target_pairs={{0,1},{1,0},{2,3},{3,2},{4,5},{5,4},{6,7},{7,6},{8,9},{9,8},{10,11... | collective-permute-start | bytes 4325384 | tf_op jit(solution)/shard_map/ppermute | solution.py:71
  576.7 25.9 %collective-permute-start.65 = (bf16[128,2048]{1,0:T(8,128)(2,1)}, bf16[128,2048]{1,0:T(8,128)(2,1)}, u32[]{:S(2)}, u32[]{:S(2)}) collective-permute-start(bf16[128,2048]{1,0:T(8,128)(2,1)} %add_convert_fusion.4), channel_id=1, source_target_pairs={{8,0},{16,8},{24,16},{28,24},{20,28},{12,20},{4,12},{0,4},{9,1},{1... | collective-permute-start | bytes 1572872 | tf_op jit(solution)/shard_map/ppermute | solution.py:45
  579.2 17.8 %collective-permute-start.72 = (bf16[1,8,64,768]{3,2,1,0:T(8,128)(2,1)S(1)}, bf16[1,8,64,768]{3,2,1,0:T(8,128)(2,1)S(1)}, u32[]{:S(2)}, u32[]{:S(2)}) collective-permute-start(bf16[1,8,64,768]{3,2,1,0:T(8,128)(2,1)S(1)} %dynamic-slice_convert_fusion), channel_id=1, source_target_pairs={{0,2},{1,3},{2,0},{3,1},{4,6},{5,7},{6,4},{7,5},{8,10},{9,11},{10,... | collective-permute-start | bytes 2359304 | tf_op jit(solution)/shard_map/ppermute | solution.py:71
  580.7 22.0 %collective-permute-start.61 = (bf16[128,2048]{1,0:T(8,128)(2,1)}, bf16[128,2048]{1,0:T(8,128)(2,1)}, u32[]{:S(2)}, u32[]{:S(2)}) collective-permute-start(bf16[128,2048]{1,0:T(8,128)(2,1)} %add_convert_fusion.7), channel_id=1, source_target_pairs={{0,8},{8,16},{16,24},{24,28},{28,20},{20,12},{12,4},{4,0},{1,9},{9... | collective-permute-start | bytes 1572872 | tf_op jit(solution)/shard_map/ppermute | solution.py:42
  583.1 24.4 %collective-permute-start.78 = (bf16[2,64,2048]{2,1,0:T(8,128)(2,1)}, bf16[2,64,2048]{2,1,0:T(8,128)(2,1)}, u32[]{:S(2)}, u32[]{:S(2)}) collective-permute-start(bf16[2,64,2048]{2,1,0:T(8,128)(2,1)} %maximum_bitcast_fusion.5), channel_id=1, source_target_pairs={{0,1},{1,0},{2,3},{3,2},{4,5},{5,4},{6,7},{7,6},{8,9},{9,8},{10,11... | collective-permute-start | bytes 1572872 | tf_op jit(solution)/shard_map/ppermute | solution.py:71
  598.1 22.6 %all-to-all-start.1 = ((bf16[8,64,768]{2,1,0:T(8,128)(2,1)}), bf16[8,64,768]{2,1,0:T(8,128)(2,1)}, u32[]{:S(2)}, u32[]{:S(2)}) async-start(bf16[8,64,768]{2,1,0:T(8,128)(2,1)} %fusion.38), calls=%async_computation.1 | async-start | bytes 1572864 | tf_op jit(solution)/shard_map/all_to_all | solution.py:405
  612.9 19.6 %collective-permute-start.67 = (f32[112,128]{1,0:T(8,128)}, f32[112,128]{1,0:T(8,128)}, u32[]{:S(2)}, u32[]{:S(2)}) collective-permute-start(f32[112,128]{1,0:T(8,128)} %bitcast_add_fusion), channel_id=1, source_target_pairs={{0,8},{4,12},{8,0},{12,4},{16,24},{20,28},{24,16},{28,20},{1,9},{5... | collective-permute-start | bytes 172040 | tf_op jit(solution)/shard_map/ppermute | solution.py:71
  629.2 17.7 %collective-permute-start.73 = (bf16[1,64,6144]{2,1,0:T(8,128)(2,1)}, bf16[1,64,6144]{2,1,0:T(8,128)(2,1)S(1)}, u32[]{:S(2)}, u32[]{:S(2)}) collective-permute-start(bf16[1,64,6144]{2,1,0:T(8,128)(2,1)} %broadcast_in_dim_reshape.2), channel_id=1, source_target_pairs={{0,2},{1,3},{2,0},{3,1},{4,6},{5,7},{6,4},{7,5},{8,10},{9,11},{10,... | collective-permute-start | bytes 2359304 | tf_op jit(solution)/shard_map/ppermute | solution.py:71
  (129 other events, 1951.0 us)

commit v2 on v1

v2 whole, which is shorter than its diff:
```python
import functools

import jax
import jax.numpy as jnp
import numpy as np
from jax import lax
from jax.experimental import pallas as pl
from jax.experimental.pallas import tpu as pltpu
from jax.sharding import PartitionSpec as P

HEADS = 32
HEAD_DIM = 64
ROT = 16
BLOCK = 128
TILE = 256

eps_norm = 1e-05
theta_base = 10000.0
masked_score = -1e30
bf16 = jnp.bfloat16
f32 = jnp.float32


def ring_order(n):
    return [0, 2, 4, 6, 7, 5, 3, 1] if n == 8 else list(range(n))


class Ring:
    def __init__(self, axis):
        self.axis = axis
        self.n = n = lax.axis_size(axis)
        order = ring_order(n)
        self.ahead = [(order[i], order[(i + 1) % n]) for i in range(n)]
        self.behind = [(b, a) for a, b in self.ahead]
        half = n // 2
        table = np.zeros((n, 2 * n), np.int32)
        for i, device in enumerate(order):
            for slot in range(n):
                step = -((slot + 1) // 2) if slot % 2 and slot < n - 1 else slot // 2 if slot < n - 1 else half
                natural = order[(i + step) % n]
                table[device, natural], table[device, n + slot] = slot, natural
        self.table = jnp.asarray(table)

    def up(self, v):
        return lax.ppermute(v, self.axis, self.ahead)

    def down(self, v):
        return lax.ppermute(v, self.axis, self.behind)


class Gather:
    def __init__(self, ring, line, v):
        self.ring, self.line, self.d = ring, line, 1
        self.half = v.shape[0] // 2
        self.blocks = [v]
        self.flying = ring.up(v), ring.down(v)

    def step(self):
        got = self.line(lambda *v: v, *self.flying)
        self.blocks += got
        self.d += 1
        last = self.ring.n // 2
        if self.d < last:
            self.flying = self.ring.up(got[0]), self.ring.down(got[1])
        elif self.d == last:
            top, bottom = halves(*got)
            self.flying = self.ring.up(top), self.ring.down(bottom)
        return got


class Line:
    def __init__(self):
        self.last = ()

    def __call__(self, work, *given):
        given, _ = lax.optimization_barrier((given, self.last))
        out = work(*given)
        self.last = out
        return out


def swap(v, axis, bit):
    n = lax.axis_size(axis)
    return lax.ppermute(v, axis, [(i, i ^ bit) for i in range(n)])


def bits_of(n):
    return [1 << i for i in range(n.bit_length() - 1)]


def after(v, *others):
    return lax.optimization_barrier((v, *others))[0]


class Places:
    def __init__(self, model):
        u = functools.partial(jnp.asarray, dtype=jnp.uint32)
        seq, batch = lax.axis_index("seq").astype(jnp.uint32), lax.axis_index("batch").astype(jnp.uint32)
        core, y = batch % u(2), batch // u(2)
        self.seq = seq
        self.quarter = [batch ^ u(k) for k in range(4)]
        self.order = [(q % u(2)) * u(2) + q // u(2) for q in self.quarter]
        self.starts = {
            (name, size): which * u(size)
            for name, which in (("core", core), ("across", u(1) - core), ("y", y), ("other", u(1) - y))
            for size in (model // 2, model // 4)
        }
        for name in ("y", "other"):
            self.starts["mine " + name, model // 4] = (
                self.starts["core", model // 2] + self.starts[name, model // 4]
            )
        self.column_place = jnp.stack([(core * u(2) + y) ^ u(k) for k in range(4)]).astype(jnp.int32)
        self.row_place = jnp.stack([batch ^ u(k) for k in (0, 2, 1, 3)]).astype(jnp.int32)
        peers = [seq ^ u(k) for k in range(lax.axis_size("seq"))]
        self.peers = jnp.stack([batch, *peers]).astype(jnp.int32)

    def scalars(self):
        return [self.seq, *self.quarter, *self.order, *self.starts.values(), self.column_place, self.row_place, self.peers]

    def tied(self, scalars):
        self.seq, self.quarter, self.order = scalars[0], scalars[1:5], scalars[5:9]
        self.starts = dict(zip(self.starts, scalars[9:-3], strict=True))
        self.column_place, self.row_place, self.peers = scalars[-3:]

    def side(self, v, which, parts=2):
        size = v.shape[1] // parts
        return lax.dynamic_slice(v, (jnp.uint32(0), self.starts[which, size]), (v.shape[0], size))


def pick(v, index, axis):
    starts = [jnp.uint32(0)] * v.ndim
    starts[axis] = index
    sizes = list(v.shape)
    sizes[axis] = 1
    return lax.squeeze(lax.dynamic_slice(v, starts, sizes), (axis,))


def norm_parts(values, gain_vector, shift_vector):
    mean_value = jnp.mean(values, axis=-1, keepdims=True)
    centred = values - mean_value
    inverse = lax.rsqrt(jnp.mean(centred * centred, axis=-1, keepdims=True) + eps_norm)
    unit_value = centred * inverse
    return (unit_value * gain_vector + shift_vector, unit_value, inverse)


def norm_back(gradient, unit_value, inverse, gain_vector):
    scaled = gradient * gain_vector
    return inverse * (
        scaled
        - jnp.mean(scaled, axis=-1, keepdims=True)
        - unit_value * jnp.mean(scaled * unit_value, axis=-1, keepdims=True)
    )


def dot(a, b):
    return jnp.dot(a, b, preferred_element_type=f32)


def dot_rows(a, b):
    return lax.dot_general(a, b, (((0,), (0,)), ((), ())), preferred_element_type=f32)


def dot_last(a, b):
    return lax.dot_general(a, b, (((1,), (1,)), ((), ())), preferred_element_type=f32)


def rotary_waves(positions):
    half = ROT // 2
    frequency = theta_base ** (-(jnp.arange(half, dtype=f32) * 2.0 / ROT))
    angles = frequency[:, None] * positions
    return jnp.concatenate([jnp.cos(angles), jnp.sin(angles)], 0)


def fill_table(table_ref, waves_ref):
    half = ROT // 2
    for start in range(0, table_ref.shape[0], BLOCK):
        here = slice(start, start + BLOCK)
        cosine, sine = waves_ref[:half, here], waves_ref[half:, here]
        rest = jnp.zeros((HEAD_DIM - ROT, BLOCK), f32)
        table_ref[here, :] = jnp.concatenate([cosine, cosine, rest + 1.0, -sine, sine, rest], 0).T


def spread_table(table, width):
    own, other = table[:, :HEAD_DIM], table[:, HEAD_DIM:]
    return (jnp.concatenate([v] * (width // HEAD_DIM), 1) for v in (own, other))


def rotate_lanes(x, own, other):
    half = ROT // 2
    width = x.shape[1]
    lane = lax.broadcasted_iota(jnp.int32, x.shape, 1) % HEAD_DIM
    partner = jnp.where(lane < half, pltpu.roll(x, width - half, 1), pltpu.roll(x, half, 1))
    return x * own + partner * other


def visible_to(first_ref, start, keys, tile):
    key = lax.broadcasted_iota(jnp.int32, (keys, tile), 0)
    query = lax.broadcasted_iota(jnp.int32, (keys, tile), 1) + start
    return (key <= query) & (key >= first_ref[0:1, start : start + tile])


def head_rows(x, h):
    if x.shape[0] == HEAD_DIM:
        return x
    row = lax.broadcasted_iota(jnp.int32, x.shape, 0) // HEAD_DIM
    return jnp.where(row == h, x, jnp.zeros_like(x))


def head_lanes(x, h):
    if x.shape[1] == HEAD_DIM:
        return x
    lane = lax.broadcasted_iota(jnp.int32, x.shape, 1) // HEAD_DIM
    return jnp.where(lane == h, x, jnp.zeros_like(x))


def row_list(refs):
    return jnp.concatenate([ref[...] for ref in refs], 0)


def at_block(ref, index):
    return pl.ds(pl.multiple_of(ref[index] * BLOCK, BLOCK), BLOCK)


def grouped(refs, rows):
    groups, held, count = [], [], 0
    for ref in refs:
        held.append(ref)
        count += ref.shape[0]
        if count == rows:
            groups.append(held)
            held, count = [], 0
    return groups


def attend_kernel(blocks, maps_ref, *refs):
    block_refs, refs = refs[:blocks], refs[blocks:]
    piece_refs, refs = refs[:4], refs[4:]
    bias_ref, waves_ref, first_ref, all_ref, qkv_ref, mixed_ref, lse_ref, q_t, v_t, table_ref = refs
    fill_table(table_ref, waves_ref)
    length, width = mixed_ref.shape
    heads = width // HEAD_DIM
    blocks = length // BLOCK
    scale = HEAD_DIM ** (-0.5)
    tile = min(TILE, length)
    depth = piece_refs[0].shape[0]
    for i, group in enumerate(grouped(block_refs, tile)):
        rows = row_list(group)
        all_ref[i * tile : (i + 1) * tile, :] = rows
        x = bias_ref[...] + sum(dot(rows[:, g * depth : (g + 1) * depth], p[...]) for g, p in enumerate(piece_refs))
        for k in range(tile // BLOCK):
            here = at_block(maps_ref, blocks + i * (tile // BLOCK) + k)
            part = x[k * BLOCK : (k + 1) * BLOCK]
            own, other = spread_table(table_ref[here, :], width)
            q = rotate_lanes(part[:, :width], own, other).astype(bf16)
            v = part[:, 2 * width :].astype(bf16)
            qkv_ref[0, here, :] = q
            qkv_ref[1, here, :] = rotate_lanes(part[:, width : 2 * width], own, other).astype(bf16)
            qkv_ref[2, here, :] = v
            q_t[:, here] = (q.astype(f32) * scale).T.astype(bf16)
            v_t[:, here] = v.astype(f32).T.astype(bf16)
    lse_ref[...] = jnp.zeros_like(lse_ref)
    for start in range(0, length, tile):
        keys = start + tile
        seen = visible_to(first_ref, start, keys, tile)
        queries = q_t[:, start : start + tile]
        outs = []
        for h in range(heads):
            scores = dot(qkv_ref[1, :keys, :], head_rows(queries, h))
            scores = jnp.where(seen, scores, masked_score)
            top = jnp.max(scores, axis=0, keepdims=True)
            weights = jnp.exp(scores - top)
            total = jnp.sum(weights, axis=0, keepdims=True)
            lse_ref[h : h + 1, start : start + tile] = top + jnp.log(total)
            prob = (weights * (1.0 / total)).astype(bf16)
            outs.append(dot(v_t[h * HEAD_DIM : (h + 1) * HEAD_DIM, :keys], prob))
        out = jnp.concatenate(outs, 0).T.astype(bf16)
        for i in range(tile // BLOCK):
            mixed_ref[at_block(maps_ref, start // BLOCK + i), :] = out[i * BLOCK : (i + 1) * BLOCK]


def attend_back_kernel(blocks, maps_ref, *refs):
    block_refs, refs = refs[:blocks], refs[blocks:]
    w_ref, qkv_ref, mixed_ref, lse_ref, waves_ref, first_ref, out_ref, outer_ref = refs[:8]
    q_t, k_t, g_t, grads, delta, dk, dv, table_ref = refs[8:]
    fill_table(table_ref, waves_ref)
    length, width = mixed_ref.shape
    blocks = length // BLOCK
    heads = width // HEAD_DIM
    scale = HEAD_DIM ** (-0.5)
    tile = min(TILE, length)
    for i, group in enumerate(grouped(block_refs, tile)):
        rows = dot_last(row_list(group), w_ref[...]).astype(bf16)
        for k in range(tile // BLOCK):
            s = i * (tile // BLOCK) + k
            here = at_block(maps_ref, blocks + s)
            g = rows[k * BLOCK : (k + 1) * BLOCK]
            g_flip = g.astype(f32).T
            both = g_flip * mixed_ref[s * BLOCK : (s + 1) * BLOCK, :].astype(f32).T
            for h in range(heads):
                delta[h : h + 1, here] = jnp.sum(both[h * HEAD_DIM : (h + 1) * HEAD_DIM], axis=0, keepdims=True)
            grads[here, :] = g
            g_t[:, here] = g_flip.astype(bf16)
    for j in range(blocks):
        here = slice(j * BLOCK, (j + 1) * BLOCK)
        q_t[:, here] = (qkv_ref[0, here, :].astype(f32) * scale).T.astype(bf16)
        k_t[:, here] = qkv_ref[1, here, :].astype(f32).T.astype(bf16)
    dk[...] = jnp.zeros_like(dk)
    dv[...] = jnp.zeros_like(dv)
    for start in range(0, length, tile):
        keys = start + tile
        here = slice(start, keys)
        seen = visible_to(first_ref, start, keys, tile)
        q_tile, g_tile = q_t[:, here], g_t[:, here]
        q_rows, g_rows = qkv_ref[0, here, :], grads[here, :]
        dq, dk_sum, dv_sum = [], dk[:keys, :], dv[:keys, :]
        for h in range(heads):
            scores = dot(qkv_ref[1, :keys, :], head_rows(q_tile, h))
            prob = jnp.where(seen, jnp.exp(scores - lse_ref[h : h + 1, here]), 0.0)
            grad_prob = dot(qkv_ref[2, :keys, :], head_rows(g_tile, h))
            grad_score = (prob * (grad_prob - delta[h : h + 1, here])).astype(bf16)
            dv_sum += dot(prob.astype(bf16), head_lanes(g_rows, h))
            dk_sum += dot(grad_score, head_lanes(q_rows, h))
            dq.append(dot(k_t[h * HEAD_DIM : (h + 1) * HEAD_DIM, :keys], grad_score))
        dk[:keys, :] = dk_sum
        dv[:keys, :] = dv_sum
        dq = jnp.concatenate(dq, 0).T * scale
        for i in range(tile // BLOCK):
            at = slice(i * BLOCK, (i + 1) * BLOCK)
            place = slice(start + i * BLOCK, start + (i + 1) * BLOCK)
            own, other = spread_table(table_ref[place, :], width)
            turned = rotate_lanes(dq[at], own, -other)
            out_ref[at_block(maps_ref, start // BLOCK + i), :width] = turned.astype(bf16)
    for j in range(blocks):
        rows = at_block(maps_ref, j)
        here = slice(j * BLOCK, (j + 1) * BLOCK)
        own, other = spread_table(table_ref[here, :], width)
        turned = rotate_lanes(dk[here, :] * scale, own, -other)
        out_ref[rows, width : 2 * width] = turned.astype(bf16)
        out_ref[rows, 2 * width :] = dv[here, :].astype(bf16)
    for start in range(0, outer_ref.shape[1], 512):
        columns = slice(start, start + 512)
        outer_ref[:, columns] = sum(
            dot_rows(
                mixed_ref[i * tile : (i + 1) * tile, :], jnp.concatenate([ref[:, columns] for ref in group], 0)
            )
            for i, group in enumerate(grouped(block_refs, tile))
        )


def once(kernel, name, megabytes, out_shape, scratch, *given, maps=None):
    vmem = pl.BlockSpec(memory_space=pltpu.VMEM)
    many = isinstance(out_shape, (tuple, list))
    small = [] if maps is None else [maps]
    return pl.pallas_call(
        kernel,
        out_shape=out_shape,
        in_specs=[pl.BlockSpec(memory_space=pltpu.SMEM)] * len(small) + [vmem] * len(given),
        out_specs=[vmem] * len(out_shape) if many else vmem,
        scratch_shapes=scratch,
        compiler_params=pltpu.CompilerParams(vmem_limit_bytes=megabytes * 2**20),
        cost_estimate=BRIEF,
        name=name,
    )(*small, *given)


BRIEF = pl.CostEstimate(flops=1, bytes_accessed=1, transcendentals=0)


def attend(maps, blocks, pieces, bias, waves, first):
    length, width = waves.shape[1], pieces[0].shape[1] // 3
    return once(
        functools.partial(attend_kernel, len(blocks)),
        "attend",
        16 if length <= 1024 else 40,
        (
            jax.ShapeDtypeStruct((length, blocks[0].shape[1]), bf16),
            jax.ShapeDtypeStruct((3, length, width), bf16),
            jax.ShapeDtypeStruct((length, width), bf16),
            jax.ShapeDtypeStruct((max(8, width // HEAD_DIM), length), f32),
        ),
        [pltpu.VMEM((width, length), bf16), pltpu.VMEM((width, length), bf16), pltpu.VMEM((length, 2 * HEAD_DIM), f32)],
        *blocks,
        *pieces,
        bias,
        waves,
        first,
        maps=maps,
    )


def attend_back(maps, blocks, w_out, qkv, mixed, lse, waves, first):
    length, width = mixed.shape
    return once(
        functools.partial(attend_back_kernel, len(blocks)),
        "attend_back",
        16 if length <= 1024 else 40,
        (
            jax.ShapeDtypeStruct((length, 3 * width), bf16),
            jax.ShapeDtypeStruct((width, blocks[0].shape[1]), f32),
        ),
        [
            pltpu.VMEM((width, length), bf16),
            pltpu.VMEM((width, length), bf16),
            pltpu.VMEM((width, length), bf16),
            pltpu.VMEM((length, width), bf16),
            pltpu.VMEM((lse.shape[0], length), f32),
            pltpu.VMEM((length, width), f32),
            pltpu.VMEM((length, width), f32),
            pltpu.VMEM((length, 2 * HEAD_DIM), f32),
        ],
        *blocks,
        w_out,
        qkv,
        mixed,
        lse,
        waves,
        first,
        maps=maps,
    )


def exchange(blocks):
    return [blocks[0]] + [swap(v, "seq", k) for k, v in enumerate(blocks) if k]


def local(kernel, name, out_shape, smem, given, anywhere=0, scratch=()):
    vmem = pl.BlockSpec(memory_space=pltpu.VMEM)
    many = isinstance(out_shape, (tuple, list))
    return pl.pallas_call(
        kernel,
        out_shape=out_shape,
        in_specs=[pl.BlockSpec(memory_space=pltpu.SMEM)]
        + [pl.BlockSpec(memory_space=pl.ANY)] * anywhere
        + [vmem] * (len(given) - anywhere),
        out_specs=[vmem] * len(out_shape) if many else vmem,
        scratch_shapes=list(scratch),
        compiler_params=pltpu.CompilerParams(vmem_limit_bytes=6 * 2**20),
        cost_estimate=BRIEF,
        name=name,
    )(smem, *given)


def cut_kernel(peers_ref, w_ref, place_ref, *refs):
    outs, semaphores = refs[:-1], refs[-1]
    extra, width = place_ref.shape[0], place_ref.shape[1] // 3
    share, model = outs[0].shape[0] - extra, w_ref.shape[1] // 3
    rows = pl.ds(pl.multiple_of(peers_ref[0] * share, share), share)
    copies = []
    for k, out in enumerate(outs):
        for c in range(3):
            columns = pl.ds(pl.multiple_of(c * model + peers_ref[1 + k] * width, BLOCK), width)
            copies.append(
                pltpu.make_async_copy(
                    w_ref.at[rows, columns],
                    out.at[pl.ds(0, share), pl.ds(c * width, width)],
                    semaphores.at[3 * k + c],
                )
            )
            copies[-1].start()
    for out in outs:
        out[share:, :] = place_ref[...]
    for copy in copies:
        copy.wait()


def cut(at, w, place, n):
    extra, columns = place.shape
    share, width = w.shape[0] // 4, columns // 3
    if width % BLOCK:
        mine = pick(w.reshape(4, share, 3 * width * n), at.quarter[0], 0).reshape(share, 3, n, width)
        mine = [pick(mine, at.seq ^ jnp.uint32(k), 2).reshape(share, columns) for k in range(n)]
        return [jnp.concatenate([v, place]) for v in mine]
    out = jax.ShapeDtypeStruct((share + extra, columns), bf16)
    return local(cut_kernel, "cut", [out] * n, at.peers, (w, place), 1, [pltpu.SemaphoreType.DMA((3 * n,))])


def stack_kernel(peers_ref, *refs):
    ins, (piece_ref, place_ref) = refs[:-2], refs[-2:]
    share = piece_ref.shape[0] // len(ins)
    tokens = place_ref.shape[1] // len(ins)
    for k, ref in enumerate(ins):
        peer = peers_ref[1 + k]
        piece_ref[pl.ds(pl.multiple_of(peer * share, share), share), :] = ref[:share, :]
        place = ref[share:, :tokens].astype(f32)
        place_ref[:, pl.ds(pl.multiple_of(peer * tokens, tokens), tokens)] = place[0:1] * 64.0 + place[1:2]


def stacked(at, blocks, extra, tokens):
    n, (rows, columns) = len(blocks), blocks[0].shape
    shapes = [
        jax.ShapeDtypeStruct((n * (rows - extra), columns), bf16),
        jax.ShapeDtypeStruct((1, n * tokens), f32),
    ]
    return local(stack_kernel, "stacked", shapes, at.peers, blocks)


def in_plain_order(x, number, n):
    share = x.shape[1] // (4 * n)
    order = [(q % 2) * 2 + q // 2 for q in (number ^ j for j in range(4))]
    starts = [order[j] * n * share + s * share for s in range(n) for j in range(4)]
    return jnp.concatenate([x[:, start : start + share] for start in starts], 1)


def last_back_kernel(n, peers_ref, term_ref, first_ref, second_ref, unit_ref, inverse_ref, gain_ref, middle_ref, out_ref):
    total = term_ref[...] + first_ref[...].astype(f32) + second_ref[...].astype(f32)
    for number in range(4):

        @pl.when(peers_ref[0] == number)
        def _(number=number):
            out_ref[...] = in_plain_order(total, number, n)

    out_ref[...] = middle_ref[...] + norm_back(out_ref[...], unit_ref[...], inverse_ref[...], gain_ref[...])


def beside_kernel(in_ref, out_ref):
    n, _, columns = in_ref.shape
    width = columns // 3
    for k in range(n):
        for c in range(3):
            start = (c * n + k) * width
            out_ref[:, start : start + width] = in_ref[k, :, c * width : (c + 1) * width]


def beside(v):
    n, rows, columns = v.shape
    return once(beside_kernel, "beside", 6, jax.ShapeDtypeStruct((rows, n * columns), bf16), [], v)


def halves_kernel(first_ref, second_ref, top_ref, bottom_ref):
    half = top_ref.shape[0]
    top_ref[...] = first_ref[:half, :]
    bottom_ref[...] = second_ref[half:, :]


def halves(first, second):
    half = jax.ShapeDtypeStruct((first.shape[0] // 2, first.shape[1]), first.dtype)
    vmem = pl.BlockSpec(memory_space=pltpu.VMEM)
    return pl.pallas_call(
        halves_kernel,
        out_shape=(half, half),
        in_specs=[vmem] * 2,
        out_specs=(vmem,) * 2,
        compiler_params=pltpu.CompilerParams(vmem_limit_bytes=4 * 2**20),
        cost_estimate=BRIEF,
        name="halves",
    )(first, second)


def hidden_kernel(at, tokens, cots, held, *refs):
    token_refs, refs = refs[:tokens], refs[tokens:]
    cot_refs, refs = refs[:cots], refs[cots:]
    gate_ref, up_ref, down_ref, refs = refs[0], refs[1], refs[2], refs[3 + held :]
    results, scratch, semaphores = refs[:5], refs[5:10], refs[10]
    rows = scratch[0].shape[0]
    copies = [
        pltpu.make_async_copy(v, out.at[pl.ds(at * rows, rows), :], semaphores.at[i])
        for i, (v, out) in enumerate(zip(scratch, results, strict=True))
    ]
    two, cot, hidden, grad_gate, grad_up = scratch
    two[...] = row_list(token_refs)
    copies[0].start()
    cot[...] = row_list(cot_refs)
    copies[1].start()
    units = gate_ref.shape[0]
    for start in range(0, units, TILE):
        here = slice(start, min(start + TILE, units))
        gate, up = dot_last(two[...], gate_ref[here, :]), dot_last(two[...], up_ref[here, :])
        grad_hidden = dot_last(cot[...], down_ref[here, :])
        sigmoid = 1.0 / (1.0 + jnp.exp(-gate))
        silu = gate * sigmoid
        hidden[:, here] = (silu * up).astype(bf16)
        grad_gate[:, here] = (grad_hidden * up * sigmoid * (1.0 + gate * (1.0 - sigmoid))).astype(bf16)
        grad_up[:, here] = (grad_hidden * silu).astype(bf16)
    for copy in copies[2:]:
        copy.start()
    for copy in copies:
        copy.wait()


def hidden_pair(at, pairs, tokens, cots, gate_rows, up_rows, w_down, held):
    rows = sum(b.shape[0] for b in tokens)
    units, model = gate_rows.shape
    widths = (model, model, units, units, units)
    first = len(tokens) + len(cots) + 3
    hbm = pl.BlockSpec(memory_space=pltpu.HBM)
    return pl.pallas_call(
        functools.partial(hidden_kernel, at, len(tokens), len(cots), len(held)),
        out_shape=[jax.ShapeDtypeStruct((rows * pairs, w), bf16) for w in widths],
        in_specs=[pl.BlockSpec(memory_space=pltpu.VMEM)] * first + [hbm] * len(held),
        out_specs=[hbm] * 5,
        scratch_shapes=[pltpu.VMEM((rows, w), bf16) for w in widths] + [pltpu.SemaphoreType.DMA((5,))],
        input_output_aliases={first + i: i for i in range(len(held))},
        compiler_params=pltpu.CompilerParams(vmem_limit_bytes=12 * 2**20),
        cost_estimate=BRIEF,
        name="hidden_pair",
    )(*tokens, *cots, gate_rows, up_rows, w_down, *held)


def place_kernel(at_ref, *refs):
    out_ref = refs[-1]
    for i, ref in enumerate(refs[:-1]):

        @pl.when(pl.program_id(0) == i)
        def _(ref=ref):
            out_ref[...] = ref[...].astype(f32)


def placed(at, pieces, axis):
    shape = list(pieces[0].shape)
    total = list(shape)
    total[axis] *= len(pieces)
    return pl.pallas_call(
        place_kernel,
        out_shape=jax.ShapeDtypeStruct(tuple(total), f32),
        grid_spec=pltpu.PrefetchScalarGridSpec(
            num_scalar_prefetch=1,
            grid=(len(pieces),),
            in_specs=[pl.BlockSpec(tuple(shape), lambda i, at: (0, 0)) for _ in pieces],
            out_specs=pl.BlockSpec(tuple(shape), lambda i, at: (0, at[i]) if axis else (at[i], 0)),
        ),
        compiler_params=pltpu.CompilerParams(vmem_limit_bytes=16 * 2**20),
        cost_estimate=BRIEF,
        name="placed",
    )(at, *pieces)


def on_device(
    inputs, positions, ln1_gain, ln1_bias, w_qkv, qkv_bias, w_out, ln2_gain, ln2_bias, w_gate, w_up, w_down, cotangent
):
    n = lax.axis_size("seq")
    ring = Ring("seq")
    line = Line()
    tokens, model = inputs.shape[0], inputs.shape[2]
    length = tokens * n
    pairs = n // 2
    width = model // n
    depth = w_qkv.shape[0]
    share = depth // 4
    x = inputs.reshape(tokens, model).astype(f32)
    cot = cotangent.reshape(tokens, model)
    gate_rows, up_rows = w_gate.T, w_up.T
    others = (0, 2, 1, 3)
    at = Places(model)
    at.tied(line(lambda *v: v, *at.scalars()))

    def other_y(v):
        return swap(v, "batch", 2)

    def other_core(v):
        return swap(v, "batch", 1)

    place = positions.reshape(tokens)
    extra = 8
    place = jnp.stack([place // 64, place % 64]).astype(bf16)
    place = jnp.pad(place, ((0, extra - 2), (0, 3 * width - tokens)))
    fetched = exchange(line(lambda w, place: cut(at, w, place, n), w_qkv, place))
    bias_heads = line(lambda v: pick(v.reshape(3, n, width), at.seq, 1).reshape(1, 3 * width), qkv_bias)

    def first_norm(x):
        normed, unit, inverse = norm_parts(x, ln1_gain, ln1_bias)
        normed = normed.astype(bf16).reshape(tokens, n, 4, share)
        normed = [pick(normed, at.quarter[k], 2).reshape(tokens, -1) for k in others]
        return jnp.concatenate(normed, 1), unit, inverse

    normed, unit_one, inverse_one = line(first_norm, x)
    normed_blocks = Gather(ring, line, normed)

    piece, places = line(lambda *v: stacked(at, v, extra, tokens), *fetched)
    piece_y, piece_core = other_y(piece), other_core(piece)
    normed_blocks.step()

    def take(places, maps):
        maps = pick(maps, at.seq, 0)
        first = jnp.arange(length, dtype=jnp.int32)[None] - places.astype(jnp.int32)
        return maps, rotary_waves(places), first

    normed_blocks.step()
    ring.maps, waves, seen_from = line(take, places, ring.table)
    piece_core = line(lambda v: v, piece_core)
    for _ in range(pairs - 3):
        normed_blocks.step()
    piece_y = line(lambda v: v, piece_y)
    piece_both = other_core(piece_y)
    normed_blocks.step()
    cot_blocks = Gather(ring, line, cot)
    pieces = [piece, piece_y, piece_core, piece_both]
    all_normed, qkv, mixed, lse = line(
        lambda pieces: attend(ring.maps, normed_blocks.blocks, pieces, bias_heads, waves, seen_from), pieces
    )

    def block(v, i):
        return v[i * tokens : (i + 1) * tokens]

    class Scatter:
        def __init__(self, given, far, pair, own):
            self.given, self.pair, self.own = given, pair, own
            top, bottom = line(lambda *v: halves(*[far(*v).astype(bf16)] * 2), *given)
            self.first, self.second = ring.up(top), ring.down(bottom)
            self.d = pairs - 1
            self.term = line(lambda *v: pair(self.d, *v), *given)

        def step(self):
            half = tokens // 2

            def add(term, first, second):
                first, second = first.astype(f32), second.astype(f32)
                if self.d == pairs - 1:
                    first = jnp.pad(first, ((0, half), (0, 0)))
                    second = jnp.pad(second, ((half, 0), (0, 0)))
                return (term[tokens:] + first).astype(bf16), (term[:tokens] + second).astype(bf16)

            first, second = line(add, self.term, self.first, self.second)
            self.first, self.second = ring.up(first), ring.down(second)
            self.d -= 1
            self.term = line(lambda *v: self.pair(self.d, *v) if self.d else self.own(*v), *self.given)

        def parts(self):
            return self.term, self.first, self.second

        def finish(self):
            return line(lambda a, b, c: a + b.astype(f32) + c.astype(f32), *self.parts())

    def scattered(given, far, pair, own, fill, whole=True):
        going = Scatter(given, far, pair, own)
        for k in range(pairs):
            for work in fill[k] if k < len(fill) else ():
                work()
            if k < pairs - 1:
                going.step()
        return going.finish() if whole else going.parts()

    def pair_rows(v, d):
        return v[(2 * d - 1) * tokens : (2 * d + 1) * tokens]

    heads = {}

    def join_heads():
        heads["w"] = line(lambda *p: jnp.concatenate(p), *pieces)

    cot_step = cot_blocks.step
    branch = scattered(
        (mixed, w_out),
        lambda v, w: dot(block(v, n - 1), w),
        lambda d, v, w: dot(pair_rows(v, d), w),
        lambda v, w: dot(block(v, 0), w),
        [(cot_step,), (cot_step,), (cot_step,), (join_heads,)],
    )

    def second_norm(x, branch):
        middle = x + branch
        normed, unit, inverse = norm_parts(middle, ln2_gain, ln2_bias)
        return normed.astype(bf16), middle, unit, inverse

    normed_two, middle, unit_two, inverse_two = line(second_norm, x, branch)
    two_blocks = Gather(ring, line, normed_two)
    while len(cot_blocks.blocks) < n + 1:
        cot_blocks.step()
    held = []
    for d in range(1, pairs + 1):
        two_blocks.step()
        first, second = (v.blocks[2 * d - 1 : 2 * d + 1] for v in (two_blocks, cot_blocks))
        if d == pairs:
            first, second = [normed_two, *first], [cot, *second]
        held = line(
            lambda t, held, c=second, d=d: hidden_pair(d - 1, pairs, t, c, gate_rows, up_rows, w_down, held), first, held
        )
    all_two, all_cot, all_hidden, all_gate, all_up = held

    def last(v):
        return v[(n - 2) * tokens :]

    def ffn_rows(v, d):
        return v[2 * (d - 1) * tokens : 2 * d * tokens]

    def both(gate, up, gate_rows, up_rows):
        return dot(gate, gate_rows) + dot(up, up_rows)

    def quarter_one(units, rows, got):
        return (dot_rows(units, at.side(rows, "mine other", 4)) + at.side(got, "other").astype(f32)).astype(bf16)

    def quarter_two(units, rows, got, got_y):
        return (dot_rows(units, at.side(rows, "mine y", 4)) + at.side(got, "y").astype(f32) + got_y.astype(f32)).astype(bf16)

    class Reduced:
        def __init__(self, units, rows):
            self.units, self.rows = units, rows

        def one(self):
            self.got = other_core(line(lambda u, r: dot_rows(u, at.side(r, "across")).astype(bf16), self.units, self.rows))

        def two(self):
            self.got_y = other_y(line(quarter_one, self.units, self.rows, self.got))

        def three(self):
            piece = line(quarter_two, self.units, self.rows, self.got, self.got_y)
            self.pieces = [piece, other_y(piece), other_core(piece)]

        def four(self):
            self.pieces[1] = line(lambda v: v, self.pieces[1])
            self.pieces.append(other_core(self.pieces[1]))

        def five(self):
            self.out = line(lambda *p: placed(at.column_place, p, 1), *self.pieces)

    down, gate, up = Reduced(all_hidden, all_cot), Reduced(all_gate, all_two), Reduced(all_up, all_two)
    last_term = line(lambda g, u, *w: both(last(g), last(u), *w), all_gate, all_up, gate_rows, up_rows)
    grad_two = scattered(
        (last_term, all_gate, all_up, gate_rows, up_rows),
        lambda v, *_: v[tokens:],
        lambda d, _, g, u, *w: both(ffn_rows(g, d), ffn_rows(u, d), *w),
        lambda v, *_: v[:tokens],
        [(down.one, gate.one, down.two), (gate.two, up.one), (up.two, down.three), (gate.three,)],
    )

    def second_back(grad_two):
        grad_middle = cot.astype(f32) + norm_back(grad_two, unit_two, inverse_two, ln2_gain)
        return grad_middle, grad_middle.astype(bf16), jnp.sum(grad_two * unit_two, axis=0), jnp.sum(grad_two, axis=0)

    grad_middle, grad_branch, gain_two_grad, bias_two_grad = line(second_back, grad_two)

    branch_blocks = Gather(ring, line, grad_branch)
    going = {}

    def start_out():
        last_out = line(lambda h, w: dot(last(h), w), all_hidden, w_down)
        going["out"] = Scatter(
            (last_out, all_hidden, w_down),
            lambda v, *_: v[tokens:],
            lambda d, _, h, w: dot(ffn_rows(h, d), w),
            lambda v, *_: v[:tokens],
        )

    fill = [(up.three,), (down.four, start_out), (gate.four,), (lambda: going["out"].step(), up.four)]
    for k in range(pairs):
        for work in fill[k] if k < len(fill) else ():
            work()
        branch_blocks.step()
    out_sum = going["out"]
    out_sum.step()
    grad_joined, outer = line(
        lambda w: attend_back(ring.maps, branch_blocks.blocks, w, qkv, mixed, lse, waves, seen_from), w_out
    )

    grad_w_out = {}

    def out_one():
        grad_w_out["mine"], give = line(lambda v: (at.side(v, "core"), at.side(v, "across").astype(bf16)), outer)
        grad_w_out["got"] = other_core(give)

    def out_two():
        def work(v, got):
            v = v + got.astype(f32)
            return at.side(v, "y"), at.side(v, "other").astype(bf16)

        grad_w_out["mine"], give = line(work, grad_w_out["mine"], grad_w_out["got"])
        grad_w_out["got"] = other_y(give)

    def out_three():
        v = line(lambda v, got: (v + got.astype(f32)).astype(bf16), grad_w_out["mine"], grad_w_out["got"])
        grad_w_out["pieces"] = [v, other_y(v), other_core(v)]

    qkv_grad = {}

    def qkv_one():
        give = line(lambda a, b: dot_rows(a[:, model // 2 :], b).astype(bf16), all_normed, grad_joined)
        qkv_grad["give"], qkv_grad["got"] = give, other_core(give)

    def qkv_two():
        def work(a, b, got):
            own = dot_rows(a[:, model // 4 : model // 2], b)
            return (own + got[got.shape[0] // 2 :].astype(f32)).astype(bf16), own

        give, qkv_grad["local_y"] = line(work, all_normed, grad_joined, qkv_grad["got"])
        qkv_grad["got_y"] = other_y(give)

    def qkv_three():
        def work(a, b, got, got_y):
            own = dot_rows(a[:, : model // 4], b)
            return (own + got[: got.shape[0] // 2].astype(f32) + got_y.astype(f32)).astype(bf16), own

        piece, qkv_grad["local"] = line(work, all_normed, grad_joined, qkv_grad["got"], qkv_grad["got_y"])
        piece = piece.reshape(n, share, 3 * width)
        qkv_grad["back"] = lax.all_to_all(piece, "seq", split_axis=0, concat_axis=0, tiled=True)

    def to_rows():
        back = line(beside, qkv_grad["back"])
        qkv_grad["rows"], qkv_grad["back_y"], qkv_grad["back_core"] = back, other_y(back), other_core(back)

    def natural(v):
        v = v.reshape(-1, 4, n, share)
        v = [pick(v, at.order[j], 1) for j in range(4)]
        return jnp.stack(v, 2).reshape(-1, model)

    vectors = {}

    def sum_vectors():
        def work(joined, w, *local):
            bias = jnp.sum(joined.astype(f32), axis=0)
            w = w.astype(f32)
            shift = natural(jnp.sum(w * bias, axis=1))[0]
            rows = jnp.concatenate([v.astype(f32) for v in local])
            gain = (natural(jnp.sum(w * rows, axis=1))[0] - ln1_bias * shift) / ln1_gain
            bias_all = jnp.zeros((3, n, width), f32)
            bias_all = lax.dynamic_update_slice(bias_all, bias.reshape(3, 1, width), (jnp.uint32(0), at.seq, jnp.uint32(0))).reshape(-1)
            return jnp.concatenate([gain, shift, gain_two_grad, bias_two_grad, bias_all]).reshape(-1, 128)

        v = line(work, grad_joined, heads["w"], qkv_grad["local"], qkv_grad["local_y"], qkv_grad["give"])
        vectors["sum"] = v
        vectors["hops"] = [("batch", 1), *(("seq", bit) for bit in bits_of(n)), ("batch", 2)]
        vectors["other"] = swap(v, *vectors["hops"][0])

    def vector_step():
        v = line(lambda a, b: a + b, vectors["sum"], vectors["other"])
        vectors["sum"] = v
        vectors["hops"].pop(0)
        if vectors["hops"]:
            vectors["other"] = swap(v, *vectors["hops"][0])

    qkv_one()
    grad_one = scattered(
        (grad_joined, heads["w"]),
        lambda v, w: dot_last(block(v, n - 1), w),
        lambda d, v, w: dot_last(pair_rows(v, d), w),
        lambda v, w: dot_last(block(v, 0), w),
        [(qkv_two,), (qkv_three,), (down.five, gate.five, to_rows), (sum_vectors,)],
        whole=False,
    )

    def last_back(term, first, second):
        if share % HEAD_DIM:
            grad_one = natural(term + first.astype(f32) + second.astype(f32))
            return grad_middle + norm_back(grad_one, unit_one, inverse_one, ln1_gain)
        given = term, first, second, unit_one, inverse_one, ln1_gain[None], grad_middle
        out = jax.ShapeDtypeStruct((tokens, model), f32)
        return once(functools.partial(last_back_kernel, n), "last_back", 8, out, [], *given, maps=at.peers)

    grad_input = line(last_back, *grad_one)
    back_y = line(lambda v: v, qkv_grad["back_y"])
    back_both = other_core(back_y)
    out_one()
    vector_step()
    for _ in range(pairs - 3):
        out_sum.step()
    out_two()
    vector_step()
    up.five()
    out_three()
    vector_step()
    grad_w_qkv = line(
        lambda *p: placed(at.row_place, p, 0), qkv_grad["rows"], back_y, qkv_grad["back_core"], back_both
    )
    while vectors["hops"]:
        vector_step()
    output = line(lambda a, b: (a + b).astype(bf16), middle, out_sum.finish())
    v = grad_w_out["pieces"]
    v[1] = line(lambda v: v, v[1])
    v.append(other_core(v[1]))
    grad_w_out = line(lambda *p: placed(at.column_place, p, 1), *v)
    gain_one_sum, bias_one_sum, gain_two_sum, bias_two_sum, qkv_bias_sum = jnp.split(
        vectors["sum"].reshape(-1), [model, 2 * model, 3 * model, 4 * model]
    )

    return (
        output.reshape(tokens, 1, model),
        grad_input.reshape(tokens, 1, model),
        gain_one_sum,
        bias_one_sum,
        grad_w_qkv,
        qkv_bias_sum,
        grad_w_out,
        gain_two_sum,
        bias_two_sum,
        gate.out.T,
        up.out.T,
        down.out,
    )


def solution(mesh):
    token, shard, column, whole = P("seq", "batch", None), P("seq", None), P(None, "seq"), P()
    in_specs = (
        token, P("seq", "batch"), whole, whole, shard, whole, shard, whole, whole, column, column, shard, token
    )
    out_specs = (token, token, whole, whole, shard, whole, shard, whole, whole, column, column, shard)
    return jax.shard_map(on_device, mesh=mesh, in_specs=in_specs, out_specs=out_specs, check_vma=False)
```

time: 667 us -> 512 us (0.77)
  local copies, waits for them, and re-layouts: 133 us -> 20.3 us
  matrix products: 106 us -> 48.1 us
  blocking collectives: 43.9 us -> 0 us
  Pallas kernels: 22.2 us -> 64.6 us
  other arithmetic: 46.5 us -> 22.8 us
  waiting for transfers between devices: 208 us -> 231 us
  starting transfers between devices: 97.2 us -> 119 us
    ppermute x32, waiting for transfers between devices: 108 us -> 30.4 us  [down(): return lax.ppermute(v, self.axis, self.behind)]
    ppermute x32, waiting for transfers between devices: 34.9 us -> 96.2 us  [up(): return lax.ppermute(v, self.axis, self.ahead)]
    ppermute x27 -> x40, waiting for transfers between devices: 57.5 us -> 104 us  [swap(): return lax.ppermute(v, axis, [(i, i ^ bit) for i in range(n)])]
    all_gather x1 -> x0, blocking collectives: 43.9 us -> none  [on_device(): lax.all_gather(positions.reshape(tokens), 'seq', axis=0, tiled=True)]
    convert_element_type x12 -> x3, local copies, waits for them, and re-layouts: 43.5 us -> 0.64 us  [the longest x1 0.27 us: first_norm(): normed = normed.astype(bf16).reshape(tokens, n, 4, share)]
    pallas_call x2 -> x23, Pallas kernels: 22.2 us -> 64.6 us  [the longest x4 27.9 us: once(): pl.pallas_call(kernel, out_shape=out_shape, in_specs=[pl.BlockSpec(memory...]
    dot_general x40 -> x5, matrix products: 51.8 us -> 11 us  [dot_last(): lax.dot_general(a, b, (((1,), (1,)), ((), ())), preferred_element_type=f32)]
    ppermute x27 -> x40, starting transfers between devices: 13.9 us -> 35.5 us  [swap(): return lax.ppermute(v, axis, [(i, i ^ bit) for i in range(n)])]
  transfers between devices with their start and end apart: 93 -> 105, of which waited for: 33 -> 58; matrix products, arithmetic and copies ran while one was open for 40% -> 12% of each run, Pallas kernels for 3% -> 9%
where the time goes in v2:
time: 512 us; the launch traced here: 508 us
  waiting for transfers between devices  231 us (45%)
  starting transfers between devices  119 us (23%)
  Pallas kernels  64.6 us (13%)
  matrix products  48.1 us (9%)
  other arithmetic  22.8 us (4%)
  local copies, waits for them, and re-layouts  20.3 us (4%)
    ppermute x40, waiting for transfers between devices, swap(): return lax.ppermute(v, axis, [(i, i ^ bit) for i in range(n)])  104 us
    ppermute x32, waiting for transfers between devices, up(): return lax.ppermute(v, self.axis, self.ahead)  96.2 us
    ppermute x32, starting transfers between devices, up(): return lax.ppermute(v, self.axis, self.ahead)  51.2 us
    ppermute x40, starting transfers between devices, swap(): return lax.ppermute(v, axis, [(i, i ^ bit) for i in range(n)])  35.5 us
    ppermute x32, waiting for transfers between devices, down(): return lax.ppermute(v, self.axis, self.behind)  30.4 us
    pallas_call x4, Pallas kernels, once(): pl.pallas_call(kernel, out_shape=out_shape, in_specs=[pl.BlockSpec(memory...  27.9 us
    ppermute x32, starting transfers between devices, down(): return lax.ppermute(v, self.axis, self.behind)  27.7 us
    dot_general x12, matrix products, dot_rows(): lax.dot_general(a, b, (((0,), (0,)), ((), ())), preferred_element_type=f32)  22.1 us
  transfers between devices with their start and end apart: 105, of which 58 were waited for; matrix products, arithmetic and copies ran while one was open for 12% of the time, Pallas kernels for 9%

profile of v2, /device:TPU:0, one launch (start us, length us, event | category | flops | bytes accessed | tf_op | source)
XLA Modules:
  0.0 508.2 jit_solution(17533816469295276149)
XLA Ops:
  9.6 3.1 collective-permute-start.7
  16.2 10.7 %collective-permute-done.refs_1_ = bf16[72,768]{1,0:T(8,128)(2,1)S(1)} collective-permute-done((bf16[72,768]{1,0:T(8,128)(2,1)S(1)}, bf16[72,768]{1,0:T(8,128)(2,1)S(1)}, u32[]{:S(2)}, u32[]{:S(2)}) %collective-permute-start) | collective-permute-done | bytes 110624 | tf_op jit(solution)/shard_map/ppermute | solution.py:84
  26.9 2.7 collective-permute-done.1.refs_2_
  29.7 2.2 collective-permute-start.4
  31.9 4.0 collective-permute-start.5
  35.8 5.1 %collective-permute-done.3.refs_4_ = bf16[72,768]{1,0:T(8,128)(2,1)S(1)} collective-permute-done((bf16[72,768]{1,0:T(8,128)(2,1)S(1)}, bf16[72,768]{1,0:T(8,128)(2,1)S(1)}, u32[]{:S(2)}, u32[]{:S(2)}) %collective-permute-start.3) | collective-permute-done | bytes 110624 | tf_op jit(solution)/shard_map/ppermute | solution.py:84
  42.5 2.9 collective-permute-done.4.refs_5_
  45.4 3.1 collective-permute-done.6.refs_7_
  51.2 2.3 collective-permute-start.16
  53.5 7.5 %collective-permute-done.10.refs_4_ = bf16[128,2048]{1,0:T(8,128)(2,1)S(1)} collective-permute-done((bf16[128,2048]{1,0:T(8,128)(2,1)S(1)}, bf16[128,2048]{1,0:T(8,128)(2,1)S(1)}, u32[]{:S(2)}, u32[]{:S(2)}) %collective-permute-start.10) | collective-permute-done | bytes 524320 | tf_op jit(solution)/shard_map/ppermute | solution.py:48
  65.7 9.4 %collective-permute-done.11.first_ref.refs_5_ = bf16[128,2048]{1,0:T(8,128)(2,1)S(1)} collective-permute-done((bf16[128,2048]{1,0:T(8,128)(2,1)S(1)}, bf16[128,2048]{1,0:T(8,128)(2,1)S(1)}, u32[]{:S(2)}, u32[]{:S(2)}) %collective-permute-start.11) | collective-permute-done | bytes 524320 | tf_op jit(solution)/shard_map/ppermute | solution.py:45
  79.5 4.8 collective-permute-done.14.refs_7_
  84.6 14.1 %attend.1 = (bf16[1024,2048]{1,0:T(8,128)(2,1)S(1)}, bf16[3,1024,256]{2,1,0:T(8,128)(2,1)S(1)}, bf16[1024,256]{1,0:T(8,128)(2,1)S(1)}, f32[8,1024]{1,0:T(8,128)S(1)}) custom-call(s32[16]{0:T(128)S(1)} %fusion.89.maps_ref, bf16[128,2048]{1,0:T(8,128)(2,1)S(1)} %pad_maximum_fusion.refs_0_, bf16[128,2048]{1,0:T(8,128)(2,1)S(1)} %collective-permute-done.7.refs_1_, ...), custom_call_target="tpu_custom_call" | custom-call | flops 1 | bytes 1 | tf_op jit(solution)/shard_map/attend/pallas_call | solution.py:354
  99.0 2.1 collective-permute-start.18
  104.2 4.1 collective-permute-done.18
  113.1 6.5 %collective-permute-done.24.refs_2_ = bf16[128,2048]{1,0:T(8,128)(2,1)S(1)} collective-permute-done((bf16[128,2048]{1,0:T(8,128)(2,1)S(1)}, bf16[128,2048]{1,0:T(8,128)(2,1)S(1)}, u32[]{:S(2)}, u32[]{:S(2)}) %collective-permute-start.24) | collective-permute-done | bytes 524320 | tf_op jit(solution)/shard_map/ppermute | solution.py:45
  123.6 7.2 %collective-permute-done.22 = bf16[128,2048]{1,0:T(8,128)(2,1)S(1)} collective-permute-done((bf16[128,2048]{1,0:T(8,128)(2,1)S(1)}, bf16[128,2048]{1,0:T(8,128)(2,1)S(1)}, u32[]{:S(2)}, u32[]{:S(2)}) %collective-permute-start.22) | collective-permute-done | bytes 524320 | tf_op jit(solution)/shard_map/ppermute | solution.py:45
  135.7 6.4 %collective-permute-done.28.first_ref.refs_2_ = bf16[128,2048]{1,0:T(8,128)(2,1)S(1)} collective-permute-done((bf16[128,2048]{1,0:T(8,128)(2,1)S(1)}, bf16[128,2048]{1,0:T(8,128)(2,1)S(1)}, u32[]{:S(2)}, u32[]{:S(2)}) %collective-permute-start.28) | collective-permute-done | bytes 524320 | tf_op jit(solution)/shard_map/ppermute | solution.py:45
  144.1 7.5 %collective-permute-done.26 = bf16[128,2048]{1,0:T(8,128)(2,1)S(1)} collective-permute-done((bf16[128,2048]{1,0:T(8,128)(2,1)S(1)}, bf16[128,2048]{1,0:T(8,128)(2,1)S(1)}, u32[]{:S(2)}, u32[]{:S(2)}) %collective-permute-start.26) | collective-permute-done | bytes 524320 | tf_op jit(solution)/shard_map/ppermute | solution.py:45
  155.7 8.7 %collective-permute-done.30 = bf16[128,2048]{1,0:T(8,128)(2,1)S(1)} collective-permute-done((bf16[128,2048]{1,0:T(8,128)(2,1)S(1)}, bf16[128,2048]{1,0:T(8,128)(2,1)S(1)}, u32[]{:S(2)}, u32[]{:S(2)}) %collective-permute-start.30) | collective-permute-done | bytes 524320 | tf_op jit(solution)/shard_map/ppermute | solution.py:45
  171.4 12.6 %collective-permute-done.34.refs_4_ = bf16[64,2048]{1,0:T(8,128)(2,1)S(1)} collective-permute-done((bf16[64,2048]{1,0:T(8,128)(2,1)S(1)}, bf16[64,2048]{1,0:T(8,128)(2,1)S(1)}, u32[]{:S(2)}, u32[]{:S(2)}) %collective-permute-start.34) | collective-permute-done | bytes 262176 | tf_op jit(solution)/shard_map/ppermute | solution.py:45
  185.3 2.1 collective-permute-start.36
  187.4 3.7 hidden_pair.4
  191.1 5.5 %collective-permute-done.36.refs_0_ = bf16[128,2048]{1,0:T(8,128)(2,1)S(1)} collective-permute-done((bf16[128,2048]{1,0:T(8,128)(2,1)S(1)}, bf16[128,2048]{1,0:T(8,128)(2,1)S(1)}, u32[]{:S(2)}, u32[]{:S(2)}) %collective-permute-start.36) | collective-permute-done | bytes 524320 | tf_op jit(solution)/shard_map/ppermute | solution.py:45
  196.6 2.8 collective-permute-done.37.refs_1_
  201.4 3.7 hidden_pair.5
  205.1 6.3 %collective-permute-done.38.first_ref.refs_0_ = bf16[128,2048]{1,0:T(8,128)(2,1)S(1)} collective-permute-done((bf16[128,2048]{1,0:T(8,128)(2,1)S(1)}, bf16[128,2048]{1,0:T(8,128)(2,1)S(1)}, u32[]{:S(2)}, u32[]{:S(2)}) %collective-permute-start.38) | collective-permute-done | bytes 524320 | tf_op jit(solution)/shard_map/ppermute | solution.py:45
  213.7 3.7 hidden_pair.6
  218.7 3.7 hidden_pair.7
  231.9 2.9 fusion.16
  249.4 3.1 collective-permute-done.48
  258.9 7.7 %collective-permute-done.43 = bf16[704,512]{1,0:T(8,128)(2,1)S(1)} collective-permute-done((bf16[704,512]{1,0:T(8,128)(2,1)}, bf16[704,512]{1,0:T(8,128)(2,1)S(1)}, u32[]{:S(2)}, u32[]{:S(2)}) %collective-permute-start.43) | collective-permute-done | bytes 720928 | tf_op jit(solution)/shard_map/ppermute | solution.py:84
  272.3 9.8 %collective-permute-done.55 = bf16[704,512]{1,0:T(8,128)(2,1)} collective-permute-done((bf16[704,512]{1,0:T(8,128)(2,1)}, bf16[704,512]{1,0:T(8,128)(2,1)}, u32[]{:S(2)}, u32[]{:S(2)}) %collective-permute-start.55) | collective-permute-done | bytes 720928 | tf_op jit(solution)/shard_map/ppermute | solution.py:84
  282.1 2.3 add_convert_fusion.3.refs_0_
  288.4 9.0 %collective-permute-done.58 = bf16[704,512]{1,0:T(8,128)(2,1)S(1)} collective-permute-done((bf16[704,512]{1,0:T(8,128)(2,1)S(1)}, bf16[704,512]{1,0:T(8,128)(2,1)S(1)}, u32[]{:S(2)}, u32[]{:S(2)}) %collective-permute-start.58) | collective-permute-done | bytes 720928 | tf_op jit(solution)/shard_map/ppermute | solution.py:84
  301.8 10.6 %collective-permute-done.50.refs_1_ = bf16[704,512]{1,0:T(8,128)(2,1)S(1)} collective-permute-done((bf16[704,512]{1,0:T(8,128)(2,1)S(1)}, bf16[704,512]{1,0:T(8,128)(2,1)S(1)}, u32[]{:S(2)}, u32[]{:S(2)}) %collective-permute-start.50) | collective-permute-done | bytes 720928 | tf_op jit(solution)/shard_map/ppermute | solution.py:84
  320.5 10.8 %collective-permute-done.65.refs_1_ = bf16[704,512]{1,0:T(8,128)(2,1)S(1)} collective-permute-done((bf16[704,512]{1,0:T(8,128)(2,1)S(1)}, bf16[704,512]{1,0:T(8,128)(2,1)S(1)}, u32[]{:S(2)}, u32[]{:S(2)}) %collective-permute-start.65) | collective-permute-done | bytes 720928 | tf_op jit(solution)/shard_map/ppermute | solution.py:84
  333.0 2.2 collective-permute-done.59
  341.1 7.0 %collective-permute-done.70.refs_1_ = bf16[704,512]{1,0:T(8,128)(2,1)S(1)} collective-permute-done((bf16[704,512]{1,0:T(8,128)(2,1)S(1)}, bf16[704,512]{1,0:T(8,128)(2,1)S(1)}, u32[]{:S(2)}, u32[]{:S(2)}) %collective-permute-start.70) | collective-permute-done | bytes 720928 | tf_op jit(solution)/shard_map/ppermute | solution.py:84
  348.1 5.4 %collective-permute-done.68.refs_7_ = bf16[64,2048]{1,0:T(8,128)(2,1)S(1)} collective-permute-done((bf16[64,2048]{1,0:T(8,128)(2,1)S(1)}, bf16[64,2048]{1,0:T(8,128)(2,1)S(1)}, u32[]{:S(2)}, u32[]{:S(2)}) %collective-permute-start.68) | collective-permute-done | bytes 262176 | tf_op jit(solution)/shard_map/ppermute | solution.py:45
  355.4 2.3 fusion.41
  357.7 11.3 %attend_back.1 = (bf16[1024,768]{1,0:T(8,128)(2,1)S(1)}, f32[256,2048]{1,0:T(8,128)S(1)}) custom-call(s32[16]{0:T(128)S(1)} %fusion.89.maps_ref, bf16[128,2048]{1,0:T(8,128)(2,1)S(1)} %get-tuple-element.708.refs_0_, bf16[128,2048]{1,0:T(8,128)(2,1)S(1)} %collective-permute-done.56.refs_1_, bf16[128,2048]{1,0:T(8,128)(2,1)S(1)} %collective-permute-done.57.refs_2_, ...), custom_call_target="tpu_custom_call" | custom-call | flops 1 | bytes 1 | tf_op jit(solution)/shard_map/attend_back/pallas_call | solution.py:354
  370.4 2.1 fusion.10
  376.9 2.2 add_convert_fusion.1
  387.3 2.4 fusion.37
  389.6 8.9 %collective-permute-done.74 = bf16[512,768]{1,0:T(8,128)(2,1)S(1)} collective-permute-done((bf16[512,768]{1,0:T(8,128)(2,1)S(1)}, bf16[512,768]{1,0:T(8,128)(2,1)S(1)}, u32[]{:S(2)}, u32[]{:S(2)}) %collective-permute-start.74) | collective-permute-done | bytes 786464 | tf_op jit(solution)/shard_map/ppermute | solution.py:84
  402.0 5.1 %all-to-all-start = ((bf16[8,64,768]{2,1,0:T(8,128)(2,1)}), bf16[8,64,768]{2,1,0:T(8,128)(2,1)S(1)}, u32[]{:S(2)}, u32[]{:S(2)}) async-start(bf16[8,64,768]{2,1,0:T(8,128)(2,1)} %bitcast.138), calls=%async_computation | async-start | bytes 1572864 | tf_op jit(solution)/shard_map/all_to_all | solution.py:883
  408.1 3.1 add_convert_fusion.10
  414.2 4.4 fusion.35
  420.7 4.6 placed.5
  425.3 4.8 placed.6
  433.3 3.1 add_convert_fusion.8
  436.4 7.2 %collective-permute-start.87 = (bf16[128,2048]{1,0:T(8,128)(2,1)}, bf16[128,2048]{1,0:T(8,128)(2,1)}, u32[]{:S(2)}, u32[]{:S(2)}) collective-permute-start(bf16[128,2048]{1,0:T(8,128)(2,1)} %get-tuple-element.719), channel_id=1, source_target_pairs={{0,8},{8,16},{16,24},{24,28},{28,20},{20,12},{12,4},{4,0},{1,9},{9... | collective-permute-start | bytes 1572872 | tf_op jit(solution)/shard_map/ppermute | solution.py:45
  445.1 2.1 fusion.61.term_ref
  453.1 2.1 collective-permute-done.88.second_ref
  456.5 2.4 last_back.1
  466.0 2.2 collective-permute-start.91
  468.2 5.0 collective-permute-start.89
  473.5 3.5 placed.7
  477.0 2.5 collective-permute-start.93
  479.5 8.8 %collective-permute-done.93 = f32[112,128]{1,0:T(8,128)S(1)} collective-permute-done((f32[112,128]{1,0:T(8,128)S(1)}, f32[112,128]{1,0:T(8,128)S(1)}, u32[]{:S(2)}, u32[]{:S(2)}) %collective-permute-start.93) | collective-permute-done | bytes 57376 | tf_op jit(solution)/shard_map/ppermute | solution.py:84
  489.9 4.7 placed.8
  500.6 3.4 collective-permute-done.101.refs_1_
  505.5 2.4 placed.9
  (395 shorter events, 176.0 us)
Async XLA Ops:
  9.6 39.4 %collective-permute-start.7 = (bf16[128,2048]{1,0:T(8,128)(2,1)S(1)}, bf16[128,2048]{1,0:T(8,128)(2,1)S(1)}, u32[]{:S(2)}, u32[]{:S(2)}) collective-permute-start(bf16[128,2048]{1,0:T(8,128)(2,1)S(1)} %pad_maximum_fusion.refs_0_), channel_id=1, source_target_pairs={{0,8},{8,16},{16,24},{24,28},{28,20},{20,12},{12,4},{4,0},{1,9},{9... | collective-permute-start | bytes 1572872 | tf_op jit(solution)/shard_map/ppermute | solution.py:45
  12.7 36.4 %collective-permute-start.8 = (bf16[128,2048]{1,0:T(8,128)(2,1)S(1)}, bf16[128,2048]{1,0:T(8,128)(2,1)S(1)}, u32[]{:S(2)}, u32[]{:S(2)}) collective-permute-start(bf16[128,2048]{1,0:T(8,128)(2,1)S(1)} %pad_maximum_fusion.refs_0_), channel_id=1, source_target_pairs={{8,0},{16,8},{24,16},{28,24},{20,28},{12,20},{4,12},{0,4},{9,1},{1... | collective-permute-start | bytes 1572872 | tf_op jit(solution)/shard_map/ppermute | solution.py:48
  12.7 14.2 %collective-permute-start = (bf16[72,768]{1,0:T(8,128)(2,1)S(1)}, bf16[72,768]{1,0:T(8,128)(2,1)S(1)}, u32[]{:S(2)}, u32[]{:S(2)}) collective-permute-start(bf16[72,768]{1,0:T(8,128)(2,1)S(1)} %get-tuple-element.366), channel_id=1, source_target_pairs={{0,4},{4,0},{8,12},{12,8},{16,20},{20,16},{24,28},{28,24},{1,5},{5... | collective-permute-start | bytes 331784 | tf_op jit(solution)/shard_map/ppermute | solution.py:84
  14.7 15.0 %collective-permute-start.1 = (bf16[72,768]{1,0:T(8,128)(2,1)S(1)}, bf16[72,768]{1,0:T(8,128)(2,1)S(1)}, u32[]{:S(2)}, u32[]{:S(2)}) collective-permute-start(bf16[72,768]{1,0:T(8,128)(2,1)S(1)} %get-tuple-element.367), channel_id=1, source_target_pairs={{0,8},{4,12},{8,0},{12,4},{16,24},{20,28},{24,16},{28,20},{1,9},{5... | collective-permute-start | bytes 331784 | tf_op jit(solution)/shard_map/ppermute | solution.py:84
  16.2 15.6 %collective-permute-start.2 = (bf16[72,768]{1,0:T(8,128)(2,1)S(1)}, bf16[72,768]{1,0:T(8,128)(2,1)S(1)}, u32[]{:S(2)}, u32[]{:S(2)}) collective-permute-start(bf16[72,768]{1,0:T(8,128)(2,1)S(1)} %get-tuple-element.368), channel_id=1, source_target_pairs={{0,12},{4,8},{8,4},{12,0},{16,28},{20,24},{24,20},{28,16},{1,13},{... | collective-permute-start | bytes 331784 | tf_op jit(solution)/shard_map/ppermute | solution.py:84
  26.9 14.0 %collective-permute-start.3 = (bf16[72,768]{1,0:T(8,128)(2,1)S(1)}, bf16[72,768]{1,0:T(8,128)(2,1)S(1)}, u32[]{:S(2)}, u32[]{:S(2)}) collective-permute-start(bf16[72,768]{1,0:T(8,128)(2,1)S(1)} %get-tuple-element.369), channel_id=1, source_target_pairs={{0,16},{4,20},{8,24},{12,28},{16,0},{20,4},{24,8},{28,12},{1,17},{... | collective-permute-start | bytes 331784 | tf_op jit(solution)/shard_map/ppermute | solution.py:84
  29.7 15.7 %collective-permute-start.4 = (bf16[72,768]{1,0:T(8,128)(2,1)S(1)}, bf16[72,768]{1,0:T(8,128)(2,1)S(1)}, u32[]{:S(2)}, u32[]{:S(2)}) collective-permute-start(bf16[72,768]{1,0:T(8,128)(2,1)S(1)} %get-tuple-element.370), channel_id=1, source_target_pairs={{0,20},{4,16},{8,28},{12,24},{16,4},{20,0},{24,12},{28,8},{1,21},{... | collective-permute-start | bytes 331784 | tf_op jit(solution)/shard_map/ppermute | solution.py:84
  31.9 13.5 %collective-permute-start.5 = (bf16[72,768]{1,0:T(8,128)(2,1)S(1)}, bf16[72,768]{1,0:T(8,128)(2,1)S(1)}, u32[]{:S(2)}, u32[]{:S(2)}) collective-permute-start(bf16[72,768]{1,0:T(8,128)(2,1)S(1)} %get-tuple-element.371), channel_id=1, source_target_pairs={{0,24},{4,28},{8,16},{12,20},{16,8},{20,12},{24,0},{28,4},{1,25},{... | collective-permute-start | bytes 331784 | tf_op jit(solution)/shard_map/ppermute | solution.py:84
  51.2 14.5 %collective-permute-start.13 = (bf16[512,768]{1,0:T(8,128)(2,1)S(1)}, bf16[512,768]{1,0:T(8,128)(2,1)S(1)}, u32[]{:S(2)}, u32[]{:S(2)}) collective-permute-start(bf16[512,768]{1,0:T(8,128)(2,1)S(1)} %get-tuple-element.434.refs_9_), channel_id=1, source_target_pairs={{0,1},{1,0},{2,3},{3,2},{4,5},{5,4},{6,7},{7,6},{8,9},{9,8},{10,11... | collective-permute-start | bytes 2359304 | tf_op jit(solution)/shard_map/ppermute | solution.py:84
  51.2 23.9 %collective-permute-start.16 = (bf16[512,768]{1,0:T(8,128)(2,1)S(1)}, bf16[512,768]{1,0:T(8,128)(2,1)S(1)}, u32[]{:S(2)}, u32[]{:S(2)}) collective-permute-start(bf16[512,768]{1,0:T(8,128)(2,1)S(1)} %get-tuple-element.434.refs_9_), channel_id=1, source_target_pairs={{0,2},{1,3},{2,0},{3,1},{4,6},{5,7},{6,4},{7,5},{8,10},{9,11},{10,... | collective-permute-start | bytes 2359304 | tf_op jit(solution)/shard_map/ppermute | solution.py:84
  61.1 14.0 %collective-permute-start.11 = (bf16[128,2048]{1,0:T(8,128)(2,1)S(1)}, bf16[128,2048]{1,0:T(8,128)(2,1)S(1)}, u32[]{:S(2)}, u32[]{:S(2)}) collective-permute-start(bf16[128,2048]{1,0:T(8,128)(2,1)S(1)} %collective-permute-done.9.refs_3_), channel_id=1, source_target_pairs={{0,8},{8,16},{16,24},{24,28},{28,20},{20,12},{12,4},{4,0},{1,9},{9... | collective-permute-start | bytes 1572872 | tf_op jit(solution)/shard_map/ppermute | solution.py:45
  77.3 24.3 %collective-permute-start.20 = (bf16[128,2048]{1,0:T(8,128)(2,1)S(1)}, bf16[128,2048]{1,0:T(8,128)(2,1)S(1)}, u32[]{:S(2)}, u32[]{:S(2)}) collective-permute-start(bf16[128,2048]{1,0:T(8,128)(2,1)S(1)} %bitcast.130), channel_id=1, source_target_pairs={{0,8},{8,16},{16,24},{24,28},{28,20},{20,12},{12,4},{4,0},{1,9},{9... | collective-permute-start | bytes 1572872 | tf_op jit(solution)/shard_map/ppermute | solution.py:45
  77.6 24.0 %collective-permute-start.21 = (bf16[128,2048]{1,0:T(8,128)(2,1)S(1)}, bf16[128,2048]{1,0:T(8,128)(2,1)S(1)}, u32[]{:S(2)}, u32[]{:S(2)}) collective-permute-start(bf16[128,2048]{1,0:T(8,128)(2,1)S(1)} %bitcast.131), channel_id=1, source_target_pairs={{8,0},{16,8},{24,16},{28,24},{20,28},{12,20},{4,12},{0,4},{9,1},{1... | collective-permute-start | bytes 1572872 | tf_op jit(solution)/shard_map/ppermute | solution.py:48
  101.6 18.0 %collective-permute-start.24 = (bf16[128,2048]{1,0:T(8,128)(2,1)S(1)}, bf16[128,2048]{1,0:T(8,128)(2,1)S(1)}, u32[]{:S(2)}, u32[]{:S(2)}) collective-permute-start(bf16[128,2048]{1,0:T(8,128)(2,1)S(1)} %collective-permute-done.20.refs_2_), channel_id=1, source_target_pairs={{0,8},{8,16},{16,24},{24,28},{28,20},{20,12},{12,4},{4,0},{1,9},{9... | collective-permute-start | bytes 1572872 | tf_op jit(solution)/shard_map/ppermute | solution.py:45
  103.7 17.9 %collective-permute-start.25 = (bf16[128,2048]{1,0:T(8,128)(2,1)S(1)}, bf16[128,2048]{1,0:T(8,128)(2,1)S(1)}, u32[]{:S(2)}, u32[]{:S(2)}) collective-permute-start(bf16[128,2048]{1,0:T(8,128)(2,1)S(1)} %collective-permute-done.21.refs_3_), channel_id=1, source_target_pairs={{8,0},{16,8},{24,16},{28,24},{20,28},{12,20},{4,12},{0,4},{9,1},{1... | collective-permute-start | bytes 1572872 | tf_op jit(solution)/shard_map/ppermute | solution.py:48
  110.6 20.2 %collective-permute-start.22 = (bf16[128,2048]{1,0:T(8,128)(2,1)S(1)}, bf16[128,2048]{1,0:T(8,128)(2,1)S(1)}, u32[]{:S(2)}, u32[]{:S(2)}) collective-permute-start(bf16[128,2048]{1,0:T(8,128)(2,1)S(1)} %get-tuple-element.739), channel_id=1, source_target_pairs={{0,8},{8,16},{16,24},{24,28},{28,20},{20,12},{12,4},{4,0},{1,9},{9... | collective-permute-start | bytes 1572872 | tf_op jit(solution)/shard_map/ppermute | solution.py:45
  112.4 20.5 %collective-permute-start.23 = (bf16[128,2048]{1,0:T(8,128)(2,1)S(1)}, bf16[128,2048]{1,0:T(8,128)(2,1)S(1)}, u32[]{:S(2)}, u32[]{:S(2)}) collective-permute-start(bf16[128,2048]{1,0:T(8,128)(2,1)S(1)} %get-tuple-element.738), channel_id=1, source_target_pairs={{8,0},{16,8},{24,16},{28,24},{20,28},{12,20},{4,12},{0,4},{9,1},{1... | collective-permute-start | bytes 1572872 | tf_op jit(solution)/shard_map/ppermute | solution.py:48
  121.6 20.4 %collective-permute-start.28 = (bf16[128,2048]{1,0:T(8,128)(2,1)S(1)}, bf16[128,2048]{1,0:T(8,128)(2,1)S(1)}, u32[]{:S(2)}, u32[]{:S(2)}) collective-permute-start(bf16[128,2048]{1,0:T(8,128)(2,1)S(1)} %collective-permute-done.24.refs_2_), channel_id=1, source_target_pairs={{0,8},{8,16},{16,24},{24,28},{28,20},{20,12},{12,4},{4,0},{1,9},{9... | collective-permute-start | bytes 1572872 | tf_op jit(solution)/shard_map/ppermute | solution.py:45
  123.4 20.7 %collective-permute-start.29 = (bf16[128,2048]{1,0:T(8,128)(2,1)S(1)}, bf16[128,2048]{1,0:T(8,128)(2,1)S(1)}, u32[]{:S(2)}, u32[]{:S(2)}) collective-permute-start(bf16[128,2048]{1,0:T(8,128)(2,1)S(1)} %collective-permute-done.25.refs_3_), channel_id=1, source_target_pairs={{8,0},{16,8},{24,16},{28,24},{20,28},{12,20},{4,12},{0,4},{9,1},{1... | collective-permute-start | bytes 1572872 | tf_op jit(solution)/shard_map/ppermute | solution.py:48
  133.1 18.4 %collective-permute-start.26 = (bf16[128,2048]{1,0:T(8,128)(2,1)S(1)}, bf16[128,2048]{1,0:T(8,128)(2,1)S(1)}, u32[]{:S(2)}, u32[]{:S(2)}) collective-permute-start(bf16[128,2048]{1,0:T(8,128)(2,1)S(1)} %get-tuple-element.737), channel_id=1, source_target_pairs={{0,8},{8,16},{16,24},{24,28},{28,20},{20,12},{12,4},{4,0},{1,9},{9... | collective-permute-start | bytes 1572872 | tf_op jit(solution)/shard_map/ppermute | solution.py:45
  135.0 17.8 %collective-permute-start.27 = (bf16[128,2048]{1,0:T(8,128)(2,1)S(1)}, bf16[128,2048]{1,0:T(8,128)(2,1)S(1)}, u32[]{:S(2)}, u32[]{:S(2)}) collective-permute-start(bf16[128,2048]{1,0:T(8,128)(2,1)S(1)} %get-tuple-element.736), channel_id=1, source_target_pairs={{8,0},{16,8},{24,16},{28,24},{20,28},{12,20},{4,12},{0,4},{9,1},{1... | collective-permute-start | bytes 1572872 | tf_op jit(solution)/shard_map/ppermute | solution.py:48
  167.2 18.1 %collective-permute-start.32 = (bf16[128,2048]{1,0:T(8,128)(2,1)S(1)}, bf16[128,2048]{1,0:T(8,128)(2,1)S(1)}, u32[]{:S(2)}, u32[]{:S(2)}) collective-permute-start(bf16[128,2048]{1,0:T(8,128)(2,1)S(1)} %get-tuple-element.488.refs_0_), channel_id=1, source_target_pairs={{0,8},{8,16},{16,24},{24,28},{28,20},{20,12},{12,4},{4,0},{1,9},{9... | collective-permute-start | bytes 1572872 | tf_op jit(solution)/shard_map/ppermute | solution.py:45
  168.7 16.5 %collective-permute-start.33 = (bf16[128,2048]{1,0:T(8,128)(2,1)S(1)}, bf16[128,2048]{1,0:T(8,128)(2,1)S(1)}, u32[]{:S(2)}, u32[]{:S(2)}) collective-permute-start(bf16[128,2048]{1,0:T(8,128)(2,1)S(1)} %get-tuple-element.488.refs_0_), channel_id=1, source_target_pairs={{8,0},{16,8},{24,16},{28,24},{20,28},{12,20},{4,12},{0,4},{9,1},{1... | collective-permute-start | bytes 1572872 | tf_op jit(solution)/shard_map/ppermute | solution.py:48
  169.3 14.7 %collective-permute-start.34 = (bf16[64,2048]{1,0:T(8,128)(2,1)S(1)}, bf16[64,2048]{1,0:T(8,128)(2,1)S(1)}, u32[]{:S(2)}, u32[]{:S(2)}) collective-permute-start(bf16[64,2048]{1,0:T(8,128)(2,1)S(1)} %get-tuple-element.443), channel_id=1, source_target_pairs={{0,8},{8,16},{16,24},{24,28},{28,20},{20,12},{12,4},{4,0},{1,9},{9... | collective-permute-start | bytes 786440 | tf_op jit(solution)/shard_map/ppermute | solution.py:45
  170.9 14.4 %collective-permute-start.35 = (bf16[64,2048]{1,0:T(8,128)(2,1)S(1)}, bf16[64,2048]{1,0:T(8,128)(2,1)S(1)}, u32[]{:S(2)}, u32[]{:S(2)}) collective-permute-start(bf16[64,2048]{1,0:T(8,128)(2,1)S(1)} %get-tuple-element.444), channel_id=1, source_target_pairs={{8,0},{16,8},{24,16},{28,24},{20,28},{12,20},{4,12},{0,4},{9,1},{1... | collective-permute-start | bytes 786440 | tf_op jit(solution)/shard_map/ppermute | solution.py:48
  239.3 13.2 %collective-permute-start.48 = (bf16[128,2048]{1,0:T(8,128)(2,1)S(1)}, bf16[128,2048]{1,0:T(8,128)(2,1)S(1)}, u32[]{:S(2)}, u32[]{:S(2)}) collective-permute-start(bf16[128,2048]{1,0:T(8,128)(2,1)S(1)} %get-tuple-element.733), channel_id=1, source_target_pairs={{0,8},{8,16},{16,24},{24,28},{28,20},{20,12},{12,4},{4,0},{1,9},{9... | collective-permute-start | bytes 1572872 | tf_op jit(solution)/shard_map/ppermute | solution.py:45
  247.3 19.2 %collective-permute-start.43 = (bf16[704,512]{1,0:T(8,128)(2,1)}, bf16[704,512]{1,0:T(8,128)(2,1)S(1)}, u32[]{:S(2)}, u32[]{:S(2)}) collective-permute-start(bf16[704,512]{1,0:T(8,128)(2,1)} %fusion.22), channel_id=1, source_target_pairs={{0,2},{1,3},{2,0},{3,1},{4,6},{5,7},{6,4},{7,5},{8,10},{9,11},{10,... | collective-permute-start | bytes 2162696 | tf_op jit(solution)/shard_map/ppermute | solution.py:84
  249.1 33.0 %collective-permute-start.55 = (bf16[704,512]{1,0:T(8,128)(2,1)}, bf16[704,512]{1,0:T(8,128)(2,1)}, u32[]{:S(2)}, u32[]{:S(2)}) collective-permute-start(bf16[704,512]{1,0:T(8,128)(2,1)} %fusion.23), channel_id=1, source_target_pairs={{0,2},{1,3},{2,0},{3,1},{4,6},{5,7},{6,4},{7,5},{8,10},{9,11},{10,... | collective-permute-start | bytes 2162696 | tf_op jit(solution)/shard_map/ppermute | solution.py:84
  253.2 14.6 %collective-permute-start.51 = (bf16[128,2048]{1,0:T(8,128)(2,1)S(1)}, bf16[128,2048]{1,0:T(8,128)(2,1)S(1)}, u32[]{:S(2)}, u32[]{:S(2)}) collective-permute-start(bf16[128,2048]{1,0:T(8,128)(2,1)S(1)} %get-tuple-element.731), channel_id=1, source_target_pairs={{0,8},{8,16},{16,24},{24,28},{28,20},{20,12},{12,4},{4,0},{1,9},{9... | collective-permute-start | bytes 1572872 | tf_op jit(solution)/shard_map/ppermute | solution.py:45
  254.0 13.8 %collective-permute-start.52 = (bf16[128,2048]{1,0:T(8,128)(2,1)S(1)}, bf16[128,2048]{1,0:T(8,128)(2,1)S(1)}, u32[]{:S(2)}, u32[]{:S(2)}) collective-permute-start(bf16[128,2048]{1,0:T(8,128)(2,1)S(1)} %get-tuple-element.730), channel_id=1, source_target_pairs={{8,0},{16,8},{24,16},{28,24},{20,28},{12,20},{4,12},{0,4},{9,1},{1... | collective-permute-start | bytes 1572872 | tf_op jit(solution)/shard_map/ppermute | solution.py:48
  268.1 16.3 %collective-permute-start.53 = (bf16[128,2048]{1,0:T(8,128)(2,1)S(1)}, bf16[128,2048]{1,0:T(8,128)(2,1)S(1)}, u32[]{:S(2)}, u32[]{:S(2)}) collective-permute-start(bf16[128,2048]{1,0:T(8,128)(2,1)S(1)} %get-tuple-element.729), channel_id=1, source_target_pairs={{0,8},{8,16},{16,24},{24,28},{28,20},{20,12},{12,4},{4,0},{1,9},{9... | collective-permute-start | bytes 1572872 | tf_op jit(solution)/shard_map/ppermute | solution.py:45
  268.9 15.6 %collective-permute-start.54 = (bf16[128,2048]{1,0:T(8,128)(2,1)S(1)}, bf16[128,2048]{1,0:T(8,128)(2,1)S(1)}, u32[]{:S(2)}, u32[]{:S(2)}) collective-permute-start(bf16[128,2048]{1,0:T(8,128)(2,1)S(1)} %get-tuple-element.728), channel_id=1, source_target_pairs={{8,0},{16,8},{24,16},{28,24},{20,28},{12,20},{4,12},{0,4},{9,1},{1... | collective-permute-start | bytes 1572872 | tf_op jit(solution)/shard_map/ppermute | solution.py:48
  270.2 27.2 %collective-permute-start.58 = (bf16[704,512]{1,0:T(8,128)(2,1)S(1)}, bf16[704,512]{1,0:T(8,128)(2,1)S(1)}, u32[]{:S(2)}, u32[]{:S(2)}) collective-permute-start(bf16[704,512]{1,0:T(8,128)(2,1)S(1)} %fusion.24), channel_id=1, source_target_pairs={{0,2},{1,3},{2,0},{3,1},{4,6},{5,7},{6,4},{7,5},{8,10},{9,11},{10,... | collective-permute-start | bytes 2162696 | tf_op jit(solution)/shard_map/ppermute | solution.py:84
  271.9 40.5 %collective-permute-start.50 = (bf16[704,512]{1,0:T(8,128)(2,1)S(1)}, bf16[704,512]{1,0:T(8,128)(2,1)S(1)}, u32[]{:S(2)}, u32[]{:S(2)}) collective-permute-start(bf16[704,512]{1,0:T(8,128)(2,1)S(1)} %add_convert_fusion.4.refs_0_), channel_id=1, source_target_pairs={{0,2},{1,3},{2,0},{3,1},{4,6},{5,7},{6,4},{7,5},{8,10},{9,11},{10,... | collective-permute-start | bytes 2162696 | tf_op jit(solution)/shard_map/ppermute | solution.py:84
  286.4 13.0 %collective-permute-start.56 = (bf16[128,2048]{1,0:T(8,128)(2,1)S(1)}, bf16[128,2048]{1,0:T(8,128)(2,1)S(1)}, u32[]{:S(2)}, u32[]{:S(2)}) collective-permute-start(bf16[128,2048]{1,0:T(8,128)(2,1)S(1)} %get-tuple-element.708.refs_0_), channel_id=1, source_target_pairs={{0,8},{8,16},{16,24},{24,28},{28,20},{20,12},{12,4},{4,0},{1,9},{9... | collective-permute-start | bytes 1572872 | tf_op jit(solution)/shard_map/ppermute | solution.py:45
  299.8 16.6 %collective-permute-start.61 = (bf16[128,2048]{1,0:T(8,128)(2,1)S(1)}, bf16[128,2048]{1,0:T(8,128)(2,1)S(1)}, u32[]{:S(2)}, u32[]{:S(2)}) collective-permute-start(bf16[128,2048]{1,0:T(8,128)(2,1)S(1)} %collective-permute-done.56.refs_1_), channel_id=1, source_target_pairs={{0,8},{8,16},{16,24},{24,28},{28,20},{20,12},{12,4},{4,0},{1,9},{9... | collective-permute-start | bytes 1572872 | tf_op jit(solution)/shard_map/ppermute | solution.py:45
  300.6 15.8 %collective-permute-start.62 = (bf16[128,2048]{1,0:T(8,128)(2,1)S(1)}, bf16[128,2048]{1,0:T(8,128)(2,1)S(1)}, u32[]{:S(2)}, u32[]{:S(2)}) collective-permute-start(bf16[128,2048]{1,0:T(8,128)(2,1)S(1)} %collective-permute-done.57.refs_2_), channel_id=1, source_target_pairs={{8,0},{16,8},{24,16},{28,24},{20,28},{12,20},{4,12},{0,4},{9,1},{1... | collective-permute-start | bytes 1572872 | tf_op jit(solution)/shard_map/ppermute | solution.py:48
  313.5 17.8 %collective-permute-start.65 = (bf16[704,512]{1,0:T(8,128)(2,1)S(1)}, bf16[704,512]{1,0:T(8,128)(2,1)S(1)}, u32[]{:S(2)}, u32[]{:S(2)}) collective-permute-start(bf16[704,512]{1,0:T(8,128)(2,1)S(1)} %add_convert_fusion.3.refs_0_), channel_id=1, source_target_pairs={{0,2},{1,3},{2,0},{3,1},{4,6},{5,7},{6,4},{7,5},{8,10},{9,11},{10,... | collective-permute-start | bytes 2162696 | tf_op jit(solution)/shard_map/ppermute | solution.py:84
  316.4 16.7 %collective-permute-start.63 = (bf16[128,2048]{1,0:T(8,128)(2,1)S(1)}, bf16[128,2048]{1,0:T(8,128)(2,1)S(1)}, u32[]{:S(2)}, u32[]{:S(2)}) collective-permute-start(bf16[128,2048]{1,0:T(8,128)(2,1)S(1)} %collective-permute-done.61.refs_3_), channel_id=1, source_target_pairs={{0,8},{8,16},{16,24},{24,28},{28,20},{20,12},{12,4},{4,0},{1,9},{9... | collective-permute-start | bytes 1572872 | tf_op jit(solution)/shard_map/ppermute | solution.py:45
  317.0 16.0 %collective-permute-start.64 = (bf16[128,2048]{1,0:T(8,128)(2,1)S(1)}, bf16[128,2048]{1,0:T(8,128)(2,1)S(1)}, u32[]{:S(2)}, u32[]{:S(2)}) collective-permute-start(bf16[128,2048]{1,0:T(8,128)(2,1)S(1)} %collective-permute-done.62.refs_4_), channel_id=1, source_target_pairs={{8,0},{16,8},{24,16},{28,24},{20,28},{12,20},{4,12},{0,4},{9,1},{1... | collective-permute-start | bytes 1572872 | tf_op jit(solution)/shard_map/ppermute | solution.py:48
  318.5 16.8 %collective-permute-start.59 = (bf16[64,2048]{1,0:T(8,128)(2,1)S(1)}, bf16[64,2048]{1,0:T(8,128)(2,1)S(1)}, u32[]{:S(2)}, u32[]{:S(2)}) collective-permute-start(bf16[64,2048]{1,0:T(8,128)(2,1)S(1)} %get-tuple-element.566), channel_id=1, source_target_pairs={{0,8},{8,16},{16,24},{24,28},{28,20},{20,12},{12,4},{4,0},{1,9},{9... | collective-permute-start | bytes 786440 | tf_op jit(solution)/shard_map/ppermute | solution.py:45
  319.0 16.5 %collective-permute-start.60 = (bf16[64,2048]{1,0:T(8,128)(2,1)S(1)}, bf16[64,2048]{1,0:T(8,128)(2,1)S(1)}, u32[]{:S(2)}, u32[]{:S(2)}) collective-permute-start(bf16[64,2048]{1,0:T(8,128)(2,1)S(1)} %get-tuple-element.567), channel_id=1, source_target_pairs={{8,0},{16,8},{24,16},{28,24},{20,28},{12,20},{4,12},{0,4},{9,1},{1... | collective-permute-start | bytes 786440 | tf_op jit(solution)/shard_map/ppermute | solution.py:48
  331.3 16.8 %collective-permute-start.70 = (bf16[704,512]{1,0:T(8,128)(2,1)S(1)}, bf16[704,512]{1,0:T(8,128)(2,1)S(1)}, u32[]{:S(2)}, u32[]{:S(2)}) collective-permute-start(bf16[704,512]{1,0:T(8,128)(2,1)S(1)} %add_convert_fusion.2.refs_0_), channel_id=1, source_target_pairs={{0,2},{1,3},{2,0},{3,1},{4,6},{5,7},{6,4},{7,5},{8,10},{9,11},{10,... | collective-permute-start | bytes 2162696 | tf_op jit(solution)/shard_map/ppermute | solution.py:84
  335.8 18.3 %collective-permute-start.66 = (bf16[128,2048]{1,0:T(8,128)(2,1)S(1)}, bf16[128,2048]{1,0:T(8,128)(2,1)S(1)}, u32[]{:S(2)}, u32[]{:S(2)}) collective-permute-start(bf16[128,2048]{1,0:T(8,128)(2,1)S(1)} %get-tuple-element.727), channel_id=1, source_target_pairs={{0,8},{8,16},{16,24},{24,28},{28,20},{20,12},{12,4},{4,0},{1,9},{9... | collective-permute-start | bytes 1572872 | tf_op jit(solution)/shard_map/ppermute | solution.py:45
  336.4 17.7 %collective-permute-start.67 = (bf16[128,2048]{1,0:T(8,128)(2,1)S(1)}, bf16[128,2048]{1,0:T(8,128)(2,1)S(1)}, u32[]{:S(2)}, u32[]{:S(2)}) collective-permute-start(bf16[128,2048]{1,0:T(8,128)(2,1)S(1)} %get-tuple-element.726), channel_id=1, source_target_pairs={{8,0},{16,8},{24,16},{28,24},{20,28},{12,20},{4,12},{0,4},{9,1},{1... | collective-permute-start | bytes 1572872 | tf_op jit(solution)/shard_map/ppermute | solution.py:48
  337.9 15.6 %collective-permute-start.68 = (bf16[64,2048]{1,0:T(8,128)(2,1)S(1)}, bf16[64,2048]{1,0:T(8,128)(2,1)S(1)}, u32[]{:S(2)}, u32[]{:S(2)}) collective-permute-start(bf16[64,2048]{1,0:T(8,128)(2,1)S(1)} %get-tuple-element.580), channel_id=1, source_target_pairs={{0,8},{8,16},{16,24},{24,28},{28,20},{20,12},{12,4},{4,0},{1,9},{9... | collective-permute-start | bytes 786440 | tf_op jit(solution)/shard_map/ppermute | solution.py:45
  338.5 15.6 %collective-permute-start.69 = (bf16[64,2048]{1,0:T(8,128)(2,1)S(1)}, bf16[64,2048]{1,0:T(8,128)(2,1)S(1)}, u32[]{:S(2)}, u32[]{:S(2)}) collective-permute-start(bf16[64,2048]{1,0:T(8,128)(2,1)S(1)} %get-tuple-element.581), channel_id=1, source_target_pairs={{8,0},{16,8},{24,16},{28,24},{20,28},{12,20},{4,12},{0,4},{9,1},{1... | collective-permute-start | bytes 786440 | tf_op jit(solution)/shard_map/ppermute | solution.py:48
  379.2 19.4 %collective-permute-start.74 = (bf16[512,768]{1,0:T(8,128)(2,1)S(1)}, bf16[512,768]{1,0:T(8,128)(2,1)S(1)}, u32[]{:S(2)}, u32[]{:S(2)}) collective-permute-start(bf16[512,768]{1,0:T(8,128)(2,1)S(1)} %get-tuple-element.762), channel_id=1, source_target_pairs={{0,2},{1,3},{2,0},{3,1},{4,6},{5,7},{6,4},{7,5},{8,10},{9,11},{10,... | collective-permute-start | bytes 2359304 | tf_op jit(solution)/shard_map/ppermute | solution.py:84
  385.2 22.4 %collective-permute-start.77 = (bf16[128,2048]{1,0:T(8,128)(2,1)}, bf16[128,2048]{1,0:T(8,128)(2,1)}, u32[]{:S(2)}, u32[]{:S(2)}) collective-permute-start(bf16[128,2048]{1,0:T(8,128)(2,1)} %get-tuple-element.723), channel_id=1, source_target_pairs={{0,8},{8,16},{16,24},{24,28},{28,20},{20,12},{12,4},{4,0},{1,9},{9... | collective-permute-start | bytes 1572872 | tf_op jit(solution)/shard_map/ppermute | solution.py:45
  386.7 21.4 %collective-permute-start.78 = (bf16[128,2048]{1,0:T(8,128)(2,1)}, bf16[128,2048]{1,0:T(8,128)(2,1)}, u32[]{:S(2)}, u32[]{:S(2)}) collective-permute-start(bf16[128,2048]{1,0:T(8,128)(2,1)} %get-tuple-element.722), channel_id=1, source_target_pairs={{8,0},{16,8},{24,16},{28,24},{20,28},{12,20},{4,12},{0,4},{9,1},{1... | collective-permute-start | bytes 1572872 | tf_op jit(solution)/shard_map/ppermute | solution.py:48
  402.0 28.1 %all-to-all-start = ((bf16[8,64,768]{2,1,0:T(8,128)(2,1)}), bf16[8,64,768]{2,1,0:T(8,128)(2,1)S(1)}, u32[]{:S(2)}, u32[]{:S(2)}) async-start(bf16[8,64,768]{2,1,0:T(8,128)(2,1)} %bitcast.138), calls=%async_computation | async-start | bytes 1572864 | tf_op jit(solution)/shard_map/all_to_all | solution.py:883
  407.1 18.2 %collective-permute-start.81 = (bf16[704,512]{1,0:T(8,128)(2,1)}, bf16[704,512]{1,0:T(8,128)(2,1)}, u32[]{:S(2)}, u32[]{:S(2)}) collective-permute-start(bf16[704,512]{1,0:T(8,128)(2,1)} %copy-done.18), channel_id=1, source_target_pairs={{0,1},{1,0},{2,3},{3,2},{4,5},{5,4},{6,7},{7,6},{8,9},{9,8},{10,11... | collective-permute-start | bytes 2162696 | tf_op jit(solution)/shard_map/ppermute | solution.py:84
  407.7 17.6 %collective-permute-start.82 = (bf16[704,512]{1,0:T(8,128)(2,1)}, bf16[704,512]{1,0:T(8,128)(2,1)}, u32[]{:S(2)}, u32[]{:S(2)}) collective-permute-start(bf16[704,512]{1,0:T(8,128)(2,1)} %copy-done.22), channel_id=1, source_target_pairs={{0,1},{1,0},{2,3},{3,2},{4,5},{5,4},{6,7},{7,6},{8,9},{9,8},{10,11... | collective-permute-start | bytes 2162696 | tf_op jit(solution)/shard_map/ppermute | solution.py:84
  411.2 21.3 %collective-permute-start.79 = (bf16[128,2048]{1,0:T(8,128)(2,1)}, bf16[128,2048]{1,0:T(8,128)(2,1)}, u32[]{:S(2)}, u32[]{:S(2)}) collective-permute-start(bf16[128,2048]{1,0:T(8,128)(2,1)} %get-tuple-element.721), channel_id=1, source_target_pairs={{0,8},{8,16},{16,24},{24,28},{28,20},{20,12},{12,4},{4,0},{1,9},{9... | collective-permute-start | bytes 1572872 | tf_op jit(solution)/shard_map/ppermute | solution.py:45
  414.1 19.2 %collective-permute-start.80 = (bf16[128,2048]{1,0:T(8,128)(2,1)}, bf16[128,2048]{1,0:T(8,128)(2,1)}, u32[]{:S(2)}, u32[]{:S(2)}) collective-permute-start(bf16[128,2048]{1,0:T(8,128)(2,1)} %get-tuple-element.720), channel_id=1, source_target_pairs={{8,0},{16,8},{24,16},{28,24},{20,28},{12,20},{4,12},{0,4},{9,1},{1... | collective-permute-start | bytes 1572872 | tf_op jit(solution)/shard_map/ppermute | solution.py:48
  418.6 42.2 %collective-permute-start.71 = (bf16[128,2048]{1,0:T(8,128)(2,1)}, bf16[128,2048]{1,0:T(8,128)(2,1)}, u32[]{:S(2)}, u32[]{:S(2)}) collective-permute-start(bf16[128,2048]{1,0:T(8,128)(2,1)} %get-tuple-element.725), channel_id=1, source_target_pairs={{0,8},{8,16},{16,24},{24,28},{28,20},{20,12},{12,4},{4,0},{1,9},{9... | collective-permute-start | bytes 1572872 | tf_op jit(solution)/shard_map/ppermute | solution.py:45
  425.2 36.0 %collective-permute-start.72 = (bf16[128,2048]{1,0:T(8,128)(2,1)}, bf16[128,2048]{1,0:T(8,128)(2,1)}, u32[]{:S(2)}, u32[]{:S(2)}) collective-permute-start(bf16[128,2048]{1,0:T(8,128)(2,1)} %get-tuple-element.724), channel_id=1, source_target_pairs={{8,0},{16,8},{24,16},{28,24},{20,28},{12,20},{4,12},{0,4},{9,1},{1... | collective-permute-start | bytes 1572872 | tf_op jit(solution)/shard_map/ppermute | solution.py:48
  436.4 16.7 %collective-permute-start.87 = (bf16[128,2048]{1,0:T(8,128)(2,1)}, bf16[128,2048]{1,0:T(8,128)(2,1)}, u32[]{:S(2)}, u32[]{:S(2)}) collective-permute-start(bf16[128,2048]{1,0:T(8,128)(2,1)} %get-tuple-element.719), channel_id=1, source_target_pairs={{0,8},{8,16},{16,24},{24,28},{28,20},{20,12},{12,4},{4,0},{1,9},{9... | collective-permute-start | bytes 1572872 | tf_op jit(solution)/shard_map/ppermute | solution.py:45
  443.9 15.5 %collective-permute-start.86 = (bf16[64,6144]{1,0:T(8,128)(2,1)S(1)}, bf16[64,6144]{1,0:T(8,128)(2,1)}, u32[]{:S(2)}, u32[]{:S(2)}) collective-permute-start(bf16[64,6144]{1,0:T(8,128)(2,1)S(1)} %beside.1.refs_0_), channel_id=1, source_target_pairs={{0,2},{1,3},{2,0},{3,1},{4,6},{5,7},{6,4},{7,5},{8,10},{9,11},{10,... | collective-permute-start | bytes 2359304 | tf_op jit(solution)/shard_map/ppermute | solution.py:84
  455.3 12.9 %collective-permute-start.96 = (bf16[704,512]{1,0:T(8,128)(2,1)}, bf16[704,512]{1,0:T(8,128)(2,1)S(1)}, u32[]{:S(2)}, u32[]{:S(2)}) collective-permute-start(bf16[704,512]{1,0:T(8,128)(2,1)} %copy-done.14), channel_id=1, source_target_pairs={{0,1},{1,0},{2,3},{3,2},{4,5},{5,4},{6,7},{7,6},{8,9},{9,8},{10,11... | collective-permute-start | bytes 2162696 | tf_op jit(solution)/shard_map/ppermute | solution.py:84
  460.6 29.3 %collective-permute-start.98 = (bf16[64,6144]{1,0:T(8,128)(2,1)S(1)}, bf16[64,6144]{1,0:T(8,128)(2,1)S(1)}, u32[]{:S(2)}, u32[]{:S(2)}) collective-permute-start(bf16[64,6144]{1,0:T(8,128)(2,1)S(1)} %beside.1.refs_0_), channel_id=1, source_target_pairs={{0,1},{1,0},{2,3},{3,2},{4,5},{5,4},{6,7},{7,6},{8,9},{9,8},{10,11... | collective-permute-start | bytes 2359304 | tf_op jit(solution)/shard_map/ppermute | solution.py:84
  461.2 28.7 %collective-permute-start.99 = (bf16[64,6144]{1,0:T(8,128)(2,1)}, bf16[64,6144]{1,0:T(8,128)(2,1)S(1)}, u32[]{:S(2)}, u32[]{:S(2)}) collective-permute-start(bf16[64,6144]{1,0:T(8,128)(2,1)} %collective-permute-done.86.refs_1_), channel_id=1, source_target_pairs={{0,1},{1,0},{2,3},{3,2},{4,5},{5,4},{6,7},{7,6},{8,9},{9,8},{10,11... | collective-permute-start | bytes 2359304 | tf_op jit(solution)/shard_map/ppermute | solution.py:84
  468.2 31.2 %collective-permute-start.89 = (bf16[128,2048]{1,0:T(8,128)(2,1)S(1)}, bf16[128,2048]{1,0:T(8,128)(2,1)S(1)}, u32[]{:S(2)}, u32[]{:S(2)}) collective-permute-start(bf16[128,2048]{1,0:T(8,128)(2,1)S(1)} %get-tuple-element.717), channel_id=1, source_target_pairs={{0,8},{8,16},{16,24},{24,28},{28,20},{20,12},{12,4},{4,0},{1,9},{9... | collective-permute-start | bytes 1572872 | tf_op jit(solution)/shard_map/ppermute | solution.py:45
  473.3 26.2 %collective-permute-start.90 = (bf16[128,2048]{1,0:T(8,128)(2,1)S(1)}, bf16[128,2048]{1,0:T(8,128)(2,1)S(1)}, u32[]{:S(2)}, u32[]{:S(2)}) collective-permute-start(bf16[128,2048]{1,0:T(8,128)(2,1)S(1)} %get-tuple-element.716), channel_id=1, source_target_pairs={{8,0},{16,8},{24,16},{28,24},{20,28},{12,20},{4,12},{0,4},{9,1},{1... | collective-permute-start | bytes 1572872 | tf_op jit(solution)/shard_map/ppermute | solution.py:48
  (91 other events, 977.2 us)

commit v3 on v2

--- a/solution.py
+++ b/solution.py
@@ -419,6 +419,84 @@
     )
 
 
+def products_kernel(items, *refs):
+    out_ref, offset = refs[-1], 0
+    rows = out_ref.shape[0]
+    for (start, last), a, b in zip(items, refs[:-1:2], refs[1:-1:2], strict=True):
+        width = b.shape[0 if last else 1]
+        left = a[start : start + rows, :]
+        for begin in range(0, width, 512):
+            columns = slice(begin, begin + 512)
+            out_ref[:, offset + begin : offset + begin + 512] = (
+                dot_last(left, b[columns, :]) if last else dot(left, b[:, columns])
+            )
+        offset += width
+
+
+def products(rows, items, *given):
+    width = sum(b.shape[0 if last else 1] for (_, last), b in zip(items, given[1::2], strict=True))
+    out = jax.ShapeDtypeStruct((rows, width), f32)
+    return once(functools.partial(products_kernel, items), "products", 8, out, [], *given)
+
+
+def hop_kernel(items, *refs):
+    given, (first_ref, second_ref, ahead_ref, behind_ref) = refs[:-4], refs[-4:]
+    rows, half, offset = ahead_ref.shape[0], first_ref.shape[0], 0
+    for (start, last), a, b in zip(items, given[::2], given[1::2], strict=True):
+        width = b.shape[0 if last else 1]
+        left = a[start : start + 2 * rows, :]
+        for begin in range(0, width, 512):
+            columns = slice(begin, begin + 512)
+            term = dot_last(left, b[columns, :]) if last else dot(left, b[:, columns])
+            here = slice(offset + begin, offset + begin + 512)
+            first, second = first_ref[:, here].astype(f32), second_ref[:, here].astype(f32)
+            ahead_ref[:half, here] = (term[rows : rows + half] + first).astype(bf16)
+            behind_ref[rows - half :, here] = (term[rows - half : rows] + second).astype(bf16)
+            if half < rows:
+                ahead_ref[half:, here] = term[rows + half :].astype(bf16)
+                behind_ref[: rows - half, here] = term[: rows - half].astype(bf16)
+        offset += width
+
+
+def hop(rows, items, given, first, second):
+    out = jax.ShapeDtypeStruct((rows, first.shape[1]), bf16)
+    return once(functools.partial(hop_kernel, items), "hop", 10, (out, out), [], *given, first, second)
+
+
+def vectors_kernel(n, peers_ref, joined_ref, w_ref, local_ref, give_ref, shift_ref, gain_ref, two_ref, out_ref, turned):
+    width = joined_ref.shape[1] // 3
+    ones = jnp.ones((8, joined_ref.shape[0]), bf16)
+    bias = dot(ones, joined_ref[...])[0:1]
+    parts = []
+    for _ in range(3):
+        parts.append(bias.astype(bf16).astype(f32))
+        bias = bias - parts[-1]
+    shift = jnp.sum(dot_last(jnp.concatenate(parts, 0).astype(bf16), w_ref[...]), axis=0, keepdims=True)
+    ones = jnp.ones((8, w_ref.shape[1]), bf16)
+    half = w_ref.shape[0] // 2
+    rows = []
+    for start, ref in ((0, local_ref), (half, give_ref)):
+        product = w_ref[start : start + half, :].astype(f32) * ref[...].astype(f32)
+        upper = product.astype(bf16)
+        lower = (product - upper.astype(f32)).astype(bf16)
+        rows.append((dot_last(ones, upper) + dot_last(ones, lower))[0:1])
+    both = jnp.concatenate([jnp.concatenate(rows, 1), shift], 0)
+    for number in range(4):
+
+        @pl.when(peers_ref[0] == number)
+        def _(number=number):
+            turned[...] = in_plain_order(both, number, n)
+
+    out_ref[...] = jnp.zeros_like(out_ref)
+    out_ref[0:1, :] = (turned[0:1, :] - shift_ref[...] * turned[1:2, :]) / gain_ref[...]
+    out_ref[1:2, :] = turned[1:2, :]
+    out_ref[2:4, :] = two_ref[...]
+    total = sum(parts)
+    for c in range(3):
+        here = pl.ds(pl.multiple_of(peers_ref[1] * width, BLOCK), width)
+        out_ref[4 + c : 5 + c, here] = total[:, c * width : (c + 1) * width]
+
+
 def exchange(blocks):
     return [blocks[0]] + [swap(v, "seq", k) for k, v in enumerate(blocks) if k]
 
@@ -501,15 +579,20 @@
     return jnp.concatenate([x[:, start : start + share] for start in starts], 1)
 
 
-def last_back_kernel(n, peers_ref, term_ref, first_ref, second_ref, unit_ref, inverse_ref, gain_ref, middle_ref, out_ref):
+def last_back_kernel(
+    n, peers_ref, term_ref, first_ref, second_ref, unit_ref, inverse_ref, gain_ref, grad_ref, middle_ref, out_ref, sum_ref
+):
     total = term_ref[...] + first_ref[...].astype(f32) + second_ref[...].astype(f32)
+    model = out_ref.shape[1]
+    sum_ref[...] = (middle_ref[...] + total[:, model:]).astype(bf16)
+    total = total[:, :model]
     for number in range(4):
 
         @pl.when(peers_ref[0] == number)
         def _(number=number):
             out_ref[...] = in_plain_order(total, number, n)
 
-    out_ref[...] = middle_ref[...] + norm_back(out_ref[...], unit_ref[...], inverse_ref[...], gain_ref[...])
+    out_ref[...] = grad_ref[...] + norm_back(out_ref[...], unit_ref[...], inverse_ref[...], gain_ref[...])
 
 
 def beside_kernel(in_ref, out_ref):
@@ -663,7 +746,7 @@
         return jnp.concatenate(normed, 1), unit, inverse
 
     normed, unit_one, inverse_one = line(first_norm, x)
-    normed_blocks = Gather(ring, line, normed)
+    normed_blocks = Gather(ring, line, after(normed, fetched[1]))
 
     piece, places = line(lambda *v: stacked(at, v, extra, tokens), *fetched)
     piece_y, piece_core = other_y(piece), other_core(piece)
@@ -692,12 +775,13 @@
         return v[i * tokens : (i + 1) * tokens]
 
     class Scatter:
-        def __init__(self, given, far, pair, own):
-            self.given, self.pair, self.own = given, pair, own
+        def __init__(self, given, far, pair, own, fused=False):
+            self.given, self.pair, self.own, self.fused = given, pair, own, fused
             top, bottom = line(lambda *v: halves(*[far(*v).astype(bf16)] * 2), *given)
             self.first, self.second = ring.up(top), ring.down(bottom)
             self.d = pairs - 1
-            self.term = line(lambda *v: pair(self.d, *v), *given)
+            if not fused:
+                self.term = line(lambda *v: pair(self.d, *v), *given)
 
         def step(self):
             half = tokens // 2
@@ -709,10 +793,16 @@
                     second = jnp.pad(second, ((half, 0), (0, 0)))
                 return (term[tokens:] + first).astype(bf16), (term[:tokens] + second).astype(bf16)
 
-            first, second = line(add, self.term, self.first, self.second)
+            if self.fused:
+                first, second = line(
+                    lambda first, second, *v: self.pair(self.d, first, second, *v), self.first, self.second, *self.given
+                )
+            else:
+                first, second = line(add, self.term, self.first, self.second)
             self.first, self.second = ring.up(first), ring.down(second)
             self.d -= 1
-            self.term = line(lambda *v: self.pair(self.d, *v) if self.d else self.own(*v), *self.given)
+            if not (self.fused and self.d):
+                self.term = line(lambda *v: self.pair(self.d, *v) if self.d else self.own(*v), *self.given)
 
         def parts(self):
             return self.term, self.first, self.second
@@ -720,8 +810,8 @@
         def finish(self):
             return line(lambda a, b, c: a + b.astype(f32) + c.astype(f32), *self.parts())
 
-    def scattered(given, far, pair, own, fill, whole=True):
-        going = Scatter(given, far, pair, own)
+    def scattered(given, far, pair, own, fill, whole=True, fused=False):
+        going = Scatter(given, far, pair, own, fused)
         for k in range(pairs):
             for work in fill[k] if k < len(fill) else ():
                 work()
@@ -809,34 +899,22 @@
         lambda v, *_: v[tokens:],
         lambda d, _, g, u, *w: both(ffn_rows(g, d), ffn_rows(u, d), *w),
         lambda v, *_: v[:tokens],
-        [(down.one, gate.one, down.two), (gate.two, up.one), (up.two, down.three), (gate.three,)],
+        [(down.one, gate.one), (down.two,), (gate.two, up.one), (down.three,)],
     )
 
     def second_back(grad_two):
         grad_middle = cot.astype(f32) + norm_back(grad_two, unit_two, inverse_two, ln2_gain)
-        return grad_middle, grad_middle.astype(bf16), jnp.sum(grad_two * unit_two, axis=0), jnp.sum(grad_two, axis=0)
-
-    grad_middle, grad_branch, gain_two_grad, bias_two_grad = line(second_back, grad_two)
+        sums = jnp.stack([jnp.sum(grad_two * unit_two, axis=0), jnp.sum(grad_two, axis=0)])
+        return grad_middle, grad_middle.astype(bf16), sums
+
+    grad_middle, grad_branch, two_grads = line(second_back, grad_two)
 
     branch_blocks = Gather(ring, line, grad_branch)
-    going = {}
-
-    def start_out():
-        last_out = line(lambda h, w: dot(last(h), w), all_hidden, w_down)
-        going["out"] = Scatter(
-            (last_out, all_hidden, w_down),
-            lambda v, *_: v[tokens:],
-            lambda d, _, h, w: dot(ffn_rows(h, d), w),
-            lambda v, *_: v[:tokens],
-        )
-
-    fill = [(up.three,), (down.four, start_out), (gate.four,), (lambda: going["out"].step(), up.four)]
+    fill = [(), (gate.three, down.four), (up.two,), (gate.four, down.five)]
     for k in range(pairs):
         for work in fill[k] if k < len(fill) else ():
             work()
         branch_blocks.step()
-    out_sum = going["out"]
-    out_sum.step()
     grad_joined, outer = line(
         lambda w: attend_back(ring.maps, branch_blocks.blocks, w, qkv, mixed, lse, waves, seen_from), w_out
     )
@@ -865,20 +943,20 @@
         give = line(lambda a, b: dot_rows(a[:, model // 2 :], b).astype(bf16), all_normed, grad_joined)
         qkv_grad["give"], qkv_grad["got"] = give, other_core(give)
 
+    def qkv_local():
+        qkv_grad["local"] = line(lambda a, b: dot_rows(a[:, : model // 2], b), all_normed, grad_joined)
+
     def qkv_two():
-        def work(a, b, got):
-            own = dot_rows(a[:, model // 4 : model // 2], b)
-            return (own + got[got.shape[0] // 2 :].astype(f32)).astype(bf16), own
-
-        give, qkv_grad["local_y"] = line(work, all_normed, grad_joined, qkv_grad["got"])
-        qkv_grad["got_y"] = other_y(give)
+        def work(v, got):
+            return (v[model // 4 :] + got[model // 4 :].astype(f32)).astype(bf16)
+
+        qkv_grad["got_y"] = other_y(line(work, qkv_grad["local"], qkv_grad["got"]))
 
     def qkv_three():
-        def work(a, b, got, got_y):
-            own = dot_rows(a[:, : model // 4], b)
-            return (own + got[: got.shape[0] // 2].astype(f32) + got_y.astype(f32)).astype(bf16), own
-
-        piece, qkv_grad["local"] = line(work, all_normed, grad_joined, qkv_grad["got"], qkv_grad["got_y"])
+        def work(v, got, got_y):
+            return (v[: model // 4] + got[: model // 4].astype(f32) + got_y.astype(f32)).astype(bf16)
+
+        piece = line(work, qkv_grad["local"], qkv_grad["got"], qkv_grad["got_y"])
         piece = piece.reshape(n, share, 3 * width)
         qkv_grad["back"] = lax.all_to_all(piece, "seq", split_axis=0, concat_axis=0, tiled=True)
 
@@ -894,78 +972,101 @@
     vectors = {}
 
     def sum_vectors():
-        def work(joined, w, *local):
+        def plain(joined, w, local, give):
             bias = jnp.sum(joined.astype(f32), axis=0)
             w = w.astype(f32)
             shift = natural(jnp.sum(w * bias, axis=1))[0]
-            rows = jnp.concatenate([v.astype(f32) for v in local])
+            rows = jnp.concatenate([local, give.astype(f32)])
             gain = (natural(jnp.sum(w * rows, axis=1))[0] - ln1_bias * shift) / ln1_gain
             bias_all = jnp.zeros((3, n, width), f32)
-            bias_all = lax.dynamic_update_slice(bias_all, bias.reshape(3, 1, width), (jnp.uint32(0), at.seq, jnp.uint32(0))).reshape(-1)
-            return jnp.concatenate([gain, shift, gain_two_grad, bias_two_grad, bias_all]).reshape(-1, 128)
-
-        v = line(work, grad_joined, heads["w"], qkv_grad["local"], qkv_grad["local_y"], qkv_grad["give"])
+            start = (jnp.uint32(0), at.seq, jnp.uint32(0))
+            bias_all = lax.dynamic_update_slice(bias_all, bias.reshape(3, 1, width), start).reshape(3, model)
+            return jnp.concatenate([jnp.stack([gain, shift]), two_grads, bias_all, jnp.zeros((1, model), f32)])
+
+        def work(*v):
+            if share % HEAD_DIM:
+                return plain(*v)
+            out = jax.ShapeDtypeStruct((8, model), f32)
+            kernel = functools.partial(vectors_kernel, n)
+            scratch = [pltpu.VMEM((2, model), f32)]
+            return once(kernel, "vectors", 16, out, scratch, *v, ln1_bias[None], ln1_gain[None], two_grads, maps=at.peers)
+
+        v = line(work, grad_joined, heads["w"], qkv_grad["local"], qkv_grad["give"])
         vectors["sum"] = v
-        vectors["hops"] = [("batch", 1), *(("seq", bit) for bit in bits_of(n)), ("batch", 2)]
-        vectors["other"] = swap(v, *vectors["hops"][0])
+        vectors["hops"] = [[("batch", 1)], [("batch", 2)], [("seq", k) for k in (1, 2, 3) if k < n]]
+        vectors["hops"] += [[("seq", bit)] for bit in bits_of(n)[2:]]
+        vectors["other"] = [swap(v, *k) for k in vectors["hops"][0]]
 
     def vector_step():
-        v = line(lambda a, b: a + b, vectors["sum"], vectors["other"])
+        v = line(lambda a, *b: sum_in_order(a, b), vectors["sum"], *vectors["other"])
         vectors["sum"] = v
         vectors["hops"].pop(0)
         if vectors["hops"]:
-            vectors["other"] = swap(v, *vectors["hops"][0])
-
+            vectors["other"] = [swap(v, *k) for k in vectors["hops"][0]]
+
+    def sum_in_order(a, b):
+        if len(b) == 1:
+            return a + b[0]
+        return (a + b[0]) + (b[1] + b[2]) if len(b) == 3 else functools.reduce(jnp.add, b, a)
+
+    def up_back():
+        up.got_y = line(lambda v: v, up.got_y)
+
+    def back_done():
+        qkv_grad["back_y"] = line(lambda v: v, qkv_grad["back_y"])
+        qkv_grad["back_both"] = other_core(qkv_grad["back_y"])
+
+    def out_done():
+        v = grad_w_out["pieces"]
+        v[1] = line(lambda v: v, v[1])
+        v.append(other_core(v[1]))
+
+    def qkv_done():
+        parts = (qkv_grad[k] for k in ("rows", "back_y", "back_core", "back_both"))
+        qkv_grad["out"] = line(lambda *p: placed(at.row_place, p, 0), *parts)
+
+    up_back()
     qkv_one()
-    grad_one = scattered(
-        (grad_joined, heads["w"]),
-        lambda v, w: dot_last(block(v, n - 1), w),
-        lambda d, v, w: dot_last(pair_rows(v, d), w),
-        lambda v, w: dot_last(block(v, 0), w),
-        [(qkv_two,), (qkv_three,), (down.five, gate.five, to_rows), (sum_vectors,)],
+    last = (n - 1) * tokens
+    summed = scattered(
+        (grad_joined, heads["w"], all_hidden, w_down),
+        lambda *v: products(tokens, ((last, True), (last, False)), *v),
+        lambda d, first, second, *v: hop(
+            tokens, (((2 * d - 1) * tokens, True), (2 * (d - 1) * tokens, False)), v, first, second
+        ),
+        lambda *v: products(tokens, ((0, True), (last - tokens, False)), *v),
+        [
+            (qkv_local, qkv_two, sum_vectors, out_one),
+            (vector_step, qkv_three, vector_step, up.three, gate.five, up.four, out_two, out_three),
+            (to_rows, up.five),
+            (back_done, qkv_done, out_done),
+        ],
         whole=False,
+        fused=True,
     )
 
     def last_back(term, first, second):
         if share % HEAD_DIM:
-            grad_one = natural(term + first.astype(f32) + second.astype(f32))
-            return grad_middle + norm_back(grad_one, unit_one, inverse_one, ln1_gain)
-        given = term, first, second, unit_one, inverse_one, ln1_gain[None], grad_middle
-        out = jax.ShapeDtypeStruct((tokens, model), f32)
-        return once(functools.partial(last_back_kernel, n), "last_back", 8, out, [], *given, maps=at.peers)
-
-    grad_input = line(last_back, *grad_one)
-    back_y = line(lambda v: v, qkv_grad["back_y"])
-    back_both = other_core(back_y)
-    out_one()
+            total = term + first.astype(f32) + second.astype(f32)
+            back = grad_middle + norm_back(natural(total[:, :model]), unit_one, inverse_one, ln1_gain)
+            return back, (middle + total[:, model:]).astype(bf16)
+        given = term, first, second, unit_one, inverse_one, ln1_gain[None], grad_middle, middle
+        out = jax.ShapeDtypeStruct((tokens, model), f32), jax.ShapeDtypeStruct((tokens, model), bf16)
+        return once(functools.partial(last_back_kernel, n), "last_back", 10, out, [], *given, maps=at.peers)
+
+    grad_input, output = line(last_back, *summed)
     vector_step()
-    for _ in range(pairs - 3):
-        out_sum.step()
-    out_two()
-    vector_step()
-    up.five()
-    out_three()
-    vector_step()
-    grad_w_qkv = line(
-        lambda *p: placed(at.row_place, p, 0), qkv_grad["rows"], back_y, qkv_grad["back_core"], back_both
-    )
     while vectors["hops"]:
         vector_step()
-    output = line(lambda a, b: (a + b).astype(bf16), middle, out_sum.finish())
-    v = grad_w_out["pieces"]
-    v[1] = line(lambda v: v, v[1])
-    v.append(other_core(v[1]))
-    grad_w_out = line(lambda *p: placed(at.column_place, p, 1), *v)
-    gain_one_sum, bias_one_sum, gain_two_sum, bias_two_sum, qkv_bias_sum = jnp.split(
-        vectors["sum"].reshape(-1), [model, 2 * model, 3 * model, 4 * model]
-    )
-
+    grad_w_out = line(lambda *p: placed(at.column_place, p, 1), *grad_w_out["pieces"])
+    gain_one_sum, bias_one_sum, gain_two_sum, bias_two_sum = (vectors["sum"][i] for i in range(4))
+    qkv_bias_sum = vectors["sum"][4:7].reshape(-1)
     return (
         output.reshape(tokens, 1, model),
         grad_input.reshape(tokens, 1, model),
         gain_one_sum,
         bias_one_sum,
-        grad_w_qkv,
+        qkv_grad["out"],
         qkv_bias_sum,
         grad_w_out,
         gain_two_sum,

time: 512 us -> 484 us (0.945)
  Pallas kernels: 64.6 us -> 84.7 us
  matrix products: 48.1 us -> 32.4 us
  other arithmetic: 22.8 us -> 8.96 us
  starting transfers between devices: 119 us -> 108 us
  waiting for transfers between devices: 231 us -> 222 us
    ppermute x40 -> x41, waiting for transfers between devices: 104 us -> 47.4 us  [swap(): return lax.ppermute(v, axis, [(i, i ^ bit) for i in range(n)])]
    ppermute x32 -> x28, waiting for transfers between devices: 96.2 us -> 123 us  [up(): return lax.ppermute(v, self.axis, self.ahead)]
    pallas_call x4 -> x10, Pallas kernels: 27.9 us -> 49.1 us  [once(): pl.pallas_call(kernel, out_shape=out_shape, in_specs=[pl.BlockSpec(memory...]
    ppermute x32 -> x28, starting transfers between devices: 51.2 us -> 31.8 us  [up(): return lax.ppermute(v, self.axis, self.ahead)]
    ppermute x32 -> x28, waiting for transfers between devices: 30.4 us -> 41.8 us  [down(): return lax.ppermute(v, self.axis, self.behind)]
    dot_general x5 -> x0, matrix products: 11 us -> none  [dot_last(): lax.dot_general(a, b, (((1,), (1,)), ((), ())), preferred_element_type=f32)]
    convert_element_type x12 -> x6, other arithmetic: 12 us -> 1.59 us  [add(): (term[:tokens] + second).astype(bf16)]
    all_to_all x1, waiting for transfers between devices: 0.01 us -> 9.76 us  [qkv_three(): lax.all_to_all(piece, 'seq', split_axis=0, concat_axis=0, tiled=True)]
  transfers between devices with their start and end apart: 105 -> 98, of which waited for: 58 -> 58; matrix products, arithmetic and copies ran while one was open for 12% -> 9% of each run, Pallas kernels for 9% -> 16%
where the time goes in v3:
time: 484 us; the launch traced here: 480 us
  waiting for transfers between devices  222 us (46%)
  starting transfers between devices  108 us (22%)
  Pallas kernels  84.7 us (18%)
  matrix products  32.4 us (7%)
  local copies, waits for them, and re-layouts  22.9 us (5%)
  other arithmetic  8.96 us (2%)
    ppermute x28, waiting for transfers between devices, up(): return lax.ppermute(v, self.axis, self.ahead)  123 us
    pallas_call x10, Pallas kernels, once(): pl.pallas_call(kernel, out_shape=out_shape, in_specs=[pl.BlockSpec(memory...  49.1 us
    ppermute x41, waiting for transfers between devices, swap(): return lax.ppermute(v, axis, [(i, i ^ bit) for i in range(n)])  47.4 us
    ppermute x28, waiting for transfers between devices, down(): return lax.ppermute(v, self.axis, self.behind)  41.8 us
    ppermute x41, starting transfers between devices, swap(): return lax.ppermute(v, axis, [(i, i ^ bit) for i in range(n)])  38.4 us
    ppermute x28, starting transfers between devices, down(): return lax.ppermute(v, self.axis, self.behind)  31.8 us
    ppermute x28, starting transfers between devices, up(): return lax.ppermute(v, self.axis, self.ahead)  31.8 us
    dot_general x11, matrix products, dot_rows(): lax.dot_general(a, b, (((0,), (0,)), ((), ())), preferred_element_type=f32)  22.1 us
  transfers between devices with their start and end apart: 98, of which 58 were waited for; matrix products, arithmetic and copies ran while one was open for 9% of the time, Pallas kernels for 16%

profile of v3, /device:TPU:0, one launch (start us, length us, event | category | flops | bytes accessed | tf_op | source)
XLA Modules:
  0.0 480.3 jit_solution(11144335606530624504)
XLA Ops:
  4.5 3.0 collective-permute-start
  15.8 2.6 collective-permute-start.3
  18.4 13.7 %collective-permute-done.1.refs_2_ = bf16[72,768]{1,0:T(8,128)(2,1)S(1)} collective-permute-done((bf16[72,768]{1,0:T(8,128)(2,1)S(1)}, bf16[72,768]{1,0:T(8,128)(2,1)S(1)}, u32[]{:S(2)}, u32[]{:S(2)}) %collective-permute-start.1) | collective-permute-done | bytes 110624 | tf_op jit(solution)/shard_map/ppermute | solution.py:84
  32.7 3.1 collective-permute-start.5
  35.8 2.2 collective-permute-start.6
  38.0 5.5 %collective-permute-done.4.refs_5_ = bf16[72,768]{1,0:T(8,128)(2,1)S(1)} collective-permute-done((bf16[72,768]{1,0:T(8,128)(2,1)S(1)}, bf16[72,768]{1,0:T(8,128)(2,1)S(1)}, u32[]{:S(2)}, u32[]{:S(2)}) %collective-permute-start.4) | collective-permute-done | bytes 110624 | tf_op jit(solution)/shard_map/ppermute | solution.py:84
  45.9 2.1 collective-permute-start.9
  49.6 8.8 %collective-permute-done.10.refs_4_ = bf16[128,2048]{1,0:T(8,128)(2,1)S(1)} collective-permute-done((bf16[128,2048]{1,0:T(8,128)(2,1)S(1)}, bf16[128,2048]{1,0:T(8,128)(2,1)S(1)}, u32[]{:S(2)}, u32[]{:S(2)}) %collective-permute-start.10) | collective-permute-done | bytes 524320 | tf_op jit(solution)/shard_map/ppermute | solution.py:48
  62.4 8.0 %collective-permute-done.11.first_ref.refs_5_ = bf16[128,2048]{1,0:T(8,128)(2,1)S(1)} collective-permute-done((bf16[128,2048]{1,0:T(8,128)(2,1)S(1)}, bf16[128,2048]{1,0:T(8,128)(2,1)S(1)}, u32[]{:S(2)}, u32[]{:S(2)}) %collective-permute-start.11) | collective-permute-done | bytes 524320 | tf_op jit(solution)/shard_map/ppermute | solution.py:45
  75.4 4.9 %collective-permute-done.14.refs_7_ = bf16[64,2048]{1,0:T(8,128)(2,1)S(1)} collective-permute-done((bf16[64,2048]{1,0:T(8,128)(2,1)S(1)}, bf16[64,2048]{1,0:T(8,128)(2,1)S(1)}, u32[]{:S(2)}, u32[]{:S(2)}) %collective-permute-start.14) | collective-permute-done | bytes 262176 | tf_op jit(solution)/shard_map/ppermute | solution.py:45
  81.9 13.9 %attend.1 = (bf16[1024,2048]{1,0:T(8,128)(2,1)S(1)}, bf16[3,1024,256]{2,1,0:T(8,128)(2,1)S(1)}, bf16[1024,256]{1,0:T(8,128)(2,1)S(1)}, f32[8,1024]{1,0:T(8,128)S(1)}) custom-call(s32[16]{0:T(128)S(1)} %fusion.68.maps_ref, bf16[128,2048]{1,0:T(8,128)(2,1)S(1)} %pad_maximum_fusion.refs_0_, bf16[128,2048]{1,0:T(8,128)(2,1)S(1)} %collective-permute-done.7.refs_1_, ...), custom_call_target="tpu_custom_call" | custom-call | flops 1 | bytes 1 | tf_op jit(solution)/shard_map/attend/pallas_call | solution.py:354
  101.1 4.5 collective-permute-done.18
  109.8 7.0 %collective-permute-done.24.refs_2_ = bf16[128,2048]{1,0:T(8,128)(2,1)S(1)} collective-permute-done((bf16[128,2048]{1,0:T(8,128)(2,1)S(1)}, bf16[128,2048]{1,0:T(8,128)(2,1)S(1)}, u32[]{:S(2)}, u32[]{:S(2)}) %collective-permute-start.24) | collective-permute-done | bytes 524320 | tf_op jit(solution)/shard_map/ppermute | solution.py:45
  120.3 7.7 %collective-permute-done.22 = bf16[128,2048]{1,0:T(8,128)(2,1)S(1)} collective-permute-done((bf16[128,2048]{1,0:T(8,128)(2,1)S(1)}, bf16[128,2048]{1,0:T(8,128)(2,1)S(1)}, u32[]{:S(2)}, u32[]{:S(2)}) %collective-permute-start.22) | collective-permute-done | bytes 524320 | tf_op jit(solution)/shard_map/ppermute | solution.py:45
  132.3 6.9 %collective-permute-done.28.first_ref.refs_2_ = bf16[128,2048]{1,0:T(8,128)(2,1)S(1)} collective-permute-done((bf16[128,2048]{1,0:T(8,128)(2,1)S(1)}, bf16[128,2048]{1,0:T(8,128)(2,1)S(1)}, u32[]{:S(2)}, u32[]{:S(2)}) %collective-permute-start.28) | collective-permute-done | bytes 524320 | tf_op jit(solution)/shard_map/ppermute | solution.py:45
  140.7 7.4 %collective-permute-done.26 = bf16[128,2048]{1,0:T(8,128)(2,1)S(1)} collective-permute-done((bf16[128,2048]{1,0:T(8,128)(2,1)S(1)}, bf16[128,2048]{1,0:T(8,128)(2,1)S(1)}, u32[]{:S(2)}, u32[]{:S(2)}) %collective-permute-start.26) | collective-permute-done | bytes 524320 | tf_op jit(solution)/shard_map/ppermute | solution.py:45
  152.3 8.7 %collective-permute-done.30 = bf16[128,2048]{1,0:T(8,128)(2,1)S(1)} collective-permute-done((bf16[128,2048]{1,0:T(8,128)(2,1)S(1)}, bf16[128,2048]{1,0:T(8,128)(2,1)S(1)}, u32[]{:S(2)}, u32[]{:S(2)}) %collective-permute-start.30) | collective-permute-done | bytes 524320 | tf_op jit(solution)/shard_map/ppermute | solution.py:45
  166.9 12.8 %collective-permute-done.34.refs_4_ = bf16[64,2048]{1,0:T(8,128)(2,1)S(1)} collective-permute-done((bf16[64,2048]{1,0:T(8,128)(2,1)S(1)}, bf16[64,2048]{1,0:T(8,128)(2,1)S(1)}, u32[]{:S(2)}, u32[]{:S(2)}) %collective-permute-start.34) | collective-permute-done | bytes 262176 | tf_op jit(solution)/shard_map/ppermute | solution.py:45
  183.0 3.7 hidden_pair.4
  186.7 5.8 %collective-permute-done.36.refs_0_ = bf16[128,2048]{1,0:T(8,128)(2,1)S(1)} collective-permute-done((bf16[128,2048]{1,0:T(8,128)(2,1)S(1)}, bf16[128,2048]{1,0:T(8,128)(2,1)S(1)}, u32[]{:S(2)}, u32[]{:S(2)}) %collective-permute-start.36) | collective-permute-done | bytes 524320 | tf_op jit(solution)/shard_map/ppermute | solution.py:45
  195.4 3.7 hidden_pair.5
  199.1 6.3 %collective-permute-done.38.first_ref.refs_0_ = bf16[128,2048]{1,0:T(8,128)(2,1)S(1)} collective-permute-done((bf16[128,2048]{1,0:T(8,128)(2,1)S(1)}, bf16[128,2048]{1,0:T(8,128)(2,1)S(1)}, u32[]{:S(2)}, u32[]{:S(2)}) %collective-permute-start.38) | collective-permute-done | bytes 524320 | tf_op jit(solution)/shard_map/ppermute | solution.py:45
  208.8 3.7 hidden_pair.6
  213.6 3.7 hidden_pair.7
  223.8 2.9 fusion.13
  226.7 2.9 fusion.16
  234.5 2.3 fusion.22
  236.8 7.4 %collective-permute-done.44 = bf16[128,2048]{1,0:T(8,128)(2,1)S(1)} collective-permute-done((bf16[128,2048]{1,0:T(8,128)(2,1)S(1)}, bf16[128,2048]{1,0:T(8,128)(2,1)S(1)}, u32[]{:S(2)}, u32[]{:S(2)}) %collective-permute-start.44) | collective-permute-done | bytes 524320 | tf_op jit(solution)/shard_map/ppermute | solution.py:45
  245.2 2.1 collective-permute-start.47
  254.3 4.0 collective-permute-done.47
  264.2 2.2 collective-permute-done.52
  266.3 2.6 add_convert_fusion.4.refs_0_
  268.9 3.5 collective-permute-done.50
  278.8 7.6 %collective-permute-done.53.refs_1_ = bf16[128,2048]{1,0:T(8,128)(2,1)S(1)} collective-permute-done((bf16[128,2048]{1,0:T(8,128)(2,1)S(1)}, bf16[128,2048]{1,0:T(8,128)(2,1)S(1)}, u32[]{:S(2)}, u32[]{:S(2)}) %collective-permute-start.53) | collective-permute-done | bytes 524320 | tf_op jit(solution)/shard_map/ppermute | solution.py:45
  291.1 4.2 collective-permute-done.57.refs_1_
  295.4 2.3 collective-permute-done.55.refs_3_
  302.8 5.5 %collective-permute-done.59.first_ref.refs_5_ = bf16[128,2048]{1,0:T(8,128)(2,1)S(1)} collective-permute-done((bf16[128,2048]{1,0:T(8,128)(2,1)S(1)}, bf16[128,2048]{1,0:T(8,128)(2,1)S(1)}, u32[]{:S(2)}, u32[]{:S(2)}) %collective-permute-start.59) | collective-permute-done | bytes 524320 | tf_op jit(solution)/shard_map/ppermute | solution.py:45
  309.8 4.6 collective-permute-done.60.second_ref.refs_6_
  314.6 2.7 collective-permute-done.66.refs_1_
  318.7 3.8 placed.5
  322.5 2.3 collective-permute-done.63.refs_8_
  324.8 11.3 %attend_back.1 = (bf16[1024,768]{1,0:T(8,128)(2,1)S(1)}, f32[256,2048]{1,0:T(8,128)S(1)}) custom-call(s32[16]{0:T(128)S(1)} %fusion.68.maps_ref, bf16[128,2048]{1,0:T(8,128)(2,1)S(1)} %get-tuple-element.678.refs_0_, bf16[128,2048]{1,0:T(8,128)(2,1)S(1)} %collective-permute-done.53.refs_1_, bf16[128,2048]{1,0:T(8,128)(2,1)S(1)} %collective-permute-done.54.refs_2_, ...), custom_call_target="tpu_custom_call" | custom-call | flops 1 | bytes 1 | tf_op jit(solution)/shard_map/attend_back/pallas_call | solution.py:354
  346.0 3.7 vectors.1
  352.6 5.4 %collective-permute-done.68.refs_4_ = bf16[64,4096]{1,0:T(8,128)(2,1)S(1)} collective-permute-done((bf16[64,4096]{1,0:T(8,128)(2,1)S(1)}, bf16[64,4096]{1,0:T(8,128)(2,1)S(1)}, u32[]{:S(2)}, u32[]{:S(2)}) %collective-permute-start.68) | collective-permute-done | bytes 524320 | tf_op jit(solution)/shard_map/ppermute | solution.py:45
  358.1 3.1 hop.3
  363.5 2.3 collective-permute-done.75
  365.8 2.1 add_convert_fusion.2.refs_0_
  372.0 5.7 %all-to-all-start = ((bf16[8,64,768]{2,1,0:T(8,128)(2,1)}), bf16[8,64,768]{2,1,0:T(8,128)(2,1)}, u32[]{:S(2)}, u32[]{:S(2)}) async-start(bf16[8,64,768]{2,1,0:T(8,128)(2,1)} %bitcast.116), calls=%async_computation | async-start | bytes 1572864 | tf_op jit(solution)/shard_map/all_to_all | solution.py:961
  382.2 3.4 placed.6
  388.0 6.0 %collective-permute-done.80 = bf16[256,512]{1,0:T(8,128)(2,1)S(1)} collective-permute-done((bf16[256,512]{1,0:T(8,128)(2,1)S(1)}, bf16[256,512]{1,0:T(8,128)(2,1)S(1)}, u32[]{:S(2)}, u32[]{:S(2)}) %collective-permute-start.80) | collective-permute-done | bytes 262176 | tf_op jit(solution)/shard_map/ppermute | solution.py:84
  396.4 4.6 hop.4
  404.5 9.8 %all-to-all-done.in_ref = bf16[8,64,768]{2,1,0:T(8,128)(2,1)} async-done(((bf16[8,64,768]{2,1,0:T(8,128)(2,1)}), bf16[8,64,768]{2,1,0:T(8,128)(2,1)}, u32[]{:S(2)}, u32[]{:S(2)}) %all-to-all-start) | async-done | bytes 786464 | tf_op jit(solution)/shard_map/all_to_all | solution.py:961
  417.2 5.5 %placed.7 = f32[704,2048]{1,0:T(8,128)} custom-call(s32[4]{0:T(128)S(1)} %get-tuple-element.343.at_ref, bf16[704,512]{1,0:T(8,128)(2,1)} %add_convert_fusion.2.refs_0_, bf16[704,512]{1,0:T(8,128)(2,1)} %collective-permute-done.77.refs_1_, bf16[704,512]{1,0:T(8,128)(2,1)} %collective-permute-done.83.refs_2_, bf16[704,512]{1,0:T(8,128)(2,1)} %collective-permute-done.84.refs_3_), custom_call_target="tpu_custom_call" | custom-call | flops 1 | bytes 1 | tf_op jit(solution)/shard_map/placed/pallas_call | solution.py:695
  422.7 5.1 %collective-permute-done.81.refs_4_ = bf16[128,4096]{1,0:T(8,128)(2,1)} collective-permute-done((bf16[128,4096]{1,0:T(8,128)(2,1)}, bf16[128,4096]{1,0:T(8,128)(2,1)}, u32[]{:S(2)}, u32[]{:S(2)}) %collective-permute-start.81) | collective-permute-done | bytes 1048608 | tf_op jit(solution)/shard_map/ppermute | solution.py:45
  427.8 4.0 collective-permute-done.82.refs_5_
  431.8 4.7 hop.5
  436.5 4.8 %collective-permute-start.85 = (bf16[128,4096]{1,0:T(8,128)(2,1)}, bf16[128,4096]{1,0:T(8,128)(2,1)}, u32[]{:S(2)}, u32[]{:S(2)}) collective-permute-start(bf16[128,4096]{1,0:T(8,128)(2,1)} %get-tuple-element.623), channel_id=1, source_target_pairs={{0,8},{8,16},{16,24},{24,28},{28,20},{20,12},{12,4},{4,0},{1,9},{9... | collective-permute-start | bytes 3145736 | tf_op jit(solution)/shard_map/ppermute | solution.py:45
  447.2 6.6 %collective-permute-done.87.refs_1_ = bf16[256,512]{1,0:T(8,128)(2,1)S(1)} collective-permute-done((bf16[256,512]{1,0:T(8,128)(2,1)S(1)}, bf16[256,512]{1,0:T(8,128)(2,1)S(1)}, u32[]{:S(2)}, u32[]{:S(2)}) %collective-permute-start.87) | collective-permute-done | bytes 262176 | tf_op jit(solution)/shard_map/ppermute | solution.py:84
  454.7 2.3 collective-permute-start.92
  461.7 3.8 placed.8
  467.3 3.2 last_back.1
  471.9 2.0 copy.49
  473.9 2.5 collective-permute-done.94
  477.7 2.4 placed.9
  (338 shorter events, 161.3 us)
Async XLA Ops:
  10.6 33.5 %collective-permute-start.7 = (bf16[128,2048]{1,0:T(8,128)(2,1)S(1)}, bf16[128,2048]{1,0:T(8,128)(2,1)S(1)}, u32[]{:S(2)}, u32[]{:S(2)}) collective-permute-start(bf16[128,2048]{1,0:T(8,128)(2,1)S(1)} %pad_maximum_fusion.refs_0_), channel_id=1, source_target_pairs={{0,8},{8,16},{16,24},{24,28},{28,20},{20,12},{12,4},{4,0},{1,9},{9... | collective-permute-start | bytes 1572872 | tf_op jit(solution)/shard_map/ppermute | solution.py:45
  12.4 31.7 %collective-permute-start.8 = (bf16[128,2048]{1,0:T(8,128)(2,1)S(1)}, bf16[128,2048]{1,0:T(8,128)(2,1)S(1)}, u32[]{:S(2)}, u32[]{:S(2)}) collective-permute-start(bf16[128,2048]{1,0:T(8,128)(2,1)S(1)} %pad_maximum_fusion.refs_0_), channel_id=1, source_target_pairs={{8,0},{16,8},{24,16},{28,24},{20,28},{12,20},{4,12},{0,4},{9,1},{1... | collective-permute-start | bytes 1572872 | tf_op jit(solution)/shard_map/ppermute | solution.py:48
  12.6 19.5 %collective-permute-start.1 = (bf16[72,768]{1,0:T(8,128)(2,1)S(1)}, bf16[72,768]{1,0:T(8,128)(2,1)S(1)}, u32[]{:S(2)}, u32[]{:S(2)}) collective-permute-start(bf16[72,768]{1,0:T(8,128)(2,1)S(1)} %get-tuple-element.349), channel_id=1, source_target_pairs={{0,8},{4,12},{8,0},{12,4},{16,24},{20,28},{24,16},{28,20},{1,9},{5... | collective-permute-start | bytes 331784 | tf_op jit(solution)/shard_map/ppermute | solution.py:84
  14.5 18.3 %collective-permute-start.2 = (bf16[72,768]{1,0:T(8,128)(2,1)S(1)}, bf16[72,768]{1,0:T(8,128)(2,1)S(1)}, u32[]{:S(2)}, u32[]{:S(2)}) collective-permute-start(bf16[72,768]{1,0:T(8,128)(2,1)S(1)} %get-tuple-element.350), channel_id=1, source_target_pairs={{0,12},{4,8},{8,4},{12,0},{16,28},{20,24},{24,20},{28,16},{1,13},{... | collective-permute-start | bytes 331784 | tf_op jit(solution)/shard_map/ppermute | solution.py:84
  15.8 20.0 %collective-permute-start.3 = (bf16[72,768]{1,0:T(8,128)(2,1)S(1)}, bf16[72,768]{1,0:T(8,128)(2,1)S(1)}, u32[]{:S(2)}, u32[]{:S(2)}) collective-permute-start(bf16[72,768]{1,0:T(8,128)(2,1)S(1)} %get-tuple-element.351), channel_id=1, source_target_pairs={{0,16},{4,20},{8,24},{12,28},{16,0},{20,4},{24,8},{28,12},{1,17},{... | collective-permute-start | bytes 331784 | tf_op jit(solution)/shard_map/ppermute | solution.py:84
  44.1 14.3 %collective-permute-start.10 = (bf16[128,2048]{1,0:T(8,128)(2,1)S(1)}, bf16[128,2048]{1,0:T(8,128)(2,1)S(1)}, u32[]{:S(2)}, u32[]{:S(2)}) collective-permute-start(bf16[128,2048]{1,0:T(8,128)(2,1)S(1)} %collective-permute-done.8.refs_2_), channel_id=1, source_target_pairs={{8,0},{16,8},{24,16},{28,24},{20,28},{12,20},{4,12},{0,4},{9,1},{1... | collective-permute-start | bytes 1572872 | tf_op jit(solution)/shard_map/ppermute | solution.py:48
  45.9 13.5 %collective-permute-start.9 = (bf16[128,2048]{1,0:T(8,128)(2,1)S(1)}, bf16[128,2048]{1,0:T(8,128)(2,1)S(1)}, u32[]{:S(2)}, u32[]{:S(2)}) collective-permute-start(bf16[128,2048]{1,0:T(8,128)(2,1)S(1)} %collective-permute-done.7.refs_1_), channel_id=1, source_target_pairs={{0,8},{8,16},{16,24},{24,28},{28,20},{20,12},{12,4},{4,0},{1,9},{9... | collective-permute-start | bytes 1572872 | tf_op jit(solution)/shard_map/ppermute | solution.py:45
  48.0 14.4 %collective-permute-start.13 = (bf16[512,768]{1,0:T(8,128)(2,1)S(1)}, bf16[512,768]{1,0:T(8,128)(2,1)S(1)}, u32[]{:S(2)}, u32[]{:S(2)}) collective-permute-start(bf16[512,768]{1,0:T(8,128)(2,1)S(1)} %get-tuple-element.417.refs_9_), channel_id=1, source_target_pairs={{0,1},{1,0},{2,3},{3,2},{4,5},{5,4},{6,7},{7,6},{8,9},{9,8},{10,11... | collective-permute-start | bytes 2359304 | tf_op jit(solution)/shard_map/ppermute | solution.py:84
  48.0 23.1 %collective-permute-start.16 = (bf16[512,768]{1,0:T(8,128)(2,1)S(1)}, bf16[512,768]{1,0:T(8,128)(2,1)S(1)}, u32[]{:S(2)}, u32[]{:S(2)}) collective-permute-start(bf16[512,768]{1,0:T(8,128)(2,1)S(1)} %get-tuple-element.417.refs_9_), channel_id=1, source_target_pairs={{0,2},{1,3},{2,0},{3,1},{4,6},{5,7},{6,4},{7,5},{8,10},{9,11},{10,... | collective-permute-start | bytes 2359304 | tf_op jit(solution)/shard_map/ppermute | solution.py:84
  73.3 25.5 %collective-permute-start.20 = (bf16[128,2048]{1,0:T(8,128)(2,1)S(1)}, bf16[128,2048]{1,0:T(8,128)(2,1)S(1)}, u32[]{:S(2)}, u32[]{:S(2)}) collective-permute-start(bf16[128,2048]{1,0:T(8,128)(2,1)S(1)} %bitcast.105), channel_id=1, source_target_pairs={{0,8},{8,16},{16,24},{24,28},{28,20},{20,12},{12,4},{4,0},{1,9},{9... | collective-permute-start | bytes 1572872 | tf_op jit(solution)/shard_map/ppermute | solution.py:45
  74.8 24.0 %collective-permute-start.21 = (bf16[128,2048]{1,0:T(8,128)(2,1)S(1)}, bf16[128,2048]{1,0:T(8,128)(2,1)S(1)}, u32[]{:S(2)}, u32[]{:S(2)}) collective-permute-start(bf16[128,2048]{1,0:T(8,128)(2,1)S(1)} %bitcast.106), channel_id=1, source_target_pairs={{8,0},{16,8},{24,16},{28,24},{20,28},{12,20},{4,12},{0,4},{9,1},{1... | collective-permute-start | bytes 1572872 | tf_op jit(solution)/shard_map/ppermute | solution.py:48
  98.8 18.0 %collective-permute-start.24 = (bf16[128,2048]{1,0:T(8,128)(2,1)S(1)}, bf16[128,2048]{1,0:T(8,128)(2,1)S(1)}, u32[]{:S(2)}, u32[]{:S(2)}) collective-permute-start(bf16[128,2048]{1,0:T(8,128)(2,1)S(1)} %collective-permute-done.20.refs_2_), channel_id=1, source_target_pairs={{0,8},{8,16},{16,24},{24,28},{28,20},{20,12},{12,4},{4,0},{1,9},{9... | collective-permute-start | bytes 1572872 | tf_op jit(solution)/shard_map/ppermute | solution.py:45
  100.3 17.9 %collective-permute-start.25 = (bf16[128,2048]{1,0:T(8,128)(2,1)S(1)}, bf16[128,2048]{1,0:T(8,128)(2,1)S(1)}, u32[]{:S(2)}, u32[]{:S(2)}) collective-permute-start(bf16[128,2048]{1,0:T(8,128)(2,1)S(1)} %collective-permute-done.21.refs_3_), channel_id=1, source_target_pairs={{8,0},{16,8},{24,16},{28,24},{20,28},{12,20},{4,12},{0,4},{9,1},{1... | collective-permute-start | bytes 1572872 | tf_op jit(solution)/shard_map/ppermute | solution.py:48
  107.2 20.8 %collective-permute-start.22 = (bf16[128,2048]{1,0:T(8,128)(2,1)S(1)}, bf16[128,2048]{1,0:T(8,128)(2,1)S(1)}, u32[]{:S(2)}, u32[]{:S(2)}) collective-permute-start(bf16[128,2048]{1,0:T(8,128)(2,1)S(1)} %get-tuple-element.697), channel_id=1, source_target_pairs={{0,8},{8,16},{16,24},{24,28},{28,20},{20,12},{12,4},{4,0},{1,9},{9... | collective-permute-start | bytes 1572872 | tf_op jit(solution)/shard_map/ppermute | solution.py:45
  107.8 21.6 %collective-permute-start.23 = (bf16[128,2048]{1,0:T(8,128)(2,1)S(1)}, bf16[128,2048]{1,0:T(8,128)(2,1)S(1)}, u32[]{:S(2)}, u32[]{:S(2)}) collective-permute-start(bf16[128,2048]{1,0:T(8,128)(2,1)S(1)} %get-tuple-element.696), channel_id=1, source_target_pairs={{8,0},{16,8},{24,16},{28,24},{20,28},{12,20},{4,12},{0,4},{9,1},{1... | collective-permute-start | bytes 1572872 | tf_op jit(solution)/shard_map/ppermute | solution.py:48
  118.2 21.0 %collective-permute-start.28 = (bf16[128,2048]{1,0:T(8,128)(2,1)S(1)}, bf16[128,2048]{1,0:T(8,128)(2,1)S(1)}, u32[]{:S(2)}, u32[]{:S(2)}) collective-permute-start(bf16[128,2048]{1,0:T(8,128)(2,1)S(1)} %collective-permute-done.24.refs_2_), channel_id=1, source_target_pairs={{0,8},{8,16},{16,24},{24,28},{28,20},{20,12},{12,4},{4,0},{1,9},{9... | collective-permute-start | bytes 1572872 | tf_op jit(solution)/shard_map/ppermute | solution.py:45
  118.8 21.9 %collective-permute-start.29 = (bf16[128,2048]{1,0:T(8,128)(2,1)S(1)}, bf16[128,2048]{1,0:T(8,128)(2,1)S(1)}, u32[]{:S(2)}, u32[]{:S(2)}) collective-permute-start(bf16[128,2048]{1,0:T(8,128)(2,1)S(1)} %collective-permute-done.25.refs_3_), channel_id=1, source_target_pairs={{8,0},{16,8},{24,16},{28,24},{20,28},{12,20},{4,12},{0,4},{9,1},{1... | collective-permute-start | bytes 1572872 | tf_op jit(solution)/shard_map/ppermute | solution.py:48
  129.8 18.4 %collective-permute-start.26 = (bf16[128,2048]{1,0:T(8,128)(2,1)S(1)}, bf16[128,2048]{1,0:T(8,128)(2,1)S(1)}, u32[]{:S(2)}, u32[]{:S(2)}) collective-permute-start(bf16[128,2048]{1,0:T(8,128)(2,1)S(1)} %get-tuple-element.695), channel_id=1, source_target_pairs={{0,8},{8,16},{16,24},{24,28},{28,20},{20,12},{12,4},{4,0},{1,9},{9... | collective-permute-start | bytes 1572872 | tf_op jit(solution)/shard_map/ppermute | solution.py:45
  130.4 18.9 %collective-permute-start.27 = (bf16[128,2048]{1,0:T(8,128)(2,1)S(1)}, bf16[128,2048]{1,0:T(8,128)(2,1)S(1)}, u32[]{:S(2)}, u32[]{:S(2)}) collective-permute-start(bf16[128,2048]{1,0:T(8,128)(2,1)S(1)} %get-tuple-element.694), channel_id=1, source_target_pairs={{8,0},{16,8},{24,16},{28,24},{20,28},{12,20},{4,12},{0,4},{9,1},{1... | collective-permute-start | bytes 1572872 | tf_op jit(solution)/shard_map/ppermute | solution.py:48
  162.7 18.2 %collective-permute-start.32 = (bf16[128,2048]{1,0:T(8,128)(2,1)S(1)}, bf16[128,2048]{1,0:T(8,128)(2,1)S(1)}, u32[]{:S(2)}, u32[]{:S(2)}) collective-permute-start(bf16[128,2048]{1,0:T(8,128)(2,1)S(1)} %get-tuple-element.471.refs_0_), channel_id=1, source_target_pairs={{0,8},{8,16},{16,24},{24,28},{28,20},{20,12},{12,4},{4,0},{1,9},{9... | collective-permute-start | bytes 1572872 | tf_op jit(solution)/shard_map/ppermute | solution.py:45
  163.6 17.4 %collective-permute-start.33 = (bf16[128,2048]{1,0:T(8,128)(2,1)S(1)}, bf16[128,2048]{1,0:T(8,128)(2,1)S(1)}, u32[]{:S(2)}, u32[]{:S(2)}) collective-permute-start(bf16[128,2048]{1,0:T(8,128)(2,1)S(1)} %get-tuple-element.471.refs_0_), channel_id=1, source_target_pairs={{8,0},{16,8},{24,16},{28,24},{20,28},{12,20},{4,12},{0,4},{9,1},{1... | collective-permute-start | bytes 1572872 | tf_op jit(solution)/shard_map/ppermute | solution.py:48
  164.9 14.8 %collective-permute-start.34 = (bf16[64,2048]{1,0:T(8,128)(2,1)S(1)}, bf16[64,2048]{1,0:T(8,128)(2,1)S(1)}, u32[]{:S(2)}, u32[]{:S(2)}) collective-permute-start(bf16[64,2048]{1,0:T(8,128)(2,1)S(1)} %get-tuple-element.426), channel_id=1, source_target_pairs={{0,8},{8,16},{16,24},{24,28},{28,20},{20,12},{12,4},{4,0},{1,9},{9... | collective-permute-start | bytes 786440 | tf_op jit(solution)/shard_map/ppermute | solution.py:45
  165.7 15.2 %collective-permute-start.35 = (bf16[64,2048]{1,0:T(8,128)(2,1)S(1)}, bf16[64,2048]{1,0:T(8,128)(2,1)S(1)}, u32[]{:S(2)}, u32[]{:S(2)}) collective-permute-start(bf16[64,2048]{1,0:T(8,128)(2,1)S(1)} %get-tuple-element.427), channel_id=1, source_target_pairs={{8,0},{16,8},{24,16},{28,24},{20,28},{12,20},{4,12},{0,4},{9,1},{1... | collective-permute-start | bytes 786440 | tf_op jit(solution)/shard_map/ppermute | solution.py:48
  181.5 11.8 %collective-permute-start.37 = (bf16[128,2048]{1,0:T(8,128)(2,1)S(1)}, bf16[128,2048]{1,0:T(8,128)(2,1)S(1)}, u32[]{:S(2)}, u32[]{:S(2)}) collective-permute-start(bf16[128,2048]{1,0:T(8,128)(2,1)S(1)} %collective-permute-done.33.refs_1_), channel_id=1, source_target_pairs={{8,0},{16,8},{24,16},{28,24},{20,28},{12,20},{4,12},{0,4},{9,1},{1... | collective-permute-start | bytes 1572872 | tf_op jit(solution)/shard_map/ppermute | solution.py:48
  193.4 12.0 %collective-permute-start.38 = (bf16[128,2048]{1,0:T(8,128)(2,1)S(1)}, bf16[128,2048]{1,0:T(8,128)(2,1)S(1)}, u32[]{:S(2)}, u32[]{:S(2)}) collective-permute-start(bf16[128,2048]{1,0:T(8,128)(2,1)S(1)} %collective-permute-done.36.refs_0_), channel_id=1, source_target_pairs={{0,8},{8,16},{16,24},{24,28},{28,20},{20,12},{12,4},{4,0},{1,9},{9... | collective-permute-start | bytes 1572872 | tf_op jit(solution)/shard_map/ppermute | solution.py:45
  194.3 12.0 %collective-permute-start.39 = (bf16[128,2048]{1,0:T(8,128)(2,1)S(1)}, bf16[128,2048]{1,0:T(8,128)(2,1)S(1)}, u32[]{:S(2)}, u32[]{:S(2)}) collective-permute-start(bf16[128,2048]{1,0:T(8,128)(2,1)S(1)} %collective-permute-done.37.refs_1_), channel_id=1, source_target_pairs={{8,0},{16,8},{24,16},{28,24},{20,28},{12,20},{4,12},{0,4},{9,1},{1... | collective-permute-start | bytes 1572872 | tf_op jit(solution)/shard_map/ppermute | solution.py:48
  229.6 21.7 %collective-permute-start.49 = (bf16[704,1024]{1,0:T(8,128)(2,1)}, bf16[704,1024]{1,0:T(8,128)(2,1)S(1)}, u32[]{:S(2)}, u32[]{:S(2)}) collective-permute-start(bf16[704,1024]{1,0:T(8,128)(2,1)} %fusion.16), channel_id=1, source_target_pairs={{0,1},{1,0},{2,3},{3,2},{4,5},{5,4},{6,7},{7,6},{8,9},{9,8},{10,11... | collective-permute-start | bytes 4325384 | tf_op jit(solution)/shard_map/ppermute | solution.py:84
  230.3 13.9 %collective-permute-start.44 = (bf16[128,2048]{1,0:T(8,128)(2,1)S(1)}, bf16[128,2048]{1,0:T(8,128)(2,1)S(1)}, u32[]{:S(2)}, u32[]{:S(2)}) collective-permute-start(bf16[128,2048]{1,0:T(8,128)(2,1)S(1)} %get-tuple-element.691), channel_id=1, source_target_pairs={{0,8},{8,16},{16,24},{24,28},{28,20},{20,12},{12,4},{4,0},{1,9},{9... | collective-permute-start | bytes 1572872 | tf_op jit(solution)/shard_map/ppermute | solution.py:45
  231.1 13.8 %collective-permute-start.45 = (bf16[128,2048]{1,0:T(8,128)(2,1)S(1)}, bf16[128,2048]{1,0:T(8,128)(2,1)S(1)}, u32[]{:S(2)}, u32[]{:S(2)}) collective-permute-start(bf16[128,2048]{1,0:T(8,128)(2,1)S(1)} %get-tuple-element.690), channel_id=1, source_target_pairs={{8,0},{16,8},{24,16},{28,24},{20,28},{12,20},{4,12},{0,4},{9,1},{1... | collective-permute-start | bytes 1572872 | tf_op jit(solution)/shard_map/ppermute | solution.py:48
  245.2 13.0 %collective-permute-start.47 = (bf16[128,2048]{1,0:T(8,128)(2,1)S(1)}, bf16[128,2048]{1,0:T(8,128)(2,1)S(1)}, u32[]{:S(2)}, u32[]{:S(2)}) collective-permute-start(bf16[128,2048]{1,0:T(8,128)(2,1)S(1)} %get-tuple-element.689), channel_id=1, source_target_pairs={{0,8},{8,16},{16,24},{24,28},{28,20},{20,12},{12,4},{4,0},{1,9},{9... | collective-permute-start | bytes 1572872 | tf_op jit(solution)/shard_map/ppermute | solution.py:45
  247.3 12.9 %collective-permute-start.48 = (bf16[128,2048]{1,0:T(8,128)(2,1)S(1)}, bf16[128,2048]{1,0:T(8,128)(2,1)S(1)}, u32[]{:S(2)}, u32[]{:S(2)}) collective-permute-start(bf16[128,2048]{1,0:T(8,128)(2,1)S(1)} %get-tuple-element.688), channel_id=1, source_target_pairs={{8,0},{16,8},{24,16},{28,24},{20,28},{12,20},{4,12},{0,4},{9,1},{1... | collective-permute-start | bytes 1572872 | tf_op jit(solution)/shard_map/ppermute | solution.py:48
  247.5 18.8 %collective-permute-start.52 = (bf16[704,512]{1,0:T(8,128)(2,1)S(1)}, bf16[704,512]{1,0:T(8,128)(2,1)}, u32[]{:S(2)}, u32[]{:S(2)}) collective-permute-start(bf16[704,512]{1,0:T(8,128)(2,1)S(1)} %fusion.22), channel_id=1, source_target_pairs={{0,2},{1,3},{2,0},{3,1},{4,6},{5,7},{6,4},{7,5},{8,10},{9,11},{10,... | collective-permute-start | bytes 2162696 | tf_op jit(solution)/shard_map/ppermute | solution.py:84
  260.5 11.9 %collective-permute-start.50 = (bf16[128,2048]{1,0:T(8,128)(2,1)S(1)}, bf16[128,2048]{1,0:T(8,128)(2,1)S(1)}, u32[]{:S(2)}, u32[]{:S(2)}) collective-permute-start(bf16[128,2048]{1,0:T(8,128)(2,1)S(1)} %get-tuple-element.687), channel_id=1, source_target_pairs={{0,8},{8,16},{16,24},{24,28},{28,20},{20,12},{12,4},{4,0},{1,9},{9... | collective-permute-start | bytes 1572872 | tf_op jit(solution)/shard_map/ppermute | solution.py:45
  262.6 27.3 %collective-permute-start.58 = (bf16[704,512]{1,0:T(8,128)(2,1)S(1)}, bf16[704,512]{1,0:T(8,128)(2,1)S(1)}, u32[]{:S(2)}, u32[]{:S(2)}) collective-permute-start(bf16[704,512]{1,0:T(8,128)(2,1)S(1)} %fusion.23), channel_id=1, source_target_pairs={{0,2},{1,3},{2,0},{3,1},{4,6},{5,7},{6,4},{7,5},{8,10},{9,11},{10,... | collective-permute-start | bytes 2162696 | tf_op jit(solution)/shard_map/ppermute | solution.py:84
  264.2 36.1 %collective-permute-start.61 = (bf16[704,1024]{1,0:T(8,128)(2,1)S(1)}, bf16[704,1024]{1,0:T(8,128)(2,1)S(1)}, u32[]{:S(2)}, u32[]{:S(2)}) collective-permute-start(bf16[704,1024]{1,0:T(8,128)(2,1)S(1)} %fusion.19), channel_id=1, source_target_pairs={{0,1},{1,0},{2,3},{3,2},{4,5},{5,4},{6,7},{7,6},{8,9},{9,8},{10,11... | collective-permute-start | bytes 4325384 | tf_op jit(solution)/shard_map/ppermute | solution.py:84
  276.1 11.8 %collective-permute-start.54 = (bf16[128,2048]{1,0:T(8,128)(2,1)S(1)}, bf16[128,2048]{1,0:T(8,128)(2,1)S(1)}, u32[]{:S(2)}, u32[]{:S(2)}) collective-permute-start(bf16[128,2048]{1,0:T(8,128)(2,1)S(1)} %get-tuple-element.678.refs_0_), channel_id=1, source_target_pairs={{8,0},{16,8},{24,16},{28,24},{20,28},{12,20},{4,12},{0,4},{9,1},{1... | collective-permute-start | bytes 1572872 | tf_op jit(solution)/shard_map/ppermute | solution.py:48
  277.2 18.2 %collective-permute-start.57 = (bf16[704,512]{1,0:T(8,128)(2,1)S(1)}, bf16[704,512]{1,0:T(8,128)(2,1)S(1)}, u32[]{:S(2)}, u32[]{:S(2)}) collective-permute-start(bf16[704,512]{1,0:T(8,128)(2,1)S(1)} %add_convert_fusion.4.refs_0_), channel_id=1, source_target_pairs={{0,2},{1,3},{2,0},{3,1},{4,6},{5,7},{6,4},{7,5},{8,10},{9,11},{10,... | collective-permute-start | bytes 2162696 | tf_op jit(solution)/shard_map/ppermute | solution.py:84
  298.3 20.3 %collective-permute-start.64 = (bf16[704,512]{1,0:T(8,128)(2,1)S(1)}, bf16[704,512]{1,0:T(8,128)(2,1)S(1)}, u32[]{:S(2)}, u32[]{:S(2)}) collective-permute-start(bf16[704,512]{1,0:T(8,128)(2,1)S(1)} %add_convert_fusion.4.refs_0_), channel_id=1, source_target_pairs={{0,1},{1,0},{2,3},{3,2},{4,5},{5,4},{6,7},{7,6},{8,9},{9,8},{10,11... | collective-permute-start | bytes 2162696 | tf_op jit(solution)/shard_map/ppermute | solution.py:84
  298.3 18.9 %collective-permute-start.66 = (bf16[704,512]{1,0:T(8,128)(2,1)S(1)}, bf16[704,512]{1,0:T(8,128)(2,1)S(1)}, u32[]{:S(2)}, u32[]{:S(2)}) collective-permute-start(bf16[704,512]{1,0:T(8,128)(2,1)S(1)} %add_convert_fusion.3.refs_0_), channel_id=1, source_target_pairs={{0,2},{1,3},{2,0},{3,1},{4,6},{5,7},{6,4},{7,5},{8,10},{9,11},{10,... | collective-permute-start | bytes 2162696 | tf_op jit(solution)/shard_map/ppermute | solution.py:84
  300.0 18.6 %collective-permute-start.65 = (bf16[704,512]{1,0:T(8,128)(2,1)S(1)}, bf16[704,512]{1,0:T(8,128)(2,1)S(1)}, u32[]{:S(2)}, u32[]{:S(2)}) collective-permute-start(bf16[704,512]{1,0:T(8,128)(2,1)S(1)} %collective-permute-done.57.refs_1_), channel_id=1, source_target_pairs={{0,1},{1,0},{2,3},{3,2},{4,5},{5,4},{6,7},{7,6},{8,9},{9,8},{10,11... | collective-permute-start | bytes 2162696 | tf_op jit(solution)/shard_map/ppermute | solution.py:84
  300.3 14.1 %collective-permute-start.60 = (bf16[128,2048]{1,0:T(8,128)(2,1)S(1)}, bf16[128,2048]{1,0:T(8,128)(2,1)S(1)}, u32[]{:S(2)}, u32[]{:S(2)}) collective-permute-start(bf16[128,2048]{1,0:T(8,128)(2,1)S(1)} %collective-permute-done.56.refs_4_), channel_id=1, source_target_pairs={{8,0},{16,8},{24,16},{28,24},{20,28},{12,20},{4,12},{0,4},{9,1},{1... | collective-permute-start | bytes 1572872 | tf_op jit(solution)/shard_map/ppermute | solution.py:48
  308.3 27.9 %collective-permute-start.67 = (bf16[704,512]{1,0:T(8,128)(2,1)S(1)}, bf16[704,512]{1,0:T(8,128)(2,1)S(1)}, u32[]{:S(2)}, u32[]{:S(2)}) collective-permute-start(bf16[704,512]{1,0:T(8,128)(2,1)S(1)} %fusion.24), channel_id=1, source_target_pairs={{0,2},{1,3},{2,0},{3,1},{4,6},{5,7},{6,4},{7,5},{8,10},{9,11},{10,... | collective-permute-start | bytes 2162696 | tf_op jit(solution)/shard_map/ppermute | solution.py:84
  342.2 20.0 %collective-permute-start.76 = (bf16[512,768]{1,0:T(8,128)(2,1)S(1)}, bf16[512,768]{1,0:T(8,128)(2,1)S(1)}, u32[]{:S(2)}, u32[]{:S(2)}) collective-permute-start(bf16[512,768]{1,0:T(8,128)(2,1)S(1)} %add_convert_fusion.1), channel_id=1, source_target_pairs={{0,2},{1,3},{2,0},{3,1},{4,6},{5,7},{6,4},{7,5},{8,10},{9,11},{10,... | collective-permute-start | bytes 2359304 | tf_op jit(solution)/shard_map/ppermute | solution.py:84
  344.0 14.1 %collective-permute-start.68 = (bf16[64,4096]{1,0:T(8,128)(2,1)S(1)}, bf16[64,4096]{1,0:T(8,128)(2,1)S(1)}, u32[]{:S(2)}, u32[]{:S(2)}) collective-permute-start(bf16[64,4096]{1,0:T(8,128)(2,1)S(1)} %get-tuple-element.565), channel_id=1, source_target_pairs={{0,8},{8,16},{16,24},{24,28},{28,20},{20,12},{12,4},{4,0},{1,9},{9... | collective-permute-start | bytes 1572872 | tf_op jit(solution)/shard_map/ppermute | solution.py:45
  344.1 13.9 %collective-permute-start.69 = (bf16[64,4096]{1,0:T(8,128)(2,1)S(1)}, bf16[64,4096]{1,0:T(8,128)(2,1)S(1)}, u32[]{:S(2)}, u32[]{:S(2)}) collective-permute-start(bf16[64,4096]{1,0:T(8,128)(2,1)S(1)} %get-tuple-element.566), channel_id=1, source_target_pairs={{8,0},{16,8},{24,16},{28,24},{20,28},{12,20},{4,12},{0,4},{9,1},{1... | collective-permute-start | bytes 1572872 | tf_op jit(solution)/shard_map/ppermute | solution.py:48
  346.0 23.0 %collective-permute-start.78 = (bf16[704,512]{1,0:T(8,128)(2,1)S(1)}, bf16[704,512]{1,0:T(8,128)(2,1)S(1)}, u32[]{:S(2)}, u32[]{:S(2)}) collective-permute-start(bf16[704,512]{1,0:T(8,128)(2,1)S(1)} %add_convert_fusion.3.refs_0_), channel_id=1, source_target_pairs={{0,1},{1,0},{2,3},{3,2},{4,5},{5,4},{6,7},{7,6},{8,9},{9,8},{10,11... | collective-permute-start | bytes 2162696 | tf_op jit(solution)/shard_map/ppermute | solution.py:84
  358.1 13.1 %collective-permute-start.79 = (bf16[704,512]{1,0:T(8,128)(2,1)S(1)}, bf16[704,512]{1,0:T(8,128)(2,1)S(1)}, u32[]{:S(2)}, u32[]{:S(2)}) collective-permute-start(bf16[704,512]{1,0:T(8,128)(2,1)S(1)} %collective-permute-done.66.refs_1_), channel_id=1, source_target_pairs={{0,1},{1,0},{2,3},{3,2},{4,5},{5,4},{6,7},{7,6},{8,9},{9,8},{10,11... | collective-permute-start | bytes 2162696 | tf_op jit(solution)/shard_map/ppermute | solution.py:84
  367.9 18.1 %collective-permute-start.77 = (bf16[704,512]{1,0:T(8,128)(2,1)}, bf16[704,512]{1,0:T(8,128)(2,1)}, u32[]{:S(2)}, u32[]{:S(2)}) collective-permute-start(bf16[704,512]{1,0:T(8,128)(2,1)} %add_convert_fusion.2.refs_0_), channel_id=1, source_target_pairs={{0,2},{1,3},{2,0},{3,1},{4,6},{5,7},{6,4},{7,5},{8,10},{9,11},{10,... | collective-permute-start | bytes 2162696 | tf_op jit(solution)/shard_map/ppermute | solution.py:84
  368.3 17.7 %collective-permute-start.73 = (bf16[256,1024]{1,0:T(8,128)(2,1)}, bf16[256,1024]{1,0:T(8,128)(2,1)S(1)}, u32[]{:S(2)}, u32[]{:S(2)}) collective-permute-start(bf16[256,1024]{1,0:T(8,128)(2,1)} %dynamic-slice_convert_fusion), channel_id=1, source_target_pairs={{0,1},{1,0},{2,3},{3,2},{4,5},{5,4},{6,7},{7,6},{8,9},{9,8},{10,11... | collective-permute-start | bytes 1572872 | tf_op jit(solution)/shard_map/ppermute | solution.py:84
  368.3 26.3 %collective-permute-start.71 = (bf16[128,4096]{1,0:T(8,128)(2,1)}, bf16[128,4096]{1,0:T(8,128)(2,1)}, u32[]{:S(2)}, u32[]{:S(2)}) collective-permute-start(bf16[128,4096]{1,0:T(8,128)(2,1)} %get-tuple-element.582), channel_id=1, source_target_pairs={{0,8},{8,16},{16,24},{24,28},{28,20},{20,12},{12,4},{4,0},{1,9},{9... | collective-permute-start | bytes 3145736 | tf_op jit(solution)/shard_map/ppermute | solution.py:45
  369.9 26.5 %collective-permute-start.72 = (bf16[128,4096]{1,0:T(8,128)(2,1)}, bf16[128,4096]{1,0:T(8,128)(2,1)}, u32[]{:S(2)}, u32[]{:S(2)}) collective-permute-start(bf16[128,4096]{1,0:T(8,128)(2,1)} %get-tuple-element.583), channel_id=1, source_target_pairs={{8,0},{16,8},{24,16},{28,24},{20,28},{12,20},{4,12},{0,4},{9,1},{1... | collective-permute-start | bytes 3145736 | tf_op jit(solution)/shard_map/ppermute | solution.py:48
  372.0 42.3 %all-to-all-start = ((bf16[8,64,768]{2,1,0:T(8,128)(2,1)}), bf16[8,64,768]{2,1,0:T(8,128)(2,1)}, u32[]{:S(2)}, u32[]{:S(2)}) async-start(bf16[8,64,768]{2,1,0:T(8,128)(2,1)} %bitcast.116), calls=%async_computation | async-start | bytes 1572864 | tf_op jit(solution)/shard_map/all_to_all | solution.py:961
  401.0 26.8 %collective-permute-start.81 = (bf16[128,4096]{1,0:T(8,128)(2,1)}, bf16[128,4096]{1,0:T(8,128)(2,1)}, u32[]{:S(2)}, u32[]{:S(2)}) collective-permute-start(bf16[128,4096]{1,0:T(8,128)(2,1)} %get-tuple-element.610), channel_id=1, source_target_pairs={{0,8},{8,16},{16,24},{24,28},{28,20},{20,12},{12,4},{4,0},{1,9},{9... | collective-permute-start | bytes 3145736 | tf_op jit(solution)/shard_map/ppermute | solution.py:45
  402.6 29.2 %collective-permute-start.82 = (bf16[128,4096]{1,0:T(8,128)(2,1)}, bf16[128,4096]{1,0:T(8,128)(2,1)}, u32[]{:S(2)}, u32[]{:S(2)}) collective-permute-start(bf16[128,4096]{1,0:T(8,128)(2,1)} %get-tuple-element.611), channel_id=1, source_target_pairs={{8,0},{16,8},{24,16},{28,24},{20,28},{12,20},{4,12},{0,4},{9,1},{1... | collective-permute-start | bytes 3145736 | tf_op jit(solution)/shard_map/ppermute | solution.py:48
  404.0 13.2 %collective-permute-start.83 = (bf16[704,512]{1,0:T(8,128)(2,1)}, bf16[704,512]{1,0:T(8,128)(2,1)}, u32[]{:S(2)}, u32[]{:S(2)}) collective-permute-start(bf16[704,512]{1,0:T(8,128)(2,1)} %add_convert_fusion.2.refs_0_), channel_id=1, source_target_pairs={{0,1},{1,0},{2,3},{3,2},{4,5},{5,4},{6,7},{7,6},{8,9},{9,8},{10,11... | collective-permute-start | bytes 2162696 | tf_op jit(solution)/shard_map/ppermute | solution.py:84
  404.0 13.2 %collective-permute-start.84 = (bf16[704,512]{1,0:T(8,128)(2,1)}, bf16[704,512]{1,0:T(8,128)(2,1)}, u32[]{:S(2)}, u32[]{:S(2)}) collective-permute-start(bf16[704,512]{1,0:T(8,128)(2,1)} %collective-permute-done.77.refs_1_), channel_id=1, source_target_pairs={{0,1},{1,0},{2,3},{3,2},{4,5},{5,4},{6,7},{7,6},{8,9},{9,8},{10,11... | collective-permute-start | bytes 2162696 | tf_op jit(solution)/shard_map/ppermute | solution.py:84
  415.5 28.7 %collective-permute-start.88 = (bf16[64,6144]{1,0:T(8,128)(2,1)S(1)}, bf16[64,6144]{1,0:T(8,128)(2,1)S(1)}, u32[]{:S(2)}, u32[]{:S(2)}) collective-permute-start(bf16[64,6144]{1,0:T(8,128)(2,1)S(1)} %beside.1.refs_0_), channel_id=1, source_target_pairs={{0,2},{1,3},{2,0},{3,1},{4,6},{5,7},{6,4},{7,5},{8,10},{9,11},{10,... | collective-permute-start | bytes 2359304 | tf_op jit(solution)/shard_map/ppermute | solution.py:84
  436.5 29.1 %collective-permute-start.85 = (bf16[128,4096]{1,0:T(8,128)(2,1)}, bf16[128,4096]{1,0:T(8,128)(2,1)}, u32[]{:S(2)}, u32[]{:S(2)}) collective-permute-start(bf16[128,4096]{1,0:T(8,128)(2,1)} %get-tuple-element.623), channel_id=1, source_target_pairs={{0,8},{8,16},{16,24},{24,28},{28,20},{20,12},{12,4},{4,0},{1,9},{9... | collective-permute-start | bytes 3145736 | tf_op jit(solution)/shard_map/ppermute | solution.py:45
  441.3 25.9 %collective-permute-start.86 = (bf16[128,4096]{1,0:T(8,128)(2,1)}, bf16[128,4096]{1,0:T(8,128)(2,1)}, u32[]{:S(2)}, u32[]{:S(2)}) collective-permute-start(bf16[128,4096]{1,0:T(8,128)(2,1)} %get-tuple-element.624), channel_id=1, source_target_pairs={{8,0},{16,8},{24,16},{28,24},{20,28},{12,20},{4,12},{0,4},{9,1},{1... | collective-permute-start | bytes 3145736 | tf_op jit(solution)/shard_map/ppermute | solution.py:48
  441.3 12.5 %collective-permute-start.89 = (bf16[64,6144]{1,0:T(8,128)(2,1)S(1)}, bf16[64,6144]{1,0:T(8,128)(2,1)S(1)}, u32[]{:S(2)}, u32[]{:S(2)}) collective-permute-start(bf16[64,6144]{1,0:T(8,128)(2,1)S(1)} %beside.1.refs_0_), channel_id=1, source_target_pairs={{0,1},{1,0},{2,3},{3,2},{4,5},{5,4},{6,7},{7,6},{8,9},{9,8},{10,11... | collective-permute-start | bytes 2359304 | tf_op jit(solution)/shard_map/ppermute | solution.py:84
  444.2 12.8 %collective-permute-start.90 = (bf16[64,6144]{1,0:T(8,128)(2,1)S(1)}, bf16[64,6144]{1,0:T(8,128)(2,1)S(1)}, u32[]{:S(2)}, u32[]{:S(2)}) collective-permute-start(bf16[64,6144]{1,0:T(8,128)(2,1)S(1)} %collective-permute-done.88.refs_1_), channel_id=1, source_target_pairs={{0,1},{1,0},{2,3},{3,2},{4,5},{5,4},{6,7},{7,6},{8,9},{9,8},{10,11... | collective-permute-start | bytes 2359304 | tf_op jit(solution)/shard_map/ppermute | solution.py:84
  453.8 16.6 %collective-permute-start.91 = (f32[8,2048]{1,0:T(8,128)S(1)}, f32[8,2048]{1,0:T(8,128)S(1)}, u32[]{:S(2)}, u32[]{:S(2)}) collective-permute-start(f32[8,2048]{1,0:T(8,128)S(1)} %add.259), channel_id=1, source_target_pairs={{0,4},{4,0},{8,12},{12,8},{16,20},{20,16},{24,28},{28,24},{1,5},{5... | collective-permute-start | bytes 196616 | tf_op jit(solution)/shard_map/ppermute | solution.py:84
  454.7 15.7 %collective-permute-start.92 = (f32[8,2048]{1,0:T(8,128)S(1)}, f32[8,2048]{1,0:T(8,128)S(1)}, u32[]{:S(2)}, u32[]{:S(2)}) collective-permute-start(f32[8,2048]{1,0:T(8,128)S(1)} %add.259), channel_id=1, source_target_pairs={{0,8},{4,12},{8,0},{12,4},{16,24},{20,28},{24,16},{28,20},{1,9},{5... | collective-permute-start | bytes 196616 | tf_op jit(solution)/shard_map/ppermute | solution.py:84
  457.1 13.4 %collective-permute-start.93 = (f32[8,2048]{1,0:T(8,128)S(1)}, f32[8,2048]{1,0:T(8,128)S(1)}, u32[]{:S(2)}, u32[]{:S(2)}) collective-permute-start(f32[8,2048]{1,0:T(8,128)S(1)} %add.259), channel_id=1, source_target_pairs={{0,12},{4,8},{8,4},{12,0},{16,28},{20,24},{24,20},{28,16},{1,13},{... | collective-permute-start | bytes 196616 | tf_op jit(solution)/shard_map/ppermute | solution.py:84
  (78 other events, 1143.3 us)

commit v4 on v3

--- a/solution.py
+++ b/solution.py
@@ -271,8 +271,8 @@
             weights = jnp.exp(scores - top)
             total = jnp.sum(weights, axis=0, keepdims=True)
             lse_ref[h : h + 1, start : start + tile] = top + jnp.log(total)
-            prob = (weights * (1.0 / total)).astype(bf16)
-            outs.append(dot(v_t[h * HEAD_DIM : (h + 1) * HEAD_DIM, :keys], prob))
+            out = dot(v_t[h * HEAD_DIM : (h + 1) * HEAD_DIM, :keys], weights.astype(bf16))
+            outs.append(out * (1.0 / total))
         out = jnp.concatenate(outs, 0).T.astype(bf16)
         for i in range(tile // BLOCK):
             mixed_ref[at_block(maps_ref, start // BLOCK + i), :] = out[i * BLOCK : (i + 1) * BLOCK]
@@ -427,40 +427,31 @@
         left = a[start : start + rows, :]
         for begin in range(0, width, 512):
             columns = slice(begin, begin + 512)
-            out_ref[:, offset + begin : offset + begin + 512] = (
-                dot_last(left, b[columns, :]) if last else dot(left, b[:, columns])
-            )
+            term = dot_last(left, b[columns, :]) if last else dot(left, b[:, columns])
+            out_ref[:, offset + begin : offset + begin + 512] = term.astype(out_ref.dtype)
         offset += width
 
 
-def products(rows, items, *given):
+def products(rows, items, *given, dtype=f32):
     width = sum(b.shape[0 if last else 1] for (_, last), b in zip(items, given[1::2], strict=True))
-    out = jax.ShapeDtypeStruct((rows, width), f32)
+    out = jax.ShapeDtypeStruct((rows, width), dtype)
     return once(functools.partial(products_kernel, items), "products", 8, out, [], *given)
 
 
-def hop_kernel(items, *refs):
-    given, (first_ref, second_ref, ahead_ref, behind_ref) = refs[:-4], refs[-4:]
-    rows, half, offset = ahead_ref.shape[0], first_ref.shape[0], 0
-    for (start, last), a, b in zip(items, given[::2], given[1::2], strict=True):
-        width = b.shape[0 if last else 1]
-        left = a[start : start + 2 * rows, :]
-        for begin in range(0, width, 512):
-            columns = slice(begin, begin + 512)
-            term = dot_last(left, b[columns, :]) if last else dot(left, b[:, columns])
-            here = slice(offset + begin, offset + begin + 512)
-            first, second = first_ref[:, here].astype(f32), second_ref[:, here].astype(f32)
-            ahead_ref[:half, here] = (term[rows : rows + half] + first).astype(bf16)
-            behind_ref[rows - half :, here] = (term[rows - half : rows] + second).astype(bf16)
-            if half < rows:
-                ahead_ref[half:, here] = term[rows + half :].astype(bf16)
-                behind_ref[: rows - half, here] = term[: rows - half].astype(bf16)
-        offset += width
-
-
-def hop(rows, items, given, first, second):
-    out = jax.ShapeDtypeStruct((rows, first.shape[1]), bf16)
-    return once(functools.partial(hop_kernel, items), "hop", 10, (out, out), [], *given, first, second)
+def hop_kernel(term_ref, first_ref, second_ref, ahead_ref, behind_ref):
+    rows, half = ahead_ref.shape[0], first_ref.shape[0]
+    ahead = term_ref[rows : rows + half, :].astype(f32) + first_ref[...].astype(f32)
+    behind = term_ref[rows - half : rows, :].astype(f32) + second_ref[...].astype(f32)
+    ahead_ref[:half, :] = ahead.astype(bf16)
+    behind_ref[rows - half :, :] = behind.astype(bf16)
+    if half < rows:
+        ahead_ref[half:, :] = term_ref[rows + half :, :]
+        behind_ref[: rows - half, :] = term_ref[: rows - half, :]
+
+
+def hop(term, first, second):
+    out = jax.ShapeDtypeStruct((term.shape[0] // 2, term.shape[1]), bf16)
+    return once(hop_kernel, "hop", 8, (out, out), [], term, first, second)
 
 
 def vectors_kernel(n, peers_ref, joined_ref, w_ref, local_ref, give_ref, shift_ref, gain_ref, two_ref, out_ref, turned):
@@ -780,8 +771,7 @@
             top, bottom = line(lambda *v: halves(*[far(*v).astype(bf16)] * 2), *given)
             self.first, self.second = ring.up(top), ring.down(bottom)
             self.d = pairs - 1
-            if not fused:
-                self.term = line(lambda *v: pair(self.d, *v), *given)
+            self.term = line(lambda *v: pair(self.d, *v), *given)
 
         def step(self):
             half = tokens // 2
@@ -794,15 +784,12 @@
                 return (term[tokens:] + first).astype(bf16), (term[:tokens] + second).astype(bf16)
 
             if self.fused:
-                first, second = line(
-                    lambda first, second, *v: self.pair(self.d, first, second, *v), self.first, self.second, *self.given
-                )
+                first, second = line(hop, self.term, self.first, self.second)
             else:
                 first, second = line(add, self.term, self.first, self.second)
             self.first, self.second = ring.up(first), ring.down(second)
             self.d -= 1
-            if not (self.fused and self.d):
-                self.term = line(lambda *v: self.pair(self.d, *v) if self.d else self.own(*v), *self.given)
+            self.term = line(lambda *v: self.pair(self.d, *v) if self.d else self.own(*v), *self.given)
 
         def parts(self):
             return self.term, self.first, self.second
@@ -1031,15 +1018,15 @@
     summed = scattered(
         (grad_joined, heads["w"], all_hidden, w_down),
         lambda *v: products(tokens, ((last, True), (last, False)), *v),
-        lambda d, first, second, *v: hop(
-            tokens, (((2 * d - 1) * tokens, True), (2 * (d - 1) * tokens, False)), v, first, second
+        lambda d, *v: products(
+            2 * tokens, (((2 * d - 1) * tokens, True), (2 * (d - 1) * tokens, False)), *v, dtype=bf16
         ),
         lambda *v: products(tokens, ((0, True), (last - tokens, False)), *v),
         [
-            (qkv_local, qkv_two, sum_vectors, out_one),
-            (vector_step, qkv_three, vector_step, up.three, gate.five, up.four, out_two, out_three),
-            (to_rows, up.five),
-            (back_done, qkv_done, out_done),
+            (qkv_local, qkv_two, sum_vectors, up.three, gate.five, vector_step),
+            (qkv_three, up.four, vector_step, out_one),
+            (out_two, to_rows, out_three, up.five),
+            (back_done, qkv_done),
         ],
         whole=False,
         fused=True,
@@ -1056,6 +1043,7 @@
 
     grad_input, output = line(last_back, *summed)
     vector_step()
+    out_done()
     while vectors["hops"]:
         vector_step()
     grad_w_out = line(lambda *p: placed(at.column_place, p, 1), *grad_w_out["pieces"])

time: 484 us -> 473 us (0.977)
  waiting for transfers between devices: 222 us -> 213 us
    ppermute x41, waiting for transfers between devices: 47.4 us -> 41.4 us  [swap(): return lax.ppermute(v, axis, [(i, i ^ bit) for i in range(n)])]
    all_to_all x1, waiting for transfers between devices: 9.76 us -> 4.92 us  [qkv_three(): lax.all_to_all(piece, 'seq', split_axis=0, concat_axis=0, tiled=True)]
    unnamed x90 -> x82, local copies, waits for them, and re-layouts: 17.2 us -> 15.4 us
    pallas_call x10 -> x13, Pallas kernels: 49.1 us -> 48.9 us  [once(): pl.pallas_call(kernel, out_shape=out_shape, in_specs=[pl.BlockSpec(memory...]
  transfers between devices with their start and end apart: 98 -> 98, of which waited for: 58 -> 58; matrix products, arithmetic and copies ran while one was open for 9% -> 10% of each run, Pallas kernels for 16% -> 16%
where the time goes in v4:
time: 473 us; the launch traced here: 469 us
  waiting for transfers between devices  213 us (45%)
  starting transfers between devices  104 us (22%)
  Pallas kernels  84.6 us (18%)
  matrix products  31.6 us (7%)
  local copies, waits for them, and re-layouts  22.8 us (5%)
  other arithmetic  10.2 us (2%)
    ppermute x28, waiting for transfers between devices, up(): return lax.ppermute(v, self.axis, self.ahead)  128 us
    pallas_call x13, Pallas kernels, once(): pl.pallas_call(kernel, out_shape=out_shape, in_specs=[pl.BlockSpec(memory...  48.9 us
    ppermute x41, waiting for transfers between devices, swap(): return lax.ppermute(v, axis, [(i, i ^ bit) for i in range(n)])  41.4 us
    ppermute x28, waiting for transfers between devices, down(): return lax.ppermute(v, self.axis, self.behind)  39.4 us
    ppermute x28, starting transfers between devices, up(): return lax.ppermute(v, self.axis, self.ahead)  34.9 us
    ppermute x41, starting transfers between devices, swap(): return lax.ppermute(v, axis, [(i, i ^ bit) for i in range(n)])  34.1 us
    ppermute x28, starting transfers between devices, down(): return lax.ppermute(v, self.axis, self.behind)  29.7 us
    dot_general x11, matrix products, dot_rows(): lax.dot_general(a, b, (((0,), (0,)), ((), ())), preferred_element_type=f32)  21.6 us
  transfers between devices with their start and end apart: 98, of which 58 were waited for; matrix products, arithmetic and copies ran while one was open for 10% of the time, Pallas kernels for 16%

profile of v4, /device:TPU:0, one launch (start us, length us, event | category | flops | bytes accessed | tf_op | source)
XLA Modules:
  0.0 468.8 jit_solution(14063573660259435018)
XLA Ops:
  4.5 3.0 collective-permute-start
  15.8 2.6 collective-permute-start.3
  18.4 13.7 %collective-permute-done.1.refs_2_ = bf16[72,768]{1,0:T(8,128)(2,1)S(1)} collective-permute-done((bf16[72,768]{1,0:T(8,128)(2,1)S(1)}, bf16[72,768]{1,0:T(8,128)(2,1)S(1)}, u32[]{:S(2)}, u32[]{:S(2)}) %collective-permute-start.1) | collective-permute-done | bytes 110624 | tf_op jit(solution)/shard_map/ppermute | solution.py:84
  32.7 3.1 collective-permute-start.5
  35.8 2.2 collective-permute-start.6
  38.0 5.5 %collective-permute-done.4.refs_5_ = bf16[72,768]{1,0:T(8,128)(2,1)S(1)} collective-permute-done((bf16[72,768]{1,0:T(8,128)(2,1)S(1)}, bf16[72,768]{1,0:T(8,128)(2,1)S(1)}, u32[]{:S(2)}, u32[]{:S(2)}) %collective-permute-start.4) | collective-permute-done | bytes 110624 | tf_op jit(solution)/shard_map/ppermute | solution.py:84
  45.9 2.1 collective-permute-start.9
  49.6 8.8 %collective-permute-done.10.refs_4_ = bf16[128,2048]{1,0:T(8,128)(2,1)S(1)} collective-permute-done((bf16[128,2048]{1,0:T(8,128)(2,1)S(1)}, bf16[128,2048]{1,0:T(8,128)(2,1)S(1)}, u32[]{:S(2)}, u32[]{:S(2)}) %collective-permute-start.10) | collective-permute-done | bytes 524320 | tf_op jit(solution)/shard_map/ppermute | solution.py:48
  62.4 8.0 %collective-permute-done.11.first_ref.refs_5_ = bf16[128,2048]{1,0:T(8,128)(2,1)S(1)} collective-permute-done((bf16[128,2048]{1,0:T(8,128)(2,1)S(1)}, bf16[128,2048]{1,0:T(8,128)(2,1)S(1)}, u32[]{:S(2)}, u32[]{:S(2)}) %collective-permute-start.11) | collective-permute-done | bytes 524320 | tf_op jit(solution)/shard_map/ppermute | solution.py:45
  75.4 4.9 %collective-permute-done.14.refs_7_ = bf16[64,2048]{1,0:T(8,128)(2,1)S(1)} collective-permute-done((bf16[64,2048]{1,0:T(8,128)(2,1)S(1)}, bf16[64,2048]{1,0:T(8,128)(2,1)S(1)}, u32[]{:S(2)}, u32[]{:S(2)}) %collective-permute-start.14) | collective-permute-done | bytes 262176 | tf_op jit(solution)/shard_map/ppermute | solution.py:45
  81.9 12.6 %attend.1 = (bf16[1024,2048]{1,0:T(8,128)(2,1)S(1)}, bf16[3,1024,256]{2,1,0:T(8,128)(2,1)S(1)}, bf16[1024,256]{1,0:T(8,128)(2,1)S(1)}, f32[8,1024]{1,0:T(8,128)S(1)}) custom-call(s32[16]{0:T(128)S(1)} %fusion.68.maps_ref, bf16[128,2048]{1,0:T(8,128)(2,1)S(1)} %pad_maximum_fusion.refs_0_, bf16[128,2048]{1,0:T(8,128)(2,1)S(1)} %collective-permute-done.7.refs_1_, ...), custom_call_target="tpu_custom_call" | custom-call | flops 1 | bytes 1 | tf_op jit(solution)/shard_map/attend/pallas_call | solution.py:354
  99.5 4.7 collective-permute-done.18
  108.4 7.0 %collective-permute-done.24.refs_2_ = bf16[128,2048]{1,0:T(8,128)(2,1)S(1)} collective-permute-done((bf16[128,2048]{1,0:T(8,128)(2,1)S(1)}, bf16[128,2048]{1,0:T(8,128)(2,1)S(1)}, u32[]{:S(2)}, u32[]{:S(2)}) %collective-permute-start.24) | collective-permute-done | bytes 524320 | tf_op jit(solution)/shard_map/ppermute | solution.py:45
  119.1 7.5 %collective-permute-done.22 = bf16[128,2048]{1,0:T(8,128)(2,1)S(1)} collective-permute-done((bf16[128,2048]{1,0:T(8,128)(2,1)S(1)}, bf16[128,2048]{1,0:T(8,128)(2,1)S(1)}, u32[]{:S(2)}, u32[]{:S(2)}) %collective-permute-start.22) | collective-permute-done | bytes 524320 | tf_op jit(solution)/shard_map/ppermute | solution.py:45
  131.0 7.0 %collective-permute-done.28.first_ref.refs_2_ = bf16[128,2048]{1,0:T(8,128)(2,1)S(1)} collective-permute-done((bf16[128,2048]{1,0:T(8,128)(2,1)S(1)}, bf16[128,2048]{1,0:T(8,128)(2,1)S(1)}, u32[]{:S(2)}, u32[]{:S(2)}) %collective-permute-start.28) | collective-permute-done | bytes 524320 | tf_op jit(solution)/shard_map/ppermute | solution.py:45
  139.4 7.4 %collective-permute-done.26 = bf16[128,2048]{1,0:T(8,128)(2,1)S(1)} collective-permute-done((bf16[128,2048]{1,0:T(8,128)(2,1)S(1)}, bf16[128,2048]{1,0:T(8,128)(2,1)S(1)}, u32[]{:S(2)}, u32[]{:S(2)}) %collective-permute-start.26) | collective-permute-done | bytes 524320 | tf_op jit(solution)/shard_map/ppermute | solution.py:45
  150.9 8.7 %collective-permute-done.30 = bf16[128,2048]{1,0:T(8,128)(2,1)S(1)} collective-permute-done((bf16[128,2048]{1,0:T(8,128)(2,1)S(1)}, bf16[128,2048]{1,0:T(8,128)(2,1)S(1)}, u32[]{:S(2)}, u32[]{:S(2)}) %collective-permute-start.30) | collective-permute-done | bytes 524320 | tf_op jit(solution)/shard_map/ppermute | solution.py:45
  165.5 12.7 %collective-permute-done.34.refs_4_ = bf16[64,2048]{1,0:T(8,128)(2,1)S(1)} collective-permute-done((bf16[64,2048]{1,0:T(8,128)(2,1)S(1)}, bf16[64,2048]{1,0:T(8,128)(2,1)S(1)}, u32[]{:S(2)}, u32[]{:S(2)}) %collective-permute-start.34) | collective-permute-done | bytes 262176 | tf_op jit(solution)/shard_map/ppermute | solution.py:45
  181.6 3.7 hidden_pair.4
  185.3 5.8 %collective-permute-done.36.refs_0_ = bf16[128,2048]{1,0:T(8,128)(2,1)S(1)} collective-permute-done((bf16[128,2048]{1,0:T(8,128)(2,1)S(1)}, bf16[128,2048]{1,0:T(8,128)(2,1)S(1)}, u32[]{:S(2)}, u32[]{:S(2)}) %collective-permute-start.36) | collective-permute-done | bytes 524320 | tf_op jit(solution)/shard_map/ppermute | solution.py:45
  194.0 3.7 hidden_pair.5
  197.7 6.3 %collective-permute-done.38.first_ref.refs_0_ = bf16[128,2048]{1,0:T(8,128)(2,1)S(1)} collective-permute-done((bf16[128,2048]{1,0:T(8,128)(2,1)S(1)}, bf16[128,2048]{1,0:T(8,128)(2,1)S(1)}, u32[]{:S(2)}, u32[]{:S(2)}) %collective-permute-start.38) | collective-permute-done | bytes 524320 | tf_op jit(solution)/shard_map/ppermute | solution.py:45
  205.4 2.2 collective-permute-start.41
  207.7 3.7 hidden_pair.6
  212.2 3.7 hidden_pair.7
  222.2 2.9 fusion.13
  225.2 2.9 fusion.16
  232.9 2.1 fusion.22
  235.0 7.8 %collective-permute-done.44 = bf16[128,2048]{1,0:T(8,128)(2,1)S(1)} collective-permute-done((bf16[128,2048]{1,0:T(8,128)(2,1)S(1)}, bf16[128,2048]{1,0:T(8,128)(2,1)S(1)}, u32[]{:S(2)}, u32[]{:S(2)}) %collective-permute-start.44) | collective-permute-done | bytes 524320 | tf_op jit(solution)/shard_map/ppermute | solution.py:45
  243.9 2.1 collective-permute-start.47
  252.8 4.1 collective-permute-done.47
  262.7 2.6 collective-permute-done.52
  265.4 2.3 add_convert_fusion.4.refs_0_
  267.7 3.3 collective-permute-done.50
  277.4 7.6 %collective-permute-done.53.refs_1_ = bf16[128,2048]{1,0:T(8,128)(2,1)S(1)} collective-permute-done((bf16[128,2048]{1,0:T(8,128)(2,1)S(1)}, bf16[128,2048]{1,0:T(8,128)(2,1)S(1)}, u32[]{:S(2)}, u32[]{:S(2)}) %collective-permute-start.53) | collective-permute-done | bytes 524320 | tf_op jit(solution)/shard_map/ppermute | solution.py:45
  289.7 4.6 collective-permute-done.57.refs_1_
  301.4 5.4 %collective-permute-done.59.first_ref.refs_5_ = bf16[128,2048]{1,0:T(8,128)(2,1)S(1)} collective-permute-done((bf16[128,2048]{1,0:T(8,128)(2,1)S(1)}, bf16[128,2048]{1,0:T(8,128)(2,1)S(1)}, u32[]{:S(2)}, u32[]{:S(2)}) %collective-permute-start.59) | collective-permute-done | bytes 524320 | tf_op jit(solution)/shard_map/ppermute | solution.py:45
  308.3 4.6 collective-permute-done.60.second_ref.refs_6_
  313.3 2.7 collective-permute-done.66.refs_1_
  317.3 3.8 placed.5
  321.2 2.4 collective-permute-done.63.refs_8_
  323.6 11.4 %attend_back.1 = (bf16[1024,768]{1,0:T(8,128)(2,1)S(1)}, f32[256,2048]{1,0:T(8,128)S(1)}) custom-call(s32[16]{0:T(128)S(1)} %fusion.68.maps_ref, bf16[128,2048]{1,0:T(8,128)(2,1)S(1)} %get-tuple-element.684.refs_0_, bf16[128,2048]{1,0:T(8,128)(2,1)S(1)} %collective-permute-done.53.refs_1_, bf16[128,2048]{1,0:T(8,128)(2,1)S(1)} %collective-permute-done.54.refs_2_, ...), custom_call_target="tpu_custom_call" | custom-call | flops 1 | bytes 1 | tf_op jit(solution)/shard_map/attend_back/pallas_call | solution.py:354
  348.5 3.8 vectors.1
  352.2 2.1 add_convert_fusion.2.refs_0_
  354.8 3.4 placed.6
  358.3 2.2 collective-permute-done.68.first_ref
  368.1 5.6 %all-to-all-start = ((bf16[8,64,768]{2,1,0:T(8,128)(2,1)}), bf16[8,64,768]{2,1,0:T(8,128)(2,1)}, u32[]{:S(2)}, u32[]{:S(2)}) async-start(bf16[8,64,768]{2,1,0:T(8,128)(2,1)} %bitcast.116), calls=%async_computation | async-start | bytes 1572864 | tf_op jit(solution)/shard_map/all_to_all | solution.py:948
  373.7 7.1 %collective-permute-done.77.refs_1_ = bf16[704,512]{1,0:T(8,128)(2,1)} collective-permute-done((bf16[704,512]{1,0:T(8,128)(2,1)}, bf16[704,512]{1,0:T(8,128)(2,1)}, u32[]{:S(2)}, u32[]{:S(2)}) %collective-permute-start.77) | collective-permute-done | bytes 720928 | tf_op jit(solution)/shard_map/ppermute | solution.py:84
  385.0 3.6 collective-permute-done.74.first_ref
  391.0 3.2 hop.4
  394.2 2.8 collective-permute-start.79
  402.5 4.9 %all-to-all-done.in_ref = bf16[8,64,768]{2,1,0:T(8,128)(2,1)} async-done(((bf16[8,64,768]{2,1,0:T(8,128)(2,1)}), bf16[8,64,768]{2,1,0:T(8,128)(2,1)}, u32[]{:S(2)}, u32[]{:S(2)}) %all-to-all-start) | async-done | bytes 786464 | tf_op jit(solution)/shard_map/all_to_all | solution.py:948
  410.4 5.5 %placed.7 = f32[704,2048]{1,0:T(8,128)} custom-call(s32[4]{0:T(128)S(1)} %get-tuple-element.346.at_ref, bf16[704,512]{1,0:T(8,128)(2,1)} %add_convert_fusion.2.refs_0_, bf16[704,512]{1,0:T(8,128)(2,1)} %collective-permute-done.77.refs_1_, bf16[704,512]{1,0:T(8,128)(2,1)} %collective-permute-done.81.refs_2_, bf16[704,512]{1,0:T(8,128)(2,1)} %collective-permute-done.82.refs_3_), custom_call_target="tpu_custom_call" | custom-call | flops 1 | bytes 1 | tf_op jit(solution)/shard_map/placed/pallas_call | solution.py:686
  416.0 4.3 collective-permute-done.79.first_ref
  420.2 2.2 collective-permute-done.80.second_ref
  422.4 3.2 hop.5
  425.6 5.8 %collective-permute-start.85 = (bf16[128,4096]{1,0:T(8,128)(2,1)}, bf16[128,4096]{1,0:T(8,128)(2,1)}, u32[]{:S(2)}, u32[]{:S(2)}) collective-permute-start(bf16[128,4096]{1,0:T(8,128)(2,1)} %get-tuple-element.629), channel_id=1, source_target_pairs={{0,8},{8,16},{16,24},{24,28},{28,20},{20,12},{12,4},{4,0},{1,9},{9... | collective-permute-start | bytes 3145736 | tf_op jit(solution)/shard_map/ppermute | solution.py:45
  437.2 2.0 collective-permute-start.91
  443.6 3.8 placed.8
  447.4 6.1 %collective-permute-done.85.first_ref = bf16[128,4096]{1,0:T(8,128)(2,1)} collective-permute-done((bf16[128,4096]{1,0:T(8,128)(2,1)}, bf16[128,4096]{1,0:T(8,128)(2,1)}, u32[]{:S(2)}, u32[]{:S(2)}) %collective-permute-start.85) | collective-permute-done | bytes 1048608 | tf_op jit(solution)/shard_map/ppermute | solution.py:45
  455.7 3.1 last_back.1
  459.9 2.0 copy.49
  461.9 2.9 collective-permute-done.93
  466.1 2.4 placed.9
  (333 shorter events, 161.5 us)
Async XLA Ops:
  10.6 33.5 %collective-permute-start.7 = (bf16[128,2048]{1,0:T(8,128)(2,1)S(1)}, bf16[128,2048]{1,0:T(8,128)(2,1)S(1)}, u32[]{:S(2)}, u32[]{:S(2)}) collective-permute-start(bf16[128,2048]{1,0:T(8,128)(2,1)S(1)} %pad_maximum_fusion.refs_0_), channel_id=1, source_target_pairs={{0,8},{8,16},{16,24},{24,28},{28,20},{20,12},{12,4},{4,0},{1,9},{9... | collective-permute-start | bytes 1572872 | tf_op jit(solution)/shard_map/ppermute | solution.py:45
  12.4 31.7 %collective-permute-start.8 = (bf16[128,2048]{1,0:T(8,128)(2,1)S(1)}, bf16[128,2048]{1,0:T(8,128)(2,1)S(1)}, u32[]{:S(2)}, u32[]{:S(2)}) collective-permute-start(bf16[128,2048]{1,0:T(8,128)(2,1)S(1)} %pad_maximum_fusion.refs_0_), channel_id=1, source_target_pairs={{8,0},{16,8},{24,16},{28,24},{20,28},{12,20},{4,12},{0,4},{9,1},{1... | collective-permute-start | bytes 1572872 | tf_op jit(solution)/shard_map/ppermute | solution.py:48
  12.6 19.5 %collective-permute-start.1 = (bf16[72,768]{1,0:T(8,128)(2,1)S(1)}, bf16[72,768]{1,0:T(8,128)(2,1)S(1)}, u32[]{:S(2)}, u32[]{:S(2)}) collective-permute-start(bf16[72,768]{1,0:T(8,128)(2,1)S(1)} %get-tuple-element.352), channel_id=1, source_target_pairs={{0,8},{4,12},{8,0},{12,4},{16,24},{20,28},{24,16},{28,20},{1,9},{5... | collective-permute-start | bytes 331784 | tf_op jit(solution)/shard_map/ppermute | solution.py:84
  14.5 18.3 %collective-permute-start.2 = (bf16[72,768]{1,0:T(8,128)(2,1)S(1)}, bf16[72,768]{1,0:T(8,128)(2,1)S(1)}, u32[]{:S(2)}, u32[]{:S(2)}) collective-permute-start(bf16[72,768]{1,0:T(8,128)(2,1)S(1)} %get-tuple-element.353), channel_id=1, source_target_pairs={{0,12},{4,8},{8,4},{12,0},{16,28},{20,24},{24,20},{28,16},{1,13},{... | collective-permute-start | bytes 331784 | tf_op jit(solution)/shard_map/ppermute | solution.py:84
  15.8 20.0 %collective-permute-start.3 = (bf16[72,768]{1,0:T(8,128)(2,1)S(1)}, bf16[72,768]{1,0:T(8,128)(2,1)S(1)}, u32[]{:S(2)}, u32[]{:S(2)}) collective-permute-start(bf16[72,768]{1,0:T(8,128)(2,1)S(1)} %get-tuple-element.354), channel_id=1, source_target_pairs={{0,16},{4,20},{8,24},{12,28},{16,0},{20,4},{24,8},{28,12},{1,17},{... | collective-permute-start | bytes 331784 | tf_op jit(solution)/shard_map/ppermute | solution.py:84
  32.1 11.4 %collective-permute-start.4 = (bf16[72,768]{1,0:T(8,128)(2,1)S(1)}, bf16[72,768]{1,0:T(8,128)(2,1)S(1)}, u32[]{:S(2)}, u32[]{:S(2)}) collective-permute-start(bf16[72,768]{1,0:T(8,128)(2,1)S(1)} %get-tuple-element.355), channel_id=1, source_target_pairs={{0,20},{4,16},{8,28},{12,24},{16,4},{20,0},{24,12},{28,8},{1,21},{... | collective-permute-start | bytes 331784 | tf_op jit(solution)/shard_map/ppermute | solution.py:84
  44.1 14.3 %collective-permute-start.10 = (bf16[128,2048]{1,0:T(8,128)(2,1)S(1)}, bf16[128,2048]{1,0:T(8,128)(2,1)S(1)}, u32[]{:S(2)}, u32[]{:S(2)}) collective-permute-start(bf16[128,2048]{1,0:T(8,128)(2,1)S(1)} %collective-permute-done.8.refs_2_), channel_id=1, source_target_pairs={{8,0},{16,8},{24,16},{28,24},{20,28},{12,20},{4,12},{0,4},{9,1},{1... | collective-permute-start | bytes 1572872 | tf_op jit(solution)/shard_map/ppermute | solution.py:48
  45.9 13.5 %collective-permute-start.9 = (bf16[128,2048]{1,0:T(8,128)(2,1)S(1)}, bf16[128,2048]{1,0:T(8,128)(2,1)S(1)}, u32[]{:S(2)}, u32[]{:S(2)}) collective-permute-start(bf16[128,2048]{1,0:T(8,128)(2,1)S(1)} %collective-permute-done.7.refs_1_), channel_id=1, source_target_pairs={{0,8},{8,16},{16,24},{24,28},{28,20},{20,12},{12,4},{4,0},{1,9},{9... | collective-permute-start | bytes 1572872 | tf_op jit(solution)/shard_map/ppermute | solution.py:45
  48.0 14.4 %collective-permute-start.13 = (bf16[512,768]{1,0:T(8,128)(2,1)S(1)}, bf16[512,768]{1,0:T(8,128)(2,1)S(1)}, u32[]{:S(2)}, u32[]{:S(2)}) collective-permute-start(bf16[512,768]{1,0:T(8,128)(2,1)S(1)} %get-tuple-element.420.refs_9_), channel_id=1, source_target_pairs={{0,1},{1,0},{2,3},{3,2},{4,5},{5,4},{6,7},{7,6},{8,9},{9,8},{10,11... | collective-permute-start | bytes 2359304 | tf_op jit(solution)/shard_map/ppermute | solution.py:84
  48.0 23.1 %collective-permute-start.16 = (bf16[512,768]{1,0:T(8,128)(2,1)S(1)}, bf16[512,768]{1,0:T(8,128)(2,1)S(1)}, u32[]{:S(2)}, u32[]{:S(2)}) collective-permute-start(bf16[512,768]{1,0:T(8,128)(2,1)S(1)} %get-tuple-element.420.refs_9_), channel_id=1, source_target_pairs={{0,2},{1,3},{2,0},{3,1},{4,6},{5,7},{6,4},{7,5},{8,10},{9,11},{10,... | collective-permute-start | bytes 2359304 | tf_op jit(solution)/shard_map/ppermute | solution.py:84
  73.3 24.2 %collective-permute-start.20 = (bf16[128,2048]{1,0:T(8,128)(2,1)S(1)}, bf16[128,2048]{1,0:T(8,128)(2,1)S(1)}, u32[]{:S(2)}, u32[]{:S(2)}) collective-permute-start(bf16[128,2048]{1,0:T(8,128)(2,1)S(1)} %bitcast.105), channel_id=1, source_target_pairs={{0,8},{8,16},{16,24},{24,28},{28,20},{20,12},{12,4},{4,0},{1,9},{9... | collective-permute-start | bytes 1572872 | tf_op jit(solution)/shard_map/ppermute | solution.py:45
  74.8 22.6 %collective-permute-start.21 = (bf16[128,2048]{1,0:T(8,128)(2,1)S(1)}, bf16[128,2048]{1,0:T(8,128)(2,1)S(1)}, u32[]{:S(2)}, u32[]{:S(2)}) collective-permute-start(bf16[128,2048]{1,0:T(8,128)(2,1)S(1)} %bitcast.106), channel_id=1, source_target_pairs={{8,0},{16,8},{24,16},{28,24},{20,28},{12,20},{4,12},{0,4},{9,1},{1... | collective-permute-start | bytes 1572872 | tf_op jit(solution)/shard_map/ppermute | solution.py:48
  97.4 18.0 %collective-permute-start.24 = (bf16[128,2048]{1,0:T(8,128)(2,1)S(1)}, bf16[128,2048]{1,0:T(8,128)(2,1)S(1)}, u32[]{:S(2)}, u32[]{:S(2)}) collective-permute-start(bf16[128,2048]{1,0:T(8,128)(2,1)S(1)} %collective-permute-done.20.refs_2_), channel_id=1, source_target_pairs={{0,8},{8,16},{16,24},{24,28},{28,20},{20,12},{12,4},{4,0},{1,9},{9... | collective-permute-start | bytes 1572872 | tf_op jit(solution)/shard_map/ppermute | solution.py:45
  99.0 17.9 %collective-permute-start.25 = (bf16[128,2048]{1,0:T(8,128)(2,1)S(1)}, bf16[128,2048]{1,0:T(8,128)(2,1)S(1)}, u32[]{:S(2)}, u32[]{:S(2)}) collective-permute-start(bf16[128,2048]{1,0:T(8,128)(2,1)S(1)} %collective-permute-done.21.refs_3_), channel_id=1, source_target_pairs={{8,0},{16,8},{24,16},{28,24},{20,28},{12,20},{4,12},{0,4},{9,1},{1... | collective-permute-start | bytes 1572872 | tf_op jit(solution)/shard_map/ppermute | solution.py:48
  105.9 20.8 %collective-permute-start.22 = (bf16[128,2048]{1,0:T(8,128)(2,1)S(1)}, bf16[128,2048]{1,0:T(8,128)(2,1)S(1)}, u32[]{:S(2)}, u32[]{:S(2)}) collective-permute-start(bf16[128,2048]{1,0:T(8,128)(2,1)S(1)} %get-tuple-element.703), channel_id=1, source_target_pairs={{0,8},{8,16},{16,24},{24,28},{28,20},{20,12},{12,4},{4,0},{1,9},{9... | collective-permute-start | bytes 1572872 | tf_op jit(solution)/shard_map/ppermute | solution.py:45
  106.5 21.7 %collective-permute-start.23 = (bf16[128,2048]{1,0:T(8,128)(2,1)S(1)}, bf16[128,2048]{1,0:T(8,128)(2,1)S(1)}, u32[]{:S(2)}, u32[]{:S(2)}) collective-permute-start(bf16[128,2048]{1,0:T(8,128)(2,1)S(1)} %get-tuple-element.702), channel_id=1, source_target_pairs={{8,0},{16,8},{24,16},{28,24},{20,28},{12,20},{4,12},{0,4},{9,1},{1... | collective-permute-start | bytes 1572872 | tf_op jit(solution)/shard_map/ppermute | solution.py:48
  116.9 21.0 %collective-permute-start.28 = (bf16[128,2048]{1,0:T(8,128)(2,1)S(1)}, bf16[128,2048]{1,0:T(8,128)(2,1)S(1)}, u32[]{:S(2)}, u32[]{:S(2)}) collective-permute-start(bf16[128,2048]{1,0:T(8,128)(2,1)S(1)} %collective-permute-done.24.refs_2_), channel_id=1, source_target_pairs={{0,8},{8,16},{16,24},{24,28},{28,20},{20,12},{12,4},{4,0},{1,9},{9... | collective-permute-start | bytes 1572872 | tf_op jit(solution)/shard_map/ppermute | solution.py:45
  117.5 21.9 %collective-permute-start.29 = (bf16[128,2048]{1,0:T(8,128)(2,1)S(1)}, bf16[128,2048]{1,0:T(8,128)(2,1)S(1)}, u32[]{:S(2)}, u32[]{:S(2)}) collective-permute-start(bf16[128,2048]{1,0:T(8,128)(2,1)S(1)} %collective-permute-done.25.refs_3_), channel_id=1, source_target_pairs={{8,0},{16,8},{24,16},{28,24},{20,28},{12,20},{4,12},{0,4},{9,1},{1... | collective-permute-start | bytes 1572872 | tf_op jit(solution)/shard_map/ppermute | solution.py:48
  128.4 18.4 %collective-permute-start.26 = (bf16[128,2048]{1,0:T(8,128)(2,1)S(1)}, bf16[128,2048]{1,0:T(8,128)(2,1)S(1)}, u32[]{:S(2)}, u32[]{:S(2)}) collective-permute-start(bf16[128,2048]{1,0:T(8,128)(2,1)S(1)} %get-tuple-element.701), channel_id=1, source_target_pairs={{0,8},{8,16},{16,24},{24,28},{28,20},{20,12},{12,4},{4,0},{1,9},{9... | collective-permute-start | bytes 1572872 | tf_op jit(solution)/shard_map/ppermute | solution.py:45
  129.1 19.0 %collective-permute-start.27 = (bf16[128,2048]{1,0:T(8,128)(2,1)S(1)}, bf16[128,2048]{1,0:T(8,128)(2,1)S(1)}, u32[]{:S(2)}, u32[]{:S(2)}) collective-permute-start(bf16[128,2048]{1,0:T(8,128)(2,1)S(1)} %get-tuple-element.700), channel_id=1, source_target_pairs={{8,0},{16,8},{24,16},{28,24},{20,28},{12,20},{4,12},{0,4},{9,1},{1... | collective-permute-start | bytes 1572872 | tf_op jit(solution)/shard_map/ppermute | solution.py:48
  148.3 11.4 %collective-permute-start.30 = (bf16[128,2048]{1,0:T(8,128)(2,1)S(1)}, bf16[128,2048]{1,0:T(8,128)(2,1)S(1)}, u32[]{:S(2)}, u32[]{:S(2)}) collective-permute-start(bf16[128,2048]{1,0:T(8,128)(2,1)S(1)} %get-tuple-element.699), channel_id=1, source_target_pairs={{0,8},{8,16},{16,24},{24,28},{28,20},{20,12},{12,4},{4,0},{1,9},{9... | collective-permute-start | bytes 1572872 | tf_op jit(solution)/shard_map/ppermute | solution.py:45
  161.3 18.3 %collective-permute-start.32 = (bf16[128,2048]{1,0:T(8,128)(2,1)S(1)}, bf16[128,2048]{1,0:T(8,128)(2,1)S(1)}, u32[]{:S(2)}, u32[]{:S(2)}) collective-permute-start(bf16[128,2048]{1,0:T(8,128)(2,1)S(1)} %get-tuple-element.474.refs_0_), channel_id=1, source_target_pairs={{0,8},{8,16},{16,24},{24,28},{28,20},{20,12},{12,4},{4,0},{1,9},{9... | collective-permute-start | bytes 1572872 | tf_op jit(solution)/shard_map/ppermute | solution.py:45
  162.2 17.4 %collective-permute-start.33 = (bf16[128,2048]{1,0:T(8,128)(2,1)S(1)}, bf16[128,2048]{1,0:T(8,128)(2,1)S(1)}, u32[]{:S(2)}, u32[]{:S(2)}) collective-permute-start(bf16[128,2048]{1,0:T(8,128)(2,1)S(1)} %get-tuple-element.474.refs_0_), channel_id=1, source_target_pairs={{8,0},{16,8},{24,16},{28,24},{20,28},{12,20},{4,12},{0,4},{9,1},{1... | collective-permute-start | bytes 1572872 | tf_op jit(solution)/shard_map/ppermute | solution.py:48
  163.5 14.8 %collective-permute-start.34 = (bf16[64,2048]{1,0:T(8,128)(2,1)S(1)}, bf16[64,2048]{1,0:T(8,128)(2,1)S(1)}, u32[]{:S(2)}, u32[]{:S(2)}) collective-permute-start(bf16[64,2048]{1,0:T(8,128)(2,1)S(1)} %get-tuple-element.429), channel_id=1, source_target_pairs={{0,8},{8,16},{16,24},{24,28},{28,20},{20,12},{12,4},{4,0},{1,9},{9... | collective-permute-start | bytes 786440 | tf_op jit(solution)/shard_map/ppermute | solution.py:45
  164.4 15.2 %collective-permute-start.35 = (bf16[64,2048]{1,0:T(8,128)(2,1)S(1)}, bf16[64,2048]{1,0:T(8,128)(2,1)S(1)}, u32[]{:S(2)}, u32[]{:S(2)}) collective-permute-start(bf16[64,2048]{1,0:T(8,128)(2,1)S(1)} %get-tuple-element.430), channel_id=1, source_target_pairs={{8,0},{16,8},{24,16},{28,24},{20,28},{12,20},{4,12},{0,4},{9,1},{1... | collective-permute-start | bytes 786440 | tf_op jit(solution)/shard_map/ppermute | solution.py:48
  179.6 11.5 %collective-permute-start.36 = (bf16[128,2048]{1,0:T(8,128)(2,1)S(1)}, bf16[128,2048]{1,0:T(8,128)(2,1)S(1)}, u32[]{:S(2)}, u32[]{:S(2)}) collective-permute-start(bf16[128,2048]{1,0:T(8,128)(2,1)S(1)} %collective-permute-done.32.refs_0_), channel_id=1, source_target_pairs={{0,8},{8,16},{16,24},{24,28},{28,20},{20,12},{12,4},{4,0},{1,9},{9... | collective-permute-start | bytes 1572872 | tf_op jit(solution)/shard_map/ppermute | solution.py:45
  180.2 11.8 %collective-permute-start.37 = (bf16[128,2048]{1,0:T(8,128)(2,1)S(1)}, bf16[128,2048]{1,0:T(8,128)(2,1)S(1)}, u32[]{:S(2)}, u32[]{:S(2)}) collective-permute-start(bf16[128,2048]{1,0:T(8,128)(2,1)S(1)} %collective-permute-done.33.refs_1_), channel_id=1, source_target_pairs={{8,0},{16,8},{24,16},{28,24},{20,28},{12,20},{4,12},{0,4},{9,1},{1... | collective-permute-start | bytes 1572872 | tf_op jit(solution)/shard_map/ppermute | solution.py:48
  192.0 12.0 %collective-permute-start.38 = (bf16[128,2048]{1,0:T(8,128)(2,1)S(1)}, bf16[128,2048]{1,0:T(8,128)(2,1)S(1)}, u32[]{:S(2)}, u32[]{:S(2)}) collective-permute-start(bf16[128,2048]{1,0:T(8,128)(2,1)S(1)} %collective-permute-done.36.refs_0_), channel_id=1, source_target_pairs={{0,8},{8,16},{16,24},{24,28},{28,20},{20,12},{12,4},{4,0},{1,9},{9... | collective-permute-start | bytes 1572872 | tf_op jit(solution)/shard_map/ppermute | solution.py:45
  193.2 12.0 %collective-permute-start.39 = (bf16[128,2048]{1,0:T(8,128)(2,1)S(1)}, bf16[128,2048]{1,0:T(8,128)(2,1)S(1)}, u32[]{:S(2)}, u32[]{:S(2)}) collective-permute-start(bf16[128,2048]{1,0:T(8,128)(2,1)S(1)} %collective-permute-done.37.refs_1_), channel_id=1, source_target_pairs={{8,0},{16,8},{24,16},{28,24},{20,28},{12,20},{4,12},{0,4},{9,1},{1... | collective-permute-start | bytes 1572872 | tf_op jit(solution)/shard_map/ppermute | solution.py:48
  228.1 21.7 %collective-permute-start.49 = (bf16[704,1024]{1,0:T(8,128)(2,1)}, bf16[704,1024]{1,0:T(8,128)(2,1)S(1)}, u32[]{:S(2)}, u32[]{:S(2)}) collective-permute-start(bf16[704,1024]{1,0:T(8,128)(2,1)} %fusion.16), channel_id=1, source_target_pairs={{0,1},{1,0},{2,3},{3,2},{4,5},{5,4},{6,7},{7,6},{8,9},{9,8},{10,11... | collective-permute-start | bytes 4325384 | tf_op jit(solution)/shard_map/ppermute | solution.py:84
  228.8 14.0 %collective-permute-start.44 = (bf16[128,2048]{1,0:T(8,128)(2,1)S(1)}, bf16[128,2048]{1,0:T(8,128)(2,1)S(1)}, u32[]{:S(2)}, u32[]{:S(2)}) collective-permute-start(bf16[128,2048]{1,0:T(8,128)(2,1)S(1)} %get-tuple-element.697), channel_id=1, source_target_pairs={{0,8},{8,16},{16,24},{24,28},{28,20},{20,12},{12,4},{4,0},{1,9},{9... | collective-permute-start | bytes 1572872 | tf_op jit(solution)/shard_map/ppermute | solution.py:45
  229.7 13.8 %collective-permute-start.45 = (bf16[128,2048]{1,0:T(8,128)(2,1)S(1)}, bf16[128,2048]{1,0:T(8,128)(2,1)S(1)}, u32[]{:S(2)}, u32[]{:S(2)}) collective-permute-start(bf16[128,2048]{1,0:T(8,128)(2,1)S(1)} %get-tuple-element.696), channel_id=1, source_target_pairs={{8,0},{16,8},{24,16},{28,24},{20,28},{12,20},{4,12},{0,4},{9,1},{1... | collective-permute-start | bytes 1572872 | tf_op jit(solution)/shard_map/ppermute | solution.py:48
  243.9 13.0 %collective-permute-start.47 = (bf16[128,2048]{1,0:T(8,128)(2,1)S(1)}, bf16[128,2048]{1,0:T(8,128)(2,1)S(1)}, u32[]{:S(2)}, u32[]{:S(2)}) collective-permute-start(bf16[128,2048]{1,0:T(8,128)(2,1)S(1)} %get-tuple-element.695), channel_id=1, source_target_pairs={{0,8},{8,16},{16,24},{24,28},{28,20},{20,12},{12,4},{4,0},{1,9},{9... | collective-permute-start | bytes 1572872 | tf_op jit(solution)/shard_map/ppermute | solution.py:45
  245.9 12.9 %collective-permute-start.48 = (bf16[128,2048]{1,0:T(8,128)(2,1)S(1)}, bf16[128,2048]{1,0:T(8,128)(2,1)S(1)}, u32[]{:S(2)}, u32[]{:S(2)}) collective-permute-start(bf16[128,2048]{1,0:T(8,128)(2,1)S(1)} %get-tuple-element.694), channel_id=1, source_target_pairs={{8,0},{16,8},{24,16},{28,24},{20,28},{12,20},{4,12},{0,4},{9,1},{1... | collective-permute-start | bytes 1572872 | tf_op jit(solution)/shard_map/ppermute | solution.py:48
  246.2 19.2 %collective-permute-start.52 = (bf16[704,512]{1,0:T(8,128)(2,1)}, bf16[704,512]{1,0:T(8,128)(2,1)}, u32[]{:S(2)}, u32[]{:S(2)}) collective-permute-start(bf16[704,512]{1,0:T(8,128)(2,1)} %fusion.22), channel_id=1, source_target_pairs={{0,2},{1,3},{2,0},{3,1},{4,6},{5,7},{6,4},{7,5},{8,10},{9,11},{10,... | collective-permute-start | bytes 2162696 | tf_op jit(solution)/shard_map/ppermute | solution.py:84
  259.1 11.9 %collective-permute-start.50 = (bf16[128,2048]{1,0:T(8,128)(2,1)S(1)}, bf16[128,2048]{1,0:T(8,128)(2,1)S(1)}, u32[]{:S(2)}, u32[]{:S(2)}) collective-permute-start(bf16[128,2048]{1,0:T(8,128)(2,1)S(1)} %get-tuple-element.693), channel_id=1, source_target_pairs={{0,8},{8,16},{16,24},{24,28},{28,20},{20,12},{12,4},{4,0},{1,9},{9... | collective-permute-start | bytes 1572872 | tf_op jit(solution)/shard_map/ppermute | solution.py:45
  261.2 27.2 %collective-permute-start.58 = (bf16[704,512]{1,0:T(8,128)(2,1)S(1)}, bf16[704,512]{1,0:T(8,128)(2,1)S(1)}, u32[]{:S(2)}, u32[]{:S(2)}) collective-permute-start(bf16[704,512]{1,0:T(8,128)(2,1)S(1)} %fusion.23), channel_id=1, source_target_pairs={{0,2},{1,3},{2,0},{3,1},{4,6},{5,7},{6,4},{7,5},{8,10},{9,11},{10,... | collective-permute-start | bytes 2162696 | tf_op jit(solution)/shard_map/ppermute | solution.py:84
  262.7 36.1 %collective-permute-start.61 = (bf16[704,1024]{1,0:T(8,128)(2,1)S(1)}, bf16[704,1024]{1,0:T(8,128)(2,1)S(1)}, u32[]{:S(2)}, u32[]{:S(2)}) collective-permute-start(bf16[704,1024]{1,0:T(8,128)(2,1)S(1)} %fusion.19), channel_id=1, source_target_pairs={{0,1},{1,0},{2,3},{3,2},{4,5},{5,4},{6,7},{7,6},{8,9},{9,8},{10,11... | collective-permute-start | bytes 4325384 | tf_op jit(solution)/shard_map/ppermute | solution.py:84
  274.8 11.6 %collective-permute-start.54 = (bf16[128,2048]{1,0:T(8,128)(2,1)S(1)}, bf16[128,2048]{1,0:T(8,128)(2,1)S(1)}, u32[]{:S(2)}, u32[]{:S(2)}) collective-permute-start(bf16[128,2048]{1,0:T(8,128)(2,1)S(1)} %get-tuple-element.684.refs_0_), channel_id=1, source_target_pairs={{8,0},{16,8},{24,16},{28,24},{20,28},{12,20},{4,12},{0,4},{9,1},{1... | collective-permute-start | bytes 1572872 | tf_op jit(solution)/shard_map/ppermute | solution.py:48
  275.8 18.4 %collective-permute-start.57 = (bf16[704,512]{1,0:T(8,128)(2,1)S(1)}, bf16[704,512]{1,0:T(8,128)(2,1)S(1)}, u32[]{:S(2)}, u32[]{:S(2)}) collective-permute-start(bf16[704,512]{1,0:T(8,128)(2,1)S(1)} %add_convert_fusion.4.refs_0_), channel_id=1, source_target_pairs={{0,2},{1,3},{2,0},{3,1},{4,6},{5,7},{6,4},{7,5},{8,10},{9,11},{10,... | collective-permute-start | bytes 2162696 | tf_op jit(solution)/shard_map/ppermute | solution.py:84
  297.1 20.3 %collective-permute-start.64 = (bf16[704,512]{1,0:T(8,128)(2,1)S(1)}, bf16[704,512]{1,0:T(8,128)(2,1)S(1)}, u32[]{:S(2)}, u32[]{:S(2)}) collective-permute-start(bf16[704,512]{1,0:T(8,128)(2,1)S(1)} %add_convert_fusion.4.refs_0_), channel_id=1, source_target_pairs={{0,1},{1,0},{2,3},{3,2},{4,5},{5,4},{6,7},{7,6},{8,9},{9,8},{10,11... | collective-permute-start | bytes 2162696 | tf_op jit(solution)/shard_map/ppermute | solution.py:84
  297.1 18.9 %collective-permute-start.66 = (bf16[704,512]{1,0:T(8,128)(2,1)S(1)}, bf16[704,512]{1,0:T(8,128)(2,1)S(1)}, u32[]{:S(2)}, u32[]{:S(2)}) collective-permute-start(bf16[704,512]{1,0:T(8,128)(2,1)S(1)} %add_convert_fusion.3.refs_0_), channel_id=1, source_target_pairs={{0,2},{1,3},{2,0},{3,1},{4,6},{5,7},{6,4},{7,5},{8,10},{9,11},{10,... | collective-permute-start | bytes 2162696 | tf_op jit(solution)/shard_map/ppermute | solution.py:84
  298.6 18.7 %collective-permute-start.65 = (bf16[704,512]{1,0:T(8,128)(2,1)S(1)}, bf16[704,512]{1,0:T(8,128)(2,1)S(1)}, u32[]{:S(2)}, u32[]{:S(2)}) collective-permute-start(bf16[704,512]{1,0:T(8,128)(2,1)S(1)} %collective-permute-done.57.refs_1_), channel_id=1, source_target_pairs={{0,1},{1,0},{2,3},{3,2},{4,5},{5,4},{6,7},{7,6},{8,9},{9,8},{10,11... | collective-permute-start | bytes 2162696 | tf_op jit(solution)/shard_map/ppermute | solution.py:84
  298.8 14.1 %collective-permute-start.60 = (bf16[128,2048]{1,0:T(8,128)(2,1)S(1)}, bf16[128,2048]{1,0:T(8,128)(2,1)S(1)}, u32[]{:S(2)}, u32[]{:S(2)}) collective-permute-start(bf16[128,2048]{1,0:T(8,128)(2,1)S(1)} %collective-permute-done.56.refs_4_), channel_id=1, source_target_pairs={{8,0},{16,8},{24,16},{28,24},{20,28},{12,20},{4,12},{0,4},{9,1},{1... | collective-permute-start | bytes 1572872 | tf_op jit(solution)/shard_map/ppermute | solution.py:48
  306.8 29.5 %collective-permute-start.67 = (bf16[704,512]{1,0:T(8,128)(2,1)S(1)}, bf16[704,512]{1,0:T(8,128)(2,1)S(1)}, u32[]{:S(2)}, u32[]{:S(2)}) collective-permute-start(bf16[704,512]{1,0:T(8,128)(2,1)S(1)} %fusion.24), channel_id=1, source_target_pairs={{0,2},{1,3},{2,0},{3,1},{4,6},{5,7},{6,4},{7,5},{8,10},{9,11},{10,... | collective-permute-start | bytes 2162696 | tf_op jit(solution)/shard_map/ppermute | solution.py:84
  338.2 16.1 %collective-permute-start.72 = (bf16[704,512]{1,0:T(8,128)(2,1)S(1)}, bf16[704,512]{1,0:T(8,128)(2,1)S(1)}, u32[]{:S(2)}, u32[]{:S(2)}) collective-permute-start(bf16[704,512]{1,0:T(8,128)(2,1)S(1)} %add_convert_fusion.3.refs_0_), channel_id=1, source_target_pairs={{0,1},{1,0},{2,3},{3,2},{4,5},{5,4},{6,7},{7,6},{8,9},{9,8},{10,11... | collective-permute-start | bytes 2162696 | tf_op jit(solution)/shard_map/ppermute | solution.py:84
  340.6 14.2 %collective-permute-start.73 = (bf16[704,512]{1,0:T(8,128)(2,1)S(1)}, bf16[704,512]{1,0:T(8,128)(2,1)S(1)}, u32[]{:S(2)}, u32[]{:S(2)}) collective-permute-start(bf16[704,512]{1,0:T(8,128)(2,1)S(1)} %collective-permute-done.66.refs_1_), channel_id=1, source_target_pairs={{0,1},{1,0},{2,3},{3,2},{4,5},{5,4},{6,7},{7,6},{8,9},{9,8},{10,11... | collective-permute-start | bytes 2162696 | tf_op jit(solution)/shard_map/ppermute | solution.py:84
  344.9 21.7 %collective-permute-start.78 = (bf16[512,768]{1,0:T(8,128)(2,1)S(1)}, bf16[512,768]{1,0:T(8,128)(2,1)S(1)}, u32[]{:S(2)}, u32[]{:S(2)}) collective-permute-start(bf16[512,768]{1,0:T(8,128)(2,1)S(1)} %add_convert_fusion.1), channel_id=1, source_target_pairs={{0,2},{1,3},{2,0},{3,1},{4,6},{5,7},{6,4},{7,5},{8,10},{9,11},{10,... | collective-permute-start | bytes 2359304 | tf_op jit(solution)/shard_map/ppermute | solution.py:84
  346.4 14.0 %collective-permute-start.68 = (bf16[64,4096]{1,0:T(8,128)(2,1)S(1)}, bf16[64,4096]{1,0:T(8,128)(2,1)S(1)}, u32[]{:S(2)}, u32[]{:S(2)}) collective-permute-start(bf16[64,4096]{1,0:T(8,128)(2,1)S(1)} %get-tuple-element.568), channel_id=1, source_target_pairs={{0,8},{8,16},{16,24},{24,28},{28,20},{20,12},{12,4},{4,0},{1,9},{9... | collective-permute-start | bytes 1572872 | tf_op jit(solution)/shard_map/ppermute | solution.py:45
  346.7 13.7 %collective-permute-start.69 = (bf16[64,4096]{1,0:T(8,128)(2,1)S(1)}, bf16[64,4096]{1,0:T(8,128)(2,1)S(1)}, u32[]{:S(2)}, u32[]{:S(2)}) collective-permute-start(bf16[64,4096]{1,0:T(8,128)(2,1)S(1)} %get-tuple-element.569), channel_id=1, source_target_pairs={{8,0},{16,8},{24,16},{28,24},{20,28},{12,20},{4,12},{0,4},{9,1},{1... | collective-permute-start | bytes 1572872 | tf_op jit(solution)/shard_map/ppermute | solution.py:48
  354.3 26.5 %collective-permute-start.77 = (bf16[704,512]{1,0:T(8,128)(2,1)}, bf16[704,512]{1,0:T(8,128)(2,1)}, u32[]{:S(2)}, u32[]{:S(2)}) collective-permute-start(bf16[704,512]{1,0:T(8,128)(2,1)} %add_convert_fusion.2.refs_0_), channel_id=1, source_target_pairs={{0,2},{1,3},{2,0},{3,1},{4,6},{5,7},{6,4},{7,5},{8,10},{9,11},{10,... | collective-permute-start | bytes 2162696 | tf_op jit(solution)/shard_map/ppermute | solution.py:84
  362.1 26.5 %collective-permute-start.74 = (bf16[128,4096]{1,0:T(8,128)(2,1)}, bf16[128,4096]{1,0:T(8,128)(2,1)}, u32[]{:S(2)}, u32[]{:S(2)}) collective-permute-start(bf16[128,4096]{1,0:T(8,128)(2,1)} %get-tuple-element.595), channel_id=1, source_target_pairs={{0,8},{8,16},{16,24},{24,28},{28,20},{20,12},{12,4},{4,0},{1,9},{9... | collective-permute-start | bytes 3145736 | tf_op jit(solution)/shard_map/ppermute | solution.py:45
  363.0 26.4 %collective-permute-start.75 = (bf16[128,4096]{1,0:T(8,128)(2,1)}, bf16[128,4096]{1,0:T(8,128)(2,1)}, u32[]{:S(2)}, u32[]{:S(2)}) collective-permute-start(bf16[128,4096]{1,0:T(8,128)(2,1)} %get-tuple-element.596), channel_id=1, source_target_pairs={{8,0},{16,8},{24,16},{28,24},{20,28},{12,20},{4,12},{0,4},{9,1},{1... | collective-permute-start | bytes 3145736 | tf_op jit(solution)/shard_map/ppermute | solution.py:48
  364.1 17.6 %collective-permute-start.76 = (f32[8,2048]{1,0:T(8,128)S(1)}, f32[8,2048]{1,0:T(8,128)S(1)}, u32[]{:S(2)}, u32[]{:S(2)}) collective-permute-start(f32[8,2048]{1,0:T(8,128)S(1)} %add.258), channel_id=1, source_target_pairs={{0,2},{1,3},{2,0},{3,1},{4,6},{5,7},{6,4},{7,5},{8,10},{9,11},{10,... | collective-permute-start | bytes 196616 | tf_op jit(solution)/shard_map/ppermute | solution.py:84
  368.1 39.4 %all-to-all-start = ((bf16[8,64,768]{2,1,0:T(8,128)(2,1)}), bf16[8,64,768]{2,1,0:T(8,128)(2,1)}, u32[]{:S(2)}, u32[]{:S(2)}) async-start(bf16[8,64,768]{2,1,0:T(8,128)(2,1)} %bitcast.116), calls=%async_computation | async-start | bytes 1572864 | tf_op jit(solution)/shard_map/all_to_all | solution.py:948
  383.1 17.0 %collective-permute-start.83 = (bf16[256,1024]{1,0:T(8,128)(2,1)S(1)}, bf16[256,1024]{1,0:T(8,128)(2,1)S(1)}, u32[]{:S(2)}, u32[]{:S(2)}) collective-permute-start(bf16[256,1024]{1,0:T(8,128)(2,1)S(1)} %dynamic-slice_convert_fusion), channel_id=1, source_target_pairs={{0,1},{1,0},{2,3},{3,2},{4,5},{5,4},{6,7},{7,6},{8,9},{9,8},{10,11... | collective-permute-start | bytes 1572872 | tf_op jit(solution)/shard_map/ppermute | solution.py:84
  394.2 26.1 %collective-permute-start.79 = (bf16[128,4096]{1,0:T(8,128)(2,1)}, bf16[128,4096]{1,0:T(8,128)(2,1)}, u32[]{:S(2)}, u32[]{:S(2)}) collective-permute-start(bf16[128,4096]{1,0:T(8,128)(2,1)} %get-tuple-element.611), channel_id=1, source_target_pairs={{0,8},{8,16},{16,24},{24,28},{28,20},{20,12},{12,4},{4,0},{1,9},{9... | collective-permute-start | bytes 3145736 | tf_op jit(solution)/shard_map/ppermute | solution.py:45
  397.0 25.4 %collective-permute-start.80 = (bf16[128,4096]{1,0:T(8,128)(2,1)}, bf16[128,4096]{1,0:T(8,128)(2,1)}, u32[]{:S(2)}, u32[]{:S(2)}) collective-permute-start(bf16[128,4096]{1,0:T(8,128)(2,1)} %get-tuple-element.612), channel_id=1, source_target_pairs={{8,0},{16,8},{24,16},{28,24},{20,28},{12,20},{4,12},{0,4},{9,1},{1... | collective-permute-start | bytes 3145736 | tf_op jit(solution)/shard_map/ppermute | solution.py:48
  408.7 25.6 %collective-permute-start.87 = (bf16[64,6144]{1,0:T(8,128)(2,1)S(1)}, bf16[64,6144]{1,0:T(8,128)(2,1)S(1)}, u32[]{:S(2)}, u32[]{:S(2)}) collective-permute-start(bf16[64,6144]{1,0:T(8,128)(2,1)S(1)} %beside.1.refs_0_), channel_id=1, source_target_pairs={{0,2},{1,3},{2,0},{3,1},{4,6},{5,7},{6,4},{7,5},{8,10},{9,11},{10,... | collective-permute-start | bytes 2359304 | tf_op jit(solution)/shard_map/ppermute | solution.py:84
  425.6 27.9 %collective-permute-start.85 = (bf16[128,4096]{1,0:T(8,128)(2,1)}, bf16[128,4096]{1,0:T(8,128)(2,1)}, u32[]{:S(2)}, u32[]{:S(2)}) collective-permute-start(bf16[128,4096]{1,0:T(8,128)(2,1)} %get-tuple-element.629), channel_id=1, source_target_pairs={{0,8},{8,16},{16,24},{24,28},{28,20},{20,12},{12,4},{4,0},{1,9},{9... | collective-permute-start | bytes 3145736 | tf_op jit(solution)/shard_map/ppermute | solution.py:45
  431.4 24.3 %collective-permute-start.86 = (bf16[128,4096]{1,0:T(8,128)(2,1)}, bf16[128,4096]{1,0:T(8,128)(2,1)}, u32[]{:S(2)}, u32[]{:S(2)}) collective-permute-start(bf16[128,4096]{1,0:T(8,128)(2,1)} %get-tuple-element.630), channel_id=1, source_target_pairs={{8,0},{16,8},{24,16},{28,24},{20,28},{12,20},{4,12},{0,4},{9,1},{1... | collective-permute-start | bytes 3145736 | tf_op jit(solution)/shard_map/ppermute | solution.py:48
  435.7 23.2 %collective-permute-start.90 = (f32[8,2048]{1,0:T(8,128)S(1)}, f32[8,2048]{1,0:T(8,128)S(1)}, u32[]{:S(2)}, u32[]{:S(2)}) collective-permute-start(f32[8,2048]{1,0:T(8,128)S(1)} %add.261), channel_id=1, source_target_pairs={{0,4},{4,0},{8,12},{12,8},{16,20},{20,16},{24,28},{28,24},{1,5},{5... | collective-permute-start | bytes 196616 | tf_op jit(solution)/shard_map/ppermute | solution.py:84
  437.2 21.6 %collective-permute-start.91 = (f32[8,2048]{1,0:T(8,128)S(1)}, f32[8,2048]{1,0:T(8,128)S(1)}, u32[]{:S(2)}, u32[]{:S(2)}) collective-permute-start(f32[8,2048]{1,0:T(8,128)S(1)} %add.261), channel_id=1, source_target_pairs={{0,8},{4,12},{8,0},{12,4},{16,24},{20,28},{24,16},{28,20},{1,9},{5... | collective-permute-start | bytes 196616 | tf_op jit(solution)/shard_map/ppermute | solution.py:84
  439.3 19.6 %collective-permute-start.92 = (f32[8,2048]{1,0:T(8,128)S(1)}, f32[8,2048]{1,0:T(8,128)S(1)}, u32[]{:S(2)}, u32[]{:S(2)}) collective-permute-start(f32[8,2048]{1,0:T(8,128)S(1)} %add.261), channel_id=1, source_target_pairs={{0,12},{4,8},{8,4},{12,0},{16,28},{20,24},{24,20},{28,16},{1,13},{... | collective-permute-start | bytes 196616 | tf_op jit(solution)/shard_map/ppermute | solution.py:84
  (74 other events, 1097.4 us)

commit v5 on v4

--- a/solution.py
+++ b/solution.py
@@ -724,7 +724,7 @@
         return swap(v, "batch", 1)
 
     place = positions.reshape(tokens)
-    extra = 8
+    extra = 16
     place = jnp.stack([place // 64, place % 64]).astype(bf16)
     place = jnp.pad(place, ((0, extra - 2), (0, 3 * width - tokens)))
     fetched = exchange(line(lambda w, place: cut(at, w, place, n), w_qkv, place))

time: 473 us -> 476 us (level)
  transfers between devices with their start and end apart: 98 -> 98, of which waited for: 58 -> 59; matrix products, arithmetic and copies ran while one was open for 10% -> 10% of each run, Pallas kernels for 16% -> 16%
where the time goes in v5:
time: 476 us; the launch traced here: 472 us
  waiting for transfers between devices  216 us (45%)
  starting transfers between devices  105 us (22%)
  Pallas kernels  84.6 us (18%)
  matrix products  31.6 us (7%)
  local copies, waits for them, and re-layouts  22.8 us (5%)
  other arithmetic  10.2 us (2%)
    ppermute x28, waiting for transfers between devices, up(): return lax.ppermute(v, self.axis, self.ahead)  127 us
    pallas_call x13, Pallas kernels, once(): pl.pallas_call(kernel, out_shape=out_shape, in_specs=[pl.BlockSpec(memory...  48.9 us
    ppermute x41, waiting for transfers between devices, swap(): return lax.ppermute(v, axis, [(i, i ^ bit) for i in range(n)])  43.7 us
    ppermute x28, waiting for transfers between devices, down(): return lax.ppermute(v, self.axis, self.behind)  40.8 us
    ppermute x28, starting transfers between devices, up(): return lax.ppermute(v, self.axis, self.ahead)  37.7 us
    ppermute x41, starting transfers between devices, swap(): return lax.ppermute(v, axis, [(i, i ^ bit) for i in range(n)])  33.8 us
    ppermute x28, starting transfers between devices, down(): return lax.ppermute(v, self.axis, self.behind)  27.4 us
    dot_general x11, matrix products, dot_rows(): lax.dot_general(a, b, (((0,), (0,)), ((), ())), preferred_element_type=f32)  21.6 us
  transfers between devices with their start and end apart: 98, of which 59 were waited for; matrix products, arithmetic and copies ran while one was open for 10% of the time, Pallas kernels for 16%

profile of v5, /device:TPU:0, one launch (start us, length us, event | category | flops | bytes accessed | tf_op | source)
XLA Modules:
  0.0 471.9 jit_solution(4647552968817974902)
XLA Ops:
  4.5 3.0 collective-permute-start
  16.1 2.6 collective-permute-start.3
  18.7 14.4 %collective-permute-done.1.refs_2_ = bf16[80,768]{1,0:T(8,128)(2,1)S(1)} collective-permute-done((bf16[80,768]{1,0:T(8,128)(2,1)S(1)}, bf16[80,768]{1,0:T(8,128)(2,1)S(1)}, u32[]{:S(2)}, u32[]{:S(2)}) %collective-permute-start.1) | collective-permute-done | bytes 122912 | tf_op jit(solution)/shard_map/ppermute | solution.py:84
  34.1 2.9 collective-permute-start.5
  36.9 2.2 collective-permute-start.6
  39.2 6.4 %collective-permute-done.4.refs_5_ = bf16[80,768]{1,0:T(8,128)(2,1)S(1)} collective-permute-done((bf16[80,768]{1,0:T(8,128)(2,1)S(1)}, bf16[80,768]{1,0:T(8,128)(2,1)S(1)}, u32[]{:S(2)}, u32[]{:S(2)}) %collective-permute-start.4) | collective-permute-done | bytes 122912 | tf_op jit(solution)/shard_map/ppermute | solution.py:84
  48.0 2.5 collective-permute-start.9
  52.0 8.6 %collective-permute-done.10.refs_4_ = bf16[128,2048]{1,0:T(8,128)(2,1)S(1)} collective-permute-done((bf16[128,2048]{1,0:T(8,128)(2,1)S(1)}, bf16[128,2048]{1,0:T(8,128)(2,1)S(1)}, u32[]{:S(2)}, u32[]{:S(2)}) %collective-permute-start.10) | collective-permute-done | bytes 524320 | tf_op jit(solution)/shard_map/ppermute | solution.py:48
  64.9 7.9 %collective-permute-done.11.first_ref.refs_5_ = bf16[128,2048]{1,0:T(8,128)(2,1)S(1)} collective-permute-done((bf16[128,2048]{1,0:T(8,128)(2,1)S(1)}, bf16[128,2048]{1,0:T(8,128)(2,1)S(1)}, u32[]{:S(2)}, u32[]{:S(2)}) %collective-permute-start.11) | collective-permute-done | bytes 524320 | tf_op jit(solution)/shard_map/ppermute | solution.py:45
  78.1 4.9 %collective-permute-done.14.refs_7_ = bf16[64,2048]{1,0:T(8,128)(2,1)S(1)} collective-permute-done((bf16[64,2048]{1,0:T(8,128)(2,1)S(1)}, bf16[64,2048]{1,0:T(8,128)(2,1)S(1)}, u32[]{:S(2)}, u32[]{:S(2)}) %collective-permute-start.14) | collective-permute-done | bytes 262176 | tf_op jit(solution)/shard_map/ppermute | solution.py:45
  84.8 12.6 %attend.1 = (bf16[1024,2048]{1,0:T(8,128)(2,1)S(1)}, bf16[3,1024,256]{2,1,0:T(8,128)(2,1)S(1)}, bf16[1024,256]{1,0:T(8,128)(2,1)S(1)}, f32[8,1024]{1,0:T(8,128)S(1)}) custom-call(s32[16]{0:T(128)S(1)} %fusion.68.maps_ref, bf16[128,2048]{1,0:T(8,128)(2,1)S(1)} %pad_maximum_fusion.refs_0_, bf16[128,2048]{1,0:T(8,128)(2,1)S(1)} %collective-permute-done.7.refs_1_, ...), custom_call_target="tpu_custom_call" | custom-call | flops 1 | bytes 1 | tf_op jit(solution)/shard_map/attend/pallas_call | solution.py:354
  102.4 4.7 collective-permute-done.18
  111.3 7.1 %collective-permute-done.24.refs_2_ = bf16[128,2048]{1,0:T(8,128)(2,1)S(1)} collective-permute-done((bf16[128,2048]{1,0:T(8,128)(2,1)S(1)}, bf16[128,2048]{1,0:T(8,128)(2,1)S(1)}, u32[]{:S(2)}, u32[]{:S(2)}) %collective-permute-start.24) | collective-permute-done | bytes 524320 | tf_op jit(solution)/shard_map/ppermute | solution.py:45
  122.0 7.6 %collective-permute-done.22 = bf16[128,2048]{1,0:T(8,128)(2,1)S(1)} collective-permute-done((bf16[128,2048]{1,0:T(8,128)(2,1)S(1)}, bf16[128,2048]{1,0:T(8,128)(2,1)S(1)}, u32[]{:S(2)}, u32[]{:S(2)}) %collective-permute-start.22) | collective-permute-done | bytes 524320 | tf_op jit(solution)/shard_map/ppermute | solution.py:45
  133.8 7.0 %collective-permute-done.28.first_ref.refs_2_ = bf16[128,2048]{1,0:T(8,128)(2,1)S(1)} collective-permute-done((bf16[128,2048]{1,0:T(8,128)(2,1)S(1)}, bf16[128,2048]{1,0:T(8,128)(2,1)S(1)}, u32[]{:S(2)}, u32[]{:S(2)}) %collective-permute-start.28) | collective-permute-done | bytes 524320 | tf_op jit(solution)/shard_map/ppermute | solution.py:45
  142.3 7.4 %collective-permute-done.26 = bf16[128,2048]{1,0:T(8,128)(2,1)S(1)} collective-permute-done((bf16[128,2048]{1,0:T(8,128)(2,1)S(1)}, bf16[128,2048]{1,0:T(8,128)(2,1)S(1)}, u32[]{:S(2)}, u32[]{:S(2)}) %collective-permute-start.26) | collective-permute-done | bytes 524320 | tf_op jit(solution)/shard_map/ppermute | solution.py:45
  153.8 8.7 %collective-permute-done.30 = bf16[128,2048]{1,0:T(8,128)(2,1)S(1)} collective-permute-done((bf16[128,2048]{1,0:T(8,128)(2,1)S(1)}, bf16[128,2048]{1,0:T(8,128)(2,1)S(1)}, u32[]{:S(2)}, u32[]{:S(2)}) %collective-permute-start.30) | collective-permute-done | bytes 524320 | tf_op jit(solution)/shard_map/ppermute | solution.py:45
  168.5 12.7 %collective-permute-done.34.refs_4_ = bf16[64,2048]{1,0:T(8,128)(2,1)S(1)} collective-permute-done((bf16[64,2048]{1,0:T(8,128)(2,1)S(1)}, bf16[64,2048]{1,0:T(8,128)(2,1)S(1)}, u32[]{:S(2)}, u32[]{:S(2)}) %collective-permute-start.34) | collective-permute-done | bytes 262176 | tf_op jit(solution)/shard_map/ppermute | solution.py:45
  184.2 3.7 hidden_pair.4
  187.9 5.4 %collective-permute-done.36.refs_0_ = bf16[128,2048]{1,0:T(8,128)(2,1)S(1)} collective-permute-done((bf16[128,2048]{1,0:T(8,128)(2,1)S(1)}, bf16[128,2048]{1,0:T(8,128)(2,1)S(1)}, u32[]{:S(2)}, u32[]{:S(2)}) %collective-permute-start.36) | collective-permute-done | bytes 524320 | tf_op jit(solution)/shard_map/ppermute | solution.py:45
  196.6 3.7 hidden_pair.5
  200.3 6.3 %collective-permute-done.38.first_ref.refs_0_ = bf16[128,2048]{1,0:T(8,128)(2,1)S(1)} collective-permute-done((bf16[128,2048]{1,0:T(8,128)(2,1)S(1)}, bf16[128,2048]{1,0:T(8,128)(2,1)S(1)}, u32[]{:S(2)}, u32[]{:S(2)}) %collective-permute-start.38) | collective-permute-done | bytes 524320 | tf_op jit(solution)/shard_map/ppermute | solution.py:45
  209.7 3.7 hidden_pair.6
  214.6 3.7 hidden_pair.7
  224.7 2.9 fusion.13
  227.6 2.9 fusion.16
  235.4 2.1 fusion.22
  237.4 7.7 %collective-permute-done.44 = bf16[128,2048]{1,0:T(8,128)(2,1)S(1)} collective-permute-done((bf16[128,2048]{1,0:T(8,128)(2,1)S(1)}, bf16[128,2048]{1,0:T(8,128)(2,1)S(1)}, u32[]{:S(2)}, u32[]{:S(2)}) %collective-permute-start.44) | collective-permute-done | bytes 524320 | tf_op jit(solution)/shard_map/ppermute | solution.py:45
  246.8 2.1 collective-permute-start.47
  255.7 4.1 collective-permute-done.47
  265.6 2.7 collective-permute-done.52
  268.3 2.3 add_convert_fusion.4.refs_0_
  270.6 3.3 collective-permute-done.50
  280.2 7.6 %collective-permute-done.53.refs_1_ = bf16[128,2048]{1,0:T(8,128)(2,1)S(1)} collective-permute-done((bf16[128,2048]{1,0:T(8,128)(2,1)S(1)}, bf16[128,2048]{1,0:T(8,128)(2,1)S(1)}, u32[]{:S(2)}, u32[]{:S(2)}) %collective-permute-start.53) | collective-permute-done | bytes 524320 | tf_op jit(solution)/shard_map/ppermute | solution.py:45
  292.1 5.0 %collective-permute-done.57.refs_1_ = bf16[704,512]{1,0:T(8,128)(2,1)S(1)} collective-permute-done((bf16[704,512]{1,0:T(8,128)(2,1)S(1)}, bf16[704,512]{1,0:T(8,128)(2,1)S(1)}, u32[]{:S(2)}, u32[]{:S(2)}) %collective-permute-start.57) | collective-permute-done | bytes 720928 | tf_op jit(solution)/shard_map/ppermute | solution.py:84
  304.2 5.3 %collective-permute-done.59.first_ref.refs_5_ = bf16[128,2048]{1,0:T(8,128)(2,1)S(1)} collective-permute-done((bf16[128,2048]{1,0:T(8,128)(2,1)S(1)}, bf16[128,2048]{1,0:T(8,128)(2,1)S(1)}, u32[]{:S(2)}, u32[]{:S(2)}) %collective-permute-start.59) | collective-permute-done | bytes 524320 | tf_op jit(solution)/shard_map/ppermute | solution.py:45
  311.0 4.9 %collective-permute-done.60.second_ref.refs_6_ = bf16[128,2048]{1,0:T(8,128)(2,1)S(1)} collective-permute-done((bf16[128,2048]{1,0:T(8,128)(2,1)S(1)}, bf16[128,2048]{1,0:T(8,128)(2,1)S(1)}, u32[]{:S(2)}, u32[]{:S(2)}) %collective-permute-start.60) | collective-permute-done | bytes 524320 | tf_op jit(solution)/shard_map/ppermute | solution.py:48
  316.6 2.5 collective-permute-done.66.refs_1_
  320.2 3.8 placed.5
  324.1 2.6 collective-permute-done.63.refs_8_
  326.7 11.4 %attend_back.1 = (bf16[1024,768]{1,0:T(8,128)(2,1)S(1)}, f32[256,2048]{1,0:T(8,128)S(1)}) custom-call(s32[16]{0:T(128)S(1)} %fusion.68.maps_ref, bf16[128,2048]{1,0:T(8,128)(2,1)S(1)} %get-tuple-element.684.refs_0_, bf16[128,2048]{1,0:T(8,128)(2,1)S(1)} %collective-permute-done.53.refs_1_, bf16[128,2048]{1,0:T(8,128)(2,1)S(1)} %collective-permute-done.54.refs_2_, ...), custom_call_target="tpu_custom_call" | custom-call | flops 1 | bytes 1 | tf_op jit(solution)/shard_map/attend_back/pallas_call | solution.py:354
  345.8 1.9 fusion.local_ref
  351.5 3.8 vectors.1
  355.3 2.1 add_convert_fusion.2.refs_0_
  357.9 3.4 placed.6
  361.4 2.1 collective-permute-done.68.first_ref
  371.5 5.6 %all-to-all-start = ((bf16[8,64,768]{2,1,0:T(8,128)(2,1)}), bf16[8,64,768]{2,1,0:T(8,128)(2,1)}, u32[]{:S(2)}, u32[]{:S(2)}) async-start(bf16[8,64,768]{2,1,0:T(8,128)(2,1)} %bitcast.116), calls=%async_computation | async-start | bytes 1572864 | tf_op jit(solution)/shard_map/all_to_all | solution.py:948
  377.1 6.9 %collective-permute-done.77.refs_1_ = bf16[704,512]{1,0:T(8,128)(2,1)} collective-permute-done((bf16[704,512]{1,0:T(8,128)(2,1)}, bf16[704,512]{1,0:T(8,128)(2,1)}, u32[]{:S(2)}, u32[]{:S(2)}) %collective-permute-start.77) | collective-permute-done | bytes 720928 | tf_op jit(solution)/shard_map/ppermute | solution.py:84
  388.1 3.5 collective-permute-done.74.first_ref
  393.9 3.2 hop.4
  397.1 2.9 collective-permute-start.79
  405.5 4.9 %all-to-all-done.in_ref = bf16[8,64,768]{2,1,0:T(8,128)(2,1)} async-done(((bf16[8,64,768]{2,1,0:T(8,128)(2,1)}), bf16[8,64,768]{2,1,0:T(8,128)(2,1)}, u32[]{:S(2)}, u32[]{:S(2)}) %all-to-all-start) | async-done | bytes 786464 | tf_op jit(solution)/shard_map/all_to_all | solution.py:948
  413.4 5.5 %placed.7 = f32[704,2048]{1,0:T(8,128)} custom-call(s32[4]{0:T(128)S(1)} %get-tuple-element.346.at_ref, bf16[704,512]{1,0:T(8,128)(2,1)} %add_convert_fusion.2.refs_0_, bf16[704,512]{1,0:T(8,128)(2,1)} %collective-permute-done.77.refs_1_, bf16[704,512]{1,0:T(8,128)(2,1)} %collective-permute-done.81.refs_2_, bf16[704,512]{1,0:T(8,128)(2,1)} %collective-permute-done.82.refs_3_), custom_call_target="tpu_custom_call" | custom-call | flops 1 | bytes 1 | tf_op jit(solution)/shard_map/placed/pallas_call | solution.py:686
  419.0 4.2 collective-permute-done.79.first_ref
  423.1 2.3 collective-permute-done.80.second_ref
  425.5 3.2 hop.5
  428.6 5.8 %collective-permute-start.85 = (bf16[128,4096]{1,0:T(8,128)(2,1)}, bf16[128,4096]{1,0:T(8,128)(2,1)}, u32[]{:S(2)}, u32[]{:S(2)}) collective-permute-start(bf16[128,4096]{1,0:T(8,128)(2,1)} %get-tuple-element.629), channel_id=1, source_target_pairs={{0,8},{8,16},{16,24},{24,28},{28,20},{20,12},{12,4},{4,0},{1,9},{9... | collective-permute-start | bytes 3145736 | tf_op jit(solution)/shard_map/ppermute | solution.py:45
  440.3 2.0 collective-permute-start.91
  446.6 3.8 placed.8
  450.4 6.3 %collective-permute-done.85.first_ref = bf16[128,4096]{1,0:T(8,128)(2,1)} collective-permute-done((bf16[128,4096]{1,0:T(8,128)(2,1)}, bf16[128,4096]{1,0:T(8,128)(2,1)}, u32[]{:S(2)}, u32[]{:S(2)}) %collective-permute-start.85) | collective-permute-done | bytes 1048608 | tf_op jit(solution)/shard_map/ppermute | solution.py:45
  458.9 3.1 last_back.1
  463.1 2.0 copy.49
  465.1 2.9 collective-permute-done.93
  469.3 2.4 placed.9
  (333 shorter events, 163.3 us)
Async XLA Ops:
  10.9 35.3 %collective-permute-start.7 = (bf16[128,2048]{1,0:T(8,128)(2,1)S(1)}, bf16[128,2048]{1,0:T(8,128)(2,1)S(1)}, u32[]{:S(2)}, u32[]{:S(2)}) collective-permute-start(bf16[128,2048]{1,0:T(8,128)(2,1)S(1)} %pad_maximum_fusion.refs_0_), channel_id=1, source_target_pairs={{0,8},{8,16},{16,24},{24,28},{28,20},{20,12},{12,4},{4,0},{1,9},{9... | collective-permute-start | bytes 1572872 | tf_op jit(solution)/shard_map/ppermute | solution.py:45
  12.7 33.5 %collective-permute-start.8 = (bf16[128,2048]{1,0:T(8,128)(2,1)S(1)}, bf16[128,2048]{1,0:T(8,128)(2,1)S(1)}, u32[]{:S(2)}, u32[]{:S(2)}) collective-permute-start(bf16[128,2048]{1,0:T(8,128)(2,1)S(1)} %pad_maximum_fusion.refs_0_), channel_id=1, source_target_pairs={{8,0},{16,8},{24,16},{28,24},{20,28},{12,20},{4,12},{0,4},{9,1},{1... | collective-permute-start | bytes 1572872 | tf_op jit(solution)/shard_map/ppermute | solution.py:48
  12.9 20.2 %collective-permute-start.1 = (bf16[80,768]{1,0:T(8,128)(2,1)S(1)}, bf16[80,768]{1,0:T(8,128)(2,1)S(1)}, u32[]{:S(2)}, u32[]{:S(2)}) collective-permute-start(bf16[80,768]{1,0:T(8,128)(2,1)S(1)} %get-tuple-element.352), channel_id=1, source_target_pairs={{0,8},{4,12},{8,0},{12,4},{16,24},{20,28},{24,16},{28,20},{1,9},{5... | collective-permute-start | bytes 368648 | tf_op jit(solution)/shard_map/ppermute | solution.py:84
  14.7 19.3 %collective-permute-start.2 = (bf16[80,768]{1,0:T(8,128)(2,1)S(1)}, bf16[80,768]{1,0:T(8,128)(2,1)S(1)}, u32[]{:S(2)}, u32[]{:S(2)}) collective-permute-start(bf16[80,768]{1,0:T(8,128)(2,1)S(1)} %get-tuple-element.353), channel_id=1, source_target_pairs={{0,12},{4,8},{8,4},{12,0},{16,28},{20,24},{24,20},{28,16},{1,13},{... | collective-permute-start | bytes 368648 | tf_op jit(solution)/shard_map/ppermute | solution.py:84
  16.1 20.8 %collective-permute-start.3 = (bf16[80,768]{1,0:T(8,128)(2,1)S(1)}, bf16[80,768]{1,0:T(8,128)(2,1)S(1)}, u32[]{:S(2)}, u32[]{:S(2)}) collective-permute-start(bf16[80,768]{1,0:T(8,128)(2,1)S(1)} %get-tuple-element.354), channel_id=1, source_target_pairs={{0,16},{4,20},{8,24},{12,28},{16,0},{20,4},{24,8},{28,12},{1,17},{... | collective-permute-start | bytes 368648 | tf_op jit(solution)/shard_map/ppermute | solution.py:84
  33.1 12.4 %collective-permute-start.4 = (bf16[80,768]{1,0:T(8,128)(2,1)S(1)}, bf16[80,768]{1,0:T(8,128)(2,1)S(1)}, u32[]{:S(2)}, u32[]{:S(2)}) collective-permute-start(bf16[80,768]{1,0:T(8,128)(2,1)S(1)} %get-tuple-element.355), channel_id=1, source_target_pairs={{0,20},{4,16},{8,28},{12,24},{16,4},{20,0},{24,12},{28,8},{1,21},{... | collective-permute-start | bytes 368648 | tf_op jit(solution)/shard_map/ppermute | solution.py:84
  34.1 11.5 %collective-permute-start.5 = (bf16[80,768]{1,0:T(8,128)(2,1)S(1)}, bf16[80,768]{1,0:T(8,128)(2,1)S(1)}, u32[]{:S(2)}, u32[]{:S(2)}) collective-permute-start(bf16[80,768]{1,0:T(8,128)(2,1)S(1)} %get-tuple-element.356), channel_id=1, source_target_pairs={{0,24},{4,28},{8,16},{12,20},{16,8},{20,12},{24,0},{28,4},{1,25},{... | collective-permute-start | bytes 368648 | tf_op jit(solution)/shard_map/ppermute | solution.py:84
  46.2 14.5 %collective-permute-start.10 = (bf16[128,2048]{1,0:T(8,128)(2,1)S(1)}, bf16[128,2048]{1,0:T(8,128)(2,1)S(1)}, u32[]{:S(2)}, u32[]{:S(2)}) collective-permute-start(bf16[128,2048]{1,0:T(8,128)(2,1)S(1)} %collective-permute-done.8.refs_2_), channel_id=1, source_target_pairs={{8,0},{16,8},{24,16},{28,24},{20,28},{12,20},{4,12},{0,4},{9,1},{1... | collective-permute-start | bytes 1572872 | tf_op jit(solution)/shard_map/ppermute | solution.py:48
  48.0 14.0 %collective-permute-start.9 = (bf16[128,2048]{1,0:T(8,128)(2,1)S(1)}, bf16[128,2048]{1,0:T(8,128)(2,1)S(1)}, u32[]{:S(2)}, u32[]{:S(2)}) collective-permute-start(bf16[128,2048]{1,0:T(8,128)(2,1)S(1)} %collective-permute-done.7.refs_1_), channel_id=1, source_target_pairs={{0,8},{8,16},{16,24},{24,28},{28,20},{20,12},{12,4},{4,0},{1,9},{9... | collective-permute-start | bytes 1572872 | tf_op jit(solution)/shard_map/ppermute | solution.py:45
  50.5 14.4 %collective-permute-start.13 = (bf16[512,768]{1,0:T(8,128)(2,1)S(1)}, bf16[512,768]{1,0:T(8,128)(2,1)S(1)}, u32[]{:S(2)}, u32[]{:S(2)}) collective-permute-start(bf16[512,768]{1,0:T(8,128)(2,1)S(1)} %get-tuple-element.420.refs_9_), channel_id=1, source_target_pairs={{0,1},{1,0},{2,3},{3,2},{4,5},{5,4},{6,7},{7,6},{8,9},{9,8},{10,11... | collective-permute-start | bytes 2359304 | tf_op jit(solution)/shard_map/ppermute | solution.py:84
  50.5 23.4 %collective-permute-start.16 = (bf16[512,768]{1,0:T(8,128)(2,1)S(1)}, bf16[512,768]{1,0:T(8,128)(2,1)S(1)}, u32[]{:S(2)}, u32[]{:S(2)}) collective-permute-start(bf16[512,768]{1,0:T(8,128)(2,1)S(1)} %get-tuple-element.420.refs_9_), channel_id=1, source_target_pairs={{0,2},{1,3},{2,0},{3,1},{4,6},{5,7},{6,4},{7,5},{8,10},{9,11},{10,... | collective-permute-start | bytes 2359304 | tf_op jit(solution)/shard_map/ppermute | solution.py:84
  76.0 24.4 %collective-permute-start.20 = (bf16[128,2048]{1,0:T(8,128)(2,1)S(1)}, bf16[128,2048]{1,0:T(8,128)(2,1)S(1)}, u32[]{:S(2)}, u32[]{:S(2)}) collective-permute-start(bf16[128,2048]{1,0:T(8,128)(2,1)S(1)} %bitcast.105), channel_id=1, source_target_pairs={{0,8},{8,16},{16,24},{24,28},{28,20},{20,12},{12,4},{4,0},{1,9},{9... | collective-permute-start | bytes 1572872 | tf_op jit(solution)/shard_map/ppermute | solution.py:45
  77.7 22.6 %collective-permute-start.21 = (bf16[128,2048]{1,0:T(8,128)(2,1)S(1)}, bf16[128,2048]{1,0:T(8,128)(2,1)S(1)}, u32[]{:S(2)}, u32[]{:S(2)}) collective-permute-start(bf16[128,2048]{1,0:T(8,128)(2,1)S(1)} %bitcast.106), channel_id=1, source_target_pairs={{8,0},{16,8},{24,16},{28,24},{20,28},{12,20},{4,12},{0,4},{9,1},{1... | collective-permute-start | bytes 1572872 | tf_op jit(solution)/shard_map/ppermute | solution.py:48
  100.3 18.0 %collective-permute-start.24 = (bf16[128,2048]{1,0:T(8,128)(2,1)S(1)}, bf16[128,2048]{1,0:T(8,128)(2,1)S(1)}, u32[]{:S(2)}, u32[]{:S(2)}) collective-permute-start(bf16[128,2048]{1,0:T(8,128)(2,1)S(1)} %collective-permute-done.20.refs_2_), channel_id=1, source_target_pairs={{0,8},{8,16},{16,24},{24,28},{28,20},{20,12},{12,4},{4,0},{1,9},{9... | collective-permute-start | bytes 1572872 | tf_op jit(solution)/shard_map/ppermute | solution.py:45
  101.9 17.9 %collective-permute-start.25 = (bf16[128,2048]{1,0:T(8,128)(2,1)S(1)}, bf16[128,2048]{1,0:T(8,128)(2,1)S(1)}, u32[]{:S(2)}, u32[]{:S(2)}) collective-permute-start(bf16[128,2048]{1,0:T(8,128)(2,1)S(1)} %collective-permute-done.21.refs_3_), channel_id=1, source_target_pairs={{8,0},{16,8},{24,16},{28,24},{20,28},{12,20},{4,12},{0,4},{9,1},{1... | collective-permute-start | bytes 1572872 | tf_op jit(solution)/shard_map/ppermute | solution.py:48
  108.7 20.8 %collective-permute-start.22 = (bf16[128,2048]{1,0:T(8,128)(2,1)S(1)}, bf16[128,2048]{1,0:T(8,128)(2,1)S(1)}, u32[]{:S(2)}, u32[]{:S(2)}) collective-permute-start(bf16[128,2048]{1,0:T(8,128)(2,1)S(1)} %get-tuple-element.703), channel_id=1, source_target_pairs={{0,8},{8,16},{16,24},{24,28},{28,20},{20,12},{12,4},{4,0},{1,9},{9... | collective-permute-start | bytes 1572872 | tf_op jit(solution)/shard_map/ppermute | solution.py:45
  109.4 21.7 %collective-permute-start.23 = (bf16[128,2048]{1,0:T(8,128)(2,1)S(1)}, bf16[128,2048]{1,0:T(8,128)(2,1)S(1)}, u32[]{:S(2)}, u32[]{:S(2)}) collective-permute-start(bf16[128,2048]{1,0:T(8,128)(2,1)S(1)} %get-tuple-element.702), channel_id=1, source_target_pairs={{8,0},{16,8},{24,16},{28,24},{20,28},{12,20},{4,12},{0,4},{9,1},{1... | collective-permute-start | bytes 1572872 | tf_op jit(solution)/shard_map/ppermute | solution.py:48
  119.8 21.0 %collective-permute-start.28 = (bf16[128,2048]{1,0:T(8,128)(2,1)S(1)}, bf16[128,2048]{1,0:T(8,128)(2,1)S(1)}, u32[]{:S(2)}, u32[]{:S(2)}) collective-permute-start(bf16[128,2048]{1,0:T(8,128)(2,1)S(1)} %collective-permute-done.24.refs_2_), channel_id=1, source_target_pairs={{0,8},{8,16},{16,24},{24,28},{28,20},{20,12},{12,4},{4,0},{1,9},{9... | collective-permute-start | bytes 1572872 | tf_op jit(solution)/shard_map/ppermute | solution.py:45
  120.4 21.9 %collective-permute-start.29 = (bf16[128,2048]{1,0:T(8,128)(2,1)S(1)}, bf16[128,2048]{1,0:T(8,128)(2,1)S(1)}, u32[]{:S(2)}, u32[]{:S(2)}) collective-permute-start(bf16[128,2048]{1,0:T(8,128)(2,1)S(1)} %collective-permute-done.25.refs_3_), channel_id=1, source_target_pairs={{8,0},{16,8},{24,16},{28,24},{20,28},{12,20},{4,12},{0,4},{9,1},{1... | collective-permute-start | bytes 1572872 | tf_op jit(solution)/shard_map/ppermute | solution.py:48
  131.3 18.4 %collective-permute-start.26 = (bf16[128,2048]{1,0:T(8,128)(2,1)S(1)}, bf16[128,2048]{1,0:T(8,128)(2,1)S(1)}, u32[]{:S(2)}, u32[]{:S(2)}) collective-permute-start(bf16[128,2048]{1,0:T(8,128)(2,1)S(1)} %get-tuple-element.701), channel_id=1, source_target_pairs={{0,8},{8,16},{16,24},{24,28},{28,20},{20,12},{12,4},{4,0},{1,9},{9... | collective-permute-start | bytes 1572872 | tf_op jit(solution)/shard_map/ppermute | solution.py:45
  131.9 19.0 %collective-permute-start.27 = (bf16[128,2048]{1,0:T(8,128)(2,1)S(1)}, bf16[128,2048]{1,0:T(8,128)(2,1)S(1)}, u32[]{:S(2)}, u32[]{:S(2)}) collective-permute-start(bf16[128,2048]{1,0:T(8,128)(2,1)S(1)} %get-tuple-element.700), channel_id=1, source_target_pairs={{8,0},{16,8},{24,16},{28,24},{20,28},{12,20},{4,12},{0,4},{9,1},{1... | collective-permute-start | bytes 1572872 | tf_op jit(solution)/shard_map/ppermute | solution.py:48
  151.2 11.4 %collective-permute-start.30 = (bf16[128,2048]{1,0:T(8,128)(2,1)S(1)}, bf16[128,2048]{1,0:T(8,128)(2,1)S(1)}, u32[]{:S(2)}, u32[]{:S(2)}) collective-permute-start(bf16[128,2048]{1,0:T(8,128)(2,1)S(1)} %get-tuple-element.699), channel_id=1, source_target_pairs={{0,8},{8,16},{16,24},{24,28},{28,20},{20,12},{12,4},{4,0},{1,9},{9... | collective-permute-start | bytes 1572872 | tf_op jit(solution)/shard_map/ppermute | solution.py:45
  164.2 17.9 %collective-permute-start.32 = (bf16[128,2048]{1,0:T(8,128)(2,1)S(1)}, bf16[128,2048]{1,0:T(8,128)(2,1)S(1)}, u32[]{:S(2)}, u32[]{:S(2)}) collective-permute-start(bf16[128,2048]{1,0:T(8,128)(2,1)S(1)} %get-tuple-element.474.refs_0_), channel_id=1, source_target_pairs={{0,8},{8,16},{16,24},{24,28},{28,20},{20,12},{12,4},{4,0},{1,9},{9... | collective-permute-start | bytes 1572872 | tf_op jit(solution)/shard_map/ppermute | solution.py:45
  165.2 17.0 %collective-permute-start.33 = (bf16[128,2048]{1,0:T(8,128)(2,1)S(1)}, bf16[128,2048]{1,0:T(8,128)(2,1)S(1)}, u32[]{:S(2)}, u32[]{:S(2)}) collective-permute-start(bf16[128,2048]{1,0:T(8,128)(2,1)S(1)} %get-tuple-element.474.refs_0_), channel_id=1, source_target_pairs={{8,0},{16,8},{24,16},{28,24},{20,28},{12,20},{4,12},{0,4},{9,1},{1... | collective-permute-start | bytes 1572872 | tf_op jit(solution)/shard_map/ppermute | solution.py:48
  166.4 14.8 %collective-permute-start.34 = (bf16[64,2048]{1,0:T(8,128)(2,1)S(1)}, bf16[64,2048]{1,0:T(8,128)(2,1)S(1)}, u32[]{:S(2)}, u32[]{:S(2)}) collective-permute-start(bf16[64,2048]{1,0:T(8,128)(2,1)S(1)} %get-tuple-element.429), channel_id=1, source_target_pairs={{0,8},{8,16},{16,24},{24,28},{28,20},{20,12},{12,4},{4,0},{1,9},{9... | collective-permute-start | bytes 786440 | tf_op jit(solution)/shard_map/ppermute | solution.py:45
  167.3 14.9 %collective-permute-start.35 = (bf16[64,2048]{1,0:T(8,128)(2,1)S(1)}, bf16[64,2048]{1,0:T(8,128)(2,1)S(1)}, u32[]{:S(2)}, u32[]{:S(2)}) collective-permute-start(bf16[64,2048]{1,0:T(8,128)(2,1)S(1)} %get-tuple-element.430), channel_id=1, source_target_pairs={{8,0},{16,8},{24,16},{28,24},{20,28},{12,20},{4,12},{0,4},{9,1},{1... | collective-permute-start | bytes 786440 | tf_op jit(solution)/shard_map/ppermute | solution.py:48
  183.1 11.5 %collective-permute-start.37 = (bf16[128,2048]{1,0:T(8,128)(2,1)S(1)}, bf16[128,2048]{1,0:T(8,128)(2,1)S(1)}, u32[]{:S(2)}, u32[]{:S(2)}) collective-permute-start(bf16[128,2048]{1,0:T(8,128)(2,1)S(1)} %collective-permute-done.33.refs_1_), channel_id=1, source_target_pairs={{8,0},{16,8},{24,16},{28,24},{20,28},{12,20},{4,12},{0,4},{9,1},{1... | collective-permute-start | bytes 1572872 | tf_op jit(solution)/shard_map/ppermute | solution.py:48
  194.6 12.0 %collective-permute-start.38 = (bf16[128,2048]{1,0:T(8,128)(2,1)S(1)}, bf16[128,2048]{1,0:T(8,128)(2,1)S(1)}, u32[]{:S(2)}, u32[]{:S(2)}) collective-permute-start(bf16[128,2048]{1,0:T(8,128)(2,1)S(1)} %collective-permute-done.36.refs_0_), channel_id=1, source_target_pairs={{0,8},{8,16},{16,24},{24,28},{28,20},{20,12},{12,4},{4,0},{1,9},{9... | collective-permute-start | bytes 1572872 | tf_op jit(solution)/shard_map/ppermute | solution.py:45
  195.2 12.0 %collective-permute-start.39 = (bf16[128,2048]{1,0:T(8,128)(2,1)S(1)}, bf16[128,2048]{1,0:T(8,128)(2,1)S(1)}, u32[]{:S(2)}, u32[]{:S(2)}) collective-permute-start(bf16[128,2048]{1,0:T(8,128)(2,1)S(1)} %collective-permute-done.37.refs_1_), channel_id=1, source_target_pairs={{8,0},{16,8},{24,16},{28,24},{20,28},{12,20},{4,12},{0,4},{9,1},{1... | collective-permute-start | bytes 1572872 | tf_op jit(solution)/shard_map/ppermute | solution.py:48
  230.5 22.1 %collective-permute-start.49 = (bf16[704,1024]{1,0:T(8,128)(2,1)}, bf16[704,1024]{1,0:T(8,128)(2,1)S(1)}, u32[]{:S(2)}, u32[]{:S(2)}) collective-permute-start(bf16[704,1024]{1,0:T(8,128)(2,1)} %fusion.16), channel_id=1, source_target_pairs={{0,1},{1,0},{2,3},{3,2},{4,5},{5,4},{6,7},{7,6},{8,9},{9,8},{10,11... | collective-permute-start | bytes 4325384 | tf_op jit(solution)/shard_map/ppermute | solution.py:84
  231.2 13.9 %collective-permute-start.44 = (bf16[128,2048]{1,0:T(8,128)(2,1)S(1)}, bf16[128,2048]{1,0:T(8,128)(2,1)S(1)}, u32[]{:S(2)}, u32[]{:S(2)}) collective-permute-start(bf16[128,2048]{1,0:T(8,128)(2,1)S(1)} %get-tuple-element.697), channel_id=1, source_target_pairs={{0,8},{8,16},{16,24},{24,28},{28,20},{20,12},{12,4},{4,0},{1,9},{9... | collective-permute-start | bytes 1572872 | tf_op jit(solution)/shard_map/ppermute | solution.py:45
  232.6 13.8 %collective-permute-start.45 = (bf16[128,2048]{1,0:T(8,128)(2,1)S(1)}, bf16[128,2048]{1,0:T(8,128)(2,1)S(1)}, u32[]{:S(2)}, u32[]{:S(2)}) collective-permute-start(bf16[128,2048]{1,0:T(8,128)(2,1)S(1)} %get-tuple-element.696), channel_id=1, source_target_pairs={{8,0},{16,8},{24,16},{28,24},{20,28},{12,20},{4,12},{0,4},{9,1},{1... | collective-permute-start | bytes 1572872 | tf_op jit(solution)/shard_map/ppermute | solution.py:48
  246.8 13.0 %collective-permute-start.47 = (bf16[128,2048]{1,0:T(8,128)(2,1)S(1)}, bf16[128,2048]{1,0:T(8,128)(2,1)S(1)}, u32[]{:S(2)}, u32[]{:S(2)}) collective-permute-start(bf16[128,2048]{1,0:T(8,128)(2,1)S(1)} %get-tuple-element.695), channel_id=1, source_target_pairs={{0,8},{8,16},{16,24},{24,28},{28,20},{20,12},{12,4},{4,0},{1,9},{9... | collective-permute-start | bytes 1572872 | tf_op jit(solution)/shard_map/ppermute | solution.py:45
  248.8 12.9 %collective-permute-start.48 = (bf16[128,2048]{1,0:T(8,128)(2,1)S(1)}, bf16[128,2048]{1,0:T(8,128)(2,1)S(1)}, u32[]{:S(2)}, u32[]{:S(2)}) collective-permute-start(bf16[128,2048]{1,0:T(8,128)(2,1)S(1)} %get-tuple-element.694), channel_id=1, source_target_pairs={{8,0},{16,8},{24,16},{28,24},{20,28},{12,20},{4,12},{0,4},{9,1},{1... | collective-permute-start | bytes 1572872 | tf_op jit(solution)/shard_map/ppermute | solution.py:48
  249.0 19.2 %collective-permute-start.52 = (bf16[704,512]{1,0:T(8,128)(2,1)}, bf16[704,512]{1,0:T(8,128)(2,1)}, u32[]{:S(2)}, u32[]{:S(2)}) collective-permute-start(bf16[704,512]{1,0:T(8,128)(2,1)} %fusion.22), channel_id=1, source_target_pairs={{0,2},{1,3},{2,0},{3,1},{4,6},{5,7},{6,4},{7,5},{8,10},{9,11},{10,... | collective-permute-start | bytes 2162696 | tf_op jit(solution)/shard_map/ppermute | solution.py:84
  262.0 11.9 %collective-permute-start.50 = (bf16[128,2048]{1,0:T(8,128)(2,1)S(1)}, bf16[128,2048]{1,0:T(8,128)(2,1)S(1)}, u32[]{:S(2)}, u32[]{:S(2)}) collective-permute-start(bf16[128,2048]{1,0:T(8,128)(2,1)S(1)} %get-tuple-element.693), channel_id=1, source_target_pairs={{0,8},{8,16},{16,24},{24,28},{28,20},{20,12},{12,4},{4,0},{1,9},{9... | collective-permute-start | bytes 1572872 | tf_op jit(solution)/shard_map/ppermute | solution.py:45
  263.5 11.3 %collective-permute-start.51 = (bf16[128,2048]{1,0:T(8,128)(2,1)S(1)}, bf16[128,2048]{1,0:T(8,128)(2,1)S(1)}, u32[]{:S(2)}, u32[]{:S(2)}) collective-permute-start(bf16[128,2048]{1,0:T(8,128)(2,1)S(1)} %get-tuple-element.692), channel_id=1, source_target_pairs={{8,0},{16,8},{24,16},{28,24},{20,28},{12,20},{4,12},{0,4},{9,1},{1... | collective-permute-start | bytes 1572872 | tf_op jit(solution)/shard_map/ppermute | solution.py:48
  264.1 26.8 %collective-permute-start.58 = (bf16[704,512]{1,0:T(8,128)(2,1)S(1)}, bf16[704,512]{1,0:T(8,128)(2,1)S(1)}, u32[]{:S(2)}, u32[]{:S(2)}) collective-permute-start(bf16[704,512]{1,0:T(8,128)(2,1)S(1)} %fusion.23), channel_id=1, source_target_pairs={{0,2},{1,3},{2,0},{3,1},{4,6},{5,7},{6,4},{7,5},{8,10},{9,11},{10,... | collective-permute-start | bytes 2162696 | tf_op jit(solution)/shard_map/ppermute | solution.py:84
  265.6 36.3 %collective-permute-start.61 = (bf16[704,1024]{1,0:T(8,128)(2,1)S(1)}, bf16[704,1024]{1,0:T(8,128)(2,1)S(1)}, u32[]{:S(2)}, u32[]{:S(2)}) collective-permute-start(bf16[704,1024]{1,0:T(8,128)(2,1)S(1)} %fusion.19), channel_id=1, source_target_pairs={{0,1},{1,0},{2,3},{3,2},{4,5},{5,4},{6,7},{7,6},{8,9},{9,8},{10,11... | collective-permute-start | bytes 4325384 | tf_op jit(solution)/shard_map/ppermute | solution.py:84
  278.7 18.4 %collective-permute-start.57 = (bf16[704,512]{1,0:T(8,128)(2,1)S(1)}, bf16[704,512]{1,0:T(8,128)(2,1)S(1)}, u32[]{:S(2)}, u32[]{:S(2)}) collective-permute-start(bf16[704,512]{1,0:T(8,128)(2,1)S(1)} %add_convert_fusion.4.refs_0_), channel_id=1, source_target_pairs={{0,2},{1,3},{2,0},{3,1},{4,6},{5,7},{6,4},{7,5},{8,10},{9,11},{10,... | collective-permute-start | bytes 2162696 | tf_op jit(solution)/shard_map/ppermute | solution.py:84
  300.2 20.0 %collective-permute-start.64 = (bf16[704,512]{1,0:T(8,128)(2,1)S(1)}, bf16[704,512]{1,0:T(8,128)(2,1)S(1)}, u32[]{:S(2)}, u32[]{:S(2)}) collective-permute-start(bf16[704,512]{1,0:T(8,128)(2,1)S(1)} %add_convert_fusion.4.refs_0_), channel_id=1, source_target_pairs={{0,1},{1,0},{2,3},{3,2},{4,5},{5,4},{6,7},{7,6},{8,9},{9,8},{10,11... | collective-permute-start | bytes 2162696 | tf_op jit(solution)/shard_map/ppermute | solution.py:84
  300.2 18.9 %collective-permute-start.66 = (bf16[704,512]{1,0:T(8,128)(2,1)S(1)}, bf16[704,512]{1,0:T(8,128)(2,1)S(1)}, u32[]{:S(2)}, u32[]{:S(2)}) collective-permute-start(bf16[704,512]{1,0:T(8,128)(2,1)S(1)} %add_convert_fusion.3.refs_0_), channel_id=1, source_target_pairs={{0,2},{1,3},{2,0},{3,1},{4,6},{5,7},{6,4},{7,5},{8,10},{9,11},{10,... | collective-permute-start | bytes 2162696 | tf_op jit(solution)/shard_map/ppermute | solution.py:84
  301.6 18.6 %collective-permute-start.65 = (bf16[704,512]{1,0:T(8,128)(2,1)S(1)}, bf16[704,512]{1,0:T(8,128)(2,1)S(1)}, u32[]{:S(2)}, u32[]{:S(2)}) collective-permute-start(bf16[704,512]{1,0:T(8,128)(2,1)S(1)} %collective-permute-done.57.refs_1_), channel_id=1, source_target_pairs={{0,1},{1,0},{2,3},{3,2},{4,5},{5,4},{6,7},{7,6},{8,9},{9,8},{10,11... | collective-permute-start | bytes 2162696 | tf_op jit(solution)/shard_map/ppermute | solution.py:84
  301.9 14.1 %collective-permute-start.60 = (bf16[128,2048]{1,0:T(8,128)(2,1)S(1)}, bf16[128,2048]{1,0:T(8,128)(2,1)S(1)}, u32[]{:S(2)}, u32[]{:S(2)}) collective-permute-start(bf16[128,2048]{1,0:T(8,128)(2,1)S(1)} %collective-permute-done.56.refs_4_), channel_id=1, source_target_pairs={{8,0},{16,8},{24,16},{28,24},{20,28},{12,20},{4,12},{0,4},{9,1},{1... | collective-permute-start | bytes 1572872 | tf_op jit(solution)/shard_map/ppermute | solution.py:48
  309.5 29.8 %collective-permute-start.67 = (bf16[704,512]{1,0:T(8,128)(2,1)S(1)}, bf16[704,512]{1,0:T(8,128)(2,1)S(1)}, u32[]{:S(2)}, u32[]{:S(2)}) collective-permute-start(bf16[704,512]{1,0:T(8,128)(2,1)S(1)} %fusion.24), channel_id=1, source_target_pairs={{0,2},{1,3},{2,0},{3,1},{4,6},{5,7},{6,4},{7,5},{8,10},{9,11},{10,... | collective-permute-start | bytes 2162696 | tf_op jit(solution)/shard_map/ppermute | solution.py:84
  341.4 16.0 %collective-permute-start.72 = (bf16[704,512]{1,0:T(8,128)(2,1)S(1)}, bf16[704,512]{1,0:T(8,128)(2,1)S(1)}, u32[]{:S(2)}, u32[]{:S(2)}) collective-permute-start(bf16[704,512]{1,0:T(8,128)(2,1)S(1)} %add_convert_fusion.3.refs_0_), channel_id=1, source_target_pairs={{0,1},{1,0},{2,3},{3,2},{4,5},{5,4},{6,7},{7,6},{8,9},{9,8},{10,11... | collective-permute-start | bytes 2162696 | tf_op jit(solution)/shard_map/ppermute | solution.py:84
  343.8 14.2 %collective-permute-start.73 = (bf16[704,512]{1,0:T(8,128)(2,1)S(1)}, bf16[704,512]{1,0:T(8,128)(2,1)S(1)}, u32[]{:S(2)}, u32[]{:S(2)}) collective-permute-start(bf16[704,512]{1,0:T(8,128)(2,1)S(1)} %collective-permute-done.66.refs_1_), channel_id=1, source_target_pairs={{0,1},{1,0},{2,3},{3,2},{4,5},{5,4},{6,7},{7,6},{8,9},{9,8},{10,11... | collective-permute-start | bytes 2162696 | tf_op jit(solution)/shard_map/ppermute | solution.py:84
  348.0 21.9 %collective-permute-start.78 = (bf16[512,768]{1,0:T(8,128)(2,1)S(1)}, bf16[512,768]{1,0:T(8,128)(2,1)S(1)}, u32[]{:S(2)}, u32[]{:S(2)}) collective-permute-start(bf16[512,768]{1,0:T(8,128)(2,1)S(1)} %add_convert_fusion.1), channel_id=1, source_target_pairs={{0,2},{1,3},{2,0},{3,1},{4,6},{5,7},{6,4},{7,5},{8,10},{9,11},{10,... | collective-permute-start | bytes 2359304 | tf_op jit(solution)/shard_map/ppermute | solution.py:84
  349.5 14.0 %collective-permute-start.68 = (bf16[64,4096]{1,0:T(8,128)(2,1)S(1)}, bf16[64,4096]{1,0:T(8,128)(2,1)S(1)}, u32[]{:S(2)}, u32[]{:S(2)}) collective-permute-start(bf16[64,4096]{1,0:T(8,128)(2,1)S(1)} %get-tuple-element.568), channel_id=1, source_target_pairs={{0,8},{8,16},{16,24},{24,28},{28,20},{20,12},{12,4},{4,0},{1,9},{9... | collective-permute-start | bytes 1572872 | tf_op jit(solution)/shard_map/ppermute | solution.py:45
  350.1 13.7 %collective-permute-start.69 = (bf16[64,4096]{1,0:T(8,128)(2,1)S(1)}, bf16[64,4096]{1,0:T(8,128)(2,1)S(1)}, u32[]{:S(2)}, u32[]{:S(2)}) collective-permute-start(bf16[64,4096]{1,0:T(8,128)(2,1)S(1)} %get-tuple-element.569), channel_id=1, source_target_pairs={{8,0},{16,8},{24,16},{28,24},{20,28},{12,20},{4,12},{0,4},{9,1},{1... | collective-permute-start | bytes 1572872 | tf_op jit(solution)/shard_map/ppermute | solution.py:48
  357.3 26.6 %collective-permute-start.77 = (bf16[704,512]{1,0:T(8,128)(2,1)}, bf16[704,512]{1,0:T(8,128)(2,1)}, u32[]{:S(2)}, u32[]{:S(2)}) collective-permute-start(bf16[704,512]{1,0:T(8,128)(2,1)} %add_convert_fusion.2.refs_0_), channel_id=1, source_target_pairs={{0,2},{1,3},{2,0},{3,1},{4,6},{5,7},{6,4},{7,5},{8,10},{9,11},{10,... | collective-permute-start | bytes 2162696 | tf_op jit(solution)/shard_map/ppermute | solution.py:84
  365.4 26.2 %collective-permute-start.74 = (bf16[128,4096]{1,0:T(8,128)(2,1)}, bf16[128,4096]{1,0:T(8,128)(2,1)}, u32[]{:S(2)}, u32[]{:S(2)}) collective-permute-start(bf16[128,4096]{1,0:T(8,128)(2,1)} %get-tuple-element.595), channel_id=1, source_target_pairs={{0,8},{8,16},{16,24},{24,28},{28,20},{20,12},{12,4},{4,0},{1,9},{9... | collective-permute-start | bytes 3145736 | tf_op jit(solution)/shard_map/ppermute | solution.py:45
  365.9 26.4 %collective-permute-start.75 = (bf16[128,4096]{1,0:T(8,128)(2,1)}, bf16[128,4096]{1,0:T(8,128)(2,1)}, u32[]{:S(2)}, u32[]{:S(2)}) collective-permute-start(bf16[128,4096]{1,0:T(8,128)(2,1)} %get-tuple-element.596), channel_id=1, source_target_pairs={{8,0},{16,8},{24,16},{28,24},{20,28},{12,20},{4,12},{0,4},{9,1},{1... | collective-permute-start | bytes 3145736 | tf_op jit(solution)/shard_map/ppermute | solution.py:48
  367.4 17.3 %collective-permute-start.76 = (f32[8,2048]{1,0:T(8,128)S(1)}, f32[8,2048]{1,0:T(8,128)S(1)}, u32[]{:S(2)}, u32[]{:S(2)}) collective-permute-start(f32[8,2048]{1,0:T(8,128)S(1)} %add.258), channel_id=1, source_target_pairs={{0,2},{1,3},{2,0},{3,1},{4,6},{5,7},{6,4},{7,5},{8,10},{9,11},{10,... | collective-permute-start | bytes 196616 | tf_op jit(solution)/shard_map/ppermute | solution.py:84
  371.5 38.9 %all-to-all-start = ((bf16[8,64,768]{2,1,0:T(8,128)(2,1)}), bf16[8,64,768]{2,1,0:T(8,128)(2,1)}, u32[]{:S(2)}, u32[]{:S(2)}) async-start(bf16[8,64,768]{2,1,0:T(8,128)(2,1)} %bitcast.116), calls=%async_computation | async-start | bytes 1572864 | tf_op jit(solution)/shard_map/all_to_all | solution.py:948
  386.3 16.9 %collective-permute-start.83 = (bf16[256,1024]{1,0:T(8,128)(2,1)S(1)}, bf16[256,1024]{1,0:T(8,128)(2,1)S(1)}, u32[]{:S(2)}, u32[]{:S(2)}) collective-permute-start(bf16[256,1024]{1,0:T(8,128)(2,1)S(1)} %dynamic-slice_convert_fusion), channel_id=1, source_target_pairs={{0,1},{1,0},{2,3},{3,2},{4,5},{5,4},{6,7},{7,6},{8,9},{9,8},{10,11... | collective-permute-start | bytes 1572872 | tf_op jit(solution)/shard_map/ppermute | solution.py:84
  397.1 26.1 %collective-permute-start.79 = (bf16[128,4096]{1,0:T(8,128)(2,1)}, bf16[128,4096]{1,0:T(8,128)(2,1)}, u32[]{:S(2)}, u32[]{:S(2)}) collective-permute-start(bf16[128,4096]{1,0:T(8,128)(2,1)} %get-tuple-element.611), channel_id=1, source_target_pairs={{0,8},{8,16},{16,24},{24,28},{28,20},{20,12},{12,4},{4,0},{1,9},{9... | collective-permute-start | bytes 3145736 | tf_op jit(solution)/shard_map/ppermute | solution.py:45
  399.9 25.5 %collective-permute-start.80 = (bf16[128,4096]{1,0:T(8,128)(2,1)}, bf16[128,4096]{1,0:T(8,128)(2,1)}, u32[]{:S(2)}, u32[]{:S(2)}) collective-permute-start(bf16[128,4096]{1,0:T(8,128)(2,1)} %get-tuple-element.612), channel_id=1, source_target_pairs={{8,0},{16,8},{24,16},{28,24},{20,28},{12,20},{4,12},{0,4},{9,1},{1... | collective-permute-start | bytes 3145736 | tf_op jit(solution)/shard_map/ppermute | solution.py:48
  411.7 25.7 %collective-permute-start.87 = (bf16[64,6144]{1,0:T(8,128)(2,1)S(1)}, bf16[64,6144]{1,0:T(8,128)(2,1)S(1)}, u32[]{:S(2)}, u32[]{:S(2)}) collective-permute-start(bf16[64,6144]{1,0:T(8,128)(2,1)S(1)} %beside.1.refs_0_), channel_id=1, source_target_pairs={{0,2},{1,3},{2,0},{3,1},{4,6},{5,7},{6,4},{7,5},{8,10},{9,11},{10,... | collective-permute-start | bytes 2359304 | tf_op jit(solution)/shard_map/ppermute | solution.py:84
  428.6 28.0 %collective-permute-start.85 = (bf16[128,4096]{1,0:T(8,128)(2,1)}, bf16[128,4096]{1,0:T(8,128)(2,1)}, u32[]{:S(2)}, u32[]{:S(2)}) collective-permute-start(bf16[128,4096]{1,0:T(8,128)(2,1)} %get-tuple-element.629), channel_id=1, source_target_pairs={{0,8},{8,16},{16,24},{24,28},{28,20},{20,12},{12,4},{4,0},{1,9},{9... | collective-permute-start | bytes 3145736 | tf_op jit(solution)/shard_map/ppermute | solution.py:45
  434.4 24.4 %collective-permute-start.86 = (bf16[128,4096]{1,0:T(8,128)(2,1)}, bf16[128,4096]{1,0:T(8,128)(2,1)}, u32[]{:S(2)}, u32[]{:S(2)}) collective-permute-start(bf16[128,4096]{1,0:T(8,128)(2,1)} %get-tuple-element.630), channel_id=1, source_target_pairs={{8,0},{16,8},{24,16},{28,24},{20,28},{12,20},{4,12},{0,4},{9,1},{1... | collective-permute-start | bytes 3145736 | tf_op jit(solution)/shard_map/ppermute | solution.py:48
  438.7 23.3 %collective-permute-start.90 = (f32[8,2048]{1,0:T(8,128)S(1)}, f32[8,2048]{1,0:T(8,128)S(1)}, u32[]{:S(2)}, u32[]{:S(2)}) collective-permute-start(f32[8,2048]{1,0:T(8,128)S(1)} %add.261), channel_id=1, source_target_pairs={{0,4},{4,0},{8,12},{12,8},{16,20},{20,16},{24,28},{28,24},{1,5},{5... | collective-permute-start | bytes 196616 | tf_op jit(solution)/shard_map/ppermute | solution.py:84
  440.3 21.8 %collective-permute-start.91 = (f32[8,2048]{1,0:T(8,128)S(1)}, f32[8,2048]{1,0:T(8,128)S(1)}, u32[]{:S(2)}, u32[]{:S(2)}) collective-permute-start(f32[8,2048]{1,0:T(8,128)S(1)} %add.261), channel_id=1, source_target_pairs={{0,8},{4,12},{8,0},{12,4},{16,24},{20,28},{24,16},{28,20},{1,9},{5... | collective-permute-start | bytes 196616 | tf_op jit(solution)/shard_map/ppermute | solution.py:84
  442.3 19.8 %collective-permute-start.92 = (f32[8,2048]{1,0:T(8,128)S(1)}, f32[8,2048]{1,0:T(8,128)S(1)}, u32[]{:S(2)}, u32[]{:S(2)}) collective-permute-start(f32[8,2048]{1,0:T(8,128)S(1)} %add.261), channel_id=1, source_target_pairs={{0,12},{4,8},{8,4},{12,0},{16,28},{20,24},{24,20},{28,16},{1,13},{... | collective-permute-start | bytes 196616 | tf_op jit(solution)/shard_map/ppermute | solution.py:84
  (74 other events, 1102.7 us)
